TPU v7x, 32 devices: a whole 2x2x4 slice. The times are simulated.
32 devices in a mesh: dp: 2 (over x), ctx: 16 (over z, y, core).
Axes of the slice: x: 2, y: 2, z: 4, core: 2. Of those that a mesh axis runs over, the one named last changes fastest.
Arguments:
- block_input: bfloat16 [2, 2048, 1600], P('dp', 'ctx'), may hold values from -48 to 48
- segments: int32 [2, 2048], P('dp'), may hold values from 0 to 15, never falling along the last dimension, each value on 1 to 256 neighbouring positions
- joint_weight: bfloat16 [1600, 4800], P('dp', 'ctx'), may hold values from -2 to 2
- output_weight: bfloat16 [1600, 1600], P('dp', 'ctx'), may hold values from -1.75 to 1.75
- up_weight: bfloat16 [1600, 6400], P('dp', 'ctx'), may hold values from -0.15625 to 0.15625
- down_weight: bfloat16 [6400, 1600], P('ctx', 'dp'), may hold values from -0.078125 to 0.078125
- vectors: bfloat16 [8, 1600], P('dp', 'ctx'), may hold values from -1 to 2
- up_bias: bfloat16 [6400], P('ctx'), may hold values from -3 to 3
- cotangent: bfloat16 [2, 2048, 1600], P('dp', 'ctx'), may hold values from -6 to 6
Outputs:
- block_output: bfloat16 [2, 2048, 1600], P('dp', 'ctx')
- input_gradient: float32 [2, 2048, 1600], P('dp', 'ctx')
- joint_gradient: float32 [1600, 4800], P('dp', 'ctx')
- output_gradient: float32 [1600, 1600], P('dp', 'ctx')
- up_gradient: float32 [1600, 6400], P('dp', 'ctx')
- down_gradient: float32 [6400, 1600], P('ctx', 'dp')
- vectors_gradient: float32 [8, 1600], P('dp', 'ctx')
- bias_gradient: float32 [6400], P('ctx')
Inputs may be any that keep to these rules, and one draw needn't show every extreme that they name: `segments`: the numbers of each sequence never fall; each document holds at most 256 tokens, and the longest holds exactly that many.
All inputs are finite; a program needn't handle non-finite values.
Results may differ from a plain program's by a relative error of at most 0.0085.
The roundings to bfloat16 on the way count: a program that leaves them out, or rounds other values in their place, can miss the bound.
Values may be sent and summed in bfloat16 or wider, within the bound.
No kernel may reach another device: no remote copies, remote signals or barrier semaphores. Data moves between devices by JAX's collectives and lax.ppermute only.
A program may use at most 448 MiB of HBM per device.

v0:
```python
import jax
import jax.numpy as jnp
from jax import lax
from jax.sharding import PartitionSpec as P

H = 25
REACH = 2


norm_epsilon = 1e-05
gelu_scale = 0.7978845608028654
masked_score = -1e30


def shifted(value, axis, by):
    count = lax.axis_size(axis)
    pairs = [(i, i + by) for i in range(count) if 0 <= i + by < count]
    return lax.ppermute(value, axis, pairs)


def layer_norm(values, norm_gain, norm_shift):
    center = jnp.mean(values, axis=-1, keepdims=True)
    deviation = values - center
    variance = jnp.mean(deviation * deviation, axis=-1, keepdims=True)
    return deviation * lax.rsqrt(variance + norm_epsilon) * norm_gain + norm_shift


def gelu_curve(values):
    return (
        0.5 * values * (1.0 + jnp.tanh(gelu_scale * (values + 0.044715 * values * values * values)))
    )


def contract_rows(left_side, right_side):
    return lax.dot_general(
        left_side, right_side, (((0,), (0,)), ((), ())), preferred_element_type=jnp.float32
    )


def contract_columns(left_side, right_side):
    return lax.dot_general(
        left_side, right_side, (((1,), (1,)), ((), ())), preferred_element_type=jnp.float32
    )


def split_heads(matrix):
    return matrix.reshape(matrix.shape[0], H, -1).transpose(1, 0, 2)


def merge_heads(stacked):
    return stacked.transpose(1, 0, 2).reshape(stacked.shape[1], -1)


def collect(joint_weight, output_weight, up_weight, down_weight, vectors, bias_rows):
    first_section = (
        lax.all_gather(joint_weight, "ctx", axis=1, tiled=True),
        lax.all_gather(output_weight, "ctx", axis=1, tiled=True),
        lax.all_gather(up_weight, "ctx", axis=1, tiled=True),
        lax.all_gather(down_weight, "ctx", axis=0, tiled=True),
        lax.all_gather(vectors, "ctx", axis=1, tiled=True),
        lax.all_gather(bias_rows, "ctx", axis=1, tiled=True),
    )
    second_section = (
        lax.all_gather(first_section[0], "dp", axis=0, tiled=True),
        lax.all_gather(first_section[1], "dp", axis=0, tiled=True),
        lax.all_gather(first_section[2], "dp", axis=0, tiled=True),
        lax.all_gather(first_section[3], "dp", axis=1, tiled=True),
        lax.all_gather(first_section[4], "dp", axis=0, tiled=True),
    )
    bias_full = first_section[5]
    return (
        second_section[0],
        second_section[1],
        second_section[2],
        second_section[3],
        second_section[4],
        bias_full,
    )


def attend_forward(queries, window_rows, allowed, scale_factor):
    features = queries.shape[1]
    operands_all = (
        split_heads(queries),
        split_heads(window_rows[:, :features]),
        split_heads(window_rows[:, features:]),
    )

    def one_head(operands):
        query_head, key_head, value_head = operands
        scores = jnp.where(
            allowed, contract_columns(query_head, key_head) * scale_factor, masked_score
        )
        row_max = jnp.max(scores, axis=1, keepdims=True)
        row_total = jnp.sum(
            jnp.where(allowed, jnp.exp(scores - row_max), 0.0), axis=1, keepdims=True
        )
        log_total = row_max + jnp.log(row_total)
        weights_low = jnp.where(allowed, jnp.exp(scores - log_total), 0.0).astype(jnp.bfloat16)
        mixed_head = jnp.dot(weights_low, value_head, preferred_element_type=jnp.float32).astype(
            jnp.bfloat16
        )
        return (mixed_head, log_total[:, 0])

    mixed_heads, log_totals = lax.map(one_head, operands_all)
    return (merge_heads(mixed_heads), log_totals)


def attend_backward(
    queries, window_rows, allowed, log_totals, attended, attended_back, scale_factor
):
    features = queries.shape[1]
    operands_all = (
        split_heads(queries),
        split_heads(window_rows[:, :features]),
        split_heads(window_rows[:, features:]),
        log_totals,
        split_heads(attended),
        split_heads(attended_back),
    )

    def one_head(operands):
        query_head, key_head, value_head, log_head, mixed_head, mixed_back = operands
        scores = contract_columns(query_head, key_head) * scale_factor
        weights = jnp.where(allowed, jnp.exp(scores - log_head[:, None]), 0.0)
        row_delta = jnp.sum(
            mixed_back.astype(jnp.float32) * mixed_head.astype(jnp.float32), axis=1, keepdims=True
        )
        weight_back = contract_columns(mixed_back, value_head)
        score_back = (weights * (weight_back - row_delta)).astype(jnp.bfloat16)
        query_back = (
            jnp.dot(score_back, key_head, preferred_element_type=jnp.float32) * scale_factor
        )
        key_back = contract_rows(score_back, query_head) * scale_factor
        value_back = contract_rows(weights.astype(jnp.bfloat16), mixed_back)
        return (query_back, key_back, value_back)

    query_backs, key_backs, value_backs = lax.map(one_head, operands_all)
    return (
        merge_heads(query_backs),
        jnp.concatenate([merge_heads(key_backs), merge_heads(value_backs)], axis=1),
    )


def shards(
    block_input,
    segments,
    joint_weight,
    output_weight,
    up_weight,
    down_weight,
    vectors,
    up_bias,
    cotangent,
):
    block_rows = block_input.shape[1]
    features = block_input.shape[2]
    reach_rows = REACH * block_rows
    window = reach_rows + block_rows
    scale_factor = (features // H) ** (-0.5)
    position = lax.axis_index("ctx")
    data_size = lax.axis_size("dp")
    context_size = lax.axis_size("ctx")
    gathered = collect(
        joint_weight, output_weight, up_weight, down_weight, vectors, up_bias.reshape(1, -1)
    )
    joint_full, output_full, up_full, down_full = (
        gathered[0],
        gathered[1],
        gathered[2],
        gathered[3],
    )
    params = gathered[4].astype(jnp.float32)
    up_shift = gathered[5].reshape(-1).astype(jnp.float32)
    padded_numbers = jnp.concatenate([jnp.full((reach_rows,), -1, jnp.int32), segments[0]])
    first_key = position * block_rows
    key_numbers = lax.dynamic_slice_in_dim(padded_numbers, first_key, window)
    key_places = first_key - reach_rows + jnp.arange(window, dtype=jnp.int32)
    same_document = key_numbers[None, :] == key_numbers[reach_rows:, None]
    allowed = same_document & (key_places[None, :] <= key_places[reach_rows:, None])
    rows_float = block_input[0].astype(jnp.float32)
    normed_one = layer_norm(rows_float, params[0], params[1]).astype(jnp.bfloat16)
    joint_bias = jnp.concatenate([params[2], jnp.zeros((features,), jnp.float32), params[3]])
    projected = (
        jnp.dot(normed_one, joint_full, preferred_element_type=jnp.float32) + joint_bias
    ).astype(jnp.bfloat16)
    queries = projected[:, :features]
    pairs = projected[:, features:]
    received = [shifted(pairs, "ctx", distance) for distance in range(1, REACH + 1)]
    window_rows = jnp.concatenate(received[::-1] + [pairs], axis=0)
    attended, log_totals = attend_forward(queries, window_rows, allowed, scale_factor)
    residual = (
        rows_float + jnp.dot(attended, output_full, preferred_element_type=jnp.float32) + params[4]
    )
    normed_two = layer_norm(residual, params[5], params[6]).astype(jnp.bfloat16)
    up_values = jnp.dot(normed_two, up_full, preferred_element_type=jnp.float32) + up_shift
    hidden = gelu_curve(up_values).astype(jnp.bfloat16)
    block_output = (
        residual + jnp.dot(hidden, down_full, preferred_element_type=jnp.float32) + params[7]
    ).astype(jnp.bfloat16)
    held_shards = lax.optimization_barrier(
        (joint_weight, output_weight, up_weight, down_weight, vectors, up_bias, block_output)
    )
    gathered_back = collect(
        held_shards[0],
        held_shards[1],
        held_shards[2],
        held_shards[3],
        held_shards[4],
        held_shards[5].reshape(1, -1),
    )
    joint_back, output_back, up_back_full, down_back = (
        gathered_back[0],
        gathered_back[1],
        gathered_back[2],
        gathered_back[3],
    )
    cotangent_rows = cotangent[0]
    cotangent_float = cotangent_rows.astype(jnp.float32)
    hidden_back = contract_columns(cotangent_rows, down_back)
    _, gelu_pull = jax.vjp(gelu_curve, up_values)
    up_back = gelu_pull(hidden_back)[0].astype(jnp.bfloat16)
    normed_two_back = contract_columns(up_back, up_back_full)
    _, norm_pull = jax.vjp(layer_norm, residual, params[5], params[6])
    residual_part, gain_two_back, shift_two_back = norm_pull(normed_two_back)
    residual_back = cotangent_float + residual_part
    residual_low = residual_back.astype(jnp.bfloat16)
    attended_back = contract_columns(residual_low, output_back).astype(jnp.bfloat16)
    query_back, key_terms = attend_backward(
        queries, window_rows, allowed, log_totals, attended, attended_back, scale_factor
    )

    def term_block(distance):
        first_row = (REACH - distance) * block_rows
        return key_terms[first_row : first_row + block_rows]

    key_total = term_block(0)
    for distance in range(1, REACH + 1):
        key_total = key_total + shifted(
            term_block(distance).astype(jnp.bfloat16), "ctx", -distance
        ).astype(jnp.float32)
    value_back = key_total[:, features:]
    projected_back = jnp.concatenate([query_back, key_total], axis=1).astype(jnp.bfloat16)
    normed_one_back = contract_columns(projected_back, joint_back)
    _, first_pull = jax.vjp(layer_norm, rows_float, params[0], params[1])
    rows_part, gain_one_back, shift_one_back = first_pull(normed_one_back)
    input_gradient = residual_back + rows_part
    vectors_gradient = jnp.stack(
        [
            gain_one_back,
            shift_one_back,
            jnp.sum(query_back, axis=0),
            jnp.sum(value_back, axis=0),
            jnp.sum(residual_back, axis=0),
            gain_two_back,
            shift_two_back,
            jnp.sum(cotangent_float, axis=0),
        ]
    )
    half = features // data_size
    joint_cols = 3 * features // context_size
    output_cols = features // context_size
    unit_cols = up_back.shape[1] // context_size

    def by_halves(matrix):
        return matrix.reshape(block_rows, data_size, -1).transpose(1, 0, 2)

    def by_slices(matrix):
        return matrix.reshape(block_rows, context_size, -1).transpose(1, 0, 2)

    row_pack = jnp.concatenate(
        [
            by_halves(normed_one),
            by_halves(attended),
            by_halves(normed_two),
            by_halves(cotangent_rows),
        ],
        axis=2,
    )
    column_pack = jnp.concatenate(
        [by_slices(projected_back), by_slices(residual_low), by_slices(up_back), by_slices(hidden)],
        axis=2,
    )
    row_shares = lax.all_to_all(row_pack, "dp", split_axis=0, concat_axis=0, tiled=True)
    column_local = lax.all_to_all(column_pack, "ctx", split_axis=0, concat_axis=0, tiled=True)
    column_width = column_pack.shape[2]
    column_all = lax.all_gather(column_local, "dp", axis=0, tiled=True).reshape(
        data_size, -1, column_width
    )
    up_start = joint_cols + output_cols
    hidden_start = up_start + unit_cols
    bias_gradient = jnp.sum(
        column_all[:, :, up_start:hidden_start].astype(jnp.float32), axis=(0, 1)
    )
    piece = lax.all_gather(row_shares, "ctx", axis=1, tiled=True)
    left_rows = piece.reshape(-1, piece.shape[2])
    right_rows = column_all.reshape(-1, column_width)
    joint_tile = contract_rows(left_rows[:, 0:half], right_rows[:, 0:joint_cols])
    output_tile = contract_rows(left_rows[:, half : 2 * half], right_rows[:, joint_cols:up_start])
    up_tile = contract_rows(left_rows[:, 2 * half : 3 * half], right_rows[:, up_start:hidden_start])
    down_tile = contract_rows(right_rows[:, hidden_start:], left_rows[:, 3 * half :])
    vector_spread = lax.psum_scatter(vectors_gradient, "ctx", scatter_dimension=1, tiled=True)
    vector_owned = lax.psum_scatter(vector_spread, "dp", scatter_dimension=0, tiled=True)
    return (
        block_output[None],
        input_gradient[None],
        joint_tile,
        output_tile,
        up_tile,
        down_tile,
        vector_owned,
        bias_gradient,
    )


def solution(mesh):
    in_specs = (
        P("dp", "ctx", None),
        P("dp", None),
        P("dp", "ctx"),
        P("dp", "ctx"),
        P("dp", "ctx"),
        P("ctx", "dp"),
        P("dp", "ctx"),
        P("ctx"),
        P("dp", "ctx", None),
    )
    out_specs = (
        P("dp", "ctx", None),
        P("dp", "ctx", None),
        P("dp", "ctx"),
        P("dp", "ctx"),
        P("dp", "ctx"),
        P("ctx", "dp"),
        P("dp", "ctx"),
        P("ctx"),
    )
    return jax.shard_map(shards, mesh=mesh, in_specs=in_specs, out_specs=out_specs, check_vma=False)
```

profile of v0, /device:TPU:0, one launch (start us, length us, event | category | flops | bytes accessed | tf_op | source)
XLA Modules:
  0.0 2645.1 jit_solution(9609876019320877117)
XLA Ops:
  9.4 80.4 %all-gather.54.cloned.1.call-done = bf16[16,300,800]{2,1,0:T(8,128)(2,1)} async-done(((bf16[1,300,800]{2,1,0:T(8,128)(2,1)}), bf16[16,300,800]{2,1,0:T(8,128)(2,1)}) %all-gather.54.cloned.1.call-update) | async-done | bytes 7680016 | tf_op jit(solution)/shard_map/all_gather | solution.py:56
  89.9 10.5 reshape.235
  100.4 12.0 copy.71
  113.0 22.2 all-gather.56.cloned.1.call-done
  141.9 87.7 %all-gather.30.cloned.1.call-done = bf16[800,6400]{0,1:T(8,128)(2,1)} async-done(((bf16[800,400]{0,1:T(8,128)(2,1)}), bf16[800,6400]{0,1:T(8,128)(2,1)}) %all-gather.30.cloned.1.call-update) | async-done | bytes 10240016 | tf_op jit(solution)/shard_map/all_gather | solution.py:58
  229.6 16.1 copy.76
  246.4 18.2 all-gather.1
  270.1 144.6 %all-gather.26.cloned.1.call-done = bf16[1600,4800]{1,0:T(8,128)(2,1)} async-done(((bf16[800,4800]{1,0:T(8,128)(2,1)}), bf16[1600,4800]{1,0:T(8,128)(2,1)}) %all-gather.26.cloned.1.call-update) | async-done | bytes 15360016 | tf_op jit(solution)/shard_map/all_gather | solution.py:64
  414.7 12.2 fusion.62
  434.8 96.7 %all-reduce.1 = bf16[6400]{0:T(1024)(128)(2,1)S(1)} all-reduce(bf16[6400]{0:T(1024)(128)(2,1)S(1)} %dynamic-update-slice), channel_id=2, replica_groups=mesh['dp'=2,'ctx'=16] {'ctx'}, use_global_device_ids=true, to_apply=%add.1 | all-reduce | flops 6400 | bytes 25600
  531.5 15.7 copy.77
  558.2 66.7 %while.28 = (s32[]{:T(128)}, bf16[25,128,64]{1,2,0:T(8,128)(2,1)S(1)}, f32[25,128]{1,0:T(8,128)S(1)}, bf16[25,128,64]{2,1,0:T(8,128)(2,1)}, bf16[25,384,64]{2,1,...) while((s32[]{:T(128)}, ...), condition=%wide.region_5.6_spmd.clone, body=%wide.region_2.5_spmd.clone.sunk | while | flops 13475714 | bytes 855681 | solution.py:105
  631.1 212.1 %all-gather.32.cloned.1.call-done = bf16[1600,6400]{1,0:T(8,128)(2,1)} async-done(((bf16[800,6400]{1,0:T(8,128)(2,1)}), bf16[1600,6400]{1,0:T(8,128)(2,1)}) %all-gather.32.cloned.1.call-update) | async-done | bytes 20480016 | tf_op jit(solution)/shard_map/all_gather | solution.py:66
  843.1 13.4 multiply_convert_fusion
  856.5 230.2 %all-gather.36.cloned.1.call-done = bf16[6400,1600]{0,1:T(8,128)(2,1)} async-done(((bf16[6400,800]{0,1:T(8,128)(2,1)}), bf16[6400,1600]{0,1:T(8,128)(2,1)}) %all-gather.36.cloned.1.call-update) | async-done | bytes 20480016 | tf_op jit(solution)/shard_map/all_gather | solution.py:67
  1086.7 10.7 fusion.75
  1099.3 12.5 all-gather.40.cloned.1.call-start
  1111.8 79.7 %all-gather.38.cloned.1.call-done = bf16[6400,800]{1,0:T(8,128)(2,1)} async-done(((bf16[400,800]{1,0:T(8,128)(2,1)}), bf16[6400,800]{1,0:T(8,128)(2,1)}) %all-gather.38.cloned.1.call-update) | async-done | bytes 10240016 | tf_op jit(solution)/shard_map/all_gather | solution.py:59
  1191.5 15.4 copy.78
  1207.0 78.7 %all-gather.42.cloned.1.call-done = bf16[800,6400]{0,1:T(8,128)(2,1)} async-done(((bf16[800,400]{0,1:T(8,128)(2,1)}), bf16[800,6400]{0,1:T(8,128)(2,1)}) %all-gather.42.cloned.1.call-update) | async-done | bytes 10240016 | tf_op jit(solution)/shard_map/all_gather | solution.py:58
  1285.7 15.3 copy.80
  1301.1 29.9 %all-gather.58.cloned.1.call-done = bf16[16,100,800]{2,1,0:T(8,128)(2,1)} async-done(((bf16[1,100,800]{2,1,0:T(8,128)(2,1)}), bf16[16,100,800]{2,1,0:T(8,128)(2,1)}) %all-gather.58.cloned.1.call-update) | async-done | bytes 2560016 | tf_op jit(solution)/shard_map/all_gather | solution.py:57
  1340.8 67.5 %all-gather.60.cloned.1.call-done = bf16[16,300,800]{2,1,0:T(8,128)(2,1)} async-done(((bf16[1,300,800]{2,1,0:T(8,128)(2,1)}), bf16[16,300,800]{2,1,0:T(8,128)(2,1)}) %all-gather.60.cloned.1.call-update) | async-done | bytes 7680016 | tf_op jit(solution)/shard_map/all_gather | solution.py:56
  1408.3 11.0 reshape.241
  1419.2 13.2 copy.84
  1440.6 38.6 %all-to-all-done = bf16[2,128,3200]{1,2,0:T(8,128)(2,1)} async-done(((bf16[2,128,3200]{1,2,0:T(8,128)(2,1)}), bf16[2,128,3200]{1,2,0:T(8,128)(2,1)}, u32[]{:S(2)}, u32[]{:S(2)}) %all-to-all-start) | async-done | bytes 1638432 | tf_op jit(solution)/shard_map/all_to_all | solution.py:284
  1479.2 188.3 %all-gather.40.cloned.1.call-done = bf16[6400,1600]{0,1:T(8,128)(2,1)} async-done(((bf16[6400,800]{0,1:T(8,128)(2,1)}), bf16[6400,1600]{0,1:T(8,128)(2,1)}) %all-gather.40.cloned.1.call-update) | async-done | bytes 20480016 | tf_op jit(solution)/shard_map/all_gather | solution.py:67
  1667.6 11.9 fusion.67
  1679.5 231.5 %all-gather.44.cloned.1.call-done = bf16[1600,6400]{1,0:T(8,128)(2,1)} async-done(((bf16[800,6400]{1,0:T(8,128)(2,1)}), bf16[1600,6400]{1,0:T(8,128)(2,1)}) %all-gather.44.cloned.1.call-update) | async-done | bytes 20480016 | tf_op jit(solution)/shard_map/all_gather | solution.py:66
  1911.0 11.9 multiply_reduce_fusion
  1924.2 57.7 %all-gather.46.cloned.1.call-done = bf16[1600,1600]{1,0:T(8,128)(2,1)} async-done(((bf16[800,1600]{1,0:T(8,128)(2,1)}), bf16[1600,1600]{1,0:T(8,128)(2,1)}) %all-gather.46.cloned.1.call-update) | async-done | bytes 5120016 | tf_op jit(solution)/shard_map/all_gather | solution.py:65
  1989.0 222.4 %while.29 = (s32[]{:T(128)}, f32[25,128,64]{1,2,0:T(8,128)}, f32[25,384,64]{1,2,0:T(8,128)}, f32[25,384,64]{1,2,0:T(8,128)}, bf16[25,128,64]{2,1,0:T(8,128)(2,1)...) while((s32[]{:T(128)}, f32[25,128,64]{1,2,0:T(8,128)}, ...), condition=%wide.region_12.13_spmd.clone, body=%wide.region_10.12_spmd.clone.sunk | while | flops 32014208 | bytes 1650337 | solution.py:138
  2224.7 30.8 %collective-permute-done.3 = bf16[128,3200]{0,1:T(8,128)(2,1)} collective-permute-done((bf16[128,3200]{0,1:T(8,128)(2,1)}, bf16[128,3200]{0,1:T(8,128)(2,1)}, u32[]{:S(2)}, u32[]{:S(2)}) %collective-permute-start.3) | collective-permute-done | bytes 819232 | tf_op jit(solution)/shard_map/ppermute | solution.py:18
  2261.2 28.2 %concatenate.27 = bf16[16,128,1200]{1,2,0:T(8,128)(2,1)} concatenate(bf16[16,128,300]{1,2,0:T(8,128)(2,1)} %bitcast.248, bf16[16,128,100]{1,2,0:T(8,128)(2,1)} %bitcast.261, bf16[16,128,400]{1,2,0:T(8,128)(2,1)} %bitcast.247, bf16[16,128,400]{1,2,0:T(8,128)(2,1)} %bitcast.246), dimensions={2} | concatenate | bytes 9830400 | tf_op jit(solution)/shard_map/concatenate | solution.py:280
  2289.4 148.6 %all_to_all.10 = bf16[16,128,1200]{1,2,0:T(8,128)(2,1)} all-to-all(bf16[16,128,1200]{1,2,0:T(8,128)(2,1)} %concatenate.27), channel_id=1, replica_groups=mesh['dp'=2,'ctx'=16] {'ctx'}, dimensions={0} | all-to-all | bytes 9830400 | tf_op jit(solution)/shard_map/all_to_all | solution.py:285
  2441.0 9.4 fusion.91
  2452.9 61.2 %all-reduce.2 = f32[8,1600]{1,0:T(8,128)S(1)} all-reduce(f32[8,1600]{1,0:T(8,128)S(1)} %stack.23), channel_id=3, replica_groups=mesh['dp'=2,'ctx'=16] {'ctx'}, use_global_device_ids=true, to_apply=%region_23.24.clone | all-reduce | flops 12800 | bytes 102400
  2514.2 6.0 all-reduce.3
  2520.8 32.2 %copy.85 = bf16[2,2048,3200]{2,1,0:T(8,128)(2,1)} copy(bf16[2,2048,3200]{1,2,0:T(8,128)(2,1)} %all-gather.50.cloned.1.call-done) | data formatting | bytes 52428800 | tf_op jit(solution)/shard_map/all_gather | solution.py:295
  2553.0 9.4 all-gather.52.cloned.1.call-done
  2562.4 9.0 copy_bitcast_fusion
  2571.4 7.7 fusion.60
  2579.1 6.9 fusion.58
  2586.0 7.5 fusion.56
  2593.4 7.3 fusion.54
  2600.7 12.0 copy.88
  2612.8 19.5 reshape.220
  2632.3 5.5 convert_reduce_fusion
  (503 shorter events, 380.1 us)
Async XLA Ops:
  7.2 82.7 %all-gather.54.cloned.1.call-start = ((), (), s32[]{:S(2)}) async-start(), calls=%async_computation.16 | async-start | bytes 9261056 | tf_op jit(solution)/shard_map/all_gather | solution.py:56
  7.9 127.2 %all-gather.56.cloned.1.call-start = ((), (), s32[]{:S(2)}) async-start(), calls=%async_computation.17 | async-start | bytes 3168256 | tf_op jit(solution)/shard_map/all_gather | solution.py:57
  8.6 221.0 %all-gather.30.cloned.1.call-start = ((), (), s32[]{:S(2)}) async-start(), calls=%async_computation.4 | async-start | bytes 12185600 | tf_op jit(solution)/shard_map/all_gather | solution.py:58
  9.4 405.4 %all-gather.26.cloned.1.call-start = ((), (), s32[]{:S(2)}) async-start(), calls=%async_computation.2 | async-start | bytes 23347200 | tf_op jit(solution)/shard_map/all_gather | solution.py:64
  112.3 419.2 %all-gather.34.cloned.1.call-start = ((), (), s32[]{:S(2)}) async-start(), calls=%async_computation.6 | async-start | bytes 12185600 | tf_op jit(solution)/shard_map/all_gather | solution.py:59
  112.9 512.0 %all-gather.28.cloned.1.call-start = ((), (), s32[]{:S(2)}) async-start(), calls=%async_computation.3 | async-start | bytes 7987200 | tf_op jit(solution)/shard_map/all_gather | solution.py:65
  141.9 701.3 %all-gather.32.cloned.1.call-start = ((), (), s32[]{:S(2)}) async-start(), calls=%async_computation.5 | async-start | bytes 30720000 | tf_op jit(solution)/shard_map/all_gather | solution.py:66
  245.7 0.7 copy-start.9
  245.7 23.9 copy-start
  245.7 840.9 %all-gather.36.cloned.1.call-start = ((), (), s32[]{:S(2)}) async-start(), calls=%async_computation.7 | async-start | bytes 30720000 | tf_op jit(solution)/shard_map/all_gather | solution.py:67
  414.7 18.5 copy-start.7
  414.7 18.6 copy-start.8
  414.7 19.8 copy-start.10
  427.0 121.8 %collective-permute-start.1 = (bf16[128,3200]{0,1:T(8,128)(2,1)S(1)}, bf16[128,3200]{0,1:T(8,128)(2,1)}, u32[]{:S(2)}, u32[]{:S(2)}) collective-permute-start(bf16[128,3200]{0,1:T(8,128)(2,1)S(1)} %slice.119), channel_id=1, source_target_pairs={{0,1},{1,2},{2,3},{3,4},{4,5},{5,6},{6,7},{7,8},{8,9},{9,10},{10,1... | collective-permute-start | bytes 2457608 | tf_op jit(solution)/shard_map/ppermute | solution.py:18
  429.7 119.1 %collective-permute-start = (bf16[128,3200]{0,1:T(8,128)(2,1)S(1)}, bf16[128,3200]{0,1:T(8,128)(2,1)}, u32[]{:S(2)}, u32[]{:S(2)}) collective-permute-start(bf16[128,3200]{0,1:T(8,128)(2,1)S(1)} %slice.119), channel_id=1, source_target_pairs={{0,2},{1,3},{2,4},{3,5},{4,6},{5,7},{6,8},{7,9},{8,10},{9,11},{10,... | collective-permute-start | bytes 2457608 | tf_op jit(solution)/shard_map/ppermute | solution.py:18
  547.3 644.2 %all-gather.38.cloned.1.call-start = ((), (), s32[]{:S(2)}) async-start(), calls=%async_computation.8 | async-start | bytes 12185600 | tf_op jit(solution)/shard_map/all_gather | solution.py:59
  624.9 5.4 copy-start.6
  1097.4 188.2 %all-gather.42.cloned.1.call-start = ((), (), s32[]{:S(2)}) async-start(), calls=%async_computation.10 | async-start | bytes 12185600 | tf_op jit(solution)/shard_map/all_gather | solution.py:58
  1098.0 232.9 %all-gather.58.cloned.1.call-start = ((), (), s32[]{:S(2)}) async-start(), calls=%async_computation.18 | async-start | bytes 3168256 | tf_op jit(solution)/shard_map/all_gather | solution.py:57
  1098.7 309.5 %all-gather.60.cloned.1.call-start = ((), (), s32[]{:S(2)}) async-start(), calls=%async_computation.19 | async-start | bytes 9261056 | tf_op jit(solution)/shard_map/all_gather | solution.py:56
  1099.3 568.3 %all-gather.40.cloned.1.call-start = ((), (), s32[]{:S(2)}) async-start(), calls=%async_computation.9 | async-start | bytes 30720000 | tf_op jit(solution)/shard_map/all_gather | solution.py:67
  1206.9 704.1 %all-gather.44.cloned.1.call-start = ((), (), s32[]{:S(2)}) async-start(), calls=%async_computation.11 | async-start | bytes 30720000 | tf_op jit(solution)/shard_map/all_gather | solution.py:66
  1301.0 680.9 %all-gather.46.cloned.1.call-start = ((), (), s32[]{:S(2)}) async-start(), calls=%async_computation.12 | async-start | bytes 7987200 | tf_op jit(solution)/shard_map/all_gather | solution.py:65
  1340.8 1100.2 %all-gather.48.cloned.1.call-start = ((), (), s32[]{:S(2)}) async-start(), calls=%async_computation.13 | async-start | bytes 23347200 | tf_op jit(solution)/shard_map/all_gather | solution.py:64
  1435.6 232.0 %copy-start.4 = (bf16[1,128,1600]{1,2,0:T(8,128)(2,1)S(1)}, bf16[1,128,1600]{1,2,0:T(8,128)(2,1)}, u32[]{:S(2)}) copy-start(bf16[1,128,1600]{1,2,0:T(8,128)(2,1)} %param.21) | copy-start | bytes 1228804
  1435.6 43.5 %all-to-all-start = ((bf16[2,128,3200]{1,2,0:T(8,128)(2,1)}), bf16[2,128,3200]{1,2,0:T(8,128)(2,1)}, u32[]{:S(2)}, u32[]{:S(2)}) async-start(bf16[2,128,3200]{1,2,0:T(8,128)(2,1)} %pad_maximum_fusion.2), calls=%async_computation | async-start | bytes 3276800 | tf_op jit(solution)/shard_map/all_to_all | solution.py:284
  1440.5 1080.3 %all-gather.50.cloned.1.call-start = ((), (), s32[]{:S(2)}) async-start(), calls=%async_computation.14 | async-start | bytes 27852800 | tf_op jit(solution)/shard_map/all_gather | solution.py:295
  1479.2 1083.2 %all-gather.52.cloned.1.call-start = ((), (), s32[]{:S(2)}) async-start(), calls=%async_computation.15 | async-start | bytes 14745600 | tf_op jit(solution)/shard_map/all_gather | solution.py:287
  1923.2 0.9 copy-start.2
  2215.3 40.3 %collective-permute-start.3 = (bf16[128,3200]{0,1:T(8,128)(2,1)}, bf16[128,3200]{0,1:T(8,128)(2,1)}, u32[]{:S(2)}, u32[]{:S(2)}) collective-permute-start(bf16[128,3200]{0,1:T(8,128)(2,1)} %get-tuple-element.318), channel_id=1, source_target_pairs={{2,0},{3,1},{4,2},{5,3},{6,4},{7,5},{8,6},{9,7},{10,8},{11,9},{12,... | collective-permute-start | bytes 2457608 | tf_op jit(solution)/shard_map/ppermute | solution.py:18
  2216.6 39.0 %collective-permute-start.2 = (bf16[128,3200]{0,1:T(8,128)(2,1)}, bf16[128,3200]{0,1:T(8,128)(2,1)}, u32[]{:S(2)}, u32[]{:S(2)}) collective-permute-start(bf16[128,3200]{0,1:T(8,128)(2,1)} %get-tuple-element.317), channel_id=1, source_target_pairs={{1,0},{2,1},{3,2},{4,3},{5,4},{6,5},{7,6},{8,7},{9,8},{10,9},{11,1... | collective-permute-start | bytes 2457608 | tf_op jit(solution)/shard_map/ppermute | solution.py:18
  2224.7 33.1 %copy-start.5 = (f32[25,128,64]{1,2,0:T(8,128)S(1)}, f32[25,128,64]{1,2,0:T(8,128)}, u32[]{:S(2)}) copy-start(f32[25,128,64]{1,2,0:T(8,128)} %get-tuple-element.114) | copy-start | bytes 2457604
  2438.0 0.7 copy-start.11
  2440.9 10.4 copy-start.3
  2571.4 7.7 copy-start.1
  2586.0 14.7 slice-start
  2586.0 14.7 slice-start.1
  2593.4 7.3 slice-start.2
Sparse Core Ops, SparseCore 0:
  10.2 79.6 all-gather.53
  92.0 43.0 all-gather.55
  137.3 92.2 all-gather.29
  231.0 183.6 all-gather.25
  416.8 113.4 all-gather.33
  531.6 67.8 all-gather.27
  601.1 242.0 all-gather.31
  844.7 241.9 all-gather.35
  1097.5 93.9 all-gather.37
  1193.5 92.0 all-gather.41
  1287.8 43.0 all-gather.57
  1333.0 75.2 all-gather.59
  1409.8 257.7 all-gather.39
  1669.0 241.9 all-gather.43
  1912.4 69.4 all-gather.45
  1983.3 185.2 all-gather.47
  2170.0 193.3 all-gather.49
  2438.2 124.2 all-gather.51
where the time goes:
time: 2670 us; the launch traced here: 2650 us
  waiting for transfers between devices  1590 us (60%)
  matrix products  348 us (13%)
  blocking collectives  335 us (13%)
  local copies, waits for them, and re-layouts  275 us (10%)
  other arithmetic  48 us (2%)
  starting transfers between devices  27.1 us (1%)
    all_gather x2, waiting for transfers between devices, collect(): lax.all_gather(first_section[2], 'dp', axis=0, tiled=True)  444 us
    all_gather x2, waiting for transfers between devices, collect(): lax.all_gather(first_section[3], 'dp', axis=1, tiled=True)  418 us
    all_gather x2, waiting for transfers between devices, collect(): lax.all_gather(up_weight, 'ctx', axis=1, tiled=True)  166 us
    unnamed x3, blocking collectives  164 us
    all_to_all x1, blocking collectives, shards(): lax.all_to_all(column_pack, 'ctx', split_axis=0, concat_axis=0, tiled=True)  149 us
    all_gather x2, waiting for transfers between devices, collect(): lax.all_gather(joint_weight, 'ctx', axis=1, tiled=True)  148 us
    all_gather x2, waiting for transfers between devices, collect(): lax.all_gather(first_section[0], 'dp', axis=0, tiled=True)  145 us
    dot_general x79, matrix products, contract_columns(): lax.dot_general(left_side, right_side, (((1,), (1,)), ((), ())), preferre...  124 us
  transfers between devices with their start and end apart: 23, of which 16 were waited for; matrix products, arithmetic and copies ran while one was open for 22% of the time, Pallas kernels for 0%

commit v1 on v0

v1 whole, which is shorter than its diff:
```python
import functools

import jax
import jax.numpy as jnp
from jax import lax
from jax.experimental import pallas as pl
from jax.experimental.pallas import tpu as pltpu
from jax.sharding import PartitionSpec as P

H = 25
REACH = 2
LANES = 128

norm_epsilon = 1e-05
gelu_scale = 0.7978845608028654
masked_score = -1e30
bf16 = jnp.bfloat16
f32 = jnp.float32
vmem_bytes = 48 * 1024 * 1024


def chip_at(place, chips):
    place %= chips
    return 2 * place if place < chips // 2 else 2 * (chips - 1 - place) + 1


def place_of(chip, chips):
    return chip // 2 if chip % 2 == 0 else chips - 1 - chip // 2


def send(value, by):
    chips = lax.axis_size("ctx") // 2
    pairs = [
        (chip_at(p, chips) * 2 + core, chip_at(p + by, chips) * 2 + core)
        for p in range(chips)
        for core in range(2)
    ]
    return lax.ppermute(value, "ctx", pairs)


def core_swap(value):
    return lax.ppermute(value, "ctx", [(i, i ^ 1) for i in range(lax.axis_size("ctx"))])


def data_swap(value):
    return lax.ppermute(value, "dp", [(i, i ^ 1) for i in range(lax.axis_size("dp"))])


def shifted(value, by):
    count = lax.axis_size("ctx")
    return lax.ppermute(
        value, "ctx", [(i, i + by) for i in range(count) if 0 <= i + by < count]
    )


def ring_gather(block):
    chips = lax.axis_size("ctx") // 2
    blocks = [None] * chips
    blocks[0] = block
    left = right = block
    for step in range(1, chips // 2):
        left, right = send(left, 1), send(right, -1)
        blocks[chips - step], blocks[step] = left, right
    half = block.shape[0] // 2
    blocks[chips // 2] = jnp.concatenate([send(left[:half], 1), send(right[half:], -1)], axis=0)
    return blocks


def ring_scatter(parts):
    chips = len(parts)
    half = parts[0].shape[0] // 2
    middle = parts[chips // 2]
    ahead = send(middle[:half].astype(bf16), 1).astype(f32)
    back = send(middle[half:].astype(bf16), -1).astype(f32)
    for step in range(chips // 2 - 1, 0, -1):
        one, two = parts[step], parts[chips - step]
        if step == chips // 2 - 1:
            one = jnp.concatenate([one[:half] + ahead, one[half:]], axis=0)
            two = jnp.concatenate([two[:half], two[half:] + back], axis=0)
        else:
            one, two = one + ahead, two + back
        ahead = send(one.astype(bf16), 1).astype(f32)
        back = send(two.astype(bf16), -1).astype(f32)
    return parts[0] + ahead + back


def ring_exchange(pieces):
    return [pieces[0]] + [send(pieces[o], o) for o in range(1, len(pieces))]


def layer_norm(values, norm_gain, norm_shift):
    center = jnp.mean(values, axis=-1, keepdims=True)
    deviation = values - center
    variance = jnp.mean(deviation * deviation, axis=-1, keepdims=True)
    return deviation * lax.rsqrt(variance + norm_epsilon) * norm_gain + norm_shift


def gelu_curve(values):
    return (
        0.5 * values * (1.0 + jnp.tanh(gelu_scale * (values + 0.044715 * values * values * values)))
    )


def rows_by_rows(left_side, right_side):
    return lax.dot_general(
        left_side, right_side, (((0,), (0,)), ((), ())), preferred_element_type=f32
    )


def cols_by_cols(left_side, right_side):
    return lax.dot_general(
        left_side, right_side, (((1,), (1,)), ((), ())), preferred_element_type=f32
    )


def times(left_side, right_side):
    return jnp.dot(left_side, right_side, preferred_element_type=f32)


def spans(first, last, widths):
    found, base = [], 0
    for number, width in enumerate(widths):
        low, high = max(first, base), min(last, base + width)
        if low < high:
            found.append((number, low - base, high - base))
        base += width
    return found


def join_kernel(widths, table, pieces, *outs):
    chips, rows, both = pieces.shape
    width = both // 2
    odd = table[chips] == 1
    for out, valid in zip(outs, widths):
        padded = out.shape[-1]
        out[:, valid:] = jnp.zeros((rows, padded - valid), out.dtype)
    for chip in range(chips):
        piece = pieces[table[chip]].astype(f32)
        piece = jnp.where(
            odd, jnp.concatenate([piece[:, width:], piece[:, :width]], axis=1), piece
        )
        first = chip * both
        done = 0
        for number, low, high in spans(first, first + both, widths):
            outs[number][:, low:high] = piece[:, done : done + high - low].astype(
                outs[number].dtype
            )
            done += high - low


def join_columns(pieces, table, widths, padded):
    rows = pieces.shape[1]
    return pl.pallas_call(
        functools.partial(join_kernel, widths),
        out_shape=[jax.ShapeDtypeStruct((rows, padded), pieces.dtype) for _ in widths],
        in_specs=[
            pl.BlockSpec(memory_space=pltpu.SMEM),
            pl.BlockSpec(memory_space=pltpu.VMEM),
        ],
        out_specs=[pl.BlockSpec(memory_space=pltpu.VMEM) for _ in widths],
        compiler_params=pltpu.CompilerParams(vmem_limit_bytes=vmem_bytes),
    )(table, pieces)


def join_weight_kernel(table, own, other, out):
    chips, rows, width = own.shape
    odd = table[chips] == 1
    for chip in range(chips):
        one = own[table[chip]].astype(f32)
        two = other[table[chip]].astype(f32)
        first = 2 * chip * width
        out[:, first : first + width] = jnp.where(odd, two, one).astype(out.dtype)
        out[:, first + width : first + 2 * width] = jnp.where(odd, one, two).astype(out.dtype)


def join_weight(own, other, table):
    chips, rows, width = own.shape
    block = rows // 13
    return pl.pallas_call(
        join_weight_kernel,
        grid=(rows // block,),
        out_shape=jax.ShapeDtypeStruct((rows, 2 * chips * width), own.dtype),
        in_specs=[
            pl.BlockSpec(memory_space=pltpu.SMEM),
            pl.BlockSpec((chips, block, width), lambda i: (0, i, 0)),
            pl.BlockSpec((chips, block, width), lambda i: (0, i, 0)),
        ],
        out_specs=pl.BlockSpec((block, 2 * chips * width), lambda i: (i, 0)),
        compiler_params=pltpu.CompilerParams(vmem_limit_bytes=vmem_bytes),
    )(table, own, other)


def cut_kernel(widths, table, *refs):
    sources, out = refs[:-1], refs[-1]
    chips, rows, both = out.shape
    width = both // 2
    odd = table[chips] == 1
    for chip in range(chips):
        first = chip * both
        parts = [
            sources[number][:, low:high].astype(f32)
            for number, low, high in spans(first, first + both, widths)
        ]
        piece = parts[0] if len(parts) == 1 else jnp.concatenate(parts, axis=1)
        piece = jnp.where(
            odd, jnp.concatenate([piece[:, width:], piece[:, :width]], axis=1), piece
        )
        out[table[chip]] = piece.astype(out.dtype)


def cut_columns(sources, table, widths, chips):
    rows = sources[0].shape[0]
    return pl.pallas_call(
        functools.partial(cut_kernel, widths),
        out_shape=jax.ShapeDtypeStruct((chips, rows, sum(widths) // chips), bf16),
        in_specs=[pl.BlockSpec(memory_space=pltpu.SMEM)]
        + [pl.BlockSpec(memory_space=pltpu.VMEM) for _ in sources],
        out_specs=pl.BlockSpec(memory_space=pltpu.VMEM),
        compiler_params=pltpu.CompilerParams(vmem_limit_bytes=vmem_bytes),
    )(table, *sources)


def both_heads(pair):
    lane = lax.broadcasted_iota(jnp.int32, pair.shape, 1)
    zero = jnp.zeros_like(pair)
    low = lane < LANES // 2
    return jnp.concatenate([jnp.where(low, pair, zero), jnp.where(low, zero, pair)], axis=0)


def one_pair(stacked):
    rows = stacked.shape[0] // 2
    lane = lax.broadcasted_iota(jnp.int32, (rows, stacked.shape[1]), 1)
    return jnp.where(lane < LANES // 2, stacked[:rows], stacked[rows:])


def forward_kernel(scale, bias, query, far, near, own, mixed, log_total):
    stacked = both_heads(query[...])
    keys = jnp.concatenate([far[0], near[0], own[0]], axis=0)
    values = jnp.concatenate([far[1], near[1], own[1]], axis=0)
    scores = cols_by_cols(stacked, keys) * scale + bias[...]
    row_max = jnp.max(scores, axis=1, keepdims=True)
    raised = jnp.exp(scores - row_max)
    log_sum = row_max + jnp.log(jnp.sum(raised, axis=1, keepdims=True))
    weights = jnp.exp(scores - log_sum).astype(bf16)
    mixed[...] = one_pair(times(weights, values)).astype(bf16)
    log_total[0] = log_sum


def backward_kernel(
    scale, bias, query, far, near, own, log_total, mixed, mixed_back, query_back, far_back,
    near_back, own_back
):
    rows = query.shape[0]
    stacked = both_heads(query[...])
    keys = jnp.concatenate([far[0], near[0], own[0]], axis=0)
    values = jnp.concatenate([far[1], near[1], own[1]], axis=0)
    scores = cols_by_cols(stacked, keys) * scale + bias[...]
    weights = jnp.exp(scores - log_total[0])
    back = both_heads(mixed_back[...])
    product = back.astype(f32) * both_heads(mixed[...]).astype(f32)
    row_delta = jnp.sum(product, axis=1, keepdims=True)
    weight_back = cols_by_cols(back, values)
    score_back = (weights * (weight_back - row_delta)).astype(bf16)
    query_back[...] = one_pair(times(score_back, keys)) * scale
    key_back = rows_by_rows(score_back, stacked) * scale
    value_back = rows_by_rows(weights.astype(bf16), back)
    for number, ref in enumerate((far_back, near_back, own_back)):
        ref[0] = key_back[number * rows : (number + 1) * rows].astype(ref.dtype)
        ref[1] = value_back[number * rows : (number + 1) * rows].astype(ref.dtype)


def attention_specs(rows, window):
    wide = pl.BlockSpec((rows, LANES), lambda p: (0, p))
    pair = pl.BlockSpec((2, rows, LANES), lambda p: (0, 0, p))
    bias = pl.BlockSpec((2 * rows, window), lambda p: (0, 0))
    total = pl.BlockSpec((1, 2 * rows, 1), lambda p: (p, 0, 0))
    return wide, pair, bias, total


def attend_forward(bias, query, far, near, own, scale):
    rows, padded = query.shape
    wide, pair, bias_spec, total = attention_specs(rows, bias.shape[1])
    return pl.pallas_call(
        functools.partial(forward_kernel, scale),
        grid=(padded // LANES,),
        out_shape=[
            jax.ShapeDtypeStruct((rows, padded), bf16),
            jax.ShapeDtypeStruct((padded // LANES, 2 * rows, 1), f32),
        ],
        in_specs=[bias_spec, wide, pair, pair, pair],
        out_specs=[wide, total],
        compiler_params=pltpu.CompilerParams(vmem_limit_bytes=vmem_bytes),
    )(bias, query, far, near, own)


def attend_backward(bias, query, far, near, own, log_total, mixed, mixed_back, scale):
    rows, padded = query.shape
    wide, pair, bias_spec, total = attention_specs(rows, bias.shape[1])
    return pl.pallas_call(
        functools.partial(backward_kernel, scale),
        grid=(padded // LANES,),
        out_shape=[
            jax.ShapeDtypeStruct((rows, padded), f32),
            jax.ShapeDtypeStruct((2, rows, padded), f32),
            jax.ShapeDtypeStruct((2, rows, padded), bf16),
            jax.ShapeDtypeStruct((2, rows, padded), f32),
        ],
        in_specs=[bias_spec, wide, pair, pair, pair, total, wide, wide],
        out_specs=[wide, pair, pair, pair],
        compiler_params=pltpu.CompilerParams(vmem_limit_bytes=vmem_bytes),
    )(bias, query, far, near, own, log_total, mixed, mixed_back)


def shards(
    block_input,
    segments,
    joint_weight,
    output_weight,
    up_weight,
    down_weight,
    vectors,
    up_bias,
    cotangent,
):
    rows = block_input.shape[1]
    features = block_input.shape[2]
    padded = -(-features // LANES) * LANES
    reach_rows = REACH * rows
    window = reach_rows + rows
    scale = (features // H) ** (-0.5)
    context = lax.axis_size("ctx")
    data = lax.axis_size("dp")
    chips = context // 2
    position = lax.axis_index("ctx")
    half_index = lax.axis_index("dp")
    chip = position // 2
    core = position % 2
    place = jnp.where(chip % 2 == 0, chip // 2, chips - 1 - chip // 2)
    places = jnp.array([place_of(m, chips) for m in range(chips)], jnp.int32)
    core_entry = core.astype(jnp.int32)[None]
    ahead_table = jnp.concatenate([(places - place) % chips, core_entry]).astype(jnp.int32)
    back_table = jnp.concatenate([(place - places) % chips, core_entry]).astype(jnp.int32)
    first_half = half_index == 0
    first_core = core == 0

    def both_halves(own, axis):
        other = data_swap(own)
        return jnp.where(
            first_half,
            jnp.concatenate([own, other], axis=axis),
            jnp.concatenate([other, own], axis=axis),
        )

    def both_cores(own, axis):
        return jnp.concatenate([own, core_swap(own)], axis=axis)

    input_blocks = ring_gather(block_input[0])
    spread = jnp.broadcast_to(vectors[None], (data * context,) + vectors.shape)
    spread = lax.all_to_all(spread, ("dp", "ctx"), 0, 0, tiled=True)
    params = (
        spread.reshape((data, context) + vectors.shape)
        .transpose(0, 2, 1, 3)
        .reshape(data * vectors.shape[0], features)
        .astype(f32)
    )
    joint_full = both_cores(both_halves(joint_weight, 0), 1)
    up_full = both_cores(both_halves(up_weight, 0), 1)
    down_full = both_cores(both_halves(down_weight, 1), 0)
    up_shift = both_cores(up_bias, 0).astype(f32)
    output_rows = jnp.pad(both_halves(output_weight, 0), ((0, padded - features), (0, 0)))
    output_own = jnp.stack(ring_gather(output_rows))
    output_full = join_weight(output_own, core_swap(output_own), ahead_table)
    cotangent_blocks = ring_gather(cotangent[0])

    joint_cols = joint_weight.shape[1]
    joint_bias = jnp.concatenate([params[2], jnp.zeros((features,), f32), params[3]])
    chip_bias = lax.dynamic_index_in_dim(joint_bias.reshape(chips, -1), chip, 0, keepdims=False)
    chip_bias = jnp.where(
        first_core,
        chip_bias,
        jnp.concatenate([chip_bias[joint_cols:], chip_bias[:joint_cols]]),
    )
    inputs_all = jnp.concatenate(input_blocks, axis=0).astype(f32)
    normed_one = layer_norm(inputs_all, params[0], params[1]).astype(bf16)
    projected = (times(normed_one, joint_full) + chip_bias).astype(bf16)
    pieces = [projected[o * rows : (o + 1) * rows] for o in range(chips)]
    joined = jnp.stack(ring_exchange(pieces))
    query, key, value = join_columns(joined, back_table, (features,) * 3, padded)

    own = jnp.stack([key, value])
    far = shifted(own, REACH)
    near = core_swap(jnp.where(first_core, own, far))
    padded_numbers = jnp.concatenate([jnp.full((reach_rows,), -1, jnp.int32), segments[0]])
    first_key = position * rows
    key_numbers = lax.dynamic_slice_in_dim(padded_numbers, first_key, window)
    key_places = jnp.arange(window, dtype=jnp.int32)
    same_document = key_numbers[None, :] == key_numbers[reach_rows:, None]
    allowed = same_document & (key_places[None, :] <= key_places[reach_rows:, None])
    bias = jnp.where(allowed, 0.0, masked_score).astype(f32)
    bias = jnp.concatenate([bias, bias], axis=0)
    attended, log_total = attend_forward(bias, query, far, near, own, scale)
    attended_blocks = ring_gather(attended[:, :features])

    rows_float = block_input[0].astype(f32)
    residual = rows_float + times(attended, output_full) + params[4]
    normed_two_own = layer_norm(residual, params[5], params[6]).astype(bf16)
    normed_two = jnp.concatenate(ring_gather(normed_two_own), axis=0)
    cotangent_all = jnp.concatenate(cotangent_blocks, axis=0)
    hidden_back = cols_by_cols(cotangent_all, down_full)
    up_values = times(normed_two, up_full) + up_shift
    hidden_float, gelu_pull = jax.vjp(gelu_curve, up_values)
    hidden = hidden_float.astype(bf16)
    up_back = gelu_pull(hidden_back)[0].astype(bf16)

    def in_blocks(matrix):
        return [matrix[o * rows : (o + 1) * rows] for o in range(chips)]

    normed_two_back = ring_scatter(in_blocks(cols_by_cols(up_back, up_full)))
    down_sum = ring_scatter(in_blocks(times(hidden, down_full)))
    block_output = (residual + down_sum + params[7]).astype(bf16)

    def finish(own_part, other_part):
        total = own_part + core_swap(other_part)
        size = total.shape[0] // data
        kept = lax.dynamic_slice_in_dim(total, half_index * size, size, 0)
        given = lax.dynamic_slice_in_dim(total, (data - 1 - half_index) * size, size, 0)
        return kept + data_swap(given.astype(bf16)).astype(f32)

    unit_cols = up_weight.shape[1]
    up_gradient = finish(
        rows_by_rows(normed_two, up_back[:, :unit_cols]),
        rows_by_rows(normed_two, up_back[:, unit_cols:]),
    )
    size = features // data
    turned = jnp.where(
        first_half,
        cotangent_all,
        jnp.concatenate([cotangent_all[:, size:], cotangent_all[:, :size]], axis=1),
    )
    down_sum_own = rows_by_rows(hidden[:, :unit_cols], turned) + core_swap(
        rows_by_rows(hidden[:, unit_cols:], turned)
    )
    down_gradient = down_sum_own[:, :size] + data_swap(
        down_sum_own[:, size:].astype(bf16)
    ).astype(f32)
    bias_sum = jnp.sum(up_back.astype(f32), axis=0)
    bias_own = bias_sum[:unit_cols] + core_swap(bias_sum[unit_cols:])
    bias_gradient = bias_own + data_swap(bias_own)

    cotangent_float = cotangent[0].astype(f32)
    _, norm_pull = jax.vjp(layer_norm, residual, params[5], params[6])
    residual_part, gain_two_back, shift_two_back = norm_pull(normed_two_back)
    residual_back = cotangent_float + residual_part
    residual_low = residual_back.astype(bf16)
    attended_back = cols_by_cols(residual_low, output_full).astype(bf16)
    query_back, far_back, near_back, own_back = attend_backward(
        bias, query, far, near, own, log_total, attended, attended_back, scale
    )
    near_got = core_swap(near_back).astype(f32)
    far_sum = jnp.where(first_core, far_back, far_back + near_got).astype(bf16)
    far_got = shifted(far_sum, -REACH).astype(f32)
    own_sum = jnp.where(first_core, own_back + near_got, own_back) + far_got

    output_cols = output_weight.shape[1]
    low_pieces = cut_columns([residual_low], ahead_table, (features,), chips)
    low_got = ring_exchange(in_blocks_of(low_pieces))
    low_all = jnp.concatenate([low_got[(chips - o) % chips] for o in range(chips)], axis=0)
    attended_all = jnp.concatenate(attended_blocks, axis=0)
    output_gradient = finish(
        rows_by_rows(attended_all, low_all[:, :output_cols]),
        rows_by_rows(attended_all, low_all[:, output_cols:]),
    )

    back_pieces = cut_columns(
        [query_back, own_sum[0], own_sum[1]], ahead_table, (features,) * 3, chips
    )
    back_got = ring_exchange(in_blocks_of(back_pieces))
    projected_back = jnp.concatenate([back_got[(chips - o) % chips] for o in range(chips)], axis=0)
    normed_one_back = ring_scatter(in_blocks(cols_by_cols(projected_back, joint_full)))
    joint_gradient = finish(
        rows_by_rows(normed_one, projected_back[:, :joint_cols]),
        rows_by_rows(normed_one, projected_back[:, joint_cols:]),
    )
    _, first_pull = jax.vjp(layer_norm, rows_float, params[0], params[1])
    rows_part, gain_one_back, shift_one_back = first_pull(normed_one_back)
    input_gradient = residual_back + rows_part
    vectors_sum = jnp.stack(
        [
            gain_one_back,
            shift_one_back,
            jnp.sum(query_back[:, :features], axis=0),
            jnp.sum(own_sum[1][:, :features], axis=0),
            jnp.sum(residual_back, axis=0),
            gain_two_back,
            shift_two_back,
            jnp.sum(cotangent_float, axis=0),
        ]
    )
    vectors_cut = (
        vectors_sum.reshape(data, vectors.shape[0], context, vectors.shape[1])
        .transpose(0, 2, 1, 3)
        .reshape((data * context,) + vectors.shape)
    )
    vectors_gradient = jnp.sum(
        lax.all_to_all(vectors_cut, ("dp", "ctx"), 0, 0, tiled=True), axis=0
    )
    return (
        block_output[None],
        input_gradient[None],
        joint_gradient,
        output_gradient,
        up_gradient,
        down_gradient,
        vectors_gradient,
        bias_gradient,
    )


def in_blocks_of(stacked):
    return [stacked[o] for o in range(stacked.shape[0])]


def solution(mesh):
    in_specs = (
        P("dp", "ctx", None),
        P("dp", None),
        P("dp", "ctx"),
        P("dp", "ctx"),
        P("dp", "ctx"),
        P("ctx", "dp"),
        P("dp", "ctx"),
        P("ctx"),
        P("dp", "ctx", None),
    )
    out_specs = (
        P("dp", "ctx", None),
        P("dp", "ctx", None),
        P("dp", "ctx"),
        P("dp", "ctx"),
        P("dp", "ctx"),
        P("ctx", "dp"),
        P("dp", "ctx"),
        P("ctx"),
    )
    return jax.shard_map(shards, mesh=mesh, in_specs=in_specs, out_specs=out_specs, check_vma=False)
```

time: 2670 us -> 621 us (0.23)
  waiting for transfers between devices: 1590 us -> 254 us
  blocking collectives: 335 us -> 0 us
  matrix products: 348 us -> 55.9 us
  local copies, waits for them, and re-layouts: 275 us -> 58.3 us
  starting transfers between devices: 27.1 us -> 168 us
  Pallas kernels: 0 us -> 38.4 us
    all_gather x18 -> x0, waiting for transfers between devices: 1520 us -> none  [the longest x2 444 us: collect(): lax.all_gather(first_section[2], 'dp', axis=0, tiled=True)]
    dot_general x187 -> x16, matrix products: 348 us -> 55.9 us  [the longest x8 23.4 us: rows_by_rows(): lax.dot_general(left_side, right_side, (((0,), (0,)), ((), ())), preferre...]
    ppermute x4 -> x108, waiting for transfers between devices: 30.9 us -> 246 us  [the longest x85 209 us: send(): return lax.ppermute(value, 'ctx', pairs)]
    unnamed x3 -> x0, blocking collectives: 164 us -> none
    ppermute x4 -> x108, starting transfers between devices: 8.8 us -> 158 us  [the longest x85 142 us: send(): return lax.ppermute(value, 'ctx', pairs)]
    all_to_all x1 -> x0, blocking collectives: 149 us -> none  [shards(): lax.all_to_all(column_pack, 'ctx', split_axis=0, concat_axis=0, tiled=True)]
    all_gather x7 -> x0, local copies, waits for them, and re-layouts: 107 us -> none  [the longest x1 32.2 us: shards(): piece = lax.all_gather(row_shares, 'ctx', axis=1, tiled=True)]
    pallas_call x0 -> x6, Pallas kernels: none -> 38.4 us  [the longest x1 12.6 us: attend_backward(): pl.pallas_call(functools.partial(backward_kernel, scale), grid=(padded //...]
  transfers between devices with their start and end apart: 23 -> 110, of which waited for: 16 -> 51; matrix products, arithmetic and copies ran while one was open for 22% -> 21% of each run, Pallas kernels for 0% -> 6%
where the time goes in v1:
time: 621 us; the launch traced here: 612 us
  waiting for transfers between devices  254 us (41%)
  starting transfers between devices  168 us (27%)
  local copies, waits for them, and re-layouts  58.3 us (9%)
  matrix products  55.9 us (9%)
  Pallas kernels  38.4 us (6%)
  other arithmetic  34.5 us (6%)
    ppermute x85, waiting for transfers between devices, send(): return lax.ppermute(value, 'ctx', pairs)  209 us
    ppermute x85, starting transfers between devices, send(): return lax.ppermute(value, 'ctx', pairs)  142 us
    ppermute x9, waiting for transfers between devices, data_swap(): lax.ppermute(value, 'dp', [(i, i ^ 1) for i in range(lax.axis_size('dp'))])  33.2 us
    unnamed x178, local copies, waits for them, and re-layouts  30.9 us
    dot_general x8, matrix products, rows_by_rows(): lax.dot_general(left_side, right_side, (((0,), (0,)), ((), ())), preferre...  23.4 us
    dot_general x4, matrix products, times(): return jnp.dot(left_side, right_side, preferred_element_type=f32)  16.3 us
    dot_general x4, matrix products, cols_by_cols(): lax.dot_general(left_side, right_side, (((1,), (1,)), ((), ())), preferre...  16.1 us
    pallas_call x1, Pallas kernels, attend_backward(): pl.pallas_call(functools.partial(backward_kernel, scale), grid=(padded //...  12.6 us
  transfers between devices with their start and end apart: 110, of which 51 were waited for; matrix products, arithmetic and copies ran while one was open for 21% of the time, Pallas kernels for 6%

profile of v1, /device:TPU:0, one launch (start us, length us, event | category | flops | bytes accessed | tf_op | source)
XLA Modules:
  0.0 612.2 jit_solution(5287423283784983249)
XLA Ops:
  11.0 6.3 %all-to-all-start = ((bf16[32,4,100]{2,1,0:T(4,128)(2,1)}), bf16[32,4,100]{2,1,0:T(4,128)(2,1)S(1)}, u32[]{:S(2)}, u32[]{:S(2)}) async-start(bf16[32,4,100]{2,1,0:T(4,128)(2,1)} %broadcast_in_dim.29), calls=%async_computation | async-start | bytes 65536 | tf_op jit(solution)/shard_map/all_to_all | solution.py:359
  25.6 5.1 all-to-all-done
  39.2 7.7 %collective-permute-done.8 = bf16[800,300]{0,1:T(8,128)(2,1)S(1)} collective-permute-done((bf16[800,300]{0,1:T(8,128)(2,1)}, bf16[800,300]{0,1:T(8,128)(2,1)S(1)}, u32[]{:S(2)}, u32[]{:S(2)}) %collective-permute-start.8) | collective-permute-done | bytes 480032 | tf_op jit(solution)/shard_map/ppermute | solution.py:46
  52.0 10.3 %collective-permute-done.40 = bf16[400,800]{1,0:T(8,128)(2,1)S(1)} collective-permute-done((bf16[400,800]{1,0:T(8,128)(2,1)}, bf16[400,800]{1,0:T(8,128)(2,1)S(1)}, u32[]{:S(2)}, u32[]{:S(2)}) %collective-permute-start.40) | collective-permute-done | bytes 640032 | tf_op jit(solution)/shard_map/ppermute | solution.py:46
  68.0 8.7 %collective-permute-done.37 = bf16[800,400]{0,1:T(8,128)(2,1)S(1)} collective-permute-done((bf16[800,400]{0,1:T(8,128)(2,1)}, bf16[800,400]{0,1:T(8,128)(2,1)S(1)}, u32[]{:S(2)}, u32[]{:S(2)}) %collective-permute-start.37) | collective-permute-done | bytes 640032 | tf_op jit(solution)/shard_map/ppermute | solution.py:46
  83.3 7.5 %collective-permute-done.21 = bf16[1664,100]{1,0:T(8,128)(2,1)S(1)} collective-permute-done((bf16[1664,100]{1,0:T(8,128)(2,1)S(1)}, bf16[1664,100]{1,0:T(8,128)(2,1)S(1)}, u32[]{:S(2)}, u32[]{:S(2)}) %collective-permute-start.21) | collective-permute-done | bytes 332832 | tf_op jit(solution)/shard_map/ppermute | solution.py:38
  91.5 5.5 collective-permute-done.24
  103.6 6.1 %collective-permute-done.25 = bf16[1664,100]{1,0:T(8,128)(2,1)S(1)} collective-permute-done((bf16[1664,100]{1,0:T(8,128)(2,1)S(1)}, bf16[1664,100]{1,0:T(8,128)(2,1)S(1)}, u32[]{:S(2)}, u32[]{:S(2)}) %collective-permute-start.25) | collective-permute-done | bytes 332832 | tf_op jit(solution)/shard_map/ppermute | solution.py:38
  110.3 8.5 %collective-permute-done.5 = bf16[128,1600]{1,0:T(8,128)(2,1)S(1)} collective-permute-done((bf16[128,1600]{1,0:T(8,128)(2,1)S(1)}, bf16[128,1600]{1,0:T(8,128)(2,1)S(1)}, u32[]{:S(2)}, u32[]{:S(2)}) %collective-permute-start.5) | collective-permute-done | bytes 409632 | tf_op jit(solution)/shard_map/ppermute | solution.py:38
  119.7 5.5 collective-permute-done.55
  129.1 4.4 collective-permute-done.26
  150.9 4.6 collective-permute-start.12
  159.5 7.6 %collective-permute-done.12 = bf16[128,600]{1,0:T(8,128)(2,1)S(1)} collective-permute-done((bf16[128,600]{1,0:T(8,128)(2,1)S(1)}, bf16[128,600]{1,0:T(8,128)(2,1)S(1)}, u32[]{:S(2)}, u32[]{:S(2)}) %collective-permute-start.12) | collective-permute-done | bytes 153632 | tf_op jit(solution)/shard_map/ppermute | solution.py:38
  177.4 4.2 collective-permute-done.16
  184.5 5.3 collective-permute-start.17
  189.9 4.3 copy.126
  205.6 10.6 %shard_map.162 = (bf16[128,1664]{1,0:T(8,128)(2,1)S(1)}, f32[13,256,1]{2,1,0:T(8,128)S(1)}) custom-call(f32[256,384]{1,0:T(8,128)S(1)} %copy-done.2, bf16[128,1664]{1,0:T(8,128)(2,1)S(1)} %copy-done.7, bf16[2,128,1664]{2,1,0:T(8,128)(2,1)} %collective-permute-done.17.far, bf16[2,128,1664]{2,1,0:T(8,128)(2,1)S(1)} %collective-permute-done.18.near, ...), custom_call_target="tpu_custom_call" | custom-call | tf_op jit(solution)/shard_map/pallas_call | solution.py:283
  223.7 5.9 collective-permute-done.85
  231.9 5.6 copy.127.other
  237.5 11.0 %shard_map.163 = bf16[1664,1600]{1,0:T(8,128)(2,1)} custom-call(s32[9]{0:T(128)S(1)} %pad_add_fusion.1.table, bf16[8,1664,100]{2,1,0:T(8,128)(2,1)S(1)} %bitcast_dynamic-update-slice_fusion.own, bf16[8,1664,100]{2,1,0:T(8,128)(2,1)} %copy.127.other), custom_call_target="tpu_custom_call" | custom-call | tf_op jit(solution)/shard_map/pallas_call | solution.py:179
  263.8 5.0 collective-permute-done.29
  272.5 5.6 collective-permute-done.90
  283.0 10.3 %collective-permute-done.91 = bf16[64,1600]{1,0:T(8,128)(2,1)S(1)} collective-permute-done((bf16[64,1600]{1,0:T(8,128)(2,1)S(1)}, bf16[64,1600]{1,0:T(8,128)(2,1)S(1)}, u32[]{:S(2)}, u32[]{:S(2)}) %collective-permute-start.91) | collective-permute-done | bytes 204832 | tf_op jit(solution)/shard_map/ppermute | solution.py:38
  306.5 7.8 %collective-permute-done.34 = bf16[128,1600]{1,0:T(8,128)(2,1)S(1)} collective-permute-done((bf16[128,1600]{1,0:T(8,128)(2,1)S(1)}, bf16[128,1600]{1,0:T(8,128)(2,1)S(1)}, u32[]{:S(2)}, u32[]{:S(2)}) %collective-permute-start.34) | collective-permute-done | bytes 409632 | tf_op jit(solution)/shard_map/ppermute | solution.py:38
  321.1 3.8 multiply_convert_fusion
  325.0 7.2 %convert_reduce_fusion.1 = (f32[800]{0:T(1024)S(1)}, bf16[1024,800]{0,1:T(8,128)(2,1)S(1)}) fusion(bf16[1024,1600]{1,0:T(8,128)(2,1)S(1)} %copy-done.17, bf16[400,1600]{1,0:T(8,128)(2,1)} %collective-permute-done.41, bf16[400,1600]{1,0:T(8,128)(2,1)} %maximum_select_fusion.2, f32[1024,800]{0,1:T(8,128)S(1)} %get-tuple-element.144, ...), kind=kOutput, calls=%fused_computation.19 | convolution fusion | flops 2648677632 | bytes 10758400 | tf_op jit(solution)/shard_map/dot_general | solution.py:111
  335.4 4.2 fusion.96
  341.9 5.8 fusion.97
  359.1 5.9 collective-permute-done.59
  366.8 7.0 %collective-permute-done.43 = bf16[128,1600]{1,0:T(8,128)(2,1)S(1)} collective-permute-done((bf16[128,1600]{1,0:T(8,128)(2,1)S(1)}, bf16[128,1600]{1,0:T(8,128)(2,1)S(1)}, u32[]{:S(2)}, u32[]{:S(2)}) %collective-permute-start.43) | collective-permute-done | bytes 409632 | tf_op jit(solution)/shard_map/ppermute | solution.py:38
  377.5 8.9 %collective-permute-done.60 = bf16[128,1600]{1,0:T(8,128)(2,1)S(1)} collective-permute-done((bf16[128,1600]{1,0:T(8,128)(2,1)S(1)}, bf16[128,1600]{1,0:T(8,128)(2,1)S(1)}, u32[]{:S(2)}, u32[]{:S(2)}) %collective-permute-start.60) | collective-permute-done | bytes 409632 | tf_op jit(solution)/shard_map/ppermute | solution.py:38
  388.7 6.9 %collective-permute-done.44 = bf16[128,1600]{1,0:T(8,128)(2,1)S(1)} collective-permute-done((bf16[128,1600]{1,0:T(8,128)(2,1)S(1)}, bf16[128,1600]{1,0:T(8,128)(2,1)S(1)}, u32[]{:S(2)}, u32[]{:S(2)}) %collective-permute-start.44) | collective-permute-done | bytes 409632 | tf_op jit(solution)/shard_map/ppermute | solution.py:38
  397.9 7.8 %collective-permute-done.48 = bf16[128,1600]{1,0:T(8,128)(2,1)S(1)} collective-permute-done((bf16[128,1600]{1,0:T(8,128)(2,1)S(1)}, bf16[128,1600]{1,0:T(8,128)(2,1)S(1)}, u32[]{:S(2)}, u32[]{:S(2)}) %collective-permute-start.48) | collective-permute-done | bytes 409632 | tf_op jit(solution)/shard_map/ppermute | solution.py:38
  409.6 8.9 %collective-permute-done.65 = bf16[128,1600]{1,0:T(8,128)(2,1)S(1)} collective-permute-done((bf16[128,1600]{1,0:T(8,128)(2,1)S(1)}, bf16[128,1600]{1,0:T(8,128)(2,1)S(1)}, u32[]{:S(2)}, u32[]{:S(2)}) %collective-permute-start.65) | collective-permute-done | bytes 409632 | tf_op jit(solution)/shard_map/ppermute | solution.py:38
  419.0 4.5 collective-permute-done.49
  427.1 12.6 %shard_map.164 = (f32[128,1664]{1,0:T(8,128)S(1)}, f32[2,128,1664]{2,1,0:T(8,128)}, bf16[2,128,1664]{2,1,0:T(8,128)(2,1)S(1)}, f32[2,128,1664]{2,1,0:T(8,128)}) custom-call(f32[256,384]{1,0:T(8,128)S(1)} %copy-done.3, bf16[128,1664]{1,0:T(8,128)(2,1)S(1)} %copy-done.8, bf16[2,128,1664]{2,1,0:T(8,128)(2,1)} %collective-permute-done.17.far, ...), custom_call_target="tpu_custom_call" | custom-call | tf_op jit(solution)/shard_map/pallas_call | solution.py:299
  439.7 4.4 fusion.46
  469.5 16.6 %collective-permute-done.99 = bf16[128,200]{1,0:T(8,128)(2,1)S(1)} collective-permute-done((bf16[128,200]{1,0:T(8,128)(2,1)S(1)}, bf16[128,200]{1,0:T(8,128)(2,1)S(1)}, u32[]{:S(2)}, u32[]{:S(2)}) %collective-permute-start.99) | collective-permute-done | bytes 51232 | tf_op jit(solution)/shard_map/ppermute | solution.py:38
  494.8 5.8 collective-permute-done.68
  500.7 7.6 %collective-permute-start.70 = (bf16[128,600]{1,0:T(8,128)(2,1)S(1)}, bf16[128,600]{1,0:T(8,128)(2,1)S(1)}, u32[]{:S(2)}, u32[]{:S(2)}) collective-permute-start(bf16[128,600]{1,0:T(8,128)(2,1)S(1)} %get-tuple-element.114), channel_id=1, source_target_pairs={{0,10},{1,11},{4,6},{5,7},{8,2},{9,3},{12,0},{13,1},{14,4},{15,5},... | collective-permute-start | bytes 460808 | tf_op jit(solution)/shard_map/ppermute | solution.py:38
  508.3 4.4 collective-permute-start.71
  512.7 5.2 collective-permute-start.72
  518.0 7.5 %collective-permute-start.73 = (bf16[128,600]{1,0:T(8,128)(2,1)S(1)}, bf16[128,600]{1,0:T(8,128)(2,1)S(1)}, u32[]{:S(2)}, u32[]{:S(2)}) collective-permute-start(bf16[128,600]{1,0:T(8,128)(2,1)S(1)} %get-tuple-element.111), channel_id=1, source_target_pairs={{0,8},{1,9},{4,12},{5,13},{8,14},{9,15},{12,10},{13,11},{14,6},{15... | collective-permute-start | bytes 460808 | tf_op jit(solution)/shard_map/ppermute | solution.py:38
  525.4 5.4 collective-permute-done.72
  531.6 5.2 collective-permute-done.74
  572.5 4.6 collective-permute-done.81
  579.7 6.5 %collective-permute-done.105 = bf16[400,800]{1,0:T(8,128)(2,1)S(1)} collective-permute-done((bf16[400,800]{1,0:T(8,128)(2,1)S(1)}, bf16[400,800]{1,0:T(8,128)(2,1)S(1)}, u32[]{:S(2)}, u32[]{:S(2)}) %collective-permute-start.105) | collective-permute-done | bytes 640032 | tf_op jit(solution)/shard_map/ppermute | solution.py:46
  598.1 4.2 all-to-all-start.1
  (499 shorter events, 285.2 us)
Async XLA Ops:
  2.7 30.6 %collective-permute-start = (bf16[128,1600]{1,0:T(8,128)(2,1)}, bf16[128,1600]{1,0:T(8,128)(2,1)}, u32[]{:S(2)}, u32[]{:S(2)}) collective-permute-start(bf16[128,1600]{1,0:T(8,128)(2,1)} %bitcast), channel_id=1, source_target_pairs={{0,2},{1,3},{4,0},{5,1},{8,4},{9,5},{12,8},{13,9},{14,12},{15,13},... | collective-permute-start | bytes 1228808 | tf_op jit(solution)/shard_map/ppermute | solution.py:38
  5.7 60.3 %collective-permute-start.3 = (bf16[128,1600]{1,0:T(8,128)(2,1)}, bf16[128,1600]{1,0:T(8,128)(2,1)}, u32[]{:S(2)}, u32[]{:S(2)}) collective-permute-start(bf16[128,1600]{1,0:T(8,128)(2,1)} %bitcast), channel_id=1, source_target_pairs={{0,4},{1,5},{4,8},{5,9},{8,12},{9,13},{12,14},{13,15},{14,10},{15,... | collective-permute-start | bytes 1228808 | tf_op jit(solution)/shard_map/ppermute | solution.py:38
  7.7 28.0 %collective-permute-start.50 = (bf16[128,1600]{1,0:T(8,128)(2,1)}, bf16[128,1600]{1,0:T(8,128)(2,1)}, u32[]{:S(2)}, u32[]{:S(2)}) collective-permute-start(bf16[128,1600]{1,0:T(8,128)(2,1)} %bitcast.24), channel_id=1, source_target_pairs={{0,2},{1,3},{4,0},{5,1},{8,4},{9,5},{12,8},{13,9},{14,12},{15,13},... | collective-permute-start | bytes 1228808 | tf_op jit(solution)/shard_map/ppermute | solution.py:38
  9.7 57.7 %collective-permute-start.53 = (bf16[128,1600]{1,0:T(8,128)(2,1)}, bf16[128,1600]{1,0:T(8,128)(2,1)}, u32[]{:S(2)}, u32[]{:S(2)}) collective-permute-start(bf16[128,1600]{1,0:T(8,128)(2,1)} %bitcast.24), channel_id=1, source_target_pairs={{0,4},{1,5},{4,8},{5,9},{8,12},{9,13},{12,14},{13,15},{14,10},{15,... | collective-permute-start | bytes 1228808 | tf_op jit(solution)/shard_map/ppermute | solution.py:38
  11.0 19.7 %all-to-all-start = ((bf16[32,4,100]{2,1,0:T(4,128)(2,1)}), bf16[32,4,100]{2,1,0:T(4,128)(2,1)S(1)}, u32[]{:S(2)}, u32[]{:S(2)}) async-start(bf16[32,4,100]{2,1,0:T(4,128)(2,1)} %broadcast_in_dim.29), calls=%async_computation | async-start | bytes 65536 | tf_op jit(solution)/shard_map/all_to_all | solution.py:359
  33.3 28.9 %collective-permute-start.40 = (bf16[400,800]{1,0:T(8,128)(2,1)}, bf16[400,800]{1,0:T(8,128)(2,1)S(1)}, u32[]{:S(2)}, u32[]{:S(2)}) collective-permute-start(bf16[400,800]{1,0:T(8,128)(2,1)} %param.15), channel_id=1, source_target_pairs={{0,16},{16,0},{1,17},{17,1},{2,18},{18,2},{3,19},{19,3},{4,20},{20... | collective-permute-start | bytes 1920008 | tf_op jit(solution)/shard_map/ppermute | solution.py:46
  46.9 29.8 %collective-permute-start.37 = (bf16[800,400]{0,1:T(8,128)(2,1)}, bf16[800,400]{0,1:T(8,128)(2,1)S(1)}, u32[]{:S(2)}, u32[]{:S(2)}) collective-permute-start(bf16[800,400]{0,1:T(8,128)(2,1)} %param.14), channel_id=1, source_target_pairs={{0,16},{16,0},{1,17},{17,1},{2,18},{18,2},{3,19},{19,3},{4,20},{20... | collective-permute-start | bytes 1920008 | tf_op jit(solution)/shard_map/ppermute | solution.py:46
  50.4 29.3 %collective-permute-start.23 = (bf16[1664,100]{1,0:T(8,128)(2,1)S(1)}, bf16[1664,100]{1,0:T(8,128)(2,1)S(1)}, u32[]{:S(2)}, u32[]{:S(2)}) collective-permute-start(bf16[1664,100]{1,0:T(8,128)(2,1)S(1)} %pad.5), channel_id=1, source_target_pairs={{0,4},{1,5},{4,8},{5,9},{8,12},{9,13},{12,14},{13,15},{14,10},{15,... | collective-permute-start | bytes 998408 | tf_op jit(solution)/shard_map/ppermute | solution.py:38
  62.2 18.5 %collective-permute-start.1 = (bf16[128,1600]{1,0:T(8,128)(2,1)}, bf16[128,1600]{1,0:T(8,128)(2,1)S(1)}, u32[]{:S(2)}, u32[]{:S(2)}) collective-permute-start(bf16[128,1600]{1,0:T(8,128)(2,1)} %collective-permute-done), channel_id=1, source_target_pairs={{0,2},{1,3},{4,0},{5,1},{8,4},{9,5},{12,8},{13,9},{14,12},{15,13},... | collective-permute-start | bytes 1228808 | tf_op jit(solution)/shard_map/ppermute | solution.py:38
  65.9 16.5 %collective-permute-start.51 = (bf16[128,1600]{1,0:T(8,128)(2,1)}, bf16[128,1600]{1,0:T(8,128)(2,1)S(1)}, u32[]{:S(2)}, u32[]{:S(2)}) collective-permute-start(bf16[128,1600]{1,0:T(8,128)(2,1)} %collective-permute-done.50), channel_id=1, source_target_pairs={{0,2},{1,3},{4,0},{5,1},{8,4},{9,5},{12,8},{13,9},{14,12},{15,13},... | collective-permute-start | bytes 1228808 | tf_op jit(solution)/shard_map/ppermute | solution.py:38
  67.3 34.2 %collective-permute-start.4 = (bf16[128,1600]{1,0:T(8,128)(2,1)}, bf16[128,1600]{1,0:T(8,128)(2,1)S(1)}, u32[]{:S(2)}, u32[]{:S(2)}) collective-permute-start(bf16[128,1600]{1,0:T(8,128)(2,1)} %collective-permute-done.3), channel_id=1, source_target_pairs={{0,4},{1,5},{4,8},{5,9},{8,12},{9,13},{12,14},{13,15},{14,10},{15,... | collective-permute-start | bytes 1228808 | tf_op jit(solution)/shard_map/ppermute | solution.py:38
  76.7 26.1 %collective-permute-start.54 = (bf16[128,1600]{1,0:T(8,128)(2,1)}, bf16[128,1600]{1,0:T(8,128)(2,1)S(1)}, u32[]{:S(2)}, u32[]{:S(2)}) collective-permute-start(bf16[128,1600]{1,0:T(8,128)(2,1)} %collective-permute-done.53), channel_id=1, source_target_pairs={{0,4},{1,5},{4,8},{5,9},{8,12},{9,13},{12,14},{13,15},{14,10},{15,... | collective-permute-start | bytes 1228808 | tf_op jit(solution)/shard_map/ppermute | solution.py:38
  80.7 16.3 %collective-permute-start.24 = (bf16[1664,100]{1,0:T(8,128)(2,1)S(1)}, bf16[1664,100]{1,0:T(8,128)(2,1)S(1)}, u32[]{:S(2)}, u32[]{:S(2)}) collective-permute-start(bf16[1664,100]{1,0:T(8,128)(2,1)S(1)} %collective-permute-done.23), channel_id=1, source_target_pairs={{0,4},{1,5},{4,8},{5,9},{8,12},{9,13},{12,14},{13,15},{14,10},{15,... | collective-permute-start | bytes 998408 | tf_op jit(solution)/shard_map/ppermute | solution.py:38
  82.4 59.1 %collective-permute-start.9 = (bf16[1600,300]{0,1:T(8,128)(2,1)S(1)}, bf16[1600,300]{0,1:T(8,128)(2,1)S(1)}, u32[]{:S(2)}, u32[]{:S(2)}) collective-permute-start(bf16[1600,300]{0,1:T(8,128)(2,1)S(1)} %maximum_select_fusion.3), channel_id=1, source_target_pairs={{0,1},{1,0},{2,3},{3,2},{4,5},{5,4},{6,7},{7,6},{8,9},{9,8},{10,11... | collective-permute-start | bytes 2880008 | tf_op jit(solution)/shard_map/ppermute | solution.py:42
  100.8 18.0 %collective-permute-start.2 = (bf16[128,1600]{1,0:T(8,128)(2,1)S(1)}, bf16[128,1600]{1,0:T(8,128)(2,1)S(1)}, u32[]{:S(2)}, u32[]{:S(2)}) collective-permute-start(bf16[128,1600]{1,0:T(8,128)(2,1)S(1)} %collective-permute-done.1), channel_id=1, source_target_pairs={{0,2},{1,3},{4,0},{5,1},{8,4},{9,5},{12,8},{13,9},{14,12},{15,13},... | collective-permute-start | bytes 1228808 | tf_op jit(solution)/shard_map/ppermute | solution.py:38
  101.5 24.7 %collective-permute-start.52 = (bf16[128,1600]{1,0:T(8,128)(2,1)S(1)}, bf16[128,1600]{1,0:T(8,128)(2,1)S(1)}, u32[]{:S(2)}, u32[]{:S(2)}) collective-permute-start(bf16[128,1600]{1,0:T(8,128)(2,1)S(1)} %collective-permute-done.51), channel_id=1, source_target_pairs={{0,2},{1,3},{4,0},{5,1},{8,4},{9,5},{12,8},{13,9},{14,12},{15,13},... | collective-permute-start | bytes 1228808 | tf_op jit(solution)/shard_map/ppermute | solution.py:38
  102.8 16.0 %collective-permute-start.5 = (bf16[128,1600]{1,0:T(8,128)(2,1)S(1)}, bf16[128,1600]{1,0:T(8,128)(2,1)S(1)}, u32[]{:S(2)}, u32[]{:S(2)}) collective-permute-start(bf16[128,1600]{1,0:T(8,128)(2,1)S(1)} %collective-permute-done.4), channel_id=1, source_target_pairs={{0,4},{1,5},{4,8},{5,9},{8,12},{9,13},{12,14},{13,15},{14,10},{15,... | collective-permute-start | bytes 1228808 | tf_op jit(solution)/shard_map/ppermute | solution.py:38
  118.8 206.1 %collective-permute-start.41 = (bf16[400,1600]{1,0:T(8,128)(2,1)}, bf16[400,1600]{1,0:T(8,128)(2,1)}, u32[]{:S(2)}, u32[]{:S(2)}) collective-permute-start(bf16[400,1600]{1,0:T(8,128)(2,1)} %maximum_select_fusion.2), channel_id=1, source_target_pairs={{0,1},{1,0},{2,3},{3,2},{4,5},{5,4},{6,7},{7,6},{8,9},{9,8},{10,11... | collective-permute-start | bytes 3840008 | tf_op jit(solution)/shard_map/ppermute | solution.py:42
  133.4 67.2 %collective-permute-start.56 = (bf16[64,1600]{1,0:T(8,128)(2,1)}, bf16[64,1600]{1,0:T(8,128)(2,1)}, u32[]{:S(2)}, u32[]{:S(2)}) collective-permute-start(bf16[64,1600]{1,0:T(8,128)(2,1)} %slice.470), channel_id=1, source_target_pairs={{0,4},{1,5},{4,8},{5,9},{8,12},{9,13},{12,14},{13,15},{14,10},{15,... | collective-permute-start | bytes 614408 | tf_op jit(solution)/shard_map/ppermute | solution.py:38
  136.7 65.7 %collective-permute-start.57 = (bf16[64,1600]{1,0:T(8,128)(2,1)}, bf16[64,1600]{1,0:T(8,128)(2,1)}, u32[]{:S(2)}, u32[]{:S(2)}) collective-permute-start(bf16[64,1600]{1,0:T(8,128)(2,1)} %slice.471), channel_id=1, source_target_pairs={{0,2},{1,3},{4,0},{5,1},{8,4},{9,5},{12,8},{13,9},{14,12},{15,13},... | collective-permute-start | bytes 614408 | tf_op jit(solution)/shard_map/ppermute | solution.py:38
  150.9 16.2 %collective-permute-start.12 = (bf16[128,600]{1,0:T(8,128)(2,1)S(1)}, bf16[128,600]{1,0:T(8,128)(2,1)S(1)}, u32[]{:S(2)}, u32[]{:S(2)}) collective-permute-start(bf16[128,600]{1,0:T(8,128)(2,1)S(1)} %get-tuple-element.121), channel_id=1, source_target_pairs={{0,12},{1,13},{4,14},{5,15},{8,10},{9,11},{12,6},{13,7},{14,2},{15... | collective-permute-start | bytes 460808 | tf_op jit(solution)/shard_map/ppermute | solution.py:38
  194.2 37.7 %collective-permute-start.28 = (bf16[8,1664,100]{1,0,2:T(8,128)(2,1)}, bf16[8,1664,100]{1,0,2:T(8,128)(2,1)}, u32[]{:S(2)}, u32[]{:S(2)}) collective-permute-start(bf16[8,1664,100]{1,0,2:T(8,128)(2,1)} %copy.126), channel_id=1, source_target_pairs={{0,1},{1,0},{2,3},{3,2},{4,5},{5,4},{6,7},{7,6},{8,9},{9,8},{10,11... | collective-permute-start | bytes 7987208 | tf_op jit(solution)/shard_map/ppermute | solution.py:42
  229.6 30.3 %collective-permute-start.86 = (bf16[128,1600]{1,0:T(8,128)(2,1)}, bf16[128,1600]{1,0:T(8,128)(2,1)}, u32[]{:S(2)}, u32[]{:S(2)}) collective-permute-start(bf16[128,1600]{1,0:T(8,128)(2,1)} %collective-permute-done.85), channel_id=1, source_target_pairs={{0,2},{1,3},{4,0},{5,1},{8,4},{9,5},{12,8},{13,9},{14,12},{15,13},... | collective-permute-start | bytes 1228808 | tf_op jit(solution)/shard_map/ppermute | solution.py:38
  231.9 28.0 %collective-permute-start.89 = (bf16[128,1600]{1,0:T(8,128)(2,1)}, bf16[128,1600]{1,0:T(8,128)(2,1)}, u32[]{:S(2)}, u32[]{:S(2)}) collective-permute-start(bf16[128,1600]{1,0:T(8,128)(2,1)} %collective-permute-done.88), channel_id=1, source_target_pairs={{0,4},{1,5},{4,8},{5,9},{8,12},{9,13},{12,14},{13,15},{14,10},{15,... | collective-permute-start | bytes 1228808 | tf_op jit(solution)/shard_map/ppermute | solution.py:38
  259.9 20.5 %collective-permute-start.87 = (bf16[128,1600]{1,0:T(8,128)(2,1)}, bf16[128,1600]{1,0:T(8,128)(2,1)S(1)}, u32[]{:S(2)}, u32[]{:S(2)}) collective-permute-start(bf16[128,1600]{1,0:T(8,128)(2,1)} %collective-permute-done.86), channel_id=1, source_target_pairs={{0,2},{1,3},{4,0},{5,1},{8,4},{9,5},{12,8},{13,9},{14,12},{15,13},... | collective-permute-start | bytes 1228808 | tf_op jit(solution)/shard_map/ppermute | solution.py:38
  259.9 18.1 %collective-permute-start.90 = (bf16[128,1600]{1,0:T(8,128)(2,1)}, bf16[128,1600]{1,0:T(8,128)(2,1)S(1)}, u32[]{:S(2)}, u32[]{:S(2)}) collective-permute-start(bf16[128,1600]{1,0:T(8,128)(2,1)} %collective-permute-done.89), channel_id=1, source_target_pairs={{0,4},{1,5},{4,8},{5,9},{8,12},{9,13},{12,14},{13,15},{14,10},{15,... | collective-permute-start | bytes 1228808 | tf_op jit(solution)/shard_map/ppermute | solution.py:38
  268.7 52.4 %collective-permute-start.38 = (bf16[1600,400]{0,1:T(8,128)(2,1)S(1)}, bf16[1600,400]{0,1:T(8,128)(2,1)S(1)}, u32[]{:S(2)}, u32[]{:S(2)}) collective-permute-start(bf16[1600,400]{0,1:T(8,128)(2,1)S(1)} %copy-done.30), channel_id=1, source_target_pairs={{0,1},{1,0},{2,3},{3,2},{4,5},{5,4},{6,7},{7,6},{8,9},{9,8},{10,11... | collective-permute-start | bytes 3840008 | tf_op jit(solution)/shard_map/ppermute | solution.py:42
  270.5 32.1 %collective-permute-start.30 = (bf16[128,1600]{1,0:T(8,128)(2,1)S(1)}, bf16[128,1600]{1,0:T(8,128)(2,1)S(1)}, u32[]{:S(2)}, u32[]{:S(2)}) collective-permute-start(bf16[128,1600]{1,0:T(8,128)(2,1)S(1)} %collective-permute-done.29), channel_id=1, source_target_pairs={{0,2},{1,3},{4,0},{5,1},{8,4},{9,5},{12,8},{13,9},{14,12},{15,13},... | collective-permute-start | bytes 1228808 | tf_op jit(solution)/shard_map/ppermute | solution.py:38
  278.0 26.3 %collective-permute-start.33 = (bf16[128,1600]{1,0:T(8,128)(2,1)S(1)}, bf16[128,1600]{1,0:T(8,128)(2,1)S(1)}, u32[]{:S(2)}, u32[]{:S(2)}) collective-permute-start(bf16[128,1600]{1,0:T(8,128)(2,1)S(1)} %collective-permute-done.32), channel_id=1, source_target_pairs={{0,4},{1,5},{4,8},{5,9},{8,12},{9,13},{12,14},{13,15},{14,10},{15,... | collective-permute-start | bytes 1228808 | tf_op jit(solution)/shard_map/ppermute | solution.py:38
  349.8 200.0 %collective-permute-start.102 = (f32[1600,400]{0,1:T(8,128)}, f32[1600,400]{0,1:T(8,128)}, u32[]{:S(2)}, u32[]{:S(2)}) collective-permute-start(f32[1600,400]{0,1:T(8,128)} %fusion.49), channel_id=1, source_target_pairs={{0,1},{1,0},{2,3},{3,2},{4,5},{5,4},{6,7},{7,6},{8,9},{9,8},{10,11... | collective-permute-start | bytes 7680008 | tf_op jit(solution)/shard_map/ppermute | solution.py:42
  350.0 94.6 %collective-permute-start.107 = (f32[400]{0:T(512)S(1)}, f32[400]{0:T(512)S(1)}, u32[]{:S(2)}, u32[]{:S(2)}) collective-permute-start(f32[400]{0:T(512)S(1)} %slice_add_fusion.22), channel_id=1, source_target_pairs={{0,16},{16,0},{1,17},{17,1},{2,18},{18,2},{3,19},{19,3},{4,20},{20... | collective-permute-start | bytes 4808 | tf_op jit(solution)/shard_map/ppermute | solution.py:46
  355.8 19.9 %collective-permute-start.63 = (bf16[128,1600]{1,0:T(8,128)(2,1)S(1)}, bf16[128,1600]{1,0:T(8,128)(2,1)S(1)}, u32[]{:S(2)}, u32[]{:S(2)}) collective-permute-start(bf16[128,1600]{1,0:T(8,128)(2,1)S(1)} %pad_maximum_fusion.15), channel_id=1, source_target_pairs={{0,2},{1,3},{4,0},{5,1},{8,4},{9,5},{12,8},{13,9},{14,12},{15,13},... | collective-permute-start | bytes 1228808 | tf_op jit(solution)/shard_map/ppermute | solution.py:38
  357.7 16.1 %collective-permute-start.43 = (bf16[128,1600]{1,0:T(8,128)(2,1)S(1)}, bf16[128,1600]{1,0:T(8,128)(2,1)S(1)}, u32[]{:S(2)}, u32[]{:S(2)}) collective-permute-start(bf16[128,1600]{1,0:T(8,128)(2,1)S(1)} %pad_maximum_fusion.12), channel_id=1, source_target_pairs={{0,4},{1,5},{4,8},{5,9},{8,12},{9,13},{12,14},{13,15},{14,10},{15,... | collective-permute-start | bytes 1228808 | tf_op jit(solution)/shard_map/ppermute | solution.py:38
  365.0 23.4 %collective-permute-start.47 = (bf16[128,1600]{1,0:T(8,128)(2,1)S(1)}, bf16[128,1600]{1,0:T(8,128)(2,1)S(1)}, u32[]{:S(2)}, u32[]{:S(2)}) collective-permute-start(bf16[128,1600]{1,0:T(8,128)(2,1)S(1)} %pad_maximum_fusion.13), channel_id=1, source_target_pairs={{0,2},{1,3},{4,0},{5,1},{8,4},{9,5},{12,8},{13,9},{14,12},{15,13},... | collective-permute-start | bytes 1228808 | tf_op jit(solution)/shard_map/ppermute | solution.py:38
  375.7 19.8 %collective-permute-start.44 = (bf16[128,1600]{1,0:T(8,128)(2,1)S(1)}, bf16[128,1600]{1,0:T(8,128)(2,1)S(1)}, u32[]{:S(2)}, u32[]{:S(2)}) collective-permute-start(bf16[128,1600]{1,0:T(8,128)(2,1)S(1)} %fusion.40), channel_id=1, source_target_pairs={{0,4},{1,5},{4,8},{5,9},{8,12},{9,13},{12,14},{13,15},{14,10},{15,... | collective-permute-start | bytes 1228808 | tf_op jit(solution)/shard_map/ppermute | solution.py:38
  388.3 19.2 %collective-permute-start.61 = (bf16[128,1600]{1,0:T(8,128)(2,1)S(1)}, bf16[128,1600]{1,0:T(8,128)(2,1)S(1)}, u32[]{:S(2)}, u32[]{:S(2)}) collective-permute-start(bf16[128,1600]{1,0:T(8,128)(2,1)S(1)} %get-tuple-element.86), channel_id=1, source_target_pairs={{0,4},{1,5},{4,8},{5,9},{8,12},{9,13},{12,14},{13,15},{14,10},{15,... | collective-permute-start | bytes 1228808 | tf_op jit(solution)/shard_map/ppermute | solution.py:38
  397.5 21.5 %collective-permute-start.45 = (bf16[128,1600]{1,0:T(8,128)(2,1)S(1)}, bf16[128,1600]{1,0:T(8,128)(2,1)S(1)}, u32[]{:S(2)}, u32[]{:S(2)}) collective-permute-start(bf16[128,1600]{1,0:T(8,128)(2,1)S(1)} %get-tuple-element.90), channel_id=1, source_target_pairs={{0,4},{1,5},{4,8},{5,9},{8,12},{9,13},{12,14},{13,15},{14,10},{15,... | collective-permute-start | bytes 1228808 | tf_op jit(solution)/shard_map/ppermute | solution.py:38
  439.7 19.7 %collective-permute-start.66 = (bf16[2,128,1664]{2,1,0:T(8,128)(2,1)S(1)}, bf16[2,128,1664]{2,1,0:T(8,128)(2,1)}, u32[]{:S(2)}, u32[]{:S(2)}) collective-permute-start(bf16[2,128,1664]{2,1,0:T(8,128)(2,1)S(1)} %get-tuple-element.24), channel_id=1, source_target_pairs={{0,1},{1,0},{2,3},{3,2},{4,5},{5,4},{6,7},{7,6},{8,9},{9,8},{10,11... | collective-permute-start | bytes 2555912 | tf_op jit(solution)/shard_map/ppermute | solution.py:42
  444.1 116.0 %collective-permute-start.104 = (f32[400,1600]{1,0:T(8,128)}, f32[400,1600]{1,0:T(8,128)}, u32[]{:S(2)}, u32[]{:S(2)}) collective-permute-start(f32[400,1600]{1,0:T(8,128)} %fusion.46), channel_id=1, source_target_pairs={{0,1},{1,0},{2,3},{3,2},{4,5},{5,4},{6,7},{7,6},{8,9},{9,8},{10,11... | collective-permute-start | bytes 7680008 | tf_op jit(solution)/shard_map/ppermute | solution.py:42
  462.7 26.4 %collective-permute-start.67 = (bf16[2,128,1664]{2,1,0:T(8,128)(2,1)S(1)}, bf16[2,128,1664]{2,1,0:T(8,128)(2,1)S(1)}, u32[]{:S(2)}, u32[]{:S(2)}) collective-permute-start(bf16[2,128,1664]{2,1,0:T(8,128)(2,1)S(1)} %fusion.18), channel_id=1, source_target_pairs={{2,0},{3,1},{4,2},{5,3},{6,4},{7,5},{8,6},{9,7},{10,8},{11,9},{12,... | collective-permute-start | bytes 2555912 | tf_op jit(solution)/shard_map/ppermute | solution.py:51
  466.3 19.7 %collective-permute-start.99 = (bf16[128,200]{1,0:T(8,128)(2,1)S(1)}, bf16[128,200]{1,0:T(8,128)(2,1)S(1)}, u32[]{:S(2)}, u32[]{:S(2)}) collective-permute-start(bf16[128,200]{1,0:T(8,128)(2,1)S(1)} %get-tuple-element.126), channel_id=1, source_target_pairs={{0,4},{1,5},{4,8},{5,9},{8,12},{9,13},{12,14},{13,15},{14,10},{15,... | collective-permute-start | bytes 153608 | tf_op jit(solution)/shard_map/ppermute | solution.py:38
  489.0 53.0 %collective-permute-start.100 = (f32[1600,100]{0,1:T(8,128)S(1)}, f32[1600,100]{0,1:T(8,128)S(1)}, u32[]{:S(2)}, u32[]{:S(2)}) collective-permute-start(f32[1600,100]{0,1:T(8,128)S(1)} %fusion.63), channel_id=1, source_target_pairs={{0,1},{1,0},{2,3},{3,2},{4,5},{5,4},{6,7},{7,6},{8,9},{9,8},{10,11... | collective-permute-start | bytes 1920008 | tf_op jit(solution)/shard_map/ppermute | solution.py:42
  512.7 18.1 %collective-permute-start.72 = (bf16[128,600]{1,0:T(8,128)(2,1)S(1)}, bf16[128,600]{1,0:T(8,128)(2,1)S(1)}, u32[]{:S(2)}, u32[]{:S(2)}) collective-permute-start(bf16[128,600]{1,0:T(8,128)(2,1)S(1)} %get-tuple-element.112), channel_id=1, source_target_pairs={{0,12},{1,13},{4,14},{5,15},{8,10},{9,11},{12,6},{13,7},{14,2},{15... | collective-permute-start | bytes 460808 | tf_op jit(solution)/shard_map/ppermute | solution.py:38
  544.9 26.4 %collective-permute-start.101 = (bf16[800,100]{0,1:T(8,128)(2,1)S(1)}, bf16[800,100]{0,1:T(8,128)(2,1)S(1)}, u32[]{:S(2)}, u32[]{:S(2)}) collective-permute-start(bf16[800,100]{0,1:T(8,128)(2,1)S(1)} %dynamic-slice_convert_fusion.2), channel_id=1, source_target_pairs={{0,16},{16,0},{1,17},{17,1},{2,18},{18,2},{3,19},{19,3},{4,20},{20... | collective-permute-start | bytes 480008 | tf_op jit(solution)/shard_map/ppermute | solution.py:46
  554.6 47.8 %collective-permute-start.103 = (bf16[800,400]{0,1:T(8,128)(2,1)}, bf16[800,400]{0,1:T(8,128)(2,1)}, u32[]{:S(2)}, u32[]{:S(2)}) collective-permute-start(bf16[800,400]{0,1:T(8,128)(2,1)} %dynamic-slice_convert_fusion), channel_id=1, source_target_pairs={{0,16},{16,0},{1,17},{17,1},{2,18},{18,2},{3,19},{19,3},{4,20},{20... | collective-permute-start | bytes 1920008 | tf_op jit(solution)/shard_map/ppermute | solution.py:46
  564.1 22.2 %collective-permute-start.105 = (bf16[400,800]{1,0:T(8,128)(2,1)S(1)}, bf16[400,800]{1,0:T(8,128)(2,1)S(1)}, u32[]{:S(2)}, u32[]{:S(2)}) collective-permute-start(bf16[400,800]{1,0:T(8,128)(2,1)S(1)} %slice.653), channel_id=1, source_target_pairs={{0,16},{16,0},{1,17},{17,1},{2,18},{18,2},{3,19},{19,3},{4,20},{20... | collective-permute-start | bytes 1920008 | tf_op jit(solution)/shard_map/ppermute | solution.py:46
  571.2 19.3 %collective-permute-start.83 = (f32[1600,300]{0,1:T(8,128)S(1)}, f32[1600,300]{0,1:T(8,128)S(1)}, u32[]{:S(2)}, u32[]{:S(2)}) collective-permute-start(f32[1600,300]{0,1:T(8,128)S(1)} %fusion.52), channel_id=1, source_target_pairs={{0,1},{1,0},{2,3},{3,2},{4,5},{5,4},{6,7},{7,6},{8,9},{9,8},{10,11... | collective-permute-start | bytes 5760008 | tf_op jit(solution)/shard_map/ppermute | solution.py:42
  593.0 17.4 %collective-permute-start.84 = (bf16[800,300]{0,1:T(8,128)(2,1)}, bf16[800,300]{0,1:T(8,128)(2,1)S(1)}, u32[]{:S(2)}, u32[]{:S(2)}) collective-permute-start(bf16[800,300]{0,1:T(8,128)(2,1)} %dynamic-slice_convert_fusion.1), channel_id=1, source_target_pairs={{0,16},{16,0},{1,17},{17,1},{2,18},{18,2},{3,19},{19,3},{4,20},{20... | collective-permute-start | bytes 1440008 | tf_op jit(solution)/shard_map/ppermute | solution.py:46
  (120 other events, 1496.9 us)

commit v2 on v1

v2 whole, which is shorter than its diff:
```python
import functools

import jax
import jax.numpy as jnp
from jax import lax
from jax.experimental import pallas as pl
from jax.experimental.pallas import tpu as pltpu
from jax.sharding import PartitionSpec as P

H = 25
REACH = 2
LANES = 128

norm_epsilon = 1e-05
gelu_scale = 0.7978845608028654
masked_score = -1e30
bf16 = jnp.bfloat16
f32 = jnp.float32
vmem_bytes = 48 * 1024 * 1024


def chip_at(place, chips):
    place %= chips
    return 2 * place if place < chips // 2 else 2 * (chips - 1 - place) + 1


def place_of(chip, chips):
    return chip // 2 if chip % 2 == 0 else chips - 1 - chip // 2


def send(value, by):
    chips = lax.axis_size("ctx") // 2
    pairs = [
        (chip_at(p, chips) * 2 + core, chip_at(p + by, chips) * 2 + core)
        for p in range(chips)
        for core in range(2)
    ]
    return lax.ppermute(value, "ctx", pairs)


def core_swap(value):
    return lax.ppermute(value, "ctx", [(i, i ^ 1) for i in range(lax.axis_size("ctx"))])


def data_swap(value):
    return lax.ppermute(value, "dp", [(i, i ^ 1) for i in range(lax.axis_size("dp"))])


def shifted(value, by):
    count = lax.axis_size("ctx")
    return lax.ppermute(
        value, "ctx", [(i, i + by) for i in range(count) if 0 <= i + by < count]
    )


def after(value, *others):
    return lax.optimization_barrier((value, others))[0]


def ring_gather(blocks, waits=None):
    chips = lax.axis_size("ctx") // 2
    waits = waits or {}
    found = [[None] * chips for _ in blocks]
    left, right = list(blocks), list(blocks)
    for step in range(1, chips // 2 + 1):
        before = waits.get(step)
        for number, block in enumerate(blocks):
            one, two = left[number], right[number]
            if before is not None:
                one, two = after((one, two), before)
            if step < chips // 2:
                one, two = send(one, 1), send(two, -1)
                found[number][chips - step], found[number][step] = one, two
                left[number], right[number] = one, two
            else:
                middle = block.shape[0] // 16 * 8
                ends = [send(one[:middle], 1), send(two[middle:], -1)]
                found[number][step] = jnp.concatenate(ends, axis=0)
            if number + 1 < len(blocks):
                before = (one, two)
    for number, block in enumerate(blocks):
        found[number][0] = block
    return found


def ring_scatter(part, chips, rows, split):
    size = rows // split
    half = split // 2
    middle = rows // 2
    ahead, back = [None] * split, [None] * split
    token = yield None
    for step in range(chips // 2, 0, -1):
        sent = []
        for i in range(split):
            for got, o, by in ((ahead, step, 1), (back, chips - step, -1)):
                first, count = i * size, size
                if step == chips // 2:
                    if split == 1:
                        first, count = (0, middle) if by == 1 else (middle, middle)
                    elif (i < half) != (by == 1):
                        continue
                piece = part(o, first, count)
                if got[i] is None:
                    piece = piece if token is None else after(piece, token)
                else:
                    arrived = after(got[i], token).astype(f32)
                    if arrived.shape[0] < count:
                        if by == 1:
                            piece = jnp.concatenate([piece[:middle] + arrived, piece[middle:]], 0)
                        else:
                            piece = jnp.concatenate([piece[:middle], piece[middle:] + arrived], 0)
                    else:
                        piece = piece + arrived
                piece = piece.astype(bf16)
                got[i] = send(piece, by)
                token = piece
                sent.append(piece)
        more = yield sent
        token = (token, more)
    yield (
        part(0, 0, rows)
        + jnp.concatenate(ahead, axis=0).astype(f32)
        + jnp.concatenate(back, axis=0).astype(f32)
    )


def ring_exchange(piece, chips):
    got = [None] * chips
    got[0] = piece(0)
    for step in range(chips // 2, 0, -1):
        for o in {step, chips - step}:
            got[o] = send(piece(o), o)
    return got


def layer_norm(values, norm_gain, norm_shift):
    center = jnp.mean(values, axis=-1, keepdims=True)
    deviation = values - center
    variance = jnp.mean(deviation * deviation, axis=-1, keepdims=True)
    return deviation * lax.rsqrt(variance + norm_epsilon) * norm_gain + norm_shift


def gelu_curve(values):
    return (
        0.5 * values * (1.0 + jnp.tanh(gelu_scale * (values + 0.044715 * values * values * values)))
    )


def rows_by_rows(left_side, right_side):
    return lax.dot_general(
        left_side, right_side, (((0,), (0,)), ((), ())), preferred_element_type=f32
    )


def cols_by_cols(left_side, right_side):
    return lax.dot_general(
        left_side, right_side, (((1,), (1,)), ((), ())), preferred_element_type=f32
    )


def times(left_side, right_side):
    return jnp.dot(left_side, right_side, preferred_element_type=f32)


def spans(first, last, widths):
    found, base = [], 0
    for number, width in enumerate(widths):
        low, high = max(first, base), min(last, base + width)
        if low < high:
            found.append((number, low - base, high - base))
        base += width
    return found


def join_kernel(widths, odd_core, pieces, query, pair):
    chips, rows, both = pieces.shape
    outs = (query, pair.at[0], pair.at[1])
    width = both // 2
    odd = odd_core[0] == 1
    for out, valid in zip(outs, widths):
        padded = out.shape[-1]
        out[:, valid:] = jnp.zeros((rows, padded - valid), out.dtype)
    for chip in range(chips):
        piece = pieces[chip].astype(f32)
        piece = jnp.where(
            odd, jnp.concatenate([piece[:, width:], piece[:, :width]], axis=1), piece
        )
        first = chip * both
        done = 0
        for number, low, high in spans(first, first + both, widths):
            outs[number][:, low:high] = piece[:, done : done + high - low].astype(
                outs[number].dtype
            )
            done += high - low


def join_columns(pieces, odd_core, widths, padded):
    rows = pieces.shape[1]
    return pl.pallas_call(
        functools.partial(join_kernel, widths),
        out_shape=[
            jax.ShapeDtypeStruct((rows, padded), pieces.dtype),
            jax.ShapeDtypeStruct((2, rows, padded), pieces.dtype),
        ],
        in_specs=[
            pl.BlockSpec(memory_space=pltpu.SMEM),
            pl.BlockSpec(memory_space=pltpu.VMEM),
        ],
        out_specs=[pl.BlockSpec(memory_space=pltpu.VMEM) for _ in range(2)],
        compiler_params=pltpu.CompilerParams(vmem_limit_bytes=vmem_bytes),
    )(odd_core, pieces)


def join_weight_kernel(odd_core, own, other, out, whole):
    chips, rows, columns = own.shape
    odd = odd_core[0] == 1
    for chip in range(chips):
        one = own[chip].astype(f32)
        two = other[chip].astype(f32)
        first = 2 * chip * rows
        whole[first : first + rows] = jnp.where(odd, two, one)
        whole[first + rows : first + 2 * rows] = jnp.where(odd, one, two)
    out[...] = whole[...].astype(out.dtype)


def join_weight(own, other, odd_core):
    chips, rows, columns = own.shape
    return pl.pallas_call(
        join_weight_kernel,
        grid=(columns // LANES,),
        out_shape=jax.ShapeDtypeStruct((2 * chips * rows, columns), own.dtype),
        in_specs=[
            pl.BlockSpec(memory_space=pltpu.SMEM),
            pl.BlockSpec((chips, rows, LANES), lambda i: (0, 0, i)),
            pl.BlockSpec((chips, rows, LANES), lambda i: (0, 0, i)),
        ],
        out_specs=pl.BlockSpec((2 * chips * rows, LANES), lambda i: (0, i)),
        scratch_shapes=[pltpu.VMEM((2 * chips * rows, LANES), f32)],
        compiler_params=pltpu.CompilerParams(vmem_limit_bytes=vmem_bytes),
    )(odd_core, own, other)


def cut_kernel(groups, odd_core, *refs):
    sources, out = refs[:-1], refs[-1]
    chips = out.shape[0]
    odd = odd_core[0] == 1
    for chip in range(chips):
        base = column = 0
        for widths in groups:
            both = sum(widths) // chips
            width = both // 2
            parts = [
                sources[base + number][:, low:high].astype(f32)
                for number, low, high in spans(chip * both, (chip + 1) * both, widths)
            ]
            piece = parts[0] if len(parts) == 1 else jnp.concatenate(parts, axis=1)
            piece = jnp.where(
                odd, jnp.concatenate([piece[:, width:], piece[:, :width]], axis=1), piece
            )
            out[chip, :, column : column + both] = piece.astype(out.dtype)
            base += len(widths)
            column += both


def cut_columns(sources, odd_core, groups, chips):
    rows = sources[0].shape[0]
    columns = sum(sum(widths) for widths in groups) // chips
    return pl.pallas_call(
        functools.partial(cut_kernel, groups),
        out_shape=jax.ShapeDtypeStruct((chips, rows, columns), bf16),
        in_specs=[pl.BlockSpec(memory_space=pltpu.SMEM)]
        + [pl.BlockSpec(memory_space=pltpu.VMEM) for _ in sources],
        out_specs=pl.BlockSpec(memory_space=pltpu.VMEM),
        compiler_params=pltpu.CompilerParams(vmem_limit_bytes=vmem_bytes),
    )(odd_core, *sources)


def both_heads(pair):
    lane = lax.broadcasted_iota(jnp.int32, pair.shape, 1)
    zero = jnp.zeros_like(pair)
    low = lane < LANES // 2
    return jnp.concatenate([jnp.where(low, pair, zero), jnp.where(low, zero, pair)], axis=0)


def one_pair(stacked):
    rows = stacked.shape[0] // 2
    lane = lax.broadcasted_iota(jnp.int32, (rows, stacked.shape[1]), 1)
    return jnp.where(lane < LANES // 2, stacked[:rows], stacked[rows:])


def forward_kernel(scale, bias, query, far, near, own, mixed, log_total):
    stacked = both_heads(query[...])
    keys = jnp.concatenate([far[0], near[0], own[0]], axis=0)
    values = jnp.concatenate([far[1], near[1], own[1]], axis=0)
    scores = cols_by_cols(stacked, keys) * scale + bias[...]
    row_max = jnp.max(scores, axis=1, keepdims=True)
    raised = jnp.exp(scores - row_max)
    log_sum = row_max + jnp.log(jnp.sum(raised, axis=1, keepdims=True))
    weights = jnp.exp(scores - log_sum).astype(bf16)
    mixed[...] = one_pair(times(weights, values)).astype(bf16)
    log_total[0] = log_sum


def backward_kernel(
    scale, bias, query, far, near, own, log_total, mixed, mixed_back, query_back, far_back,
    near_back, own_back
):
    rows = query.shape[0]
    stacked = both_heads(query[...])
    keys = jnp.concatenate([far[0], near[0], own[0]], axis=0)
    values = jnp.concatenate([far[1], near[1], own[1]], axis=0)
    scores = cols_by_cols(stacked, keys) * scale + bias[...]
    weights = jnp.exp(scores - log_total[0])
    back = both_heads(mixed_back[...])
    product = back.astype(f32) * both_heads(mixed[...]).astype(f32)
    row_delta = jnp.sum(product, axis=1, keepdims=True)
    weight_back = cols_by_cols(back, values)
    score_back = (weights * (weight_back - row_delta)).astype(bf16)
    query_back[...] = one_pair(times(score_back, keys)) * scale
    key_back = rows_by_rows(score_back, stacked) * scale
    value_back = rows_by_rows(weights.astype(bf16), back)
    for number, ref in enumerate((far_back, near_back, own_back)):
        ref[0] = key_back[number * rows : (number + 1) * rows].astype(ref.dtype)
        ref[1] = value_back[number * rows : (number + 1) * rows].astype(ref.dtype)


def attention_specs(rows, window):
    wide = pl.BlockSpec((rows, LANES), lambda p: (0, p))
    pair = pl.BlockSpec((2, rows, LANES), lambda p: (0, 0, p))
    bias = pl.BlockSpec((2 * rows, window), lambda p: (0, 0))
    total = pl.BlockSpec((1, 2 * rows, 1), lambda p: (p, 0, 0))
    return wide, pair, bias, total


def attend_forward(bias, query, far, near, own, scale):
    rows, padded = query.shape
    wide, pair, bias_spec, total = attention_specs(rows, bias.shape[1])
    return pl.pallas_call(
        functools.partial(forward_kernel, scale),
        grid=(padded // LANES,),
        out_shape=[
            jax.ShapeDtypeStruct((rows, padded), bf16),
            jax.ShapeDtypeStruct((padded // LANES, 2 * rows, 1), f32),
        ],
        in_specs=[bias_spec, wide, pair, pair, pair],
        out_specs=[wide, total],
        compiler_params=pltpu.CompilerParams(vmem_limit_bytes=vmem_bytes),
    )(bias, query, far, near, own)


def attend_backward(bias, query, far, near, own, log_total, mixed, mixed_back, scale):
    rows, padded = query.shape
    wide, pair, bias_spec, total = attention_specs(rows, bias.shape[1])
    return pl.pallas_call(
        functools.partial(backward_kernel, scale),
        grid=(padded // LANES,),
        out_shape=[
            jax.ShapeDtypeStruct((rows, padded), f32),
            jax.ShapeDtypeStruct((2, rows, padded), f32),
            jax.ShapeDtypeStruct((2, rows, padded), bf16),
            jax.ShapeDtypeStruct((2, rows, padded), f32),
        ],
        in_specs=[bias_spec, wide, pair, pair, pair, total, wide, wide],
        out_specs=[wide, pair, pair, pair],
        compiler_params=pltpu.CompilerParams(vmem_limit_bytes=vmem_bytes),
    )(bias, query, far, near, own, log_total, mixed, mixed_back)


def standardised(values):
    center = jnp.mean(values, axis=-1, keepdims=True)
    deviation = values - center
    variance = jnp.mean(deviation * deviation, axis=-1, keepdims=True)
    return deviation * lax.rsqrt(variance + norm_epsilon)


def feed_forward_kernel(
    chip, attended, inputs, cotangent, output_full, up_own, up_mate, down_own, down_mate, shift,
    vectors, normed, hidden_own, hidden_mate, back_own, back_mate, parts, bias_sum, residual_own
):
    step = pl.program_id(0)
    rows, features = residual_own.shape
    plain = inputs[:, :rows].astype(f32).reshape(-1, features)
    residual = plain + cols_by_cols(attended[...], output_full[...]) + vectors[0:1]
    for part in range(attended.shape[0] // rows):

        @pl.when(chip[0] == step * (attended.shape[0] // rows) + part)
        def _():
            residual_own[...] = residual[part * rows : (part + 1) * rows]

    normed_low = (standardised(residual) * vectors[1:2] + vectors[2:3]).astype(bf16)
    normed[...] = normed_low
    product = None

    @pl.when(step == 0)
    def _():
        bias_sum[...] = jnp.zeros_like(bias_sum)

    for number, (up, down, hidden, up_back) in enumerate(
        ((up_own, down_own, hidden_own, back_own), (up_mate, down_mate, hidden_mate, back_mate))
    ):
        value = cols_by_cols(normed_low, up[...]) + shift[number : number + 1]
        square = value * value
        bent = jnp.tanh(gelu_scale * (value + 0.044715 * square * value))
        hidden[...] = (0.5 * value * (1.0 + bent)).astype(bf16)
        slope = 0.5 * (1.0 + bent) + 0.5 * value * (1.0 - bent * bent) * (
            gelu_scale * (1.0 + 3.0 * 0.044715 * square)
        )
        back = (cols_by_cols(cotangent[...], down[...]) * slope).astype(bf16)
        up_back[...] = back
        bias_sum[number : number + 1] += jnp.sum(back.astype(f32), axis=0, keepdims=True)
        term = times(back, up[...])
        product = term if product is None else product + term
    parts[...] = product


def feed_forward(
    chip, attended, inputs, cotangent, output_full, up_own, up_mate, down_own, down_mate, shift,
    vectors, rows
):
    total, padded = attended.shape
    features = inputs.shape[2]
    units = up_own.shape[0]
    block = 2 * rows
    along = lambda columns: pl.BlockSpec((block, columns), lambda i: (i, 0))
    whole = lambda shape: pl.BlockSpec(shape, lambda i: (0, 0))
    return pl.pallas_call(
        feed_forward_kernel,
        grid=(total // block,),
        out_shape=[jax.ShapeDtypeStruct((total, features), bf16)]
        + [jax.ShapeDtypeStruct((total, units), bf16) for _ in range(4)]
        + [
            jax.ShapeDtypeStruct((total, features), f32),
            jax.ShapeDtypeStruct(shift.shape, f32),
            jax.ShapeDtypeStruct((rows, features), f32),
        ],
        in_specs=[
            pl.BlockSpec(memory_space=pltpu.SMEM),
            along(padded),
            pl.BlockSpec((block // rows,) + inputs.shape[1:], lambda i: (i, 0, 0)),
            along(features),
            whole(output_full.shape),
            whole(up_own.shape),
            whole(up_own.shape),
            whole(up_own.shape),
            whole(up_own.shape),
            whole(shift.shape),
            whole(vectors.shape),
        ],
        out_specs=[along(features)]
        + [along(units) for _ in range(4)]
        + [along(features), whole(shift.shape), whole((rows, features))],
        compiler_params=pltpu.CompilerParams(vmem_limit_bytes=vmem_bytes),
    )(
        chip, attended, inputs, cotangent, output_full, up_own, up_mate, down_own, down_mate,
        shift, vectors
    )


def back_through_kernel(rows, back, weight, inputs, parts, sums):
    columns = weight.shape[0]
    product = times(back[:, :columns], weight[...])
    parts[...] = product

    @pl.when(pl.program_id(0) == 0)
    def _():
        sums[...] = jnp.zeros_like(sums)

    plain = standardised(inputs[:, :rows].astype(f32).reshape(product.shape))
    sums[0:1] += jnp.sum(product * plain, axis=0, keepdims=True)
    sums[1:2] += jnp.sum(product, axis=0, keepdims=True)


def back_through(back, weight, inputs, rows):
    total = back.shape[0]
    features = inputs.shape[2]
    block = 2 * rows
    along = lambda columns: pl.BlockSpec((block, columns), lambda i: (i, 0))
    return pl.pallas_call(
        functools.partial(back_through_kernel, rows),
        grid=(total // block,),
        out_shape=[
            jax.ShapeDtypeStruct((total, features), f32),
            jax.ShapeDtypeStruct((8, features), f32),
        ],
        in_specs=[
            along(back.shape[1]),
            pl.BlockSpec(weight.shape, lambda i: (0, 0)),
            pl.BlockSpec((block // rows,) + inputs.shape[1:], lambda i: (i, 0, 0)),
        ],
        out_specs=[along(features), pl.BlockSpec((8, features), lambda i: (0, 0))],
        compiler_params=pltpu.CompilerParams(vmem_limit_bytes=vmem_bytes),
    )(back, weight, inputs)


def shards(
    block_input,
    segments,
    joint_weight,
    output_weight,
    up_weight,
    down_weight,
    vectors,
    up_bias,
    cotangent,
):
    rows = block_input.shape[1]
    features = block_input.shape[2]
    padded = -(-features // LANES) * LANES
    reach_rows = REACH * rows
    window = reach_rows + rows
    scale = (features // H) ** (-0.5)
    context = lax.axis_size("ctx")
    data = lax.axis_size("dp")
    chips = context // 2
    position = lax.axis_index("ctx")
    half_index = lax.axis_index("dp")
    chip = position // 2
    core = position % 2
    place = jnp.where(chip % 2 == 0, chip // 2, chips - 1 - chip // 2)
    ring_chips = jnp.array([chip_at(p, chips) for p in range(chips)], jnp.int32)
    chip_on = [ring_chips[(place + o) % chips] for o in range(chips)]
    odd_core = core.astype(jnp.int32)[None]
    first_half = half_index == 0
    first_core = core == 0

    half = features // data

    def both_halves(own):
        other = data_swap(own)
        return jnp.where(
            first_half,
            jnp.concatenate([own, other], axis=-1),
            jnp.concatenate([other, own], axis=-1),
        )

    def in_place(blocks, sign):
        count, columns = blocks[0].shape
        whole = jnp.zeros((chips * count, columns), blocks[0].dtype)
        for o in range(chips):
            first = chip_on[sign * o % chips] * count
            whole = lax.dynamic_update_slice(whole, blocks[o], (first, jnp.int32(0)))
        return whole

    def block_of(matrix):
        return lambda o, first=0, count=rows: lax.dynamic_slice_in_dim(
            matrix, chip_on[o] * rows + first, count, 0
        )

    output_cols = output_weight.shape[1]
    with jax.named_scope("input_ring"):
        output_rows = jnp.pad(output_weight.T, ((0, output_cols % 2), (0, 0)))
        fold = output_rows.shape[0] // 2
        output_rows = jnp.concatenate([output_rows[:fold], output_rows[fold:]], axis=1)
        output_rows = jnp.pad(output_rows, ((0, -fold % 8), (0, 0)))
        input_blocks, cotangent_blocks = ring_gather(
            [jnp.concatenate([block_input[0], output_rows], axis=0), cotangent[0]]
        )
        inputs = in_place(input_blocks, 1).reshape(chips, -1, features)
        cotangent_all = in_place(cotangent_blocks, 1)
        last = input_blocks[chips // 2]
    with jax.named_scope("joint_weight"):
        joint_own = both_halves(joint_weight.T)
        joint_full = jnp.concatenate([joint_own, core_swap(joint_own)], axis=0)
    with jax.named_scope("parameters"):
        spread = jnp.broadcast_to(vectors[None], (data * context,) + vectors.shape)
        spread = lax.all_to_all(spread, ("dp", "ctx"), 0, 0, tiled=True)
        params = (
            spread.reshape((data, context) + vectors.shape)
            .transpose(0, 2, 1, 3)
            .reshape(data * vectors.shape[0], features)
            .astype(f32)
        )
    with jax.named_scope("output_weight"):
        mine = inputs[:, rows : rows + fold]
        got = data_swap(mine)
        unfold = lambda v: jnp.concatenate([v[:, :, :half], v[:, :, half:]], axis=1)[:, :output_cols]
        parity = jnp.where(
            first_half,
            jnp.concatenate([unfold(mine), unfold(got)], axis=2),
            jnp.concatenate([unfold(got), unfold(mine)], axis=2),
        )
        parity = jnp.pad(parity, ((0, 0), (0, 0), (0, padded - features)))
        output_full = join_weight(parity, core_swap(parity), odd_core)
    with jax.named_scope("feed_forward_weights"):
        up_own = both_halves(after(up_weight, last).T)
        down_own = both_halves(after(down_weight, last))
        up_mate, down_mate = core_swap(up_own), core_swap(down_own)
        up_shift = up_bias[None].astype(f32)
        up_shift = jnp.concatenate([up_shift, core_swap(up_shift)], axis=0)
        up_shift = jnp.pad(up_shift, ((0, 6), (0, 0)))

    joint_cols = joint_weight.shape[1]
    joint_bias = jnp.concatenate([params[2], jnp.zeros((features,), f32), params[3]])
    chip_bias = lax.dynamic_index_in_dim(joint_bias.reshape(chips, -1), chip, 0, keepdims=False)
    chip_bias = jnp.where(
        first_core,
        chip_bias,
        jnp.concatenate([chip_bias[joint_cols:], chip_bias[:joint_cols]]),
    )
    with jax.named_scope("projection"):
        plain = inputs[:, :rows].reshape(chips * rows, features).astype(f32)
        normed_one = layer_norm(plain, params[0], params[1]).astype(bf16)
        projected = (cols_by_cols(normed_one, joint_full) + chip_bias).astype(bf16)
    with jax.named_scope("projection_exchange"):
        joined = in_place(ring_exchange(block_of(projected), chips), -1).reshape(chips, rows, -1)
        joined = after(joined, mine)
    query, own = join_columns(joined, odd_core, (features,) * 3, padded)

    far = shifted(own, REACH)
    near = core_swap(jnp.where(first_core, own, far))
    padded_numbers = jnp.concatenate([jnp.full((reach_rows,), -1, jnp.int32), segments[0]])
    first_key = position * rows
    key_numbers = lax.dynamic_slice_in_dim(padded_numbers, first_key, window)
    key_places = jnp.arange(window, dtype=jnp.int32)
    same_document = key_numbers[None, :] == key_numbers[reach_rows:, None]
    allowed = same_document & (key_places[None, :] <= key_places[reach_rows:, None])
    bias = jnp.where(allowed, 0.0, masked_score).astype(f32)
    bias = jnp.concatenate([bias, bias], axis=0)
    attended, log_total = attend_forward(bias, query, far, near, own, scale)
    with jax.named_scope("attended_ring"):
        waits = {2: (up_own, down_own, parity), chips // 2: output_full}
        attended_all = in_place(ring_gather([attended], waits)[0], 1)

    normed_two, hidden_own, hidden_mate, back_own, back_mate, normed_parts, bias_sum, residual = (
        feed_forward(
            chip.astype(jnp.int32)[None],
            attended_all,
            inputs,
            cotangent_all,
            output_full,
            up_own,
            up_mate,
            down_own,
            down_mate,
            up_shift,
            jnp.pad(params[4:7], ((0, 5), (0, 0))),
            rows,
        )
    )
    with jax.named_scope("normed_two_back_ring"):
        ring = ring_scatter(block_of(normed_parts), chips, rows, 2)
        next(ring)
        for step in range(chips // 2):
            sent = next(ring)
            if step == 0:
                down_parts = times(hidden_own, down_own) + times(hidden_mate, down_mate)
        normed_two_back = next(ring)
    with jax.named_scope("down_ring"):
        down_ring = ring_scatter(block_of(down_parts), chips, rows, 1)
        next(down_ring)
        down_sent = down_ring.send(sent)

    rows_float = block_input[0].astype(f32)
    cotangent_float = cotangent[0].astype(f32)
    _, norm_pull = jax.vjp(layer_norm, residual, params[5], params[6])
    residual_part, gain_two_back, shift_two_back = norm_pull(after(normed_two_back, down_sent))
    residual_back = cotangent_float + residual_part
    residual_low = residual_back.astype(bf16)
    attended_back = times(residual_low, output_full).astype(bf16)
    with jax.named_scope("down_ring"):
        down_sent = next(down_ring)
    query_back, far_back, near_back, own_back = attend_backward(
        bias, query, far, near, own, log_total, attended, after(attended_back, down_sent), scale
    )
    near_got = core_swap(near_back).astype(f32)
    far_sum = jnp.where(first_core, far_back, far_back + near_got).astype(bf16)
    far_got = shifted(far_sum, -REACH).astype(f32)
    own_sum = jnp.where(first_core, own_back + near_got, own_back) + far_got
    with jax.named_scope("down_ring"):
        down_sent = down_ring.send(own_sum)

    def pieces_of(own_rows, mate_rows, columns):
        total = (
            rows_by_rows(own_rows, columns) + core_swap(rows_by_rows(mate_rows, columns))
        )[:, :features]
        one, two = total[:, :half], total[:, half:]
        return jnp.where(first_half, one, two), jnp.where(first_half, two, one).astype(bf16)

    def finish(kept, given):
        return kept + data_swap(given).astype(f32)

    with jax.named_scope("up_gradient"):
        up_gradient = finish(*pieces_of(back_own, back_mate, normed_two)).T
    with jax.named_scope("down_gradient"):
        down_gradient = finish(*pieces_of(hidden_own, hidden_mate, cotangent_all))
    bias_own = bias_sum[0] + core_swap(bias_sum[1])
    bias_gradient = bias_own + data_swap(bias_own)

    back_pieces = cut_columns(
        [query_back, own_sum[0], own_sum[1], residual_low],
        odd_core,
        ((features,) * 3, (features,)),
        chips,
    ).reshape(chips * rows, -1)
    with jax.named_scope("back_exchange"):
        back_all = in_place(ring_exchange(block_of(back_pieces), chips), -1)
    with jax.named_scope("down_ring"):
        down_sent = down_ring.send(back_all)
        for step in range(4, chips // 2):
            down_sent = next(down_ring)
        block_output = (residual + next(down_ring) + params[7]).astype(bf16)
    normed_parts, norm_sums = back_through(back_all, joint_full, inputs, rows)
    vectors_sum = jnp.stack(
        [
            norm_sums[0],
            norm_sums[1],
            jnp.sum(query_back[:, :features], axis=0),
            jnp.sum(own_sum[1][:, :features], axis=0),
            jnp.sum(residual_back, axis=0),
            gain_two_back,
            shift_two_back,
            jnp.sum(cotangent_float, axis=0),
        ]
    )
    vectors_cut = (
        vectors_sum.reshape(data, vectors.shape[0], context, vectors.shape[1])
        .transpose(0, 2, 1, 3)
        .reshape((data * context,) + vectors.shape)
    )
    with jax.named_scope("joint_gradient"):
        joint_kept, joint_given = pieces_of(
            back_all[:, :joint_cols], back_all[:, joint_cols : 2 * joint_cols], normed_one
        )
        joint_gradient = finish(joint_kept, joint_given).T
    with jax.named_scope("output_gradient"):
        first = 2 * joint_cols
        output_kept, output_given = pieces_of(
            back_all[:, first : first + output_cols], back_all[:, first + output_cols :], attended_all
        )
        output_gradient = finish(output_kept, output_given).T
    with jax.named_scope("vectors_gradient"):
        vectors_gradient = jnp.sum(
            lax.all_to_all(vectors_cut, ("dp", "ctx"), 0, 0, tiled=True), axis=0
        )
    with jax.named_scope("normed_one_back_ring"):
        ring = ring_scatter(block_of(normed_parts), chips, rows, 1)
        next(ring)
        for step in range(chips // 2):
            if step == 2:
                ring.send(joint_given)
            elif step == 3:
                ring.send((output_given, vectors_cut))
            else:
                next(ring)
        normed_one_back = next(ring)
    with jax.named_scope("input_gradient"):
        _, first_pull = jax.vjp(layer_norm, rows_float, params[0], params[1])
        input_gradient = residual_back + first_pull(normed_one_back)[0]
    return (
        block_output[None],
        input_gradient[None],
        joint_gradient,
        output_gradient,
        up_gradient,
        down_gradient,
        vectors_gradient,
        bias_gradient,
    )


def solution(mesh):
    in_specs = (
        P("dp", "ctx", None),
        P("dp", None),
        P("dp", "ctx"),
        P("dp", "ctx"),
        P("dp", "ctx"),
        P("ctx", "dp"),
        P("dp", "ctx"),
        P("ctx"),
        P("dp", "ctx", None),
    )
    out_specs = (
        P("dp", "ctx", None),
        P("dp", "ctx", None),
        P("dp", "ctx"),
        P("dp", "ctx"),
        P("dp", "ctx"),
        P("ctx", "dp"),
        P("dp", "ctx"),
        P("ctx"),
    )
    return jax.shard_map(shards, mesh=mesh, in_specs=in_specs, out_specs=out_specs, check_vma=False)
```

time: 621 us -> 533 us (0.86)
  waiting for transfers between devices: 254 us -> 165 us
  starting transfers between devices: 168 us -> 118 us
  Pallas kernels: 38.4 us -> 68.8 us
  matrix products: 55.9 us -> 35.4 us
  other arithmetic: 34.5 us -> 54.6 us
  between operations: 2.83 us -> 13.4 us
  local copies, waits for them, and re-layouts: 58.3 us -> 66.8 us
    ppermute x85 -> x68, waiting for transfers between devices: 209 us -> 140 us  [send(): return lax.ppermute(value, 'ctx', pairs)]
    ppermute x85 -> x68, starting transfers between devices: 142 us -> 90.2 us  [send(): return lax.ppermute(value, 'ctx', pairs)]
    pallas_call x3 -> x4, Pallas kernels: 13.5 us -> 47.5 us  [the longest x1 30.6 us: feed_forward(): pl.pallas_call(feed_forward_kernel, grid=(total // block,), out_shape=[ja...]
    ppermute x9, waiting for transfers between devices: 33.2 us -> 0.02 us  [data_swap(): lax.ppermute(value, 'dp', [(i, i ^ 1) for i in range(lax.axis_size('dp'))])]
    dynamic_update_slice x0 -> x36, local copies, waits for them, and re-layouts: none -> 21 us  [in_place(): whole = lax.dynamic_update_slice(whole, blocks[o], (first, jnp.int32(0)))]
    unnamed x178 -> x153, local copies, waits for them, and re-layouts: 30.9 us -> 11.8 us
    dot_general x4 -> x1, matrix products: 16.1 us -> 2.43 us  [cols_by_cols(): lax.dot_general(left_side, right_side, (((1,), (1,)), ((), ())), preferre...]
    convert_element_type x12 -> x25, other arithmetic: 3.83 us -> 16.9 us  [the longest x18 9.85 us: ring_scatter(): piece = piece.astype(bf16)]
  transfers between devices with their start and end apart: 110 -> 93, of which waited for: 51 -> 32; matrix products, arithmetic and copies ran while one was open for 21% -> 26% of each run, Pallas kernels for 6% -> 5%
where the time goes in v2:
time: 533 us; the launch traced here: 522 us
  waiting for transfers between devices  165 us (31%)
  starting transfers between devices  118 us (22%)
  Pallas kernels  68.8 us (13%)
  local copies, waits for them, and re-layouts  66.8 us (13%)
  other arithmetic  54.6 us (10%)
  matrix products  35.4 us (7%)
  between operations  13.4 us (3%)
    ppermute x68, waiting for transfers between devices, send(): return lax.ppermute(value, 'ctx', pairs)  140 us
    ppermute x68, starting transfers between devices, send(): return lax.ppermute(value, 'ctx', pairs)  90.2 us
    pallas_call x1, Pallas kernels, feed_forward(): pl.pallas_call(feed_forward_kernel, grid=(total // block,), out_shape=[ja...  30.6 us
    dot_general x8, matrix products, rows_by_rows(): lax.dot_general(left_side, right_side, (((0,), (0,)), ((), ())), preferre...  25.9 us
    dynamic_update_slice x36, local copies, waits for them, and re-layouts, in_place(): whole = lax.dynamic_update_slice(whole, blocks[o], (first, jnp.int32(0)))  21 us
    ppermute x2, waiting for transfers between devices, shifted(): lax.ppermute(value, 'ctx', [(i, i + by) for i in range(count) if 0 <= i +...  15.5 us
    pallas_call x1, Pallas kernels, attend_backward(): pl.pallas_call(functools.partial(backward_kernel, scale), grid=(padded //...  12 us
    unnamed x153, local copies, waits for them, and re-layouts  11.8 us
  transfers between devices with their start and end apart: 93, of which 32 were waited for; matrix products, arithmetic and copies ran while one was open for 26% of the time, Pallas kernels for 5%

profile of v2, /device:TPU:0, one launch (start us, length us, event | category | flops | bytes accessed | tf_op | source)
XLA Modules:
  0.0 522.1 jit_solution(9553276691531542793)
XLA Ops:
  9.0 3.0 collective-permute-start
  12.8 6.4 %all-to-all-start = ((bf16[32,4,100]{2,1,0:T(4,128)(2,1)}), bf16[32,4,100]{2,1,0:T(4,128)(2,1)S(1)}, u32[]{:S(2)}, u32[]{:S(2)}) async-start(bf16[32,4,100]{2,1,0:T(4,128)(2,1)} %broadcast_in_dim.76), calls=%async_computation | async-start | bytes 65536 | tf_op jit(solution)/shard_map/parameters/all_to_all | solution.py:566
  39.7 11.4 %collective-permute-done.4 = bf16[184,1600]{1,0:T(8,128)(2,1)} collective-permute-done((bf16[184,1600]{1,0:T(8,128)(2,1)}, bf16[184,1600]{1,0:T(8,128)(2,1)}, u32[]{:S(2)}, u32[]{:S(2)}) %collective-permute-start.4) | collective-permute-done | bytes 588832 | tf_op jit(solution)/shard_map/input_ring/ppermute | solution.py:38
  55.2 6.8 %collective-permute-done.31 = bf16[128,1600]{1,0:T(8,128)(2,1)} collective-permute-done((bf16[128,1600]{1,0:T(8,128)(2,1)S(1)}, bf16[128,1600]{1,0:T(8,128)(2,1)}, u32[]{:S(2)}, u32[]{:S(2)}) %collective-permute-start.31) | collective-permute-done | bytes 409632 | tf_op jit(solution)/shard_map/input_ring/ppermute | solution.py:38
  67.8 5.5 %collective-permute-done.5 = bf16[184,1600]{1,0:T(8,128)(2,1)S(1)} collective-permute-done((bf16[184,1600]{1,0:T(8,128)(2,1)}, bf16[184,1600]{1,0:T(8,128)(2,1)S(1)}, u32[]{:S(2)}, u32[]{:S(2)}) %collective-permute-start.5) | collective-permute-done | bytes 588832 | tf_op jit(solution)/shard_map/input_ring/ppermute | solution.py:38
  75.8 8.3 %collective-permute-done.33 = bf16[128,1600]{1,0:T(8,128)(2,1)S(1)} collective-permute-done((bf16[128,1600]{1,0:T(8,128)(2,1)}, bf16[128,1600]{1,0:T(8,128)(2,1)S(1)}, u32[]{:S(2)}, u32[]{:S(2)}) %collective-permute-start.33) | collective-permute-done | bytes 409632 | tf_op jit(solution)/shard_map/input_ring/ppermute | solution.py:38
  103.1 3.0 multiply_reduce_fusion
  113.6 2.7 collective-permute-start.15
  123.2 13.1 %collective-permute-done.15 = bf16[128,600]{0,1:T(8,128)(2,1)S(1)} collective-permute-done((bf16[128,600]{0,1:T(8,128)(2,1)S(1)}, bf16[128,600]{0,1:T(8,128)(2,1)S(1)}, u32[]{:S(2)}, u32[]{:S(2)}) %collective-permute-start.15) | collective-permute-done | bytes 153632 | tf_op jit(solution)/shard_map/projection_exchange/ppermute | solution.py:38
  137.3 2.9 fusion.36
  146.8 3.6 collective-permute-start.38
  155.1 4.1 collective-permute-start.17
  161.1 3.8 maximum_select_fusion
  165.5 6.7 %collective-permute-done.17.far = bf16[2,128,1664]{2,1,0:T(8,128)(2,1)S(1)} collective-permute-done((bf16[2,128,1664]{2,1,0:T(8,128)(2,1)S(1)}, bf16[2,128,1664]{2,1,0:T(8,128)(2,1)S(1)}, u32[]{:S(2)}, u32[]{:S(2)}) %collective-permute-start.17) | collective-permute-done | bytes 852000 | tf_op jit(solution)/shard_map/ppermute | solution.py:51
  177.3 8.2 %shard_map.162 = (bf16[128,1664]{1,0:T(8,128)(2,1)S(1)}, f32[13,256,1]{2,1,0:T(8,128)S(1)}) custom-call(f32[256,384]{1,0:T(8,128)S(1)} %pad_maximum_fusion.6.bias, bf16[128,1664]{1,0:T(8,128)(2,1)S(1)} %get-tuple-element.72.query, bf16[2,128,1664]{2,1,0:T(8,128)(2,1)S(1)} %collective-permute-done.17.far, ...), custom_call_target="tpu_custom_call" | custom-call | tf_op jit(solution)/shard_map/pallas_call | solution.py:338
  185.6 4.8 collective-permute-start.20
  190.4 2.7 maximum_select_fusion.1.up_own
  194.1 5.7 %collective-permute-done.20 = bf16[128,1664]{1,0:T(8,128)(2,1)S(1)} collective-permute-done((bf16[128,1664]{1,0:T(8,128)(2,1)S(1)}, bf16[128,1664]{1,0:T(8,128)(2,1)S(1)}, u32[]{:S(2)}, u32[]{:S(2)}) %collective-permute-start.20) | collective-permute-done | bytes 426016 | tf_op jit(solution)/shard_map/attended_ring/ppermute | solution.py:38
  205.6 7.2 %collective-permute-done.24 = bf16[128,1664]{1,0:T(8,128)(2,1)} collective-permute-done((bf16[128,1664]{1,0:T(8,128)(2,1)S(1)}, bf16[128,1664]{1,0:T(8,128)(2,1)}, u32[]{:S(2)}, u32[]{:S(2)}) %collective-permute-start.24) | collective-permute-done | bytes 426016 | tf_op jit(solution)/shard_map/attended_ring/ppermute | solution.py:38
  218.1 6.9 %output_weight.1.output_full = bf16[1600,1664]{1,0:T(8,128)(2,1)} custom-call(s32[1]{0:T(128)} %bitcast.2.odd_core, bf16[8,100,1664]{2,1,0:T(8,128)(2,1)S(1)} %pad.18.own, bf16[8,100,1664]{2,1,0:T(8,128)(2,1)S(1)} %copy.63.other), custom_call_target="tpu_custom_call" | custom-call | tf_op jit(solution)/shard_map/output_weight/pallas_call | solution.py:228
  236.7 30.6 %shard_map.163 = (bf16[1024,1600]{1,0:T(8,128)(2,1)}, bf16[1024,400]{1,0:T(8,128)(2,1)S(1)}, bf16[1024,400]{1,0:T(8,128)(2,1)S(1)}, bf16[1024,400]{1,0:T(8,128)(...) custom-call(s32[1]{0:T(128)} %bitcast.chip, ...), custom_call_target="tpu_custom_call" | custom-call | tf_op jit(solution)/shard_map/pallas_call | solution.py:426
  274.1 3.8 fusion.42
  284.6 4.0 collective-permute-done.43
  305.8 4.3 collective-permute-done.58
  312.8 3.4 collective-permute-done.54
  318.1 12.0 %shard_map.164 = (f32[128,1664]{1,0:T(8,128)S(1)}, f32[2,128,1664]{2,1,0:T(8,128)}, bf16[2,128,1664]{2,1,0:T(8,128)(2,1)S(1)}, f32[2,128,1664]{2,1,0:T(8,128)}) custom-call(f32[256,384]{1,0:T(8,128)S(1)} %pad_maximum_fusion.6.bias, bf16[128,1664]{1,0:T(8,128)(2,1)S(1)} %copy-done.11, bf16[2,128,1664]{2,1,0:T(8,128)(2,1)S(1)} %copy-done.5, ...), custom_call_target="tpu_custom_call" | custom-call | tf_op jit(solution)/shard_map/pallas_call | solution.py:354
  335.7 5.1 fusion.44
  342.5 3.3 fusion.43
  349.3 8.8 %collective-permute-done.60 = bf16[2,128,1664]{2,1,0:T(8,128)(2,1)S(1)} collective-permute-done((bf16[2,128,1664]{2,1,0:T(8,128)(2,1)S(1)}, bf16[2,128,1664]{2,1,0:T(8,128)(2,1)S(1)}, u32[]{:S(2)}, u32[]{:S(2)}) %collective-permute-start.60) | collective-permute-done | bytes 852000 | tf_op jit(solution)/shard_map/ppermute | solution.py:51
  358.4 8.0 %collective-permute-done.53 = bf16[128,1600]{1,0:T(8,128)(2,1)S(1)} collective-permute-done((bf16[128,1600]{1,0:T(8,128)(2,1)S(1)}, bf16[128,1600]{1,0:T(8,128)(2,1)S(1)}, u32[]{:S(2)}, u32[]{:S(2)}) %collective-permute-start.53) | collective-permute-done | bytes 409632 | tf_op jit(solution)/shard_map/down_ring/ppermute | solution.py:38
  376.5 3.7 convolution_add_fusion.1
  382.2 3.5 convolution_add_fusion.2
  386.9 3.2 collective-permute-done.63
  392.7 7.7 %collective-permute-start.66 = (bf16[128,800]{1,0:T(8,128)(2,1)S(1)}, bf16[128,800]{1,0:T(8,128)(2,1)S(1)}, u32[]{:S(2)}, u32[]{:S(2)}) collective-permute-start(bf16[128,800]{1,0:T(8,128)(2,1)S(1)} %get-tuple-element.192), channel_id=1, source_target_pairs={{0,14},{1,15},{4,10},{5,11},{8,6},{9,7},{12,2},{13,3},{14,0},{15,1... | collective-permute-start | bytes 614408 | tf_op jit(solution)/shard_map/back_exchange/ppermute | solution.py:38
  400.5 11.1 %collective-permute-done.66 = bf16[128,800]{1,0:T(8,128)(2,1)S(1)} collective-permute-done((bf16[128,800]{1,0:T(8,128)(2,1)S(1)}, bf16[128,800]{1,0:T(8,128)(2,1)S(1)}, u32[]{:S(2)}, u32[]{:S(2)}) %collective-permute-start.66) | collective-permute-done | bytes 204832 | tf_op jit(solution)/shard_map/back_exchange/ppermute | solution.py:38
  411.6 7.0 %collective-permute-start.68 = (bf16[128,800]{1,0:T(8,128)(2,1)S(1)}, bf16[128,800]{1,0:T(8,128)(2,1)S(1)}, u32[]{:S(2)}, u32[]{:S(2)}) collective-permute-start(bf16[128,800]{1,0:T(8,128)(2,1)S(1)} %get-tuple-element.190), channel_id=1, source_target_pairs={{0,6},{1,7},{4,2},{5,3},{8,0},{9,1},{12,4},{13,5},{14,8},{15,9},{1... | collective-permute-start | bytes 614408 | tf_op jit(solution)/shard_map/back_exchange/ppermute | solution.py:38
  420.0 10.9 %collective-permute-done.68 = bf16[128,800]{1,0:T(8,128)(2,1)S(1)} collective-permute-done((bf16[128,800]{1,0:T(8,128)(2,1)S(1)}, bf16[128,800]{1,0:T(8,128)(2,1)S(1)}, u32[]{:S(2)}, u32[]{:S(2)}) %collective-permute-start.68) | collective-permute-done | bytes 204832 | tf_op jit(solution)/shard_map/back_exchange/ppermute | solution.py:38
  432.4 2.8 fusion.12
  436.9 8.1 %shard_map.166 = (f32[1024,1600]{1,0:T(8,128)}, f32[8,1600]{1,0:T(8,128)S(1)}) custom-call(bf16[1024,800]{1,0:T(8,128)(2,1)S(1)} %constant_dynamic-update-slice_fusion.back, bf16[600,1600]{1,0:T(8,128)(2,1)S(1)} %copy-done.3, bf16[8,184,1600]{2,1,0:T(8,128)(2,1)} %bitcast.13.inputs), custom_call_target="tpu_custom_call" | custom-call | tf_op jit(solution)/shard_map/pallas_call | solution.py:478
  452.3 7.9 %all-to-all-done.1 = f32[32,4,100]{2,1,0:T(4,128)S(1)} async-done(((f32[32,4,100]{2,1,0:T(4,128)}), f32[32,4,100]{2,1,0:T(4,128)S(1)}, u32[]{:S(2)}, u32[]{:S(2)}) %all-to-all-start.1) | async-done | bytes 51232 | tf_op jit(solution)/shard_map/vectors_gradient/all_to_all | solution.py:733
  466.8 3.4 collective-permute-done.75
  474.1 2.7 convert_add_fusion
  476.8 2.6 add_bitcast_fusion
  479.4 3.9 collective-permute-done.72
  489.2 3.0 convolution_add_fusion.4
  493.8 2.9 convolution_add_fusion.3
  502.5 6.7 %collective-permute-done.77 = bf16[128,1600]{1,0:T(8,128)(2,1)S(1)} collective-permute-done((bf16[128,1600]{1,0:T(8,128)(2,1)S(1)}, bf16[128,1600]{1,0:T(8,128)(2,1)S(1)}, u32[]{:S(2)}, u32[]{:S(2)}) %collective-permute-start.77) | collective-permute-done | bytes 409632 | tf_op jit(solution)/shard_map/normed_one_back_ring/ppermute | solution.py:38
  514.8 4.6 collective-permute-done.82
  (492 shorter events, 213.1 us)
Async XLA Ops:
  9.0 26.8 %collective-permute-start = (bf16[184,1600]{1,0:T(8,128)(2,1)S(1)}, bf16[184,1600]{1,0:T(8,128)(2,1)}, u32[]{:S(2)}, u32[]{:S(2)}) collective-permute-start(bf16[184,1600]{1,0:T(8,128)(2,1)S(1)} %get-tuple-element.210), channel_id=1, source_target_pairs={{0,2},{1,3},{4,0},{5,1},{8,4},{9,5},{12,8},{13,9},{14,12},{15,13},... | collective-permute-start | bytes 1766408 | tf_op jit(solution)/shard_map/input_ring/ppermute | solution.py:38
  12.0 22.1 %collective-permute-start.3 = (bf16[184,1600]{1,0:T(8,128)(2,1)S(1)}, bf16[184,1600]{1,0:T(8,128)(2,1)}, u32[]{:S(2)}, u32[]{:S(2)}) collective-permute-start(bf16[184,1600]{1,0:T(8,128)(2,1)S(1)} %get-tuple-element.210), channel_id=1, source_target_pairs={{0,4},{1,5},{4,8},{5,9},{8,12},{9,13},{12,14},{13,15},{14,10},{15,... | collective-permute-start | bytes 1766408 | tf_op jit(solution)/shard_map/input_ring/ppermute | solution.py:38
  12.1 21.9 %collective-permute-start.41 = (f32[1,400]{1,0:T(1,128)S(1)}, f32[1,400]{1,0:T(1,128)S(1)}, u32[]{:S(2)}, u32[]{:S(2)}) collective-permute-start(f32[1,400]{1,0:T(1,128)S(1)} %bitcast.117), channel_id=1, source_target_pairs={{0,1},{1,0},{2,3},{3,2},{4,5},{5,4},{6,7},{7,6},{8,9},{9,8},{10,11... | collective-permute-start | bytes 4808 | tf_op jit(solution)/shard_map/feed_forward_weights/ppermute | solution.py:42
  12.8 21.3 %all-to-all-start = ((bf16[32,4,100]{2,1,0:T(4,128)(2,1)}), bf16[32,4,100]{2,1,0:T(4,128)(2,1)S(1)}, u32[]{:S(2)}, u32[]{:S(2)}) async-start(bf16[32,4,100]{2,1,0:T(4,128)(2,1)} %broadcast_in_dim.76), calls=%async_computation | async-start | bytes 65536 | tf_op jit(solution)/shard_map/parameters/all_to_all | solution.py:566
  19.1 17.2 %collective-permute-start.8 = (bf16[300,800]{1,0:T(8,128)(2,1)S(1)}, bf16[300,800]{1,0:T(8,128)(2,1)S(1)}, u32[]{:S(2)}, u32[]{:S(2)}) collective-permute-start(bf16[300,800]{1,0:T(8,128)(2,1)S(1)} %bitcast.112), channel_id=1, source_target_pairs={{0,16},{16,0},{1,17},{17,1},{2,18},{18,2},{3,19},{19,3},{4,20},{20... | collective-permute-start | bytes 1440008 | tf_op jit(solution)/shard_map/joint_weight/ppermute | solution.py:46
  34.1 17.1 %collective-permute-start.4 = (bf16[184,1600]{1,0:T(8,128)(2,1)}, bf16[184,1600]{1,0:T(8,128)(2,1)}, u32[]{:S(2)}, u32[]{:S(2)}) collective-permute-start(bf16[184,1600]{1,0:T(8,128)(2,1)} %collective-permute-done.3), channel_id=1, source_target_pairs={{0,4},{1,5},{4,8},{5,9},{8,12},{9,13},{12,14},{13,15},{14,10},{15,... | collective-permute-start | bytes 1766408 | tf_op jit(solution)/shard_map/input_ring/ppermute | solution.py:38
  35.8 18.9 %collective-permute-start.1 = (bf16[184,1600]{1,0:T(8,128)(2,1)}, bf16[184,1600]{1,0:T(8,128)(2,1)}, u32[]{:S(2)}, u32[]{:S(2)}) collective-permute-start(bf16[184,1600]{1,0:T(8,128)(2,1)} %collective-permute-done), channel_id=1, source_target_pairs={{0,2},{1,3},{4,0},{5,1},{8,4},{9,5},{12,8},{13,9},{14,12},{15,13},... | collective-permute-start | bytes 1766408 | tf_op jit(solution)/shard_map/input_ring/ppermute | solution.py:38
  37.0 37.9 %collective-permute-start.9 = (bf16[300,1600]{1,0:T(8,128)(2,1)S(1)}, bf16[300,1600]{1,0:T(8,128)(2,1)S(1)}, u32[]{:S(2)}, u32[]{:S(2)}) collective-permute-start(bf16[300,1600]{1,0:T(8,128)(2,1)S(1)} %maximum_select_fusion.3), channel_id=1, source_target_pairs={{0,1},{1,0},{2,3},{3,2},{4,5},{5,4},{6,7},{7,6},{8,9},{9,8},{10,11... | collective-permute-start | bytes 2880008 | tf_op jit(solution)/shard_map/joint_weight/ppermute | solution.py:42
  37.1 24.9 %collective-permute-start.31 = (bf16[128,1600]{1,0:T(8,128)(2,1)S(1)}, bf16[128,1600]{1,0:T(8,128)(2,1)}, u32[]{:S(2)}, u32[]{:S(2)}) collective-permute-start(bf16[128,1600]{1,0:T(8,128)(2,1)S(1)} %bitcast.108), channel_id=1, source_target_pairs={{0,2},{1,3},{4,0},{5,1},{8,4},{9,5},{12,8},{13,9},{14,12},{15,13},... | collective-permute-start | bytes 1228808 | tf_op jit(solution)/shard_map/input_ring/ppermute | solution.py:38
  39.1 24.7 %collective-permute-start.32 = (bf16[128,1600]{1,0:T(8,128)(2,1)S(1)}, bf16[128,1600]{1,0:T(8,128)(2,1)S(1)}, u32[]{:S(2)}, u32[]{:S(2)}) collective-permute-start(bf16[128,1600]{1,0:T(8,128)(2,1)S(1)} %bitcast.109), channel_id=1, source_target_pairs={{0,4},{1,5},{4,8},{5,9},{8,12},{9,13},{12,14},{13,15},{14,10},{15,... | collective-permute-start | bytes 1228808 | tf_op jit(solution)/shard_map/input_ring/ppermute | solution.py:38
  51.2 22.1 %collective-permute-start.5 = (bf16[184,1600]{1,0:T(8,128)(2,1)}, bf16[184,1600]{1,0:T(8,128)(2,1)S(1)}, u32[]{:S(2)}, u32[]{:S(2)}) collective-permute-start(bf16[184,1600]{1,0:T(8,128)(2,1)} %collective-permute-done.4), channel_id=1, source_target_pairs={{0,4},{1,5},{4,8},{5,9},{8,12},{9,13},{12,14},{13,15},{14,10},{15,... | collective-permute-start | bytes 1766408 | tf_op jit(solution)/shard_map/input_ring/ppermute | solution.py:38
  54.6 20.6 %collective-permute-start.2 = (bf16[184,1600]{1,0:T(8,128)(2,1)}, bf16[184,1600]{1,0:T(8,128)(2,1)S(1)}, u32[]{:S(2)}, u32[]{:S(2)}) collective-permute-start(bf16[184,1600]{1,0:T(8,128)(2,1)} %collective-permute-done.1), channel_id=1, source_target_pairs={{0,2},{1,3},{4,0},{5,1},{8,4},{9,5},{12,8},{13,9},{14,12},{15,13},... | collective-permute-start | bytes 1766408 | tf_op jit(solution)/shard_map/input_ring/ppermute | solution.py:38
  63.8 20.3 %collective-permute-start.33 = (bf16[128,1600]{1,0:T(8,128)(2,1)}, bf16[128,1600]{1,0:T(8,128)(2,1)S(1)}, u32[]{:S(2)}, u32[]{:S(2)}) collective-permute-start(bf16[128,1600]{1,0:T(8,128)(2,1)} %collective-permute-done.31), channel_id=1, source_target_pairs={{0,2},{1,3},{4,0},{5,1},{8,4},{9,5},{12,8},{13,9},{14,12},{15,13},... | collective-permute-start | bytes 1228808 | tf_op jit(solution)/shard_map/input_ring/ppermute | solution.py:38
  64.4 19.8 %collective-permute-start.34 = (bf16[128,1600]{1,0:T(8,128)(2,1)S(1)}, bf16[128,1600]{1,0:T(8,128)(2,1)S(1)}, u32[]{:S(2)}, u32[]{:S(2)}) collective-permute-start(bf16[128,1600]{1,0:T(8,128)(2,1)S(1)} %collective-permute-done.32), channel_id=1, source_target_pairs={{0,4},{1,5},{4,8},{5,9},{8,12},{9,13},{12,14},{13,15},{14,10},{15,... | collective-permute-start | bytes 1228808 | tf_op jit(solution)/shard_map/input_ring/ppermute | solution.py:38
  84.1 32.2 %collective-permute-start.35 = (bf16[128,1600]{1,0:T(8,128)(2,1)S(1)}, bf16[128,1600]{1,0:T(8,128)(2,1)S(1)}, u32[]{:S(2)}, u32[]{:S(2)}) collective-permute-start(bf16[128,1600]{1,0:T(8,128)(2,1)S(1)} %collective-permute-done.33), channel_id=1, source_target_pairs={{0,2},{1,3},{4,0},{5,1},{8,4},{9,5},{12,8},{13,9},{14,12},{15,13},... | collective-permute-start | bytes 1228808 | tf_op jit(solution)/shard_map/input_ring/ppermute | solution.py:38
  84.7 34.8 %collective-permute-start.36 = (bf16[128,1600]{1,0:T(8,128)(2,1)S(1)}, bf16[128,1600]{1,0:T(8,128)(2,1)S(1)}, u32[]{:S(2)}, u32[]{:S(2)}) collective-permute-start(bf16[128,1600]{1,0:T(8,128)(2,1)S(1)} %collective-permute-done.34), channel_id=1, source_target_pairs={{0,4},{1,5},{4,8},{5,9},{8,12},{9,13},{12,14},{13,15},{14,10},{15,... | collective-permute-start | bytes 1228808 | tf_op jit(solution)/shard_map/input_ring/ppermute | solution.py:38
  107.4 51.8 %collective-permute-start.23 = (bf16[8,50,1600]{2,0,1:T(8,128)(2,1)}, bf16[8,50,1600]{2,0,1:T(8,128)(2,1)}, u32[]{:S(2)}, u32[]{:S(2)}) collective-permute-start(bf16[8,50,1600]{2,0,1:T(8,128)(2,1)} %copy.59), channel_id=1, source_target_pairs={{0,16},{16,0},{1,17},{17,1},{2,18},{18,2},{3,19},{19,3},{4,20},{20... | collective-permute-start | bytes 3840008 | tf_op jit(solution)/shard_map/output_weight/ppermute | solution.py:46
  113.6 22.7 %collective-permute-start.15 = (bf16[128,600]{0,1:T(8,128)(2,1)S(1)}, bf16[128,600]{0,1:T(8,128)(2,1)S(1)}, u32[]{:S(2)}, u32[]{:S(2)}) collective-permute-start(bf16[128,600]{0,1:T(8,128)(2,1)S(1)} %get-tuple-element.203), channel_id=1, source_target_pairs={{0,6},{1,7},{4,2},{5,3},{8,0},{9,1},{12,4},{13,5},{14,8},{15,9},{1... | collective-permute-start | bytes 460808 | tf_op jit(solution)/shard_map/projection_exchange/ppermute | solution.py:38
  116.4 20.0 %collective-permute-start.14 = (bf16[128,600]{0,1:T(8,128)(2,1)S(1)}, bf16[128,600]{0,1:T(8,128)(2,1)S(1)}, u32[]{:S(2)}, u32[]{:S(2)}) collective-permute-start(bf16[128,600]{0,1:T(8,128)(2,1)S(1)} %get-tuple-element.204), channel_id=1, source_target_pairs={{0,10},{1,11},{4,6},{5,7},{8,2},{9,3},{12,0},{13,1},{14,4},{15,5},... | collective-permute-start | bytes 460808 | tf_op jit(solution)/shard_map/projection_exchange/ppermute | solution.py:38
  119.5 24.7 %collective-permute-start.13 = (bf16[128,600]{0,1:T(8,128)(2,1)S(1)}, bf16[128,600]{0,1:T(8,128)(2,1)}, u32[]{:S(2)}, u32[]{:S(2)}) collective-permute-start(bf16[128,600]{0,1:T(8,128)(2,1)S(1)} %get-tuple-element.205), channel_id=1, source_target_pairs={{0,14},{1,15},{4,10},{5,11},{8,6},{9,7},{12,2},{13,3},{14,0},{15,1... | collective-permute-start | bytes 460808 | tf_op jit(solution)/shard_map/projection_exchange/ppermute | solution.py:38
  122.1 24.7 %collective-permute-start.12 = (bf16[128,600]{0,1:T(8,128)(2,1)S(1)}, bf16[128,600]{0,1:T(8,128)(2,1)}, u32[]{:S(2)}, u32[]{:S(2)}) collective-permute-start(bf16[128,600]{0,1:T(8,128)(2,1)S(1)} %get-tuple-element.206), channel_id=1, source_target_pairs={{0,12},{1,13},{4,14},{5,15},{8,10},{9,11},{12,6},{13,7},{14,2},{15... | collective-permute-start | bytes 460808 | tf_op jit(solution)/shard_map/projection_exchange/ppermute | solution.py:38
  144.2 46.2 %collective-permute-start.21 = (bf16[400,800]{1,0:T(8,128)(2,1)}, bf16[400,800]{1,0:T(8,128)(2,1)}, u32[]{:S(2)}, u32[]{:S(2)}) collective-permute-start(bf16[400,800]{1,0:T(8,128)(2,1)} %bitcast.29), channel_id=1, source_target_pairs={{0,16},{16,0},{1,17},{17,1},{2,18},{18,2},{3,19},{19,3},{4,20},{20... | collective-permute-start | bytes 1920008 | tf_op jit(solution)/shard_map/feed_forward_weights/ppermute | solution.py:46
  146.8 26.5 %collective-permute-start.38 = (bf16[64,1600]{1,0:T(8,128)(2,1)}, bf16[64,1600]{1,0:T(8,128)(2,1)}, u32[]{:S(2)}, u32[]{:S(2)}) collective-permute-start(bf16[64,1600]{1,0:T(8,128)(2,1)} %slice.196), channel_id=1, source_target_pairs={{0,2},{1,3},{4,0},{5,1},{8,4},{9,5},{12,8},{13,9},{14,12},{15,13},... | collective-permute-start | bytes 614408 | tf_op jit(solution)/shard_map/input_ring/ppermute | solution.py:38
  151.5 22.4 %collective-permute-start.37 = (bf16[64,1600]{1,0:T(8,128)(2,1)}, bf16[64,1600]{1,0:T(8,128)(2,1)}, u32[]{:S(2)}, u32[]{:S(2)}) collective-permute-start(bf16[64,1600]{1,0:T(8,128)(2,1)} %slice.195), channel_id=1, source_target_pairs={{0,4},{1,5},{4,8},{5,9},{8,12},{9,13},{12,14},{13,15},{14,10},{15,... | collective-permute-start | bytes 614408 | tf_op jit(solution)/shard_map/input_ring/ppermute | solution.py:38
  155.1 17.1 %collective-permute-start.17 = (bf16[2,128,1664]{2,1,0:T(8,128)(2,1)S(1)}, bf16[2,128,1664]{2,1,0:T(8,128)(2,1)S(1)}, u32[]{:S(2)}, u32[]{:S(2)}) collective-permute-start(bf16[2,128,1664]{2,1,0:T(8,128)(2,1)S(1)} %get-tuple-element.73.own), channel_id=1, source_target_pairs={{0,2},{1,3},{2,4},{3,5},{4,6},{5,7},{6,8},{7,9},{8,10},{9,11},{10,... | collective-permute-start | bytes 2555912 | tf_op jit(solution)/shard_map/ppermute | solution.py:51
  165.4 50.5 %collective-permute-start.28 = (bf16[8,100,1664]{2,0,1:T(8,128)(2,1)S(1)}, bf16[8,100,1664]{2,0,1:T(8,128)(2,1)}, u32[]{:S(2)}, u32[]{:S(2)}) collective-permute-start(bf16[8,100,1664]{2,0,1:T(8,128)(2,1)S(1)} %copy.62), channel_id=1, source_target_pairs={{0,1},{1,0},{2,3},{3,2},{4,5},{5,4},{6,7},{7,6},{8,9},{9,8},{10,11... | collective-permute-start | bytes 7987208 | tf_op jit(solution)/shard_map/output_weight/ppermute | solution.py:42
  173.3 19.8 %collective-permute-start.22 = (bf16[400,800]{1,0:T(8,128)(2,1)S(1)}, bf16[400,800]{1,0:T(8,128)(2,1)S(1)}, u32[]{:S(2)}, u32[]{:S(2)}) collective-permute-start(bf16[400,800]{1,0:T(8,128)(2,1)S(1)} %copy-done.50), channel_id=1, source_target_pairs={{0,16},{16,0},{1,17},{17,1},{2,18},{18,2},{3,19},{19,3},{4,20},{20... | collective-permute-start | bytes 1920008 | tf_op jit(solution)/shard_map/feed_forward_weights/ppermute | solution.py:46
  204.8 29.2 %collective-permute-start.40 = (bf16[400,1600]{1,0:T(8,128)(2,1)S(1)}, bf16[400,1600]{1,0:T(8,128)(2,1)S(1)}, u32[]{:S(2)}, u32[]{:S(2)}) collective-permute-start(bf16[400,1600]{1,0:T(8,128)(2,1)S(1)} %maximum_select_fusion.2.down_own), channel_id=1, source_target_pairs={{0,1},{1,0},{2,3},{3,2},{4,5},{5,4},{6,7},{7,6},{8,9},{9,8},{10,11... | collective-permute-start | bytes 3840008 | tf_op jit(solution)/shard_map/feed_forward_weights/ppermute | solution.py:42
  204.8 29.3 %collective-permute-start.39 = (bf16[400,1600]{1,0:T(8,128)(2,1)S(1)}, bf16[400,1600]{1,0:T(8,128)(2,1)S(1)}, u32[]{:S(2)}, u32[]{:S(2)}) collective-permute-start(bf16[400,1600]{1,0:T(8,128)(2,1)S(1)} %maximum_select_fusion.1.up_own), channel_id=1, source_target_pairs={{0,1},{1,0},{2,3},{3,2},{4,5},{5,4},{6,7},{7,6},{8,9},{9,8},{10,11... | collective-permute-start | bytes 3840008 | tf_op jit(solution)/shard_map/feed_forward_weights/ppermute | solution.py:42
  334.2 23.9 %collective-permute-start.60 = (bf16[2,128,1664]{2,1,0:T(8,128)(2,1)S(1)}, bf16[2,128,1664]{2,1,0:T(8,128)(2,1)S(1)}, u32[]{:S(2)}, u32[]{:S(2)}) collective-permute-start(bf16[2,128,1664]{2,1,0:T(8,128)(2,1)S(1)} %fusion.6), channel_id=1, source_target_pairs={{2,0},{3,1},{4,2},{5,3},{6,4},{7,5},{8,6},{9,7},{10,8},{11,9},{12,... | collective-permute-start | bytes 2555912 | tf_op jit(solution)/shard_map/ppermute | solution.py:51
  340.9 34.2 %collective-permute-start.87 = (f32[400,1600]{1,0:T(8,128)}, f32[400,1600]{1,0:T(8,128)S(1)}, u32[]{:S(2)}, u32[]{:S(2)}) collective-permute-start(f32[400,1600]{1,0:T(8,128)} %fusion.44), channel_id=1, source_target_pairs={{0,1},{1,0},{2,3},{3,2},{4,5},{5,4},{6,7},{7,6},{8,9},{9,8},{10,11... | collective-permute-start | bytes 7680008 | tf_op jit(solution)/shard_map/down_gradient/ppermute | solution.py:42
  345.8 35.6 %collective-permute-start.85 = (f32[400,1600]{1,0:T(8,128)}, f32[400,1600]{1,0:T(8,128)}, u32[]{:S(2)}, u32[]{:S(2)}) collective-permute-start(f32[400,1600]{1,0:T(8,128)} %fusion.43), channel_id=1, source_target_pairs={{0,1},{1,0},{2,3},{3,2},{4,5},{5,4},{6,7},{7,6},{8,9},{9,8},{10,11... | collective-permute-start | bytes 7680008 | tf_op jit(solution)/shard_map/up_gradient/ppermute | solution.py:42
  346.5 22.0 %collective-permute-start.62 = (bf16[128,1600]{1,0:T(8,128)(2,1)S(1)}, bf16[128,1600]{1,0:T(8,128)(2,1)S(1)}, u32[]{:S(2)}, u32[]{:S(2)}) collective-permute-start(bf16[128,1600]{1,0:T(8,128)(2,1)S(1)} %pad_maximum_fusion.3), channel_id=1, source_target_pairs={{0,2},{1,3},{4,0},{5,1},{8,4},{9,5},{12,8},{13,9},{14,12},{15,13},... | collective-permute-start | bytes 1228808 | tf_op jit(solution)/shard_map/down_ring/ppermute | solution.py:38
  349.1 17.3 %collective-permute-start.53 = (bf16[128,1600]{1,0:T(8,128)(2,1)S(1)}, bf16[128,1600]{1,0:T(8,128)(2,1)S(1)}, u32[]{:S(2)}, u32[]{:S(2)}) collective-permute-start(bf16[128,1600]{1,0:T(8,128)(2,1)S(1)} %copy-done.58), channel_id=1, source_target_pairs={{0,4},{1,5},{4,8},{5,9},{8,12},{9,13},{12,14},{13,15},{14,10},{15,... | collective-permute-start | bytes 1228808 | tf_op jit(solution)/shard_map/down_ring/ppermute | solution.py:38
  368.4 92.4 %collective-permute-start.61 = (bf16[128,1600]{1,0:T(8,128)(2,1)}, bf16[128,1600]{1,0:T(8,128)(2,1)}, u32[]{:S(2)}, u32[]{:S(2)}) collective-permute-start(bf16[128,1600]{1,0:T(8,128)(2,1)} %add_convert_fusion.9), channel_id=1, source_target_pairs={{0,4},{1,5},{4,8},{5,9},{8,12},{9,13},{12,14},{13,15},{14,10},{15,... | collective-permute-start | bytes 1228808 | tf_op jit(solution)/shard_map/down_ring/ppermute | solution.py:38
  370.4 91.9 %collective-permute-start.71 = (bf16[128,1600]{1,0:T(8,128)(2,1)}, bf16[128,1600]{1,0:T(8,128)(2,1)}, u32[]{:S(2)}, u32[]{:S(2)}) collective-permute-start(bf16[128,1600]{1,0:T(8,128)(2,1)} %add_convert_fusion.8), channel_id=1, source_target_pairs={{0,2},{1,3},{4,0},{5,1},{8,4},{9,5},{12,8},{13,9},{14,12},{15,13},... | collective-permute-start | bytes 1228808 | tf_op jit(solution)/shard_map/down_ring/ppermute | solution.py:38
  375.0 57.4 %collective-permute-start.69 = (bf16[128,800]{1,0:T(8,128)(2,1)S(1)}, bf16[128,800]{1,0:T(8,128)(2,1)S(1)}, u32[]{:S(2)}, u32[]{:S(2)}) collective-permute-start(bf16[128,800]{1,0:T(8,128)(2,1)S(1)} %get-tuple-element.189), channel_id=1, source_target_pairs={{0,2},{1,3},{4,0},{5,1},{8,4},{9,5},{12,8},{13,9},{14,12},{15,13},... | collective-permute-start | bytes 614408 | tf_op jit(solution)/shard_map/back_exchange/ppermute | solution.py:38
  375.0 17.6 %collective-permute-start.64 = (bf16[128,800]{1,0:T(8,128)(2,1)S(1)}, bf16[128,800]{1,0:T(8,128)(2,1)S(1)}, u32[]{:S(2)}, u32[]{:S(2)}) collective-permute-start(bf16[128,800]{1,0:T(8,128)(2,1)S(1)} %get-tuple-element.194), channel_id=1, source_target_pairs={{0,8},{1,9},{4,12},{5,13},{8,14},{9,15},{12,10},{13,11},{14,6},{15... | collective-permute-start | bytes 614408 | tf_op jit(solution)/shard_map/back_exchange/ppermute | solution.py:38
  392.7 18.9 %collective-permute-start.66 = (bf16[128,800]{1,0:T(8,128)(2,1)S(1)}, bf16[128,800]{1,0:T(8,128)(2,1)S(1)}, u32[]{:S(2)}, u32[]{:S(2)}) collective-permute-start(bf16[128,800]{1,0:T(8,128)(2,1)S(1)} %get-tuple-element.192), channel_id=1, source_target_pairs={{0,14},{1,15},{4,10},{5,11},{8,6},{9,7},{12,2},{13,3},{14,0},{15,1... | collective-permute-start | bytes 614408 | tf_op jit(solution)/shard_map/back_exchange/ppermute | solution.py:38
  400.4 18.2 %collective-permute-start.67 = (bf16[128,800]{1,0:T(8,128)(2,1)S(1)}, bf16[128,800]{1,0:T(8,128)(2,1)S(1)}, u32[]{:S(2)}, u32[]{:S(2)}) collective-permute-start(bf16[128,800]{1,0:T(8,128)(2,1)S(1)} %get-tuple-element.191), channel_id=1, source_target_pairs={{0,10},{1,11},{4,6},{5,7},{8,2},{9,3},{12,0},{13,1},{14,4},{15,5},... | collective-permute-start | bytes 614408 | tf_op jit(solution)/shard_map/back_exchange/ppermute | solution.py:38
  411.6 19.4 %collective-permute-start.68 = (bf16[128,800]{1,0:T(8,128)(2,1)S(1)}, bf16[128,800]{1,0:T(8,128)(2,1)S(1)}, u32[]{:S(2)}, u32[]{:S(2)}) collective-permute-start(bf16[128,800]{1,0:T(8,128)(2,1)S(1)} %get-tuple-element.190), channel_id=1, source_target_pairs={{0,6},{1,7},{4,2},{5,3},{8,0},{9,1},{12,4},{13,5},{14,8},{15,9},{1... | collective-permute-start | bytes 614408 | tf_op jit(solution)/shard_map/back_exchange/ppermute | solution.py:38
  418.6 53.5 %collective-permute-start.88 = (bf16[400,800]{1,0:T(8,128)(2,1)}, bf16[400,800]{1,0:T(8,128)(2,1)}, u32[]{:S(2)}, u32[]{:S(2)}) collective-permute-start(bf16[400,800]{1,0:T(8,128)(2,1)} %select_convert_fusion), channel_id=1, source_target_pairs={{0,16},{16,0},{1,17},{17,1},{2,18},{18,2},{3,19},{19,3},{4,20},{20... | collective-permute-start | bytes 1920008 | tf_op jit(solution)/shard_map/down_gradient/ppermute | solution.py:46
  431.0 45.8 %collective-permute-start.86 = (bf16[400,800]{1,0:T(8,128)(2,1)}, bf16[400,800]{1,0:T(8,128)(2,1)}, u32[]{:S(2)}, u32[]{:S(2)}) collective-permute-start(bf16[400,800]{1,0:T(8,128)(2,1)} %select_convert_fusion.1), channel_id=1, source_target_pairs={{0,16},{16,0},{1,17},{17,1},{2,18},{18,2},{3,19},{19,3},{4,20},{20... | collective-permute-start | bytes 1920008 | tf_op jit(solution)/shard_map/up_gradient/ppermute | solution.py:46
  460.8 28.3 %collective-permute-start.79 = (f32[100,1664]{1,0:T(8,128)}, f32[100,1664]{1,0:T(8,128)}, u32[]{:S(2)}, u32[]{:S(2)}) collective-permute-start(f32[100,1664]{1,0:T(8,128)} %fusion.22), channel_id=1, source_target_pairs={{0,1},{1,0},{2,3},{3,2},{4,5},{5,4},{6,7},{7,6},{8,9},{9,8},{10,11... | collective-permute-start | bytes 1996808 | tf_op jit(solution)/shard_map/output_gradient/ppermute | solution.py:42
  464.5 29.3 %collective-permute-start.76 = (f32[300,1600]{1,0:T(8,128)}, f32[300,1600]{1,0:T(8,128)}, u32[]{:S(2)}, u32[]{:S(2)}) collective-permute-start(f32[300,1600]{1,0:T(8,128)} %fusion.12), channel_id=1, source_target_pairs={{0,1},{1,0},{2,3},{3,2},{4,5},{5,4},{6,7},{7,6},{8,9},{9,8},{10,11... | collective-permute-start | bytes 5760008 | tf_op jit(solution)/shard_map/joint_gradient/ppermute | solution.py:42
  476.8 21.2 %collective-permute-start.74 = (bf16[128,1600]{1,0:T(8,128)(2,1)}, bf16[128,1600]{1,0:T(8,128)(2,1)}, u32[]{:S(2)}, u32[]{:S(2)}) collective-permute-start(bf16[128,1600]{1,0:T(8,128)(2,1)} %pad_maximum_fusion.4), channel_id=1, source_target_pairs={{0,4},{1,5},{4,8},{5,9},{8,12},{9,13},{12,14},{13,15},{14,10},{15,... | collective-permute-start | bytes 1228808 | tf_op jit(solution)/shard_map/normed_one_back_ring/ppermute | solution.py:38
  492.3 20.2 %collective-permute-start.84 = (bf16[100,800]{1,0:T(8,128)(2,1)S(1)}, bf16[100,800]{1,0:T(8,128)(2,1)S(1)}, u32[]{:S(2)}, u32[]{:S(2)}) collective-permute-start(bf16[100,800]{1,0:T(8,128)(2,1)S(1)} %select_convert_fusion.3), channel_id=1, source_target_pairs={{0,16},{16,0},{1,17},{17,1},{2,18},{18,2},{3,19},{19,3},{4,20},{20... | collective-permute-start | bytes 480008 | tf_op jit(solution)/shard_map/output_gradient/ppermute | solution.py:46
  496.9 16.5 %collective-permute-start.83 = (bf16[300,800]{1,0:T(8,128)(2,1)S(1)}, bf16[300,800]{1,0:T(8,128)(2,1)S(1)}, u32[]{:S(2)}, u32[]{:S(2)}) collective-permute-start(bf16[300,800]{1,0:T(8,128)(2,1)S(1)} %select_convert_fusion.2), channel_id=1, source_target_pairs={{0,16},{16,0},{1,17},{17,1},{2,18},{18,2},{3,19},{19,3},{4,20},{20... | collective-permute-start | bytes 1440008 | tf_op jit(solution)/shard_map/joint_gradient/ppermute | solution.py:46
  (118 other events, 1199.5 us)

commit v3 on v2

v3 whole, which is shorter than its diff:
```python
import functools
import random

import jax
import jax.numpy as jnp
from jax import lax
from jax.experimental import pallas as pl
from jax.experimental.pallas import tpu as pltpu
from jax.sharding import PartitionSpec as P

H = 25
REACH = 2
LANES = 128

norm_epsilon = 1e-05
gelu_scale = 0.7978845608028654
masked_score = -1e30
bf16 = jnp.bfloat16
f32 = jnp.float32
vmem_bytes = 60 * 1024 * 1024
most_resident = 8


def chip_at(place, chips):
    place %= chips
    return 2 * place if place < chips // 2 else 2 * (chips - 1 - place) + 1


def place_of(chip, chips):
    return chip // 2 if chip % 2 == 0 else chips - 1 - chip // 2


def send(value, by):
    chips = lax.axis_size("ctx") // 2
    pairs = [
        (chip_at(p, chips) * 2 + core, chip_at(p + by, chips) * 2 + core)
        for p in range(chips)
        for core in range(2)
    ]
    return lax.ppermute(value, "ctx", pairs)


def core_swap(value):
    return lax.ppermute(value, "ctx", [(i, i ^ 1) for i in range(lax.axis_size("ctx"))])


def data_swap(value):
    return lax.ppermute(value, "dp", [(i, i ^ 1) for i in range(lax.axis_size("dp"))])


def shifted(value, by):
    count = lax.axis_size("ctx")
    return lax.ppermute(
        value, "ctx", [(i, i + by) for i in range(count) if 0 <= i + by < count]
    )


def after(value, *others):
    return lax.optimization_barrier((value, others))[0]


def ring_gather(block):
    chips = lax.axis_size("ctx") // 2
    found = [None] * chips
    found[0] = left = right = block
    token = yield None
    for step in range(1, chips // 2):
        if token is not None:
            left, right = after((left, right), token)
        left, right = send(left, 1), send(right, -1)
        found[chips - step], found[step] = left, right
        token = yield left, right
    middle = block.shape[0] // 16 * 8
    if token is not None:
        left, right = after((left, right), token)
    ends = [send(left[:middle], 1), send(right[middle:], -1)]
    found[chips // 2] = jnp.concatenate(ends, axis=0)
    yield ends
    yield found


def ring_scatter(part, chips, rows, split):
    size = rows // split
    half = split // 2
    middle = rows // 2
    ahead, back = [None] * split, [None] * split
    token = yield None
    for step in range(chips // 2, 0, -1):
        sent = []
        for i in range(split):
            for got, o, by in ((ahead, step, 1), (back, chips - step, -1)):
                first, count = i * size, size
                if step == chips // 2:
                    if split == 1:
                        first, count = (0, middle) if by == 1 else (middle, middle)
                    elif (i < half) != (by == 1):
                        continue
                piece = part(o, first, count)
                if got[i] is None:
                    piece = piece if token is None else after(piece, token)
                else:
                    piece = piece.astype(f32)
                    arrived = after(got[i], token).astype(f32)
                    if arrived.shape[0] < count:
                        if by == 1:
                            piece = jnp.concatenate([piece[:middle] + arrived, piece[middle:]], 0)
                        else:
                            piece = jnp.concatenate([piece[:middle], piece[middle:] + arrived], 0)
                    else:
                        piece = piece + arrived
                piece = piece.astype(bf16)
                got[i] = send(piece, by)
                token = piece
                sent.append(piece)
        more = yield sent, [v for v in ahead + back if v is not None]
        token = (token, more)
    yield (
        part(0, 0, rows).astype(f32)
        + jnp.concatenate(ahead, axis=0).astype(f32)
        + jnp.concatenate(back, axis=0).astype(f32)
    )


def exchange(stacked):
    count = lax.axis_size("ctx")
    groups = [list(range(core, count, 2)) for core in range(2)]
    return lax.all_to_all(stacked, "ctx", 0, 0, axis_index_groups=groups, tiled=True)


def head_spans(chips):
    firsts = [H * m // chips for m in range(chips + 1)]
    most = max(firsts[m + 1] - firsts[m] for m in range(chips))
    return firsts, most + most % 2


def head_rows(chip, chips, size):
    firsts, slots = head_spans(chips)
    return [
        section * H * size + (firsts[chip] + slot) * size + row
        if firsts[chip] + slot < firsts[chip + 1]
        else -1
        for section in range(3)
        for slot in range(slots)
        for row in range(size)
    ]


def plan_route(held, wanted):
    devices = len(held)
    edges = []
    for core in range(2):
        want = [set(wanted[d]) for d in range(core, devices, 2)]
        for source in range(core, devices, 2):
            for chip, rows in enumerate(want):
                moved = [r for r in held[source] if r >= 0 and r in rows]
                if moved:
                    edges.append((len(moved), source, 2 * chip + core, moved))
    draw, best = random.Random(0), None
    for trial in range(64):
        rounds = []
        for edge in sorted(edges, key=lambda e: (-e[0] - trial * draw.random(), e[1], e[2])):
            for found in rounds:
                if all(edge[1] != e[1] and edge[2] != e[2] for e in found):
                    found.append(edge)
                    break
            else:
                rounds.append([edge])
        cost = sum(-(-max(e[0] for e in found) // 16) * 16 + 32 for found in rounds)
        if best is None or cost < best[0]:
            best = cost, rounds
    rounds = best[1]
    sizes = [-(-max(e[0] for e in found) // 16) * 16 for found in rounds]
    total = sum(sizes)
    sends = [[-1] * total for _ in range(devices)]
    has = [[-1] * total for _ in range(devices)]
    first = 0
    for found, size in zip(rounds, sizes):
        for count, source, target, moved in found:
            places = {r: i for i, r in enumerate(held[source])}
            sends[source][first : first + count] = [places[r] for r in moved]
            has[target][first : first + count] = moved
        first += size
    pairs = [[(e[1], e[2]) for e in found] for found in rounds]
    return pairs, sizes, sends, has


def run_route(pieces, pairs):
    return jnp.concatenate(
        [lax.ppermute(piece, "ctx", group) for piece, group in zip(pieces, pairs)], axis=0
    )


def places_in(lists, wanted):
    found = []
    for has, want in zip(lists, wanted):
        where = {r: i for i, r in enumerate(has) if r >= 0}
        found.append([where.get(r, -1) for r in want])
    return found


def layer_norm(values, norm_gain, norm_shift):
    center = jnp.mean(values, axis=-1, keepdims=True)
    deviation = values - center
    variance = jnp.mean(deviation * deviation, axis=-1, keepdims=True)
    return deviation * lax.rsqrt(variance + norm_epsilon) * norm_gain + norm_shift


def gelu_curve(values):
    return (
        0.5 * values * (1.0 + jnp.tanh(gelu_scale * (values + 0.044715 * values * values * values)))
    )


def rows_by_rows(left_side, right_side):
    return lax.dot_general(
        left_side, right_side, (((0,), (0,)), ((), ())), preferred_element_type=f32
    )


def cols_by_cols(left_side, right_side):
    return lax.dot_general(
        left_side, right_side, (((1,), (1,)), ((), ())), preferred_element_type=f32
    )


def cost_of(flops, moved):
    return pl.CostEstimate(flops=0, bytes_accessed=0, transcendentals=0)


def times(left_side, right_side):
    return jnp.dot(left_side, right_side, preferred_element_type=f32)


def chosen_by(rows, count):
    places = lax.broadcasted_iota(jnp.int32, (count, rows.shape[1]), 0)
    return (rows == places).astype(bf16)


def choose_kernel(rows, matrix, *outs):
    found = rows_by_rows(chosen_by(rows[0:1], matrix.shape[0]), matrix[...])
    first = 0
    columns = matrix.shape[1]
    for out in outs:
        out[:, :columns] = found[first : first + out.shape[0]].astype(bf16)
        out[:, columns:] = jnp.zeros((out.shape[0], out.shape[1] - columns), bf16)
        first += out.shape[0]


def choose_rows(rows, matrix, sizes):
    return pl.pallas_call(
        choose_kernel,
        out_shape=[
            jax.ShapeDtypeStruct((count, -(-matrix.shape[1] // LANES) * LANES), bf16)
            for count in sizes
        ],
        in_specs=[pl.BlockSpec(memory_space=pltpu.VMEM) for _ in range(2)],
        out_specs=[pl.BlockSpec(memory_space=pltpu.VMEM) for _ in sizes],
        compiler_params=pltpu.CompilerParams(vmem_limit_bytes=vmem_bytes),
    )(rows, matrix)


def pick_kernel(flag, own_rows, mate_rows, own, got, mate_own, mate_got, out):
    half = out.shape[1] // 2
    chosen = [chosen_by(rows[0:1], own.shape[0]) for rows in (own_rows, mate_rows)]
    first = flag[0] == 0
    for side in range(2):
        total = 0.0
        for pick, one, two in ((chosen[0], own, got), (chosen[1], mate_own, mate_got)):
            total += rows_by_rows(pick, jnp.where(first == (side == 0), one[...], two[...]))
        out[:, side * half : (side + 1) * half] = total[:, :half].astype(bf16)


def pick_rows(flag, own_rows, mate_rows, own, got, mate_own, mate_got, half):
    count = own_rows.shape[1]
    return pl.pallas_call(
        pick_kernel,
        out_shape=jax.ShapeDtypeStruct((count, 2 * half), bf16),
        in_specs=[pl.BlockSpec(memory_space=pltpu.SMEM)]
        + [pl.BlockSpec(memory_space=pltpu.VMEM) for _ in range(6)],
        out_specs=pl.BlockSpec(memory_space=pltpu.VMEM),
        compiler_params=pltpu.CompilerParams(vmem_limit_bytes=vmem_bytes),
    )(flag, own_rows, mate_rows, own, got, mate_own, mate_got)


def join_weight_kernel(size, count, flags, own, got, mate_own, mate_got, out, whole):
    chips, _, features = own.shape
    half, fold = features // 2, (count + 1) // 2
    first_half, odd = flags[0] == 0, flags[1] == 1
    for chip in range(chips):
        sides = []
        for one, two in ((own, got), (mate_own, mate_got)):
            one, two = one[chip].astype(f32), two[chip].astype(f32)
            sides.append((jnp.where(first_half, one, two), jnp.where(first_half, two, one)))
        for core in range(2):
            base = (2 * chip + core) * count
            for side in range(2):
                piece = jnp.where(odd == (core == 1), sides[0][side], sides[1][side])
                columns = slice(side * half, (side + 1) * half)
                whole[base : base + fold, columns] = piece[:fold, :half]
                whole[base + fold : base + count, columns] = piece[: count - fold, half:]
    firsts, slots = head_spans(chips)
    for chip in range(chips):
        low, high = firsts[chip] * size, firsts[chip + 1] * size
        first, last = chip * slots * size, (chip + 1) * slots * size
        if low < high:
            out[:, first : first + high - low] = whole[:, low:high].astype(out.dtype)
        if first + high - low < last:
            out[:, first + high - low : last] = jnp.zeros(
                (out.shape[0], last - first - high + low), out.dtype
            )


def join_weight(flags, own, got, mate_own, mate_got, size, count):
    chips, fold, features = own.shape
    slots = head_spans(chips)[1]
    return pl.pallas_call(
        functools.partial(join_weight_kernel, size, count),
        out_shape=jax.ShapeDtypeStruct((2 * chips * count, chips * slots * size), own.dtype),
        in_specs=[pl.BlockSpec(memory_space=pltpu.SMEM)]
        + [pl.BlockSpec(memory_space=pltpu.VMEM) for _ in range(4)],
        out_specs=pl.BlockSpec(memory_space=pltpu.VMEM),
        scratch_shapes=[pltpu.VMEM((2 * chips * count, features), f32)],
        compiler_params=pltpu.CompilerParams(vmem_limit_bytes=vmem_bytes),
    )(flags, own, got, mate_own, mate_got)


def cut_kernel(width, table, back, low, out):
    chips = out.shape[0]
    odd = table[chips] == 1
    both = low.shape[1] // chips
    half = both // 2
    for chip in range(chips):
        out[chip, :, :width] = back[:, chip * width : (chip + 1) * width]
        piece = low[:, chip * both : (chip + 1) * both].astype(f32)
        piece = jnp.where(odd, jnp.concatenate([piece[:, half:], piece[:, :half]], axis=1), piece)
        out[chip, :, width : width + both] = piece.astype(out.dtype)
        out[chip, :, width + both :] = jnp.zeros(
            (out.shape[1], out.shape[2] - width - both), out.dtype
        )


def cut_columns(back, low, table, chips):
    rows = low.shape[0]
    width = back.shape[1] // chips
    return pl.pallas_call(
        functools.partial(cut_kernel, width),
        out_shape=jax.ShapeDtypeStruct(
            (chips, rows, -(-(width + low.shape[1] // chips) // LANES) * LANES), bf16
        ),
        in_specs=[pl.BlockSpec(memory_space=pltpu.SMEM)]
        + [pl.BlockSpec(memory_space=pltpu.VMEM) for _ in range(2)],
        out_specs=pl.BlockSpec(memory_space=pltpu.VMEM),
        compiler_params=pltpu.CompilerParams(vmem_limit_bytes=vmem_bytes),
    )(table, back, low)


def both_heads(pair):
    lane = lax.broadcasted_iota(jnp.int32, pair.shape, 1)
    zero = jnp.zeros_like(pair)
    low = lane < LANES // 2
    return jnp.concatenate([jnp.where(low, pair, zero), jnp.where(low, zero, pair)], axis=0)


def one_pair(stacked):
    rows = stacked.shape[0] // 2
    lane = lax.broadcasted_iota(jnp.int32, (rows, stacked.shape[1]), 1)
    return jnp.where(lane < LANES // 2, stacked[:rows], stacked[rows:])


def window_of(far, near, own, number, columns):
    return jnp.concatenate(
        [far[number, :, columns], near[number, :, columns], own[number, :, columns]], axis=0
    )


def forward_kernel(scale, odd_core, bias, query, far, near, own, mixed, log_total):
    masked = jnp.concatenate([bias[0], bias[0]], axis=0)
    for pair in range(query.shape[1] // LANES):
        columns = slice(pair * LANES, (pair + 1) * LANES)
        stacked = both_heads(query[:, columns])
        keys = window_of(far, near, own, 0, columns)
        values = window_of(far, near, own, 1, columns)
        scores = cols_by_cols(stacked, keys) * scale + masked
        row_max = jnp.max(scores, axis=1, keepdims=True)
        raised = jnp.exp(scores - row_max)
        row_total = jnp.sum(raised, axis=1, keepdims=True)
        log_sum = row_max + jnp.log(row_total)
        weights = (raised * (1.0 / row_total)).astype(bf16)
        mixed[:, columns] = one_pair(times(weights, values)).astype(bf16)
        log_total[0, pair] = log_sum


def backward_kernel(
    scale, odd_core, bias, query, far, near, own, log_total, mixed, mixed_back, query_back,
    own_back, mate_back, query_sum
):
    step = pl.program_id(0)
    rows = query.shape[0]
    masked = jnp.concatenate([bias[0], bias[0]], axis=0)

    @pl.when(step == 0)
    def _():
        query_sum[...] = jnp.zeros_like(query_sum)
        mate_back[...] = jnp.zeros_like(mate_back)

    here = pl.multiple_of(step * rows, rows)
    before = pl.multiple_of(jnp.maximum(step - 1, 0) * rows, rows)
    beside = pl.multiple_of(jnp.maximum(step - 1 + odd_core[0], 0) * rows, rows)
    for pair in range(query.shape[1] // LANES):
        columns = slice(pair * LANES, (pair + 1) * LANES)
        stacked = both_heads(query[:, columns])
        keys = window_of(far, near, own, 0, columns)
        values = window_of(far, near, own, 1, columns)
        scores = cols_by_cols(stacked, keys) * scale + masked
        weights = jnp.exp(scores - log_total[0, pair])
        back = both_heads(mixed_back[:, columns])
        product = back.astype(f32) * both_heads(mixed[:, columns]).astype(f32)
        row_delta = jnp.sum(product, axis=1, keepdims=True)
        weight_back = cols_by_cols(back, values)
        score_back = (weights * (weight_back - row_delta)).astype(bf16)
        query_part = one_pair(times(score_back, keys)) * scale
        query_back[:, columns] = query_part.astype(bf16)
        query_sum[0:1, columns] += jnp.sum(query_part, axis=0, keepdims=True)
        terms = (
            rows_by_rows(score_back, stacked) * scale,
            rows_by_rows(weights.astype(bf16), back),
        )
        for number, term in enumerate(terms):
            own_back[number, pl.ds(here, rows), columns] = term[2 * rows :]

            @pl.when(step > 0)
            def _():
                own_back[number, pl.ds(before, rows), columns] += term[:rows]

            @pl.when(step + odd_core[0] > 0)
            def _():
                mate_back[number, pl.ds(beside, rows), columns] = term[rows : 2 * rows].astype(bf16)


def attention_specs(rows, width, window):
    wide = pl.BlockSpec((rows, width), lambda m, odd: (m, 0))
    own = pl.BlockSpec((2, rows, width), lambda m, odd: (0, m, 0))
    far = pl.BlockSpec((2, rows, width), lambda m, odd: (0, jnp.maximum(m - 1, 0), 0))
    near = pl.BlockSpec((2, rows, width), lambda m, odd: (0, jnp.maximum(m - 1 + odd[0], 0), 0))
    bias = pl.BlockSpec((1, rows, window), lambda m, odd: (m, 0, 0))
    total = pl.BlockSpec((1, width // LANES, 2 * rows, 1), lambda m, odd: (m, 0, 0, 0))
    return wide, own, far, near, bias, total


def attend_forward(odd_core, bias, query, pair, mate, scale):
    total, width = query.shape
    chips, rows, window = bias.shape
    wide, own, far, near, bias_spec, sums = attention_specs(rows, width, window)
    return pl.pallas_call(
        functools.partial(forward_kernel, scale),
        grid_spec=pltpu.PrefetchScalarGridSpec(
            num_scalar_prefetch=1,
            grid=(chips,),
            in_specs=[bias_spec, wide, far, near, own],
            out_specs=[wide, sums],
        ),
        out_shape=[
            jax.ShapeDtypeStruct((total, width), bf16),
            jax.ShapeDtypeStruct((chips, width // LANES, 2 * rows, 1), f32),
        ],
        cost_estimate=cost_of(8 * total * window * 2 * width, 16 * total * width),
        compiler_params=pltpu.CompilerParams(vmem_limit_bytes=vmem_bytes),
    )(odd_core, bias, query, pair, mate, pair)


def attend_backward(odd_core, bias, query, pair, mate, log_total, mixed, mixed_back, scale):
    total, width = query.shape
    chips, rows, window = bias.shape
    wide, own, far, near, bias_spec, sums = attention_specs(rows, width, window)
    back = pl.BlockSpec((rows, mixed_back.shape[1]), lambda m, odd: (m, 0))
    whole = pl.BlockSpec((2, total, width), lambda m, odd: (0, 0, 0))
    return pl.pallas_call(
        functools.partial(backward_kernel, scale),
        grid_spec=pltpu.PrefetchScalarGridSpec(
            num_scalar_prefetch=1,
            grid=(chips,),
            in_specs=[bias_spec, wide, far, near, own, sums, wide, back],
            out_specs=[wide, whole, whole, pl.BlockSpec((8, width), lambda m, odd: (0, 0))],
        ),
        out_shape=[
            jax.ShapeDtypeStruct((total, width), bf16),
            jax.ShapeDtypeStruct((2, total, width), f32),
            jax.ShapeDtypeStruct((2, total, width), bf16),
            jax.ShapeDtypeStruct((8, width), f32),
        ],
        cost_estimate=cost_of(20 * total * window * 2 * width, 32 * total * width),
        compiler_params=pltpu.CompilerParams(vmem_limit_bytes=vmem_bytes),
    )(odd_core, bias, query, pair, mate, pair, log_total, mixed, mixed_back)


def standardised(values):
    center = jnp.mean(values, axis=-1, keepdims=True)
    deviation = values - center
    variance = jnp.mean(deviation * deviation, axis=-1, keepdims=True)
    return deviation * lax.rsqrt(variance + norm_epsilon)


def project_kernel(rows, table, weight, bias, vectors, *refs):
    blocks, (inputs, below, cotangent, normed, query, pair) = refs[:-6], refs[-6:]
    last = blocks[0].shape[0] - rows
    width = query.shape[1]
    for o in range(0, len(blocks), 2):
        values = jnp.concatenate([blocks[o][:rows], blocks[o + 1][:rows]], axis=0)
        normed_low = standardised(values.astype(f32)) * vectors[0:1] + vectors[1:2]
        normed_low = normed_low.astype(bf16)
        product = (cols_by_cols(normed_low, weight[...]) + bias[0:1]).astype(bf16)
        for part in range(2):
            here = slice(part * rows, (part + 1) * rows)
            place = pl.ds(pl.multiple_of(table[o + part] * rows, rows), rows)
            inputs[place] = values[here]
            below[table[o + part]] = blocks[o + part][rows:last]
            cotangent[place] = blocks[o + part][last:]
            normed[place] = normed_low[here]
            query[place] = product[here, :width]
            pair[0, place] = product[here, width : 2 * width]
            pair[1, place] = product[here, 2 * width :]


def project(blocks, table, weight, bias, vectors, rows):
    chips, (count, features) = len(blocks), blocks[0].shape
    if chips > most_resident:
        own_order = jnp.arange(most_resident, dtype=jnp.int32)
        found = [
            project(blocks[first : first + most_resident], own_order, weight, bias, vectors, rows)
            for first in range(0, chips, most_resident)
        ]
        by_chip = lambda value, axis: taken(value, table[chips + 1 :], axis)
        joined = []
        for number, parts in enumerate(zip(*found)):
            axis = 1 if number == 5 else 0
            value = jnp.concatenate(parts, axis=axis)
            shape = value.shape
            split = shape[:axis] + (chips, shape[axis] // chips) + shape[axis + 1 :]
            joined.append(by_chip(value.reshape(split), axis).reshape(shape))
        return joined
    total, width = chips * rows, weight.shape[0] // 3
    return pl.pallas_call(
        functools.partial(project_kernel, rows),
        out_shape=[
            jax.ShapeDtypeStruct((total, features), bf16),
            jax.ShapeDtypeStruct((chips, count - 2 * rows, features), bf16),
            jax.ShapeDtypeStruct((total, features), bf16),
            jax.ShapeDtypeStruct((total, features), bf16),
            jax.ShapeDtypeStruct((total, width), bf16),
            jax.ShapeDtypeStruct((2, total, width), bf16),
        ],
        in_specs=[pl.BlockSpec(memory_space=pltpu.SMEM)]
        + [pl.BlockSpec(memory_space=pltpu.VMEM) for _ in range(3 + chips)],
        out_specs=[pl.BlockSpec(memory_space=pltpu.VMEM) for _ in range(6)],
        cost_estimate=cost_of(6 * total * features * width, 8 * total * features),
        compiler_params=pltpu.CompilerParams(vmem_limit_bytes=vmem_bytes),
    )(table, weight, bias, vectors, *blocks)


def taken(value, places, axis):
    return jnp.concatenate(
        [
            lax.dynamic_slice_in_dim(value, places[i], 1, axis)
            for i in range(places.shape[0])
        ],
        axis=axis,
    )


def parts_spec(chips, rows, features):
    if chips <= most_resident:
        return pl.BlockSpec((chips, rows, features), lambda i, table: (0, 0, 0))
    return pl.BlockSpec((2, rows, features), lambda i, table: (i, 0, 0))


def by_place(parts, table):
    chips = parts.shape[0]
    return parts if chips <= most_resident else taken(parts, table[:chips], 0)


def feed_forward_kernel(
    table, inputs, cotangent, output_full, up_own, up_mate, down_own, down_mate, shift, vectors,
    *refs
):
    attended, refs = refs[:-9], refs[-9:]
    (
        normed, hidden_own, hidden_mate, back_own, back_mate, parts, bias_sum, residual_own,
        attended_wide,
    ) = refs
    step = pl.program_id(0)
    rows, features = residual_own.shape
    width = attended[0].shape[1]
    for o, ref in enumerate(attended):
        columns = pl.ds(pl.multiple_of(table[o] * width, width), width)
        attended_wide[:, columns] = ref[...]
    residual = inputs[...].astype(f32) + vectors[0:1]
    residual += cols_by_cols(attended_wide[...], output_full[...])
    cotangent_rows = cotangent[...]
    for part in range(inputs.shape[0] // rows):

        @pl.when(table[0] == step * (inputs.shape[0] // rows) + part)
        def _():
            residual_own[...] = residual[part * rows : (part + 1) * rows]

    normed_low = (standardised(residual) * vectors[1:2] + vectors[2:3]).astype(bf16)
    normed[...] = normed_low
    product = output = None

    @pl.when(step == 0)
    def _():
        bias_sum[...] = jnp.zeros_like(bias_sum)

    for number, (up, down, hidden, up_back) in enumerate(
        ((up_own, down_own, hidden_own, back_own), (up_mate, down_mate, hidden_mate, back_mate))
    ):
        value = cols_by_cols(normed_low, up[...]) + shift[number : number + 1]
        square = value * value
        bent = jnp.tanh(gelu_scale * (value + 0.044715 * square * value))
        hidden_low = (0.5 * value * (1.0 + bent)).astype(bf16)
        hidden[...] = hidden_low
        term = times(hidden_low, down[...])
        output = term if output is None else output + term
        slope = 0.5 * (1.0 + bent) + 0.5 * value * (1.0 - bent * bent) * (
            gelu_scale * (1.0 + 3.0 * 0.044715 * square)
        )
        back = (cols_by_cols(cotangent_rows, down[...]) * slope).astype(bf16)
        up_back[...] = back
        bias_sum[number : number + 1] += jnp.sum(back.astype(f32), axis=0, keepdims=True)
        term = times(back, up[...])
        product = term if product is None else product + term
    for part in range(inputs.shape[0] // rows):
        place = part
        if len(attended) <= most_resident:
            place = table[len(attended) + 1 + step * (inputs.shape[0] // rows) + part]
        here = slice(part * rows, (part + 1) * rows)
        parts[place, :rows] = product[here].astype(bf16)
        parts[place, rows:] = output[here].astype(bf16)


def feed_forward(
    table, attended, inputs, cotangent, output_full, up_own, up_mate, down_own, down_mate, shift,
    vectors, rows
):
    chips, (total, width) = len(attended), attended[0].shape
    features = inputs.shape[1]
    units = up_own.shape[0]
    block = 2 * rows
    along = lambda columns: pl.BlockSpec((block, columns), lambda i, table: (i, 0))
    whole = lambda shape: pl.BlockSpec(shape, lambda i, table: (0, 0))
    return pl.pallas_call(
        feed_forward_kernel,
        grid_spec=pltpu.PrefetchScalarGridSpec(
            num_scalar_prefetch=1,
            grid=(total // block,),
            in_specs=[
                along(features),
                along(features),
                whole(output_full.shape),
                whole(up_own.shape),
                whole(up_own.shape),
                whole(up_own.shape),
                whole(up_own.shape),
                whole(shift.shape),
                whole(vectors.shape),
            ]
            + [along(width) for _ in attended],
            out_specs=[along(features)]
            + [along(units) for _ in range(4)]
            + [
                parts_spec(chips, 2 * rows, features),
                whole(shift.shape),
                whole((rows, features)),
                along(chips * width),
            ],
        ),
        out_shape=[jax.ShapeDtypeStruct((total, features), bf16)]
        + [jax.ShapeDtypeStruct((total, units), bf16) for _ in range(4)]
        + [
            jax.ShapeDtypeStruct((chips, 2 * rows, features), bf16),
            jax.ShapeDtypeStruct(shift.shape, f32),
            jax.ShapeDtypeStruct((rows, features), f32),
            jax.ShapeDtypeStruct((total, chips * width), bf16),
        ],
        cost_estimate=cost_of(
            2 * total * features * (chips * width + 6 * units), 16 * total * features
        ),
        compiler_params=pltpu.CompilerParams(vmem_limit_bytes=vmem_bytes),
    )(
        table, inputs, cotangent, output_full, up_own, up_mate, down_own, down_mate, shift, vectors,
        *attended
    )


def back_through_kernel(
    chips, table, query_back, own_back, mate_back, weight, inputs, own_rows, mate_rows, own_wide,
    mate_wide, parts, sums, value_sum, own_chosen, mate_chosen
):
    step = pl.program_id(0)
    rows = parts.shape[1]

    @pl.when(step == 0)
    def _():
        sums[...] = jnp.zeros_like(sums)
        value_sum[...] = jnp.zeros_like(value_sum)
        own_chosen[...] = chosen_by(own_rows[0:1], own_chosen.shape[0])
        mate_chosen[...] = chosen_by(mate_rows[0:1], mate_chosen.shape[0])

    key = own_back[0] + mate_back[0].astype(f32)
    value = own_back[1] + mate_back[1].astype(f32)
    value_sum[0:1] += jnp.sum(value, axis=0, keepdims=True)
    back = jnp.concatenate([query_back[...], key.astype(bf16), value.astype(bf16)], axis=1)
    own_wide[...] = times(back, own_chosen[...]).astype(bf16)
    mate_wide[...] = times(back, mate_chosen[...]).astype(bf16)
    product = times(back, weight[...])
    for part in range(back.shape[0] // rows):
        place = part
        if chips <= most_resident:
            place = table[chips + 1 + step * (back.shape[0] // rows) + part]
        parts[place] = product[part * rows : (part + 1) * rows].astype(bf16)
    plain = standardised(inputs[...].astype(f32))
    sums[0:1] += jnp.sum(product * plain, axis=0, keepdims=True)
    sums[1:2] += jnp.sum(product, axis=0, keepdims=True)


def back_through(
    table, query_back, own_back, mate_back, weight, inputs, own_rows, mate_rows, rows
):
    total, width = query_back.shape
    features = inputs.shape[1]
    chips, share = total // rows, own_rows.shape[1]
    block = 2 * rows
    along = lambda columns: pl.BlockSpec((block, columns), lambda i, table: (i, 0))
    pair = pl.BlockSpec((2, block, width), lambda i, table: (0, i, 0))
    whole = lambda shape: pl.BlockSpec(shape, lambda i, table: (0,) * len(shape))
    return pl.pallas_call(
        functools.partial(back_through_kernel, chips),
        grid_spec=pltpu.PrefetchScalarGridSpec(
            num_scalar_prefetch=1,
            grid=(total // block,),
            in_specs=[
                along(width),
                pair,
                pair,
                whole(weight.shape),
                along(features),
                whole(own_rows.shape),
                whole(mate_rows.shape),
            ],
            out_specs=[
                along(share),
                along(share),
                parts_spec(chips, rows, features),
                whole((8, features)),
                whole((8, width)),
            ],
            scratch_shapes=[pltpu.VMEM((3 * width, share), bf16) for _ in range(2)],
        ),
        out_shape=[
            jax.ShapeDtypeStruct((total, share), bf16),
            jax.ShapeDtypeStruct((total, share), bf16),
            jax.ShapeDtypeStruct((chips, rows, features), bf16),
            jax.ShapeDtypeStruct((8, features), f32),
            jax.ShapeDtypeStruct((8, width), f32),
        ],
        compiler_params=pltpu.CompilerParams(vmem_limit_bytes=vmem_bytes),
    )(table, query_back, own_back, mate_back, weight, inputs, own_rows, mate_rows)


def shards(
    block_input,
    segments,
    joint_weight,
    output_weight,
    up_weight,
    down_weight,
    vectors,
    up_bias,
    cotangent,
):
    rows = block_input.shape[1]
    features = block_input.shape[2]
    size = features // H
    reach_rows = REACH * rows
    window = reach_rows + rows
    scale = size ** (-0.5)
    context = lax.axis_size("ctx")
    data = lax.axis_size("dp")
    chips = context // 2
    position = lax.axis_index("ctx")
    half_index = lax.axis_index("dp")
    chip = position // 2
    core = position % 2
    place = jnp.where(chip % 2 == 0, chip // 2, chips - 1 - chip // 2)
    steps = jnp.arange(chips, dtype=jnp.int32)

    def chip_of(places):
        return jnp.where(places < chips // 2, 2 * places, 2 * (chips - 1 - places) + 1)

    here = chip_of((place + steps) % chips)
    back_table = chip_of((place - steps) % chips)
    places = jnp.where(steps % 2 == 0, steps // 2, chips - 1 - steps // 2)
    chip_on = [here[o] for o in range(chips)]
    table = jnp.concatenate(
        [here, core[None].astype(jnp.int32), (places - place) % chips]
    ).astype(jnp.int32)
    odd_core = core.astype(jnp.int32)[None]
    first_half = half_index == 0
    first_core = core == 0

    half = features // data

    def block_of(matrix):
        return lambda o, first=0, count=rows: lax.dynamic_slice_in_dim(
            matrix, chip_on[o] * rows + first, count, 0
        )

    def part_of(stacked):
        return lambda o, first=0, count=rows: stacked[o, first : first + count]

    joint_cols = joint_weight.shape[1]
    firsts, slots = head_spans(chips)
    width = slots * size
    devices = range(context)
    wanted = [head_rows(d // 2, chips, size) for d in devices]
    owned = [list(range(d * joint_cols, (d + 1) * joint_cols)) for d in devices]
    shares = [
        [r for r in wanted[d] if r >= 0 and r // joint_cols % 2 == d % 2] for d in devices
    ]
    most = -(-max(len(share) for share in shares) // 16) * 16
    shares = [share + [-1] * (most - len(share)) for share in shares]
    route = plan_route(owned, shares)
    back_route = plan_route(shares, owned)
    lists = [
        route[2],
        places_in(route[3], wanted),
        places_in([route[3][d ^ 1] for d in devices], wanted),
        places_in(wanted, shares),
        places_in(wanted, [shares[d ^ 1] for d in devices]),
        back_route[2],
        places_in(back_route[3], owned),
    ]
    longest = -(-max(len(one[0]) for one in lists) // LANES) * LANES
    rows_here = lax.dynamic_index_in_dim(
        jnp.array(
            [[one[d] + [-1] * (longest - len(one[d])) for one in lists] for d in devices], jnp.int32
        ),
        position,
        0,
        keepdims=False,
    )
    rows_here = [rows_here[i : i + 1, : len(one[0])] for i, one in enumerate(lists)]

    output_cols = output_weight.shape[1]
    with jax.named_scope("parameters"):
        spread = jnp.broadcast_to(vectors[None], (data * context,) + vectors.shape)
        spread = lax.all_to_all(spread, ("dp", "ctx"), 0, 0, tiled=True)
        params = (
            spread.reshape((data, context) + vectors.shape)
            .transpose(0, 2, 1, 3)
            .reshape(data * vectors.shape[0], features)
            .astype(f32)
        )
    with jax.named_scope("input_ring"):
        output_rows = jnp.pad(output_weight.T, ((0, output_cols % 2), (0, 0)))
        fold = output_rows.shape[0] // 2
        output_rows = jnp.concatenate([output_rows[:fold], output_rows[fold:]], axis=1)
        output_rows = jnp.pad(output_rows, ((0, -fold % 16), (0, 0)))
        block = jnp.concatenate([block_input[0], output_rows, cotangent[0]], axis=0)
        input_ring = ring_gather(after(block, spread))
        next(input_ring)
        arrived = next(input_ring)
    with jax.named_scope("joint_weight"):
        mine = choose_rows(rows_here[0], after(joint_weight, spread).T, route[1])
        mine = run_route(mine, route[0])
        got = data_swap(mine)
    with jax.named_scope("input_ring"):
        arrived = input_ring.send(mine)
    with jax.named_scope("joint_weight"):
        joint_heads = pick_rows(
            half_index.astype(jnp.int32)[None],
            rows_here[1],
            rows_here[2],
            mine,
            got,
            core_swap(after(mine, got)),
            core_swap(got),
            half,
        )
    with jax.named_scope("feed_forward_weights"):
        up_mine, down_mine = up_weight.T, down_weight
        up_got = data_swap(after(up_mine, got))
        down_got = data_swap(after(down_mine, got))
    with jax.named_scope("input_ring"):
        for step in range(3, chips // 2 + 1):
            if step == 3:
                arrived = input_ring.send(got)
            elif step == chips // 2:
                arrived = input_ring.send((joint_heads, up_got))
            else:
                arrived = next(input_ring)
        input_blocks = next(input_ring)
    with jax.named_scope("masks"):
        padded_numbers = jnp.concatenate([jnp.full((reach_rows,), -1, jnp.int32), segments[0]])
        numbers = jnp.stack(
            [
                lax.dynamic_slice_in_dim(padded_numbers, (2 * m + core) * rows, window)
                for m in range(chips)
            ]
        )
        key_places = jnp.arange(window, dtype=jnp.int32)
        allowed = (numbers[:, None, :] == numbers[:, reach_rows:, None]) & (
            key_places[None, None, :] <= key_places[None, reach_rows:, None]
        )
        bias = jnp.where(allowed, 0.0, masked_score).astype(f32)

    with jax.named_scope("projection"):
        first_column = jnp.array(firsts[:chips], jnp.int32)[chip] * size
        last_column = jnp.array(firsts[1:], jnp.int32)[chip] * size
        inside = first_column + jnp.arange(width, dtype=jnp.int32) < last_column

        def of_heads(row):
            row = lax.dynamic_slice_in_dim(jnp.pad(row, (0, width)), first_column, width)
            return jnp.where(inside, row, 0.0)

        def at_heads(row):
            whole = jnp.zeros((features + width,), f32)
            return lax.dynamic_update_slice_in_dim(whole, row, first_column, 0)[:features]

        head_bias = jnp.concatenate(
            [of_heads(params[2]), jnp.zeros((width,), f32), of_heads(params[3])]
        )
        inputs, below, cotangent_all, normed_one, query, own = project(
            input_blocks,
            table,
            joint_heads,
            jnp.pad(head_bias[None], ((0, 7), (0, 0))),
            jnp.pad(params[0:2], ((0, 6), (0, 0))),
            rows,
        )

    with jax.named_scope("feed_forward_weights"):
        up_shift = core_swap(up_bias[None].astype(f32))
        up_shift = jnp.concatenate([up_bias[None].astype(f32), up_shift], axis=0)
        up_shift = jnp.pad(up_shift, ((0, 6), (0, 0)))

        def both_halves(mine, got):
            return jnp.where(
                first_half,
                jnp.concatenate([mine, got], axis=-1),
                jnp.concatenate([got, mine], axis=-1),
            )

        up_own, down_own = both_halves(up_mine, up_got), both_halves(down_mine, down_got)
    mate = core_swap(after(own, down_got))
    attended, log_total = attend_forward(odd_core, bias, query, own, mate, scale)
    with jax.named_scope("attended_ring"):
        attended_ring = ring_gather(attended)
        next(attended_ring)
        arrived = next(attended_ring)
    arrived_first = arrived
    with jax.named_scope("attended_ring"):
        arrived = next(attended_ring)
    with jax.named_scope("output_weight"):
        below_got = data_swap(below)
        below_mate = core_swap(after(below, arrived_first))
        below_both = core_swap(after(below_got, arrived))
        flags = jnp.stack([half_index, core]).astype(jnp.int32)
        output_full = join_weight(
            flags, below, below_got, below_mate, below_both, size, output_cols
        )
    with jax.named_scope("feed_forward_weights"):
        up_mate, down_mate = core_swap(up_own), core_swap(down_own)
    with jax.named_scope("attended_ring"):
        arrived = attended_ring.send((up_own, down_own, below_both))
        for step in range(4, chips // 2 + 1):
            arrived = attended_ring.send(output_full) if step == 4 else next(attended_ring)
        attended_blocks = next(attended_ring)

    (
        normed_two,
        hidden_own,
        hidden_mate,
        back_own,
        back_mate,
        normed_parts,
        bias_sum,
        residual,
        attended_wide,
    ) = (
        feed_forward(
            table,
            attended_blocks,
            inputs,
            cotangent_all,
            output_full,
            up_own,
            up_mate,
            down_own,
            down_mate,
            up_shift,
            jnp.pad(params[4:7], ((0, 5), (0, 0))),
            rows,
        )
    )
    def pieces_of(own_rows, other, columns, order=lambda matrix: matrix):
        total = order(rows_by_rows(own_rows, columns) + core_swap(other))
        one, two = total[:, :half], total[:, half:]
        return jnp.where(first_half, one, two), jnp.where(first_half, two, one).astype(bf16)

    def finish(kept, given):
        return kept + data_swap(given).astype(f32)

    with jax.named_scope("normed_two_back_ring"):
        normed_parts = by_place(normed_parts, table)
        ring = ring_scatter(part_of(normed_parts), chips, rows, 2)
        next(ring)
        sent, _ = next(ring)
        sent, _ = next(ring)
    with jax.named_scope("up_gradient"):
        up_other = rows_by_rows(after(back_mate, sent), normed_two)
    with jax.named_scope("down_gradient"):
        down_other = rows_by_rows(after(hidden_mate, sent), cotangent_all)
    with jax.named_scope("normed_two_back_ring"):
        sent, _ = next(ring)
    with jax.named_scope("up_gradient"):
        up_kept, up_given = pieces_of(after(back_own, sent), up_other, normed_two)
        up_arrived = data_swap(up_given)
    with jax.named_scope("down_gradient"):
        down_kept, down_given = pieces_of(after(hidden_own, sent), down_other, cotangent_all)
        down_arrived = data_swap(down_given)
    with jax.named_scope("normed_two_back_ring"):
        for step in range(3, chips // 2):
            sent, _ = ring.send((up_other, down_other)) if step == 3 else next(ring)
        normed_two_back = next(ring)
    with jax.named_scope("down_ring"):
        down_ring = ring_scatter(
            lambda o, first=0, count=rows, held=normed_parts: held[
                o, rows + first : rows + first + count
            ],
            chips,
            rows,
            1,
        )
        next(down_ring)
        sent, arrived = down_ring.send(sent)

    rows_float = block_input[0].astype(f32)
    cotangent_float = cotangent[0].astype(f32)
    _, norm_pull = jax.vjp(layer_norm, residual, params[5], params[6])
    residual_part, gain_two_back, shift_two_back = norm_pull(normed_two_back)
    residual_back = cotangent_float + residual_part
    residual_low = residual_back.astype(bf16)
    attended_back = times(residual_low, output_full).astype(bf16)
    pieces = cut_columns(attended_back, residual_low, table, chips)
    with jax.named_scope("back_exchange"):
        back_got = exchange(pieces)
    with jax.named_scope("down_ring"):
        sent, arrived = down_ring.send(pieces)
    with jax.named_scope("back_exchange"):
        bias_own = bias_sum[0] + core_swap(bias_sum[1])
        bias_gradient = bias_own + data_swap(bias_own)
        back_got = after(back_got, (up_given, down_given, arrived, bias_gradient))
        back_all = back_got.reshape(chips * rows, -1)
    with jax.named_scope("down_ring"):
        sent, arrived = down_ring.send(back_all)
    query_back, own_back, mate_back, query_sum = attend_backward(
        odd_core, bias, query, own, mate, log_total, attended, back_all, scale
    )
    with jax.named_scope("mate_back"):
        mate_back = core_swap(after(mate_back, (up_arrived, arrived)))
    with jax.named_scope("up_gradient"):
        up_gradient = up_kept + after(up_arrived, own_back).astype(f32)
    with jax.named_scope("down_ring"):
        sent, arrived = down_ring.send(own_back)

    own_wide, mate_wide, normed_parts, norm_sums, value_sum = back_through(
        table,
        query_back,
        own_back,
        mate_back,
        joint_heads,
        inputs,
        rows_here[3],
        rows_here[4],
        rows,
    )

    vectors_sum = jnp.stack(
        [
            norm_sums[0],
            norm_sums[1],
            at_heads(query_sum[0]),
            at_heads(value_sum[0]),
            jnp.sum(residual_back, axis=0),
            gain_two_back,
            shift_two_back,
            jnp.sum(cotangent_float, axis=0),
        ]
    )
    vectors_cut = (
        vectors_sum.reshape(data, vectors.shape[0], context, vectors.shape[1])
        .transpose(0, 2, 1, 3)
        .reshape((data * context,) + vectors.shape)
    )
    with jax.named_scope("last_ring"):
        normed_parts = by_place(normed_parts, table)
        ring = ring_scatter(part_of(normed_parts), chips, rows, 2)
        next(ring)
        sent, _ = ring.send(arrived)

    with jax.named_scope("joint_gradient"):
        joint_other = rows_by_rows(after(mate_wide, sent), normed_one)
    with jax.named_scope("last_ring"):
        sent, _ = ring.send(joint_other)
    with jax.named_scope("joint_gradient"):
        mine, joint_given = pieces_of(after(own_wide, sent), joint_other, normed_one)
    with jax.named_scope("down_ring"):
        for step in range(4, chips // 2):
            next(down_ring)
        block_output = (residual + next(down_ring) + params[7]).astype(bf16)
    with jax.named_scope("last_ring"):
        sent, _ = ring.send(joint_given)
    with jax.named_scope("output_gradient"):
        low = after(back_all, sent)[:, width:]

        def by_heads(matrix):
            return jnp.concatenate(
                [
                    matrix[:, m * width : m * width + (firsts[m + 1] - firsts[m]) * size]
                    for m in range(chips)
                ],
                axis=1,
            )

        output_other = rows_by_rows(low[:, output_cols : 2 * output_cols], attended_wide)
    with jax.named_scope("down_gradient"):
        down_gradient = down_kept + after(down_arrived, sent).astype(f32)
    with jax.named_scope("joint_gradient"):
        mine = (mine + data_swap(joint_given).astype(f32)).astype(bf16)
        joint_sent = choose_rows(rows_here[5], mine, back_route[1])
    with jax.named_scope("last_ring"):
        for step in range(3, chips // 2):
            sent, _ = ring.send((output_other, joint_sent)) if step == 3 else next(ring)
    with jax.named_scope("output_gradient"):
        output_kept, output_given = pieces_of(
            after(low, sent)[:, :output_cols], output_other, attended_wide, by_heads
        )
        output_gradient = finish(output_kept, output_given).T
    with jax.named_scope("joint_gradient"):
        mine = run_route(joint_sent, back_route[0])
        joint_gradient = rows_by_rows(chosen_by(rows_here[6], mine.shape[0]), mine)[:, :half].T
    with jax.named_scope("vectors_gradient"):
        vectors_gradient = jnp.sum(
            lax.all_to_all(after(vectors_cut, sent), ("dp", "ctx"), 0, 0, tiled=True), axis=0
        )
    with jax.named_scope("last_ring"):
        normed_one_back = next(ring)
    with jax.named_scope("input_gradient"):
        _, first_pull = jax.vjp(layer_norm, rows_float, params[0], params[1])
        input_gradient = residual_back + first_pull(normed_one_back)[0]
    return (
        block_output[None],
        input_gradient[None],
        joint_gradient,
        output_gradient,
        up_gradient.T,
        down_gradient,
        vectors_gradient,
        bias_gradient,
    )


def solution(mesh):
    in_specs = (
        P("dp", "ctx", None),
        P("dp", None),
        P("dp", "ctx"),
        P("dp", "ctx"),
        P("dp", "ctx"),
        P("ctx", "dp"),
        P("dp", "ctx"),
        P("ctx"),
        P("dp", "ctx", None),
    )
    out_specs = (
        P("dp", "ctx", None),
        P("dp", "ctx", None),
        P("dp", "ctx"),
        P("dp", "ctx"),
        P("dp", "ctx"),
        P("ctx", "dp"),
        P("dp", "ctx"),
        P("ctx"),
    )
    return jax.shard_map(shards, mesh=mesh, in_specs=in_specs, out_specs=out_specs, check_vma=False)
```

time: 533 us -> 506 us (0.949)
  Pallas kernels: 68.8 us -> 112 us
  waiting for transfers between devices: 165 us -> 131 us
  local copies, waits for them, and re-layouts: 66.8 us -> 40.2 us
  other arithmetic: 54.6 us -> 69.9 us
  starting transfers between devices: 118 us -> 105 us
  between operations: 13.4 us -> 2.54 us
    ppermute x68 -> x52, waiting for transfers between devices: 140 us -> 61.4 us  [send(): return lax.ppermute(value, 'ctx', pairs)]
    pallas_call x7 -> x10, Pallas kernels: 68.8 us -> 112 us  [the longest x1 38.2 us: feed_forward(): pl.pallas_call(feed_forward_kernel, grid_spec=pltpu.PrefetchScalarGridSpe...]
    ppermute x9, waiting for transfers between devices: 0.02 us -> 41.1 us  [data_swap(): lax.ppermute(value, 'dp', [(i, i ^ 1) for i in range(lax.axis_size('dp'))])]
    ppermute x68 -> x52, starting transfers between devices: 90.2 us -> 68.5 us  [send(): return lax.ppermute(value, 'ctx', pairs)]
    dynamic_update_slice x36 -> x2, local copies, waits for them, and re-layouts: 21 us -> 0.36 us  [at_heads(): lax.dynamic_update_slice_in_dim(whole, row, first_column, 0)[:features]]
    convert_element_type x18 -> x24, other arithmetic: 9.85 us -> 26.3 us  [ring_scatter(): piece = piece.astype(bf16)]
    dot_general x8 -> x9, matrix products: 25.9 us -> 35.1 us  [rows_by_rows(): lax.dot_general(left_side, right_side, (((0,), (0,)), ((), ())), preferre...]
    ppermute x8 -> x0, local copies, waits for them, and re-layouts: 8.62 us -> none  [the longest x7 6.54 us: send(): return lax.ppermute(value, 'ctx', pairs)]
  transfers between devices with their start and end apart: 93 -> 84, of which waited for: 32 -> 31; matrix products, arithmetic and copies ran while one was open for 26% -> 25% of each run, Pallas kernels for 5% -> 15%
where the time goes in v3:
time: 506 us; the launch traced here: 498 us
  waiting for transfers between devices  131 us (26%)
  Pallas kernels  112 us (22%)
  starting transfers between devices  105 us (21%)
  other arithmetic  69.9 us (14%)
  local copies, waits for them, and re-layouts  40.2 us (8%)
  matrix products  37.1 us (7%)
    ppermute x52, starting transfers between devices, send(): return lax.ppermute(value, 'ctx', pairs)  68.5 us
    ppermute x52, waiting for transfers between devices, send(): return lax.ppermute(value, 'ctx', pairs)  61.4 us
    ppermute x9, waiting for transfers between devices, data_swap(): lax.ppermute(value, 'dp', [(i, i ^ 1) for i in range(lax.axis_size('dp'))])  41.1 us
    pallas_call x1, Pallas kernels, feed_forward(): pl.pallas_call(feed_forward_kernel, grid_spec=pltpu.PrefetchScalarGridSpe...  38.2 us
    dot_general x9, matrix products, rows_by_rows(): lax.dot_general(left_side, right_side, (((0,), (0,)), ((), ())), preferre...  35.1 us
    convert_element_type x24, other arithmetic, ring_scatter(): piece = piece.astype(bf16)  26.3 us
    ppermute x6, waiting for transfers between devices, run_route(): lax.ppermute(piece, 'ctx', group)  22.8 us
    unnamed x134, local copies, waits for them, and re-layouts  15.6 us
  transfers between devices with their start and end apart: 84, of which 31 were waited for; matrix products, arithmetic and copies ran while one was open for 25% of the time, Pallas kernels for 15%

profile of v3, /device:TPU:0, one launch (start us, length us, event | category | flops | bytes accessed | tf_op | source)
XLA Modules:
  0.0 497.5 jit_solution(3025089652642120048)
XLA Ops:
  1.9 7.3 %all-to-all-start = ((bf16[32,4,100]{2,1,0:T(4,128)(2,1)}), bf16[32,4,100]{2,1,0:T(4,128)(2,1)S(1)}, u32[]{:S(2)}, u32[]{:S(2)}) async-start(bf16[32,4,100]{2,1,0:T(4,128)(2,1)} %broadcast_in_dim.61), calls=%async_computation | async-start | bytes 65536 | tf_op jit(solution)/shard_map/parameters/all_to_all | solution.py:856
  13.9 2.6 all-to-all-done
  19.1 2.6 joint_weight.2
  26.4 22.8 %collective-permute-done.1 = bf16[160,896]{1,0:T(8,128)(2,1)S(1)} collective-permute-done((bf16[160,896]{1,0:T(8,128)(2,1)}, bf16[160,896]{1,0:T(8,128)(2,1)S(1)}, u32[]{:S(2)}, u32[]{:S(2)}) %collective-permute-start.1) | collective-permute-done | bytes 286752 | tf_op jit(solution)/shard_map/joint_weight/ppermute | solution.py:189
  50.6 10.2 %collective-permute-start.8 = (bf16[320,1600]{1,0:T(8,128)(2,1)}, bf16[320,1600]{1,0:T(8,128)(2,1)}, u32[]{:S(2)}, u32[]{:S(2)}) collective-permute-start(bf16[320,1600]{1,0:T(8,128)(2,1)} %collective-permute-done.6.refs_1_), channel_id=1, source_target_pairs={{0,2},{1,3},{4,0},{5,1},{8,4},{9,5},{12,8},{13,9},{14,12},{15,13},... | collective-permute-start | bytes 3072008 | tf_op jit(solution)/shard_map/input_ring/ppermute | solution.py:40
  61.4 19.7 %collective-permute-done.3.got = bf16[480,896]{1,0:T(8,128)(2,1)} collective-permute-done((bf16[480,896]{1,0:T(8,128)(2,1)}, bf16[480,896]{1,0:T(8,128)(2,1)}, u32[]{:S(2)}, u32[]{:S(2)}) %collective-permute-start.3) | collective-permute-done | bytes 860192 | tf_op jit(solution)/shard_map/joint_weight/ppermute | solution.py:48
  81.0 2.2 collective-permute-done.8.refs_2_
  92.5 7.0 %joint_weight.3.weight = bf16[768,1600]{1,0:T(8,128)(2,1)} custom-call(s32[1]{0:T(128)} %bitcast.1.flag, s32[1,768]{1,0:T(1,128)} %get-tuple-element.265.own_rows, s32[1,768]{1,0:T(1,128)} %get-tuple-element.264.mate_rows, bf16[480,896]{1,0:T(8,128)(2,1)} %constant_dynamic-update-slice_fusion.own, bf16[480,896]{1,0:T(8,128)(2,1)} %collective-permute-done.3.got, ...), custom_call_target="tpu_custom_call" | custom-call | tf_op jit(solution)/shard_map/joint_weight/pallas_call | solution.py:275
  99.6 7.8 %collective-permute-done.12 = bf16[400,800]{1,0:T(8,128)(2,1)} collective-permute-done((bf16[400,800]{1,0:T(8,128)(2,1)}, bf16[400,800]{1,0:T(8,128)(2,1)}, u32[]{:S(2)}, u32[]{:S(2)}) %collective-permute-start.12) | collective-permute-done | bytes 640032 | tf_op jit(solution)/shard_map/feed_forward_weights/ppermute | solution.py:48
  108.2 2.4 collective-permute-done.11.refs_5_
  117.1 5.9 %collective-permute-done.14 = bf16[160,1600]{1,0:T(8,128)(2,1)S(1)} collective-permute-done((bf16[160,1600]{1,0:T(8,128)(2,1)S(1)}, bf16[160,1600]{1,0:T(8,128)(2,1)S(1)}, u32[]{:S(2)}, u32[]{:S(2)}) %collective-permute-start.14) | collective-permute-done | bytes 512032 | tf_op jit(solution)/shard_map/input_ring/ppermute | solution.py:40
  123.1 4.5 collective-permute-done.13
  128.6 13.4 %projection.1 = (bf16[1024,1600]{1,0:T(8,128)(2,1)}, bf16[8,64,1600]{2,1,0:T(8,128)(2,1)}, bf16[1024,1600]{1,0:T(8,128)(2,1)}, bf16[1024,1600]{1,0:T(8,128)(2,1)...) custom-call(s32[17]{0:T(128)} %pad_add_fusion.table, bf16[768,1600]{1,0:T(8,128)(2,1)} %joint_weight.3.weight, ...), custom_call_target="tpu_custom_call" | custom-call | tf_op jit(solution)/shard_map/projection/pallas_call | solution.py:542
  146.7 10.4 %shard_map.179 = (bf16[1024,256]{1,0:T(8,128)(2,1)}, f32[8,2,256,1]{3,2,1,0:T(8,128)}) custom-call(s32[1]{0:T(128)} %bitcast.odd_core, f32[8,128,384]{2,1,0:T(8,128)} %and_select_fusion.bias, bf16[1024,256]{1,0:T(8,128)(2,1)} %get-tuple-element.122.query, bf16[2,1024,256]{2,1,0:T(8,128)(2,1)} %get-tuple-element.125.far.own, ...), custom_call_target="tpu_custom_call" | custom-call | tf_op jit(solution)/shard_map/pallas_call | solution.py:454
  159.1 12.2 %collective-permute-done.19.refs_1_ = bf16[1024,256]{1,0:T(8,128)(2,1)S(1)} collective-permute-done((bf16[1024,256]{1,0:T(8,128)(2,1)}, bf16[1024,256]{1,0:T(8,128)(2,1)S(1)}, u32[]{:S(2)}, u32[]{:S(2)}) %collective-permute-start.19) | collective-permute-done | bytes 524320 | tf_op jit(solution)/shard_map/attended_ring/ppermute | solution.py:40
  174.1 8.7 %collective-permute-done.15.got = bf16[8,64,1600]{2,1,0:T(8,128)(2,1)} collective-permute-done((bf16[8,64,1600]{2,1,0:T(8,128)(2,1)}, bf16[8,64,1600]{2,1,0:T(8,128)(2,1)}, u32[]{:S(2)}, u32[]{:S(2)}) %collective-permute-start.15) | collective-permute-done | bytes 1638432 | tf_op jit(solution)/shard_map/output_weight/ppermute | solution.py:48
  182.8 2.6 collective-permute-done.22.refs_2_
  187.4 2.3 maximum_select_fusion.up_own
  189.8 3.0 maximum_select_fusion.1.down_own
  195.9 9.8 %output_weight.1.output_full = bf16[1600,2048]{1,0:T(8,128)(2,1)} custom-call(s32[2]{0:T(128)} %pad_add_fusion.1.flags, bf16[8,64,1600]{2,1,0:T(8,128)(2,1)} %get-tuple-element.127.own, bf16[8,64,1600]{2,1,0:T(8,128)(2,1)} %collective-permute-done.15.got, bf16[8,64,1600]{2,1,0:T(8,128)(2,1)} %collective-permute-done.20.mate_own, ...), custom_call_target="tpu_custom_call" | custom-call | tf_op jit(solution)/shard_map/output_weight/pallas_call | solution.py:316
  215.3 3.0 collective-permute-done.30
  220.9 38.2 %shard_map.180 = (bf16[1024,1600]{1,0:T(8,128)(2,1)}, bf16[1024,400]{1,0:T(8,128)(2,1)}, bf16[1024,400]{1,0:T(8,128)(2,1)}, bf16[1024,400]{1,0:T(8,128)(2,1)}, b...) custom-call(s32[17]{0:T(128)} %pad_add_fusion.table, ...), custom_call_target="tpu_custom_call" | custom-call | tf_op jit(solution)/shard_map/pallas_call | solution.py:650
  259.9 2.8 slice_bitcast_fusion.4
  277.1 4.5 fusion.66
  281.6 3.2 fusion.65
  303.0 4.7 collective-permute-done.45
  309.7 2.1 multiply_reduce_fusion
  316.4 2.6 shard_map.181
  319.0 4.2 all-to-all-start.1
  329.6 4.5 convolution_add_fusion.2
  336.5 3.5 convolution_add_fusion.1
  342.7 9.3 %collective-permute-done.50 = bf16[128,1600]{1,0:T(8,128)(2,1)} collective-permute-done((bf16[128,1600]{1,0:T(8,128)(2,1)S(1)}, bf16[128,1600]{1,0:T(8,128)(2,1)}, u32[]{:S(2)}, u32[]{:S(2)}) %collective-permute-start.50) | collective-permute-done | bytes 409632 | tf_op jit(solution)/shard_map/down_ring/ppermute | solution.py:40
  356.0 6.2 %collective-permute-start.53 = (bf16[128,1600]{1,0:T(8,128)(2,1)S(1)}, bf16[128,1600]{1,0:T(8,128)(2,1)S(1)}, u32[]{:S(2)}, u32[]{:S(2)}) collective-permute-start(bf16[128,1600]{1,0:T(8,128)(2,1)S(1)} %fusion.11), channel_id=1, source_target_pairs={{0,4},{1,5},{4,8},{5,9},{8,12},{9,13},{12,14},{13,15},{14,10},{15,... | collective-permute-start | bytes 1228808 | tf_op jit(solution)/shard_map/down_ring/ppermute | solution.py:40
  362.1 13.7 %shard_map.182 = (bf16[1024,256]{1,0:T(8,128)(2,1)}, f32[2,1024,256]{2,1,0:T(8,128)}, bf16[2,1024,256]{2,1,0:T(8,128)(2,1)}, f32[8,256]{1,0:T(8,128)}) custom-call(s32[1]{0:T(128)} %bitcast.odd_core, f32[8,128,384]{2,1,0:T(8,128)} %and_select_fusion.bias, bf16[1024,256]{1,0:T(8,128)(2,1)} %get-tuple-element.122.query, ...), custom_call_target="tpu_custom_call" | custom-call | tf_op jit(solution)/shard_map/pallas_call | solution.py:477
  381.8 11.2 %shard_map.183 = (bf16[1024,416]{1,0:T(8,128)(2,1)}, bf16[1024,416]{1,0:T(8,128)(2,1)}, bf16[8,128,1600]{2,1,0:T(8,128)(2,1)}, f32[8,1600]{1,0:T(8,128)}, f32[8,256]{1,0:T(8,128)}) custom-call(s32[17]{0:T(128)} %pad_add_fusion.table, bf16[1024,256]{1,0:T(8,128)(2,1)} %get-tuple-element.169.query_back, f32[2,1024,256]{2,1,0:T(8,128)} %get-tuple-element.166.own_back, ...), custom_call_target="tpu_custom_call" | custom-call | tf_op jit(solution)/shard_map/pallas_call | solution.py:735
  393.0 2.2 slice_bitcast_fusion
  396.1 5.8 %fusion.67 = f32[416,1600]{1,0:T(8,128)} fusion(bf16[1024,416]{1,0:T(8,128)(2,1)} %get-tuple-element.176, bf16[1024,1600]{1,0:T(8,128)(2,1)} %get-tuple-element.177), kind=kOutput, calls=%fused_computation.201 | convolution fusion | flops 1363148800 | bytes 6791168 | tf_op jit(solution)/shard_map/joint_gradient/dot_general | solution.py:215
  406.5 2.6 add_bitcast_fusion
  423.4 4.9 convolution_add_fusion
  439.6 2.8 fusion.44
  442.4 5.0 collective-permute-done.67
  448.8 2.7 joint_gradient.1
  464.0 3.2 convolution_add_fusion.3
  468.5 5.1 %collective-permute-start.75 = (bf16[256,896]{1,0:T(8,128)(2,1)}, bf16[256,896]{1,0:T(8,128)(2,1)}, u32[]{:S(2)}, u32[]{:S(2)}) collective-permute-start(bf16[256,896]{1,0:T(8,128)(2,1)} %get-tuple-element.190), channel_id=1, source_target_pairs={{15,15},{14,10},{0,0},{1,5},{3,11},{5,1},{7,7},{9,13},{11,3},{13,9... | collective-permute-start | bytes 1376264 | tf_op jit(solution)/shard_map/joint_gradient/ppermute | solution.py:189
  480.6 3.3 all-to-all-start.2
  483.9 2.7 convert_add_fusion
  487.4 2.3 copy.37
  494.7 2.6 convolution_bitcast_fusion
  (407 shorter events, 178.8 us)
Async XLA Ops:
  1.9 14.6 %all-to-all-start = ((bf16[32,4,100]{2,1,0:T(4,128)(2,1)}), bf16[32,4,100]{2,1,0:T(4,128)(2,1)S(1)}, u32[]{:S(2)}, u32[]{:S(2)}) async-start(bf16[32,4,100]{2,1,0:T(4,128)(2,1)} %broadcast_in_dim.61), calls=%async_computation | async-start | bytes 65536 | tf_op jit(solution)/shard_map/parameters/all_to_all | solution.py:856
  16.5 34.1 %collective-permute-start.7 = (bf16[320,1600]{1,0:T(8,128)(2,1)S(1)}, bf16[320,1600]{1,0:T(8,128)(2,1)S(1)}, u32[]{:S(2)}, u32[]{:S(2)}) collective-permute-start(bf16[320,1600]{1,0:T(8,128)(2,1)S(1)} %pad_maximum_fusion.refs_0_), channel_id=1, source_target_pairs={{0,4},{1,5},{4,8},{5,9},{8,12},{9,13},{12,14},{13,15},{14,10},{15,... | collective-permute-start | bytes 3072008 | tf_op jit(solution)/shard_map/input_ring/ppermute | solution.py:40
  16.9 33.7 %collective-permute-start.6 = (bf16[320,1600]{1,0:T(8,128)(2,1)S(1)}, bf16[320,1600]{1,0:T(8,128)(2,1)}, u32[]{:S(2)}, u32[]{:S(2)}) collective-permute-start(bf16[320,1600]{1,0:T(8,128)(2,1)S(1)} %pad_maximum_fusion.refs_0_), channel_id=1, source_target_pairs={{0,2},{1,3},{4,0},{5,1},{8,4},{9,5},{12,8},{13,9},{14,12},{15,13},... | collective-permute-start | bytes 3072008 | tf_op jit(solution)/shard_map/input_ring/ppermute | solution.py:40
  23.4 25.8 %collective-permute-start.1 = (bf16[160,896]{1,0:T(8,128)(2,1)}, bf16[160,896]{1,0:T(8,128)(2,1)S(1)}, u32[]{:S(2)}, u32[]{:S(2)}) collective-permute-start(bf16[160,896]{1,0:T(8,128)(2,1)} %get-tuple-element.108), channel_id=1, source_target_pairs={{4,14},{14,12},{8,10},{2,8},{12,6},{6,4},{0,2},{5,15},{10,0},{11,1... | collective-permute-start | bytes 860168 | tf_op jit(solution)/shard_map/joint_weight/ppermute | solution.py:189
  24.9 25.0 %collective-permute-start.2 = (bf16[64,896]{1,0:T(8,128)(2,1)}, bf16[64,896]{1,0:T(8,128)(2,1)S(1)}, u32[]{:S(2)}, u32[]{:S(2)}) collective-permute-start(bf16[64,896]{1,0:T(8,128)(2,1)} %get-tuple-element.109), channel_id=1, source_target_pairs={{9,15},{3,13},{13,11},{7,9},{1,7},{11,5},{5,3},{25,31},{19,29},{29... | collective-permute-start | bytes 344072 | tf_op jit(solution)/shard_map/joint_weight/ppermute | solution.py:189
  50.6 32.6 %collective-permute-start.8 = (bf16[320,1600]{1,0:T(8,128)(2,1)}, bf16[320,1600]{1,0:T(8,128)(2,1)}, u32[]{:S(2)}, u32[]{:S(2)}) collective-permute-start(bf16[320,1600]{1,0:T(8,128)(2,1)} %collective-permute-done.6.refs_1_), channel_id=1, source_target_pairs={{0,2},{1,3},{4,0},{5,1},{8,4},{9,5},{12,8},{13,9},{14,12},{15,13},... | collective-permute-start | bytes 3072008 | tf_op jit(solution)/shard_map/input_ring/ppermute | solution.py:40
  60.8 24.4 %collective-permute-start.9 = (bf16[320,1600]{1,0:T(8,128)(2,1)S(1)}, bf16[320,1600]{1,0:T(8,128)(2,1)}, u32[]{:S(2)}, u32[]{:S(2)}) collective-permute-start(bf16[320,1600]{1,0:T(8,128)(2,1)S(1)} %collective-permute-done.7.refs_7_), channel_id=1, source_target_pairs={{0,4},{1,5},{4,8},{5,9},{8,12},{9,13},{12,14},{13,15},{14,10},{15,... | collective-permute-start | bytes 3072008 | tf_op jit(solution)/shard_map/input_ring/ppermute | solution.py:40
  60.8 20.3 %collective-permute-start.3 = (bf16[480,896]{1,0:T(8,128)(2,1)}, bf16[480,896]{1,0:T(8,128)(2,1)}, u32[]{:S(2)}, u32[]{:S(2)}) collective-permute-start(bf16[480,896]{1,0:T(8,128)(2,1)} %constant_dynamic-update-slice_fusion.own), channel_id=1, source_target_pairs={{0,16},{16,0},{1,17},{17,1},{2,18},{18,2},{3,19},{19,3},{4,20},{20... | collective-permute-start | bytes 2580488 | tf_op jit(solution)/shard_map/joint_weight/ppermute | solution.py:48
  85.2 23.0 %collective-permute-start.10 = (bf16[320,1600]{1,0:T(8,128)(2,1)}, bf16[320,1600]{1,0:T(8,128)(2,1)S(1)}, u32[]{:S(2)}, u32[]{:S(2)}) collective-permute-start(bf16[320,1600]{1,0:T(8,128)(2,1)} %collective-permute-done.8.refs_2_), channel_id=1, source_target_pairs={{0,2},{1,3},{4,0},{5,1},{8,4},{9,5},{12,8},{13,9},{14,12},{15,13},... | collective-permute-start | bytes 3072008 | tf_op jit(solution)/shard_map/input_ring/ppermute | solution.py:40
  86.7 23.9 %collective-permute-start.11 = (bf16[320,1600]{1,0:T(8,128)(2,1)}, bf16[320,1600]{1,0:T(8,128)(2,1)}, u32[]{:S(2)}, u32[]{:S(2)}) collective-permute-start(bf16[320,1600]{1,0:T(8,128)(2,1)} %collective-permute-done.9.refs_6_), channel_id=1, source_target_pairs={{0,4},{1,5},{4,8},{5,9},{8,12},{9,13},{12,14},{13,15},{14,10},{15,... | collective-permute-start | bytes 3072008 | tf_op jit(solution)/shard_map/input_ring/ppermute | solution.py:40
  89.0 18.3 %collective-permute-start.12 = (bf16[400,800]{1,0:T(8,128)(2,1)}, bf16[400,800]{1,0:T(8,128)(2,1)}, u32[]{:S(2)}, u32[]{:S(2)}) collective-permute-start(bf16[400,800]{1,0:T(8,128)(2,1)} %bitcast.197), channel_id=1, source_target_pairs={{0,16},{16,0},{1,17},{17,1},{2,18},{18,2},{3,19},{19,3},{4,20},{20... | collective-permute-start | bytes 1920008 | tf_op jit(solution)/shard_map/feed_forward_weights/ppermute | solution.py:48
  115.0 27.0 %collective-permute-start.16 = (bf16[400,800]{1,0:T(8,128)(2,1)S(1)}, bf16[400,800]{1,0:T(8,128)(2,1)S(1)}, u32[]{:S(2)}, u32[]{:S(2)}) collective-permute-start(bf16[400,800]{1,0:T(8,128)(2,1)S(1)} %copy-done.39), channel_id=1, source_target_pairs={{0,16},{16,0},{1,17},{17,1},{2,18},{18,2},{3,19},{19,3},{4,20},{20... | collective-permute-start | bytes 1920008 | tf_op jit(solution)/shard_map/feed_forward_weights/ppermute | solution.py:48
  142.9 39.9 %collective-permute-start.15 = (bf16[8,64,1600]{2,1,0:T(8,128)(2,1)}, bf16[8,64,1600]{2,1,0:T(8,128)(2,1)}, u32[]{:S(2)}, u32[]{:S(2)}) collective-permute-start(bf16[8,64,1600]{2,1,0:T(8,128)(2,1)} %get-tuple-element.127.own), channel_id=1, source_target_pairs={{0,16},{16,0},{1,17},{17,1},{2,18},{18,2},{3,19},{19,3},{4,20},{20... | collective-permute-start | bytes 4915208 | tf_op jit(solution)/shard_map/output_weight/ppermute | solution.py:48
  158.8 15.0 %collective-permute-start.18 = (bf16[1024,256]{1,0:T(8,128)(2,1)}, bf16[1024,256]{1,0:T(8,128)(2,1)S(1)}, u32[]{:S(2)}, u32[]{:S(2)}) collective-permute-start(bf16[1024,256]{1,0:T(8,128)(2,1)} %get-tuple-element.126.refs_0_.mixed), channel_id=1, source_target_pairs={{0,4},{1,5},{4,8},{5,9},{8,12},{9,13},{12,14},{13,15},{14,10},{15,... | collective-permute-start | bytes 1572872 | tf_op jit(solution)/shard_map/attended_ring/ppermute | solution.py:40
  189.7 30.1 %collective-permute-start.24 = (bf16[400,1600]{1,0:T(8,128)(2,1)S(1)}, bf16[400,1600]{1,0:T(8,128)(2,1)S(1)}, u32[]{:S(2)}, u32[]{:S(2)}) collective-permute-start(bf16[400,1600]{1,0:T(8,128)(2,1)S(1)} %maximum_select_fusion.up_own), channel_id=1, source_target_pairs={{0,1},{1,0},{2,3},{3,2},{4,5},{5,4},{6,7},{7,6},{8,9},{9,8},{10,11... | collective-permute-start | bytes 3840008 | tf_op jit(solution)/shard_map/feed_forward_weights/ppermute | solution.py:44
  192.9 27.0 %collective-permute-start.25 = (bf16[400,1600]{1,0:T(8,128)(2,1)S(1)}, bf16[400,1600]{1,0:T(8,128)(2,1)}, u32[]{:S(2)}, u32[]{:S(2)}) collective-permute-start(bf16[400,1600]{1,0:T(8,128)(2,1)S(1)} %maximum_select_fusion.1.down_own), channel_id=1, source_target_pairs={{0,1},{1,0},{2,3},{3,2},{4,5},{5,4},{6,7},{7,6},{8,9},{9,8},{10,11... | collective-permute-start | bytes 3840008 | tf_op jit(solution)/shard_map/feed_forward_weights/ppermute | solution.py:44
  193.1 14.5 %collective-permute-start.27 = (bf16[1024,256]{1,0:T(8,128)(2,1)}, bf16[1024,256]{1,0:T(8,128)(2,1)}, u32[]{:S(2)}, u32[]{:S(2)}) collective-permute-start(bf16[1024,256]{1,0:T(8,128)(2,1)} %collective-permute-done.22.refs_2_), channel_id=1, source_target_pairs={{0,2},{1,3},{4,0},{5,1},{8,4},{9,5},{12,8},{13,9},{14,12},{15,13},... | collective-permute-start | bytes 1572872 | tf_op jit(solution)/shard_map/attended_ring/ppermute | solution.py:40
  267.5 34.8 %collective-permute-start.52 = (f32[400]{0:T(512)S(1)}, f32[400]{0:T(512)S(1)}, u32[]{:S(2)}, u32[]{:S(2)}) collective-permute-start(f32[400]{0:T(512)S(1)} %add.307), channel_id=1, source_target_pairs={{0,16},{16,0},{1,17},{17,1},{2,18},{18,2},{3,19},{19,3},{4,20},{20... | collective-permute-start | bytes 4808 | tf_op jit(solution)/shard_map/back_exchange/ppermute | solution.py:48
  270.0 14.8 %collective-permute-start.32 = (bf16[64,1600]{1,0:T(8,128)(2,1)S(1)}, bf16[64,1600]{1,0:T(8,128)(2,1)S(1)}, u32[]{:S(2)}, u32[]{:S(2)}) collective-permute-start(bf16[64,1600]{1,0:T(8,128)(2,1)S(1)} %fusion.38), channel_id=1, source_target_pairs={{0,4},{1,5},{4,8},{5,9},{8,12},{9,13},{12,14},{13,15},{14,10},{15,... | collective-permute-start | bytes 614408 | tf_op jit(solution)/shard_map/normed_two_back_ring/ppermute | solution.py:40
  271.1 15.9 %collective-permute-start.37 = (bf16[64,1600]{1,0:T(8,128)(2,1)}, bf16[64,1600]{1,0:T(8,128)(2,1)S(1)}, u32[]{:S(2)}, u32[]{:S(2)}) collective-permute-start(bf16[64,1600]{1,0:T(8,128)(2,1)} %get-tuple-element.137), channel_id=1, source_target_pairs={{0,2},{1,3},{4,0},{5,1},{8,4},{9,5},{12,8},{13,9},{14,12},{15,13},... | collective-permute-start | bytes 614408 | tf_op jit(solution)/shard_map/normed_two_back_ring/ppermute | solution.py:40
  272.0 17.0 %collective-permute-start.36 = (bf16[64,1600]{1,0:T(8,128)(2,1)}, bf16[64,1600]{1,0:T(8,128)(2,1)S(1)}, u32[]{:S(2)}, u32[]{:S(2)}) collective-permute-start(bf16[64,1600]{1,0:T(8,128)(2,1)} %get-tuple-element.138), channel_id=1, source_target_pairs={{0,4},{1,5},{4,8},{5,9},{8,12},{9,13},{12,14},{13,15},{14,10},{15,... | collective-permute-start | bytes 614408 | tf_op jit(solution)/shard_map/normed_two_back_ring/ppermute | solution.py:40
  275.8 15.3 %collective-permute-start.35 = (bf16[64,1600]{1,0:T(8,128)(2,1)S(1)}, bf16[64,1600]{1,0:T(8,128)(2,1)S(1)}, u32[]{:S(2)}, u32[]{:S(2)}) collective-permute-start(bf16[64,1600]{1,0:T(8,128)(2,1)S(1)} %fusion.37), channel_id=1, source_target_pairs={{0,2},{1,3},{4,0},{5,1},{8,4},{9,5},{12,8},{13,9},{14,12},{15,13},... | collective-permute-start | bytes 614408 | tf_op jit(solution)/shard_map/normed_two_back_ring/ppermute | solution.py:40
  294.1 15.5 %collective-permute-start.42 = (bf16[64,1600]{1,0:T(8,128)(2,1)S(1)}, bf16[64,1600]{1,0:T(8,128)(2,1)S(1)}, u32[]{:S(2)}, u32[]{:S(2)}) collective-permute-start(bf16[64,1600]{1,0:T(8,128)(2,1)S(1)} %fusion.40), channel_id=1, source_target_pairs={{0,4},{1,5},{4,8},{5,9},{8,12},{9,13},{12,14},{13,15},{14,10},{15,... | collective-permute-start | bytes 614408 | tf_op jit(solution)/shard_map/normed_two_back_ring/ppermute | solution.py:40
  303.0 33.5 %collective-permute-start.49 = (f32[400,1600]{1,0:T(8,128)}, f32[400,1600]{1,0:T(8,128)}, u32[]{:S(2)}, u32[]{:S(2)}) collective-permute-start(f32[400,1600]{1,0:T(8,128)} %fusion.66), channel_id=1, source_target_pairs={{0,1},{1,0},{2,3},{3,2},{4,5},{5,4},{6,7},{7,6},{8,9},{9,8},{10,11... | collective-permute-start | bytes 7680008 | tf_op jit(solution)/shard_map/down_gradient/ppermute | solution.py:44
  307.6 22.0 %collective-permute-start.48 = (f32[400,1600]{1,0:T(8,128)}, f32[400,1600]{1,0:T(8,128)}, u32[]{:S(2)}, u32[]{:S(2)}) collective-permute-start(f32[400,1600]{1,0:T(8,128)} %fusion.65), channel_id=1, source_target_pairs={{0,1},{1,0},{2,3},{3,2},{4,5},{5,4},{6,7},{7,6},{8,9},{9,8},{10,11... | collective-permute-start | bytes 7680008 | tf_op jit(solution)/shard_map/up_gradient/ppermute | solution.py:44
  307.6 15.6 %collective-permute-start.41 = (bf16[64,1600]{1,0:T(8,128)(2,1)}, bf16[64,1600]{1,0:T(8,128)(2,1)}, u32[]{:S(2)}, u32[]{:S(2)}) collective-permute-start(bf16[64,1600]{1,0:T(8,128)(2,1)} %get-tuple-element.153), channel_id=1, source_target_pairs={{0,4},{1,5},{4,8},{5,9},{8,12},{9,13},{12,14},{13,15},{14,10},{15,... | collective-permute-start | bytes 614408 | tf_op jit(solution)/shard_map/down_ring/ppermute | solution.py:40
  308.2 19.1 %collective-permute-start.47 = (bf16[64,1600]{1,0:T(8,128)(2,1)}, bf16[64,1600]{1,0:T(8,128)(2,1)}, u32[]{:S(2)}, u32[]{:S(2)}) collective-permute-start(bf16[64,1600]{1,0:T(8,128)(2,1)} %get-tuple-element.154), channel_id=1, source_target_pairs={{0,2},{1,3},{4,0},{5,1},{8,4},{9,5},{12,8},{13,9},{14,12},{15,13},... | collective-permute-start | bytes 614408 | tf_op jit(solution)/shard_map/down_ring/ppermute | solution.py:40
  319.0 33.0 %all-to-all-start.1 = ((bf16[8,128,512]{2,1,0:T(8,128)(2,1)}), bf16[8,128,512]{2,1,0:T(8,128)(2,1)}, u32[]{:S(2)}, u32[]{:S(2)}) async-start(bf16[8,128,512]{2,1,0:T(8,128)(2,1)} %shard_map.181), calls=%async_computation.1 | async-start | bytes 2097152 | tf_op jit(solution)/shard_map/back_exchange/all_to_all | solution.py:127
  325.4 26.6 %collective-permute-start.46 = (bf16[128,1600]{1,0:T(8,128)(2,1)S(1)}, bf16[128,1600]{1,0:T(8,128)(2,1)}, u32[]{:S(2)}, u32[]{:S(2)}) collective-permute-start(bf16[128,1600]{1,0:T(8,128)(2,1)S(1)} %pad_maximum_fusion.7), channel_id=1, source_target_pairs={{0,4},{1,5},{4,8},{5,9},{8,12},{9,13},{12,14},{13,15},{14,10},{15,... | collective-permute-start | bytes 1228808 | tf_op jit(solution)/shard_map/down_ring/ppermute | solution.py:40
  329.4 22.6 %collective-permute-start.50 = (bf16[128,1600]{1,0:T(8,128)(2,1)S(1)}, bf16[128,1600]{1,0:T(8,128)(2,1)}, u32[]{:S(2)}, u32[]{:S(2)}) collective-permute-start(bf16[128,1600]{1,0:T(8,128)(2,1)S(1)} %pad_maximum_fusion.8), channel_id=1, source_target_pairs={{0,2},{1,3},{4,0},{5,1},{8,4},{9,5},{12,8},{13,9},{14,12},{15,13},... | collective-permute-start | bytes 1228808 | tf_op jit(solution)/shard_map/down_ring/ppermute | solution.py:40
  335.4 40.5 %collective-permute-start.57 = (bf16[400,800]{1,0:T(8,128)(2,1)}, bf16[400,800]{1,0:T(8,128)(2,1)}, u32[]{:S(2)}, u32[]{:S(2)}) collective-permute-start(bf16[400,800]{1,0:T(8,128)(2,1)} %select_convert_fusion.2), channel_id=1, source_target_pairs={{0,16},{16,0},{1,17},{17,1},{2,18},{18,2},{3,19},{19,3},{4,20},{20... | collective-permute-start | bytes 1920008 | tf_op jit(solution)/shard_map/up_gradient/ppermute | solution.py:48
  354.5 21.3 %collective-permute-start.55 = (bf16[128,1600]{1,0:T(8,128)(2,1)S(1)}, bf16[128,1600]{1,0:T(8,128)(2,1)S(1)}, u32[]{:S(2)}, u32[]{:S(2)}) collective-permute-start(bf16[128,1600]{1,0:T(8,128)(2,1)S(1)} %fusion.9), channel_id=1, source_target_pairs={{0,2},{1,3},{4,0},{5,1},{8,4},{9,5},{12,8},{13,9},{14,12},{15,13},... | collective-permute-start | bytes 1228808 | tf_op jit(solution)/shard_map/down_ring/ppermute | solution.py:40
  356.0 19.9 %collective-permute-start.53 = (bf16[128,1600]{1,0:T(8,128)(2,1)S(1)}, bf16[128,1600]{1,0:T(8,128)(2,1)S(1)}, u32[]{:S(2)}, u32[]{:S(2)}) collective-permute-start(bf16[128,1600]{1,0:T(8,128)(2,1)S(1)} %fusion.11), channel_id=1, source_target_pairs={{0,4},{1,5},{4,8},{5,9},{8,12},{9,13},{12,14},{13,15},{14,10},{15,... | collective-permute-start | bytes 1228808 | tf_op jit(solution)/shard_map/down_ring/ppermute | solution.py:40
  377.6 17.5 %collective-permute-start.54 = (bf16[128,1600]{1,0:T(8,128)(2,1)S(1)}, bf16[128,1600]{1,0:T(8,128)(2,1)S(1)}, u32[]{:S(2)}, u32[]{:S(2)}) collective-permute-start(bf16[128,1600]{1,0:T(8,128)(2,1)S(1)} %fusion.12), channel_id=1, source_target_pairs={{0,4},{1,5},{4,8},{5,9},{8,12},{9,13},{12,14},{13,15},{14,10},{15,... | collective-permute-start | bytes 1228808 | tf_op jit(solution)/shard_map/down_ring/ppermute | solution.py:40
  401.8 20.5 %collective-permute-start.62 = (f32[416,1600]{1,0:T(8,128)}, f32[416,1600]{1,0:T(8,128)}, u32[]{:S(2)}, u32[]{:S(2)}) collective-permute-start(f32[416,1600]{1,0:T(8,128)} %fusion.67), channel_id=1, source_target_pairs={{0,1},{1,0},{2,3},{3,2},{4,5},{5,4},{6,7},{7,6},{8,9},{9,8},{10,11... | collective-permute-start | bytes 7987208 | tf_op jit(solution)/shard_map/joint_gradient/ppermute | solution.py:44
  403.9 34.1 %collective-permute-start.80 = (bf16[400,800]{1,0:T(8,128)(2,1)}, bf16[400,800]{1,0:T(8,128)(2,1)}, u32[]{:S(2)}, u32[]{:S(2)}) collective-permute-start(bf16[400,800]{1,0:T(8,128)(2,1)} %select_convert_fusion.1), channel_id=1, source_target_pairs={{0,16},{16,0},{1,17},{17,1},{2,18},{18,2},{3,19},{19,3},{4,20},{20... | collective-permute-start | bytes 1920008 | tf_op jit(solution)/shard_map/down_gradient/ppermute | solution.py:48
  417.6 14.5 %collective-permute-start.66 = (bf16[64,1600]{1,0:T(8,128)(2,1)}, bf16[64,1600]{1,0:T(8,128)(2,1)S(1)}, u32[]{:S(2)}, u32[]{:S(2)}) collective-permute-start(bf16[64,1600]{1,0:T(8,128)(2,1)} %get-tuple-element.179), channel_id=1, source_target_pairs={{0,2},{1,3},{4,0},{5,1},{8,4},{9,5},{12,8},{13,9},{14,12},{15,13},... | collective-permute-start | bytes 614408 | tf_op jit(solution)/shard_map/last_ring/ppermute | solution.py:40
  430.5 16.9 %collective-permute-start.67 = (bf16[416,800]{1,0:T(8,128)(2,1)S(1)}, bf16[416,800]{1,0:T(8,128)(2,1)S(1)}, u32[]{:S(2)}, u32[]{:S(2)}) collective-permute-start(bf16[416,800]{1,0:T(8,128)(2,1)S(1)} %select_convert_fusion), channel_id=1, source_target_pairs={{0,16},{16,0},{1,17},{17,1},{2,18},{18,2},{3,19},{19,3},{4,20},{20... | collective-permute-start | bytes 1996808 | tf_op jit(solution)/shard_map/joint_gradient/ppermute | solution.py:48
  434.3 25.0 %collective-permute-start.73 = (bf16[64,1600]{1,0:T(8,128)(2,1)}, bf16[64,1600]{1,0:T(8,128)(2,1)}, u32[]{:S(2)}, u32[]{:S(2)}) collective-permute-start(bf16[64,1600]{1,0:T(8,128)(2,1)} %fusion.25), channel_id=1, source_target_pairs={{0,2},{1,3},{4,0},{5,1},{8,4},{9,5},{12,8},{13,9},{14,12},{15,13},... | collective-permute-start | bytes 614408 | tf_op jit(solution)/shard_map/last_ring/ppermute | solution.py:40
  436.0 20.8 %collective-permute-start.69 = (bf16[64,1600]{1,0:T(8,128)(2,1)}, bf16[64,1600]{1,0:T(8,128)(2,1)}, u32[]{:S(2)}, u32[]{:S(2)}) collective-permute-start(bf16[64,1600]{1,0:T(8,128)(2,1)} %fusion.24), channel_id=1, source_target_pairs={{0,4},{1,5},{4,8},{5,9},{8,12},{9,13},{12,14},{13,15},{14,10},{15,... | collective-permute-start | bytes 614408 | tf_op jit(solution)/shard_map/last_ring/ppermute | solution.py:40
  436.3 17.7 %collective-permute-start.70 = (bf16[64,1600]{1,0:T(8,128)(2,1)}, bf16[64,1600]{1,0:T(8,128)(2,1)}, u32[]{:S(2)}, u32[]{:S(2)}) collective-permute-start(bf16[64,1600]{1,0:T(8,128)(2,1)} %fusion.23), channel_id=1, source_target_pairs={{0,2},{1,3},{4,0},{5,1},{8,4},{9,5},{12,8},{13,9},{14,12},{15,13},... | collective-permute-start | bytes 614408 | tf_op jit(solution)/shard_map/last_ring/ppermute | solution.py:40
  447.4 14.8 %collective-permute-start.78 = (f32[100,2048]{1,0:T(8,128)}, f32[100,2048]{1,0:T(8,128)}, u32[]{:S(2)}, u32[]{:S(2)}) collective-permute-start(f32[100,2048]{1,0:T(8,128)} %fusion.44), channel_id=1, source_target_pairs={{0,1},{1,0},{2,3},{3,2},{4,5},{5,4},{6,7},{7,6},{8,9},{9,8},{10,11... | collective-permute-start | bytes 2457608 | tf_op jit(solution)/shard_map/output_gradient/ppermute | solution.py:44
  453.1 21.4 %collective-permute-start.68 = (bf16[64,1600]{1,0:T(8,128)(2,1)}, bf16[64,1600]{1,0:T(8,128)(2,1)}, u32[]{:S(2)}, u32[]{:S(2)}) collective-permute-start(bf16[64,1600]{1,0:T(8,128)(2,1)} %fusion.29), channel_id=1, source_target_pairs={{0,4},{1,5},{4,8},{5,9},{8,12},{9,13},{12,14},{13,15},{14,10},{15,... | collective-permute-start | bytes 614408 | tf_op jit(solution)/shard_map/last_ring/ppermute | solution.py:40
  455.6 18.9 %collective-permute-start.72 = (bf16[64,1600]{1,0:T(8,128)(2,1)}, bf16[64,1600]{1,0:T(8,128)(2,1)}, u32[]{:S(2)}, u32[]{:S(2)}) collective-permute-start(bf16[64,1600]{1,0:T(8,128)(2,1)} %fusion.21), channel_id=1, source_target_pairs={{0,2},{1,3},{4,0},{5,1},{8,4},{9,5},{12,8},{13,9},{14,12},{15,13},... | collective-permute-start | bytes 614408 | tf_op jit(solution)/shard_map/last_ring/ppermute | solution.py:40
  458.5 15.1 %collective-permute-start.71 = (bf16[64,1600]{1,0:T(8,128)(2,1)}, bf16[64,1600]{1,0:T(8,128)(2,1)}, u32[]{:S(2)}, u32[]{:S(2)}) collective-permute-start(bf16[64,1600]{1,0:T(8,128)(2,1)} %fusion.22), channel_id=1, source_target_pairs={{0,4},{1,5},{4,8},{5,9},{8,12},{9,13},{12,14},{13,15},{14,10},{15,... | collective-permute-start | bytes 614408 | tf_op jit(solution)/shard_map/last_ring/ppermute | solution.py:40
  462.2 32.5 %collective-permute-start.76 = (bf16[160,896]{1,0:T(8,128)(2,1)}, bf16[160,896]{1,0:T(8,128)(2,1)}, u32[]{:S(2)}, u32[]{:S(2)}) collective-permute-start(bf16[160,896]{1,0:T(8,128)(2,1)} %get-tuple-element.191), channel_id=1, source_target_pairs={{14,4},{12,14},{10,8},{8,2},{6,12},{4,6},{2,0},{0,10},{15,5},{1,11... | collective-permute-start | bytes 860168 | tf_op jit(solution)/shard_map/joint_gradient/ppermute | solution.py:189
  468.5 26.1 %collective-permute-start.75 = (bf16[256,896]{1,0:T(8,128)(2,1)}, bf16[256,896]{1,0:T(8,128)(2,1)}, u32[]{:S(2)}, u32[]{:S(2)}) collective-permute-start(bf16[256,896]{1,0:T(8,128)(2,1)} %get-tuple-element.190), channel_id=1, source_target_pairs={{15,15},{14,10},{0,0},{1,5},{3,11},{5,1},{7,7},{9,13},{11,3},{13,9... | collective-permute-start | bytes 1376264 | tf_op jit(solution)/shard_map/joint_gradient/ppermute | solution.py:189
  473.6 19.1 %collective-permute-start.79 = (bf16[100,800]{1,0:T(8,128)(2,1)}, bf16[100,800]{1,0:T(8,128)(2,1)}, u32[]{:S(2)}, u32[]{:S(2)}) collective-permute-start(bf16[100,800]{1,0:T(8,128)(2,1)} %select_convert_fusion.3), channel_id=1, source_target_pairs={{0,16},{16,0},{1,17},{17,1},{2,18},{18,2},{3,19},{19,3},{4,20},{20... | collective-permute-start | bytes 480008 | tf_op jit(solution)/shard_map/output_gradient/ppermute | solution.py:48
  (100 other events, 1174.5 us)

commit v4 on v3

--- a/solution.py
+++ b/solution.py
@@ -79,7 +79,7 @@
     yield found
 
 
-def ring_scatter(part, chips, rows, split):
+def ring_scatter(part, chips, rows, split, terms=False):
     size = rows // split
     half = split // 2
     middle = rows // 2
@@ -114,6 +114,8 @@
                 sent.append(piece)
         more = yield sent, [v for v in ahead + back if v is not None]
         token = (token, more)
+    if terms:
+        yield [part(0, 0, rows)] + ahead + back
     yield (
         part(0, 0, rows).astype(f32)
         + jnp.concatenate(ahead, axis=0).astype(f32)
@@ -324,34 +326,55 @@
     )(flags, own, got, mate_own, mate_got)
 
 
-def cut_kernel(width, table, back, low, out):
-    chips = out.shape[0]
-    odd = table[chips] == 1
-    both = low.shape[1] // chips
+def between_kernel(
+    chips, odd_core, own, ahead_one, ahead_two, back_one, back_two, residual, cotangent, weight,
+    vectors, out, residual_back, sums
+):
+    rows = own.shape[0]
+    odd = odd_core[0] == 1
+    arrived = jnp.concatenate([ahead_one[...], ahead_two[...]], axis=0).astype(f32)
+    arrived += jnp.concatenate([back_one[...], back_two[...]], axis=0).astype(f32)
+    pulled = own[...].astype(f32) + arrived
+    values = residual[...]
+    deviation = values - jnp.mean(values, axis=-1, keepdims=True)
+    variance = jnp.mean(deviation * deviation, axis=-1, keepdims=True)
+    scale = lax.rsqrt(variance + norm_epsilon)
+    plain = deviation * scale
+    inner = pulled * vectors[0:1]
+    outer = inner - jnp.mean(inner, axis=-1, keepdims=True)
+    outer -= plain * jnp.mean(inner * plain, axis=-1, keepdims=True)
+    straight = cotangent[...].astype(f32)
+    total = straight + scale * outer
+    residual_back[...] = total
+    for number, value in enumerate((total, pulled * plain, pulled, straight)):
+        sums[number : number + 1] = jnp.sum(value, axis=0, keepdims=True)
+    low = total.astype(bf16)
+    back = times(low, weight[...]).astype(bf16)
+    width, both = back.shape[1] // chips, low.shape[1] // chips
     half = both // 2
     for chip in range(chips):
         out[chip, :, :width] = back[:, chip * width : (chip + 1) * width]
-        piece = low[:, chip * both : (chip + 1) * both].astype(f32)
+        piece = total[:, chip * both : (chip + 1) * both].astype(bf16).astype(f32)
         piece = jnp.where(odd, jnp.concatenate([piece[:, half:], piece[:, :half]], axis=1), piece)
         out[chip, :, width : width + both] = piece.astype(out.dtype)
-        out[chip, :, width + both :] = jnp.zeros(
-            (out.shape[1], out.shape[2] - width - both), out.dtype
-        )
-
-
-def cut_columns(back, low, table, chips):
-    rows = low.shape[0]
-    width = back.shape[1] // chips
+        out[chip, :, width + both :] = jnp.zeros((rows, out.shape[2] - width - both), out.dtype)
+
+
+def between(odd_core, terms, residual, cotangent, weight, vectors, chips):
+    rows, features = residual.shape
+    columns = (weight.shape[1] + features) // chips
     return pl.pallas_call(
-        functools.partial(cut_kernel, width),
-        out_shape=jax.ShapeDtypeStruct(
-            (chips, rows, -(-(width + low.shape[1] // chips) // LANES) * LANES), bf16
-        ),
+        functools.partial(between_kernel, chips),
+        out_shape=[
+            jax.ShapeDtypeStruct((chips, rows, -(-columns // LANES) * LANES), bf16),
+            jax.ShapeDtypeStruct((rows, features), f32),
+            jax.ShapeDtypeStruct((8, features), f32),
+        ],
         in_specs=[pl.BlockSpec(memory_space=pltpu.SMEM)]
-        + [pl.BlockSpec(memory_space=pltpu.VMEM) for _ in range(2)],
-        out_specs=pl.BlockSpec(memory_space=pltpu.VMEM),
+        + [pl.BlockSpec(memory_space=pltpu.VMEM) for _ in range(9)],
+        out_specs=[pl.BlockSpec(memory_space=pltpu.VMEM) for _ in range(3)],
         compiler_params=pltpu.CompilerParams(vmem_limit_bytes=vmem_bytes),
-    )(table, back, low)
+    )(odd_core, *terms, residual, cotangent, weight, vectors)
 
 
 def both_heads(pair):
@@ -692,8 +715,8 @@
 
 
 def back_through_kernel(
-    chips, table, query_back, own_back, mate_back, weight, inputs, own_rows, mate_rows, own_wide,
-    mate_wide, parts, sums, value_sum, own_chosen, mate_chosen
+    chips, table, query_back, own_back, mate_back, weight, inputs, normed, own_rows, mate_rows,
+    own_total, mate_total, parts, sums, value_sum, own_chosen, mate_chosen
 ):
     step = pl.program_id(0)
     rows = parts.shape[1]
@@ -702,6 +725,8 @@
     def _():
         sums[...] = jnp.zeros_like(sums)
         value_sum[...] = jnp.zeros_like(value_sum)
+        own_total[...] = jnp.zeros_like(own_total)
+        mate_total[...] = jnp.zeros_like(mate_total)
         own_chosen[...] = chosen_by(own_rows[0:1], own_chosen.shape[0])
         mate_chosen[...] = chosen_by(mate_rows[0:1], mate_chosen.shape[0])
 
@@ -709,8 +734,8 @@
     value = own_back[1] + mate_back[1].astype(f32)
     value_sum[0:1] += jnp.sum(value, axis=0, keepdims=True)
     back = jnp.concatenate([query_back[...], key.astype(bf16), value.astype(bf16)], axis=1)
-    own_wide[...] = times(back, own_chosen[...]).astype(bf16)
-    mate_wide[...] = times(back, mate_chosen[...]).astype(bf16)
+    for chosen, total in ((own_chosen, own_total), (mate_chosen, mate_total)):
+        total[...] += rows_by_rows(times(back, chosen[...]).astype(bf16), normed[...])
     product = times(back, weight[...])
     for part in range(back.shape[0] // rows):
         place = part
@@ -723,7 +748,7 @@
 
 
 def back_through(
-    table, query_back, own_back, mate_back, weight, inputs, own_rows, mate_rows, rows
+    table, query_back, own_back, mate_back, weight, inputs, normed, own_rows, mate_rows, rows
 ):
     total, width = query_back.shape
     features = inputs.shape[1]
@@ -743,12 +768,13 @@
                 pair,
                 whole(weight.shape),
                 along(features),
+                along(features),
                 whole(own_rows.shape),
                 whole(mate_rows.shape),
             ],
             out_specs=[
-                along(share),
-                along(share),
+                whole((share, features)),
+                whole((share, features)),
                 parts_spec(chips, rows, features),
                 whole((8, features)),
                 whole((8, width)),
@@ -756,14 +782,14 @@
             scratch_shapes=[pltpu.VMEM((3 * width, share), bf16) for _ in range(2)],
         ),
         out_shape=[
-            jax.ShapeDtypeStruct((total, share), bf16),
-            jax.ShapeDtypeStruct((total, share), bf16),
+            jax.ShapeDtypeStruct((share, features), f32),
+            jax.ShapeDtypeStruct((share, features), f32),
             jax.ShapeDtypeStruct((chips, rows, features), bf16),
             jax.ShapeDtypeStruct((8, features), f32),
             jax.ShapeDtypeStruct((8, width), f32),
         ],
         compiler_params=pltpu.CompilerParams(vmem_limit_bytes=vmem_bytes),
-    )(table, query_back, own_back, mate_back, weight, inputs, own_rows, mate_rows)
+    )(table, query_back, own_back, mate_back, weight, inputs, normed, own_rows, mate_rows)
 
 
 def shards(
@@ -850,28 +876,43 @@
     )
     rows_here = [rows_here[i : i + 1, : len(one[0])] for i, one in enumerate(lists)]
 
+    with jax.named_scope("masks"):
+        padded_numbers = jnp.concatenate([jnp.full((reach_rows,), -1, jnp.int32), segments[0]])
+        numbers = jnp.stack(
+            [
+                lax.dynamic_slice_in_dim(padded_numbers, (2 * m + core) * rows, window)
+                for m in range(chips)
+            ]
+        )
+        key_places = jnp.arange(window, dtype=jnp.int32)
+        allowed = (numbers[:, None, :] == numbers[:, reach_rows:, None]) & (
+            key_places[None, None, :] <= key_places[None, reach_rows:, None]
+        )
+        bias = jnp.where(allowed, 0.0, masked_score).astype(f32)
+
     output_cols = output_weight.shape[1]
-    with jax.named_scope("parameters"):
-        spread = jnp.broadcast_to(vectors[None], (data * context,) + vectors.shape)
-        spread = lax.all_to_all(spread, ("dp", "ctx"), 0, 0, tiled=True)
-        params = (
-            spread.reshape((data, context) + vectors.shape)
-            .transpose(0, 2, 1, 3)
-            .reshape(data * vectors.shape[0], features)
-            .astype(f32)
-        )
     with jax.named_scope("input_ring"):
         output_rows = jnp.pad(output_weight.T, ((0, output_cols % 2), (0, 0)))
         fold = output_rows.shape[0] // 2
         output_rows = jnp.concatenate([output_rows[:fold], output_rows[fold:]], axis=1)
         output_rows = jnp.pad(output_rows, ((0, -fold % 16), (0, 0)))
         block = jnp.concatenate([block_input[0], output_rows, cotangent[0]], axis=0)
-        input_ring = ring_gather(after(block, spread))
+        input_ring = ring_gather(block)
         next(input_ring)
         arrived = next(input_ring)
     with jax.named_scope("joint_weight"):
-        mine = choose_rows(rows_here[0], after(joint_weight, spread).T, route[1])
-        mine = run_route(mine, route[0])
+        chosen = choose_rows(rows_here[0], joint_weight.T, route[1])
+    with jax.named_scope("parameters"):
+        spread = jnp.broadcast_to(vectors[None], (data * context,) + vectors.shape)
+        spread = lax.all_to_all(after(spread, chosen), ("dp", "ctx"), 0, 0, tiled=True)
+        params = (
+            spread.reshape((data, context) + vectors.shape)
+            .transpose(0, 2, 1, 3)
+            .reshape(data * vectors.shape[0], features)
+            .astype(f32)
+        )
+    with jax.named_scope("joint_weight"):
+        mine = after(run_route(chosen, route[0]), params)
         got = data_swap(mine)
     with jax.named_scope("input_ring"):
         arrived = input_ring.send(mine)
@@ -895,24 +936,11 @@
             if step == 3:
                 arrived = input_ring.send(got)
             elif step == chips // 2:
-                arrived = input_ring.send((joint_heads, up_got))
+                arrived = input_ring.send(joint_heads)
             else:
                 arrived = next(input_ring)
         input_blocks = next(input_ring)
-    with jax.named_scope("masks"):
-        padded_numbers = jnp.concatenate([jnp.full((reach_rows,), -1, jnp.int32), segments[0]])
-        numbers = jnp.stack(
-            [
-                lax.dynamic_slice_in_dim(padded_numbers, (2 * m + core) * rows, window)
-                for m in range(chips)
-            ]
-        )
-        key_places = jnp.arange(window, dtype=jnp.int32)
-        allowed = (numbers[:, None, :] == numbers[:, reach_rows:, None]) & (
-            key_places[None, None, :] <= key_places[None, reach_rows:, None]
-        )
-        bias = jnp.where(allowed, 0.0, masked_score).astype(f32)
-
+        joint_heads = after(joint_heads, (up_got, bias))
     with jax.named_scope("projection"):
         first_column = jnp.array(firsts[:chips], jnp.int32)[chip] * size
         last_column = jnp.array(firsts[1:], jnp.int32)[chip] * size
@@ -959,7 +987,7 @@
         arrived = next(attended_ring)
     arrived_first = arrived
     with jax.named_scope("attended_ring"):
-        arrived = next(attended_ring)
+        arrived = attended_ring.send((up_own, down_own))
     with jax.named_scope("output_weight"):
         below_got = data_swap(below)
         below_mate = core_swap(after(below, arrived_first))
@@ -971,7 +999,7 @@
     with jax.named_scope("feed_forward_weights"):
         up_mate, down_mate = core_swap(up_own), core_swap(down_own)
     with jax.named_scope("attended_ring"):
-        arrived = attended_ring.send((up_own, down_own, below_both))
+        arrived = next(attended_ring)
         for step in range(4, chips // 2 + 1):
             arrived = attended_ring.send(output_full) if step == 4 else next(attended_ring)
         attended_blocks = next(attended_ring)
@@ -1003,7 +1031,9 @@
         )
     )
     def pieces_of(own_rows, other, columns, order=lambda matrix: matrix):
-        total = order(rows_by_rows(own_rows, columns) + core_swap(other))
+        return halves_of(order(rows_by_rows(own_rows, columns) + core_swap(other)))
+
+    def halves_of(total):
         one, two = total[:, :half], total[:, half:]
         return jnp.where(first_half, one, two), jnp.where(first_half, two, one).astype(bf16)
 
@@ -1012,9 +1042,10 @@
 
     with jax.named_scope("normed_two_back_ring"):
         normed_parts = by_place(normed_parts, table)
-        ring = ring_scatter(part_of(normed_parts), chips, rows, 2)
+        ring = ring_scatter(part_of(normed_parts), chips, rows, 2, True)
         next(ring)
         sent, _ = next(ring)
+    with jax.named_scope("normed_two_back_ring"):
         sent, _ = next(ring)
     with jax.named_scope("up_gradient"):
         up_other = rows_by_rows(after(back_mate, sent), normed_two)
@@ -1031,7 +1062,7 @@
     with jax.named_scope("normed_two_back_ring"):
         for step in range(3, chips // 2):
             sent, _ = ring.send((up_other, down_other)) if step == 3 else next(ring)
-        normed_two_back = next(ring)
+        normed_terms = next(ring)
     with jax.named_scope("down_ring"):
         down_ring = ring_scatter(
             lambda o, first=0, count=rows, held=normed_parts: held[
@@ -1045,21 +1076,21 @@
         sent, arrived = down_ring.send(sent)
 
     rows_float = block_input[0].astype(f32)
-    cotangent_float = cotangent[0].astype(f32)
-    _, norm_pull = jax.vjp(layer_norm, residual, params[5], params[6])
-    residual_part, gain_two_back, shift_two_back = norm_pull(normed_two_back)
-    residual_back = cotangent_float + residual_part
-    residual_low = residual_back.astype(bf16)
-    attended_back = times(residual_low, output_full).astype(bf16)
-    pieces = cut_columns(attended_back, residual_low, table, chips)
+    pieces, residual_back, middle_sums = between(
+        odd_core,
+        normed_terms,
+        residual,
+        cotangent[0],
+        output_full,
+        jnp.pad(params[5:6], ((0, 7), (0, 0))),
+        chips,
+    )
     with jax.named_scope("back_exchange"):
-        back_got = exchange(pieces)
-    with jax.named_scope("down_ring"):
-        sent, arrived = down_ring.send(pieces)
+        back_got = exchange(after(pieces, arrived))
     with jax.named_scope("back_exchange"):
         bias_own = bias_sum[0] + core_swap(bias_sum[1])
         bias_gradient = bias_own + data_swap(bias_own)
-        back_got = after(back_got, (up_given, down_given, arrived, bias_gradient))
+        back_got = after(back_got, (up_given, down_given, bias_gradient))
         back_all = back_got.reshape(chips * rows, -1)
     with jax.named_scope("down_ring"):
         sent, arrived = down_ring.send(back_all)
@@ -1073,13 +1104,14 @@
     with jax.named_scope("down_ring"):
         sent, arrived = down_ring.send(own_back)
 
-    own_wide, mate_wide, normed_parts, norm_sums, value_sum = back_through(
+    joint_own, joint_other, normed_parts, norm_sums, value_sum = back_through(
         table,
         query_back,
         own_back,
-        mate_back,
+        after(mate_back, up_gradient),
         joint_heads,
         inputs,
+        normed_one,
         rows_here[3],
         rows_here[4],
         rows,
@@ -1091,10 +1123,10 @@
             norm_sums[1],
             at_heads(query_sum[0]),
             at_heads(value_sum[0]),
-            jnp.sum(residual_back, axis=0),
-            gain_two_back,
-            shift_two_back,
-            jnp.sum(cotangent_float, axis=0),
+            middle_sums[0],
+            middle_sums[1],
+            middle_sums[2],
+            middle_sums[3],
         ]
     )
     vectors_cut = (
@@ -1104,20 +1136,18 @@
     )
     with jax.named_scope("last_ring"):
         normed_parts = by_place(normed_parts, table)
-        ring = ring_scatter(part_of(normed_parts), chips, rows, 2)
+        ring = ring_scatter(part_of(normed_parts), chips, rows, 1)
         next(ring)
         sent, _ = ring.send(arrived)
 
     with jax.named_scope("joint_gradient"):
-        joint_other = rows_by_rows(after(mate_wide, sent), normed_one)
+        mine, joint_given = halves_of(joint_own + core_swap(after(joint_other, arrived)))
     with jax.named_scope("last_ring"):
-        sent, _ = ring.send(joint_other)
-    with jax.named_scope("joint_gradient"):
-        mine, joint_given = pieces_of(after(own_wide, sent), joint_other, normed_one)
+        sent, _ = next(ring)
     with jax.named_scope("down_ring"):
+        _, arrived = down_ring.send(sent)
         for step in range(4, chips // 2):
-            next(down_ring)
-        block_output = (residual + next(down_ring) + params[7]).astype(bf16)
+            _, arrived = next(down_ring)
     with jax.named_scope("last_ring"):
         sent, _ = ring.send(joint_given)
     with jax.named_scope("output_gradient"):
@@ -1135,26 +1165,30 @@
         output_other = rows_by_rows(low[:, output_cols : 2 * output_cols], attended_wide)
     with jax.named_scope("down_gradient"):
         down_gradient = down_kept + after(down_arrived, sent).astype(f32)
+    with jax.named_scope("vectors_gradient"):
+        vectors_gradient = jnp.sum(
+            lax.all_to_all(after(vectors_cut, sent), ("dp", "ctx"), 0, 0, tiled=True), axis=0
+        )
     with jax.named_scope("joint_gradient"):
-        mine = (mine + data_swap(joint_given).astype(f32)).astype(bf16)
+        joint_arrived = after(data_swap(joint_given), vectors_gradient)
+        mine = (mine + joint_arrived.astype(f32)).astype(bf16)
         joint_sent = choose_rows(rows_here[5], mine, back_route[1])
     with jax.named_scope("last_ring"):
         for step in range(3, chips // 2):
-            sent, _ = ring.send((output_other, joint_sent)) if step == 3 else next(ring)
+            sent, _ = ring.send((output_other, joint_sent, arrived)) if step == 3 else next(ring)
+    with jax.named_scope("down_ring"):
+        block_output = (after(residual, sent) + next(down_ring) + params[7]).astype(bf16)
     with jax.named_scope("output_gradient"):
         output_kept, output_given = pieces_of(
             after(low, sent)[:, :output_cols], output_other, attended_wide, by_heads
         )
-        output_gradient = finish(output_kept, output_given).T
     with jax.named_scope("joint_gradient"):
-        mine = run_route(joint_sent, back_route[0])
+        mine = routed = run_route(joint_sent, back_route[0])
         joint_gradient = rows_by_rows(chosen_by(rows_here[6], mine.shape[0]), mine)[:, :half].T
-    with jax.named_scope("vectors_gradient"):
-        vectors_gradient = jnp.sum(
-            lax.all_to_all(after(vectors_cut, sent), ("dp", "ctx"), 0, 0, tiled=True), axis=0
-        )
+    with jax.named_scope("output_gradient"):
+        output_gradient = finish(output_kept, after(output_given, routed)).T
     with jax.named_scope("last_ring"):
-        normed_one_back = next(ring)
+        normed_one_back = after(next(ring), (down_gradient, output_given, routed))
     with jax.named_scope("input_gradient"):
         _, first_pull = jax.vjp(layer_norm, rows_float, params[0], params[1])
         input_gradient = residual_back + first_pull(normed_one_back)[0]

time: 506 us -> 477 us (0.943)
  the two profiles are of different devices: /device:TPU:0 before, /device:TPU:8 now
where the time goes in v4:
time: 477 us; the launch traced here: 469 us
  waiting for transfers between devices  131 us (27%)
  Pallas kernels  121 us (25%)
  starting transfers between devices  84.5 us (18%)
  other arithmetic  62.4 us (13%)
  local copies, waits for them, and re-layouts  43.3 us (9%)
  matrix products  23.7 us (5%)
    ppermute x46, waiting for transfers between devices, send(): return lax.ppermute(value, 'ctx', pairs)  52.7 us
    ppermute x46, starting transfers between devices, send(): return lax.ppermute(value, 'ctx', pairs)  48.3 us
    pallas_call x1, Pallas kernels, feed_forward(): pl.pallas_call(feed_forward_kernel, grid_spec=pltpu.PrefetchScalarGridSpe...  38.4 us
    ppermute x9, waiting for transfers between devices, data_swap(): lax.ppermute(value, 'dp', [(i, i ^ 1) for i in range(lax.axis_size('dp'))])  30.3 us
    all_to_all x1, waiting for transfers between devices, shards(): lax.all_to_all(after(spread, chosen), ('dp', 'ctx'), 0, 0, tiled=True)  26.9 us
    dot_general x7, matrix products, rows_by_rows(): lax.dot_general(left_side, right_side, (((0,), (0,)), ((), ())), preferre...  23.7 us
    convert_element_type x18, other arithmetic, ring_scatter(): piece = piece.astype(bf16)  23.7 us
    pallas_call x1, Pallas kernels, back_through(): pl.pallas_call(functools.partial(back_through_kernel, chips), grid_spec=p...  16.5 us
  transfers between devices with their start and end apart: 78, of which 33 were waited for; matrix products, arithmetic and copies ran while one was open for 24% of the time, Pallas kernels for 18%

profile of v4, /device:TPU:8, one launch (start us, length us, event | category | flops | bytes accessed | tf_op | source)
XLA Modules:
  0.0 469.1 jit_solution(5773683091926916165)
XLA Ops:
  4.6 2.0 collective-permute-start.8
  7.9 2.6 joint_weight.2
  10.6 4.5 collective-permute-start
  17.2 4.6 all-to-all-start
  22.5 26.9 %all-to-all-done = bf16[32,4,100]{2,1,0:T(4,128)(2,1)S(1)} async-done(((bf16[32,4,100]{2,1,0:T(4,128)(2,1)}), bf16[32,4,100]{2,1,0:T(4,128)(2,1)S(1)}, u32[]{:S(2)}, u32[]{:S(2)}) %all-to-all-start) | async-done | bytes 25632 | tf_op jit(solution)/shard_map/parameters/all_to_all | solution.py:907
  56.3 18.0 %collective-permute-done.3.got = bf16[480,896]{1,0:T(8,128)(2,1)} collective-permute-done((bf16[480,896]{1,0:T(8,128)(2,1)S(1)}, bf16[480,896]{1,0:T(8,128)(2,1)}, u32[]{:S(2)}, u32[]{:S(2)}) %collective-permute-start.3) | collective-permute-done | bytes 860192 | tf_op jit(solution)/shard_map/joint_weight/ppermute | solution.py:48
  74.4 3.1 collective-permute-done.9.refs_2_
  87.8 7.1 %joint_weight.3.weight = bf16[768,1600]{1,0:T(8,128)(2,1)} custom-call(s32[1]{0:T(128)} %bitcast.1.flag, s32[1,768]{1,0:T(1,128)} %get-tuple-element.260.own_rows, s32[1,768]{1,0:T(1,128)} %get-tuple-element.259.mate_rows, bf16[480,896]{1,0:T(8,128)(2,1)} %copy-done.13, bf16[480,896]{1,0:T(8,128)(2,1)} %collective-permute-done.3.got, ...), custom_call_target="tpu_custom_call" | custom-call | tf_op jit(solution)/shard_map/joint_weight/pallas_call | solution.py:277
  94.9 8.7 %collective-permute-done.11.refs_3_ = bf16[320,1600]{1,0:T(8,128)(2,1)} collective-permute-done((bf16[320,1600]{1,0:T(8,128)(2,1)}, bf16[320,1600]{1,0:T(8,128)(2,1)}, u32[]{:S(2)}, u32[]{:S(2)}) %collective-permute-start.11) | collective-permute-done | bytes 1024032 | tf_op jit(solution)/shard_map/input_ring/ppermute | solution.py:40
  112.2 5.4 %collective-permute-done.14 = bf16[160,1600]{1,0:T(8,128)(2,1)S(1)} collective-permute-done((bf16[160,1600]{1,0:T(8,128)(2,1)S(1)}, bf16[160,1600]{1,0:T(8,128)(2,1)S(1)}, u32[]{:S(2)}, u32[]{:S(2)}) %collective-permute-start.14) | collective-permute-done | bytes 512032 | tf_op jit(solution)/shard_map/input_ring/ppermute | solution.py:40
  117.6 2.2 collective-permute-done.13
  120.9 13.4 %projection.1 = (bf16[1024,1600]{1,0:T(8,128)(2,1)}, bf16[8,64,1600]{2,1,0:T(8,128)(2,1)}, bf16[1024,1600]{1,0:T(8,128)(2,1)}, bf16[1024,1600]{1,0:T(8,128)(2,1)...) custom-call(s32[17]{0:T(128)} %pad_add_fusion.table, bf16[768,1600]{1,0:T(8,128)(2,1)} %joint_weight.3.weight, ...), custom_call_target="tpu_custom_call" | custom-call | tf_op jit(solution)/shard_map/projection/pallas_call | solution.py:565
  135.7 2.4 collective-permute-done.17.near
  139.1 10.4 %shard_map.179 = (bf16[1024,256]{1,0:T(8,128)(2,1)}, f32[8,2,256,1]{3,2,1,0:T(8,128)}) custom-call(s32[1]{0:T(128)} %bitcast.odd_core, f32[8,128,384]{2,1,0:T(8,128)} %and_select_fusion.bias, bf16[1024,256]{1,0:T(8,128)(2,1)} %get-tuple-element.126.query, bf16[2,1024,256]{2,1,0:T(8,128)(2,1)} %get-tuple-element.129.far.own, ...), custom_call_target="tpu_custom_call" | custom-call | tf_op jit(solution)/shard_map/pallas_call | solution.py:477
  151.5 2.2 maximum_select_fusion.up_own
  154.7 9.0 %collective-permute-done.18.refs_7_ = bf16[1024,256]{1,0:T(8,128)(2,1)S(1)} collective-permute-done((bf16[1024,256]{1,0:T(8,128)(2,1)}, bf16[1024,256]{1,0:T(8,128)(2,1)S(1)}, u32[]{:S(2)}, u32[]{:S(2)}) %collective-permute-start.18) | collective-permute-done | bytes 524320 | tf_op jit(solution)/shard_map/attended_ring/ppermute | solution.py:40
  166.6 8.5 %collective-permute-done.15.got = bf16[8,64,1600]{2,1,0:T(8,128)(2,1)} collective-permute-done((bf16[8,64,1600]{2,1,0:T(8,128)(2,1)}, bf16[8,64,1600]{2,1,0:T(8,128)(2,1)}, u32[]{:S(2)}, u32[]{:S(2)}) %collective-permute-start.15) | collective-permute-done | bytes 1638432 | tf_op jit(solution)/shard_map/output_weight/ppermute | solution.py:48
  175.2 2.5 collective-permute-done.21.refs_6_
  184.4 9.8 %output_weight.1.output_full.weight = bf16[1600,2048]{1,0:T(8,128)(2,1)} custom-call(s32[2]{0:T(128)} %pad_add_fusion.1.flags, bf16[8,64,1600]{2,1,0:T(8,128)(2,1)} %get-tuple-element.131.own, bf16[8,64,1600]{2,1,0:T(8,128)(2,1)} %collective-permute-done.15.got, bf16[8,64,1600]{2,1,0:T(8,128)(2,1)} %copy-done.19, ...), custom_call_target="tpu_custom_call" | custom-call | tf_op jit(solution)/shard_map/output_weight/pallas_call | solution.py:318
  202.1 2.1 collective-permute-done.30
  207.7 38.4 %shard_map.180 = (bf16[1024,1600]{1,0:T(8,128)(2,1)}, bf16[1024,400]{1,0:T(8,128)(2,1)}, bf16[1024,400]{1,0:T(8,128)(2,1)}, bf16[1024,400]{1,0:T(8,128)(2,1)}, b...) custom-call(s32[17]{0:T(128)} %pad_add_fusion.table, ...), custom_call_target="tpu_custom_call" | custom-call | tf_op jit(solution)/shard_map/pallas_call | solution.py:673
  246.1 2.5 slice_bitcast_fusion.5
  251.3 3.2 collective-permute-done.31
  260.9 3.2 fusion.54
  264.1 3.2 fusion.53
  287.2 2.5 collective-permute-done.41.ahead_two
  294.2 6.6 %shard_map.181 = (bf16[8,128,512]{2,1,0:T(8,128)(2,1)}, f32[128,1600]{1,0:T(8,128)}, f32[8,1600]{1,0:T(8,128)}) custom-call(s32[1]{0:T(128)} %bitcast.odd_core, bf16[128,1600]{1,0:T(8,128)(2,1)} %slice_bitcast_fusion.own, bf16[64,1600]{1,0:T(8,128)(2,1)} %copy-done.36, bf16[64,1600]{1,0:T(8,128)(2,1)} %copy-done.38, bf16[64,1600]{1,0:T(8,128)(2,1)} %copy-done.37, ...), custom_call_target="tpu_custom_call" | custom-call | tf_op jit(solution)/shard_map/pallas_call | solution.py:366
  300.8 4.8 %all-to-all-start.1 = ((bf16[8,128,512]{2,1,0:T(8,128)(2,1)}), bf16[8,128,512]{2,1,0:T(8,128)(2,1)}, u32[]{:S(2)}, u32[]{:S(2)}) async-start(bf16[8,128,512]{2,1,0:T(8,128)(2,1)} %get-tuple-element.161), calls=%async_computation.1 | async-start | bytes 2097152 | tf_op jit(solution)/shard_map/back_exchange/all_to_all | solution.py:129
  311.8 4.8 %convolution_add_fusion.1 = f32[400,1600]{1,0:T(8,128)S(1)} fusion(f32[400,1600]{1,0:T(8,128)} %collective-permute-done.47, bf16[1024,400]{1,0:T(8,128)(2,1)} %get-tuple-element.163, bf16[1024,1600]{1,0:T(8,128)(2,1)} %get-tuple-element.151), kind=kOutput, calls=%fused_computation.1 | convolution fusion | flops 1311360000 | bytes 9216000 | tf_op jit(solution)/shard_map/up_gradient/dot_general | solution.py:217
  319.1 3.5 convolution_add_fusion
  325.4 2.4 all-to-all-done.1
  331.2 2.3 collective-permute-start.53
  335.4 13.8 %shard_map.182 = (bf16[1024,256]{1,0:T(8,128)(2,1)}, f32[2,1024,256]{2,1,0:T(8,128)}, bf16[2,1024,256]{2,1,0:T(8,128)(2,1)}, f32[8,256]{1,0:T(8,128)}) custom-call(s32[1]{0:T(128)} %bitcast.odd_core, f32[8,128,384]{2,1,0:T(8,128)} %and_select_fusion.bias, bf16[1024,256]{1,0:T(8,128)(2,1)} %get-tuple-element.126.query, ...), custom_call_target="tpu_custom_call" | custom-call | tf_op jit(solution)/shard_map/pallas_call | solution.py:500
  358.8 2.6 convert_add_fusion.1
  361.5 16.5 %shard_map.183 = (f32[416,1600]{1,0:T(8,128)}, f32[416,1600]{1,0:T(8,128)}, bf16[8,128,1600]{2,1,0:T(8,128)(2,1)}, f32[8,1600]{1,0:T(8,128)}, f32[8,256]{1,0:T(8,128)}) custom-call(s32[17]{0:T(128)} %pad_add_fusion.table, bf16[1024,256]{1,0:T(8,128)(2,1)} %get-tuple-element.168.query_back, f32[2,1024,256]{2,1,0:T(8,128)} %get-tuple-element.169.own_back, ...), custom_call_target="tpu_custom_call" | custom-call | tf_op jit(solution)/shard_map/pallas_call | solution.py:760
  379.5 2.1 slice_bitcast_fusion.1
  386.2 2.8 collective-permute-done.57
  399.1 2.1 add.284
  409.7 4.2 all-to-all-start.2
  414.2 4.3 fusion.38
  418.5 2.7 convert_add_fusion
  422.9 2.4 add_convert_fusion.matrix
  425.4 2.7 joint_gradient.1
  432.7 4.6 collective-permute-start.71
  441.0 3.2 convolution_add_fusion.2
  446.5 8.3 %collective-permute-done.71 = bf16[256,896]{1,0:T(8,128)(2,1)S(1)} collective-permute-done((bf16[256,896]{1,0:T(8,128)(2,1)}, bf16[256,896]{1,0:T(8,128)(2,1)S(1)}, u32[]{:S(2)}, u32[]{:S(2)}) %collective-permute-start.71) | collective-permute-done | bytes 458784 | tf_op jit(solution)/shard_map/joint_gradient/ppermute | solution.py:191
  454.8 4.3 collective-permute-done.72
  465.4 2.6 collective-permute-done.74
  (358 shorter events, 164.4 us)
Async XLA Ops:
  4.5 47.6 %collective-permute-start.7 = (bf16[320,1600]{1,0:T(8,128)(2,1)S(1)}, bf16[320,1600]{1,0:T(8,128)(2,1)}, u32[]{:S(2)}, u32[]{:S(2)}) collective-permute-start(bf16[320,1600]{1,0:T(8,128)(2,1)S(1)} %pad_maximum_fusion.refs_0_), channel_id=1, source_target_pairs={{0,2},{1,3},{4,0},{5,1},{8,4},{9,5},{12,8},{13,9},{14,12},{15,13},... | collective-permute-start | bytes 3072008 | tf_op jit(solution)/shard_map/input_ring/ppermute | solution.py:40
  4.6 47.6 %collective-permute-start.8 = (bf16[320,1600]{1,0:T(8,128)(2,1)S(1)}, bf16[320,1600]{1,0:T(8,128)(2,1)}, u32[]{:S(2)}, u32[]{:S(2)}) collective-permute-start(bf16[320,1600]{1,0:T(8,128)(2,1)S(1)} %pad_maximum_fusion.refs_0_), channel_id=1, source_target_pairs={{0,4},{1,5},{4,8},{5,9},{8,12},{9,13},{12,14},{13,15},{14,10},{15,... | collective-permute-start | bytes 3072008 | tf_op jit(solution)/shard_map/input_ring/ppermute | solution.py:40
  10.6 40.3 %collective-permute-start = (bf16[256,896]{1,0:T(8,128)(2,1)}, bf16[256,896]{1,0:T(8,128)(2,1)}, u32[]{:S(2)}, u32[]{:S(2)}) collective-permute-start(bf16[256,896]{1,0:T(8,128)(2,1)} %get-tuple-element.109), channel_id=1, source_target_pairs={{15,15},{10,14},{0,0},{1,5},{3,11},{5,1},{7,7},{9,13},{11,3},{13,9... | collective-permute-start | bytes 1376264 | tf_op jit(solution)/shard_map/joint_weight/ppermute | solution.py:191
  15.1 34.5 %collective-permute-start.1 = (bf16[160,896]{1,0:T(8,128)(2,1)}, bf16[160,896]{1,0:T(8,128)(2,1)S(1)}, u32[]{:S(2)}, u32[]{:S(2)}) collective-permute-start(bf16[160,896]{1,0:T(8,128)(2,1)} %get-tuple-element.110), channel_id=1, source_target_pairs={{4,14},{14,12},{8,10},{2,8},{12,6},{6,4},{0,2},{5,15},{10,0},{11,1... | collective-permute-start | bytes 860168 | tf_op jit(solution)/shard_map/joint_weight/ppermute | solution.py:191
  17.2 32.2 %all-to-all-start = ((bf16[32,4,100]{2,1,0:T(4,128)(2,1)}), bf16[32,4,100]{2,1,0:T(4,128)(2,1)S(1)}, u32[]{:S(2)}, u32[]{:S(2)}) async-start(bf16[32,4,100]{2,1,0:T(4,128)(2,1)} %broadcast_in_dim.53), calls=%async_computation | async-start | bytes 65536 | tf_op jit(solution)/shard_map/parameters/all_to_all | solution.py:907
  21.8 27.7 %collective-permute-start.2 = (bf16[64,896]{1,0:T(8,128)(2,1)}, bf16[64,896]{1,0:T(8,128)(2,1)S(1)}, u32[]{:S(2)}, u32[]{:S(2)}) collective-permute-start(bf16[64,896]{1,0:T(8,128)(2,1)} %get-tuple-element.111), channel_id=1, source_target_pairs={{9,15},{3,13},{13,11},{7,9},{1,7},{11,5},{5,3},{25,31},{19,29},{29... | collective-permute-start | bytes 344072 | tf_op jit(solution)/shard_map/joint_weight/ppermute | solution.py:191
  52.2 25.3 %collective-permute-start.9 = (bf16[320,1600]{1,0:T(8,128)(2,1)}, bf16[320,1600]{1,0:T(8,128)(2,1)}, u32[]{:S(2)}, u32[]{:S(2)}) collective-permute-start(bf16[320,1600]{1,0:T(8,128)(2,1)} %collective-permute-done.7.refs_1_), channel_id=1, source_target_pairs={{0,2},{1,3},{4,0},{5,1},{8,4},{9,5},{12,8},{13,9},{14,12},{15,13},... | collective-permute-start | bytes 3072008 | tf_op jit(solution)/shard_map/input_ring/ppermute | solution.py:40
  53.4 25.6 %collective-permute-start.10 = (bf16[320,1600]{1,0:T(8,128)(2,1)}, bf16[320,1600]{1,0:T(8,128)(2,1)}, u32[]{:S(2)}, u32[]{:S(2)}) collective-permute-start(bf16[320,1600]{1,0:T(8,128)(2,1)} %collective-permute-done.8.refs_7_), channel_id=1, source_target_pairs={{0,4},{1,5},{4,8},{5,9},{8,12},{9,13},{12,14},{13,15},{14,10},{15,... | collective-permute-start | bytes 3072008 | tf_op jit(solution)/shard_map/input_ring/ppermute | solution.py:40
  54.3 20.1 %collective-permute-start.3 = (bf16[480,896]{1,0:T(8,128)(2,1)S(1)}, bf16[480,896]{1,0:T(8,128)(2,1)}, u32[]{:S(2)}, u32[]{:S(2)}) collective-permute-start(bf16[480,896]{1,0:T(8,128)(2,1)S(1)} %pad_maximum_fusion.2.own), channel_id=1, source_target_pairs={{0,16},{16,0},{1,17},{17,1},{2,18},{18,2},{3,19},{19,3},{4,20},{20... | collective-permute-start | bytes 2580488 | tf_op jit(solution)/shard_map/joint_weight/ppermute | solution.py:48
  79.0 24.7 %collective-permute-start.11 = (bf16[320,1600]{1,0:T(8,128)(2,1)}, bf16[320,1600]{1,0:T(8,128)(2,1)}, u32[]{:S(2)}, u32[]{:S(2)}) collective-permute-start(bf16[320,1600]{1,0:T(8,128)(2,1)} %collective-permute-done.9.refs_2_), channel_id=1, source_target_pairs={{0,2},{1,3},{4,0},{5,1},{8,4},{9,5},{12,8},{13,9},{14,12},{15,13},... | collective-permute-start | bytes 3072008 | tf_op jit(solution)/shard_map/input_ring/ppermute | solution.py:40
  80.3 24.4 %collective-permute-start.12 = (bf16[320,1600]{1,0:T(8,128)(2,1)}, bf16[320,1600]{1,0:T(8,128)(2,1)}, u32[]{:S(2)}, u32[]{:S(2)}) collective-permute-start(bf16[320,1600]{1,0:T(8,128)(2,1)} %collective-permute-done.10.refs_6_), channel_id=1, source_target_pairs={{0,4},{1,5},{4,8},{5,9},{8,12},{9,13},{12,14},{13,15},{14,10},{15,... | collective-permute-start | bytes 3072008 | tf_op jit(solution)/shard_map/input_ring/ppermute | solution.py:40
  87.0 25.1 %collective-permute-start.6 = (bf16[400,800]{1,0:T(8,128)(2,1)S(1)}, bf16[400,800]{1,0:T(8,128)(2,1)}, u32[]{:S(2)}, u32[]{:S(2)}) collective-permute-start(bf16[400,800]{1,0:T(8,128)(2,1)S(1)} %bitcast.161), channel_id=1, source_target_pairs={{0,16},{16,0},{1,17},{17,1},{2,18},{18,2},{3,19},{19,3},{4,20},{20... | collective-permute-start | bytes 1920008 | tf_op jit(solution)/shard_map/feed_forward_weights/ppermute | solution.py:48
  110.2 24.2 %collective-permute-start.16 = (bf16[400,800]{1,0:T(8,128)(2,1)S(1)}, bf16[400,800]{1,0:T(8,128)(2,1)S(1)}, u32[]{:S(2)}, u32[]{:S(2)}) collective-permute-start(bf16[400,800]{1,0:T(8,128)(2,1)S(1)} %copy-done.25), channel_id=1, source_target_pairs={{0,16},{16,0},{1,17},{17,1},{2,18},{18,2},{3,19},{19,3},{4,20},{20... | collective-permute-start | bytes 1920008 | tf_op jit(solution)/shard_map/feed_forward_weights/ppermute | solution.py:48
  135.2 39.9 %collective-permute-start.15 = (bf16[8,64,1600]{2,1,0:T(8,128)(2,1)}, bf16[8,64,1600]{2,1,0:T(8,128)(2,1)}, u32[]{:S(2)}, u32[]{:S(2)}) collective-permute-start(bf16[8,64,1600]{2,1,0:T(8,128)(2,1)} %get-tuple-element.131.own), channel_id=1, source_target_pairs={{0,16},{16,0},{1,17},{17,1},{2,18},{18,2},{3,19},{19,3},{4,20},{20... | collective-permute-start | bytes 4915208 | tf_op jit(solution)/shard_map/output_weight/ppermute | solution.py:48
  149.4 14.2 %collective-permute-start.18 = (bf16[1024,256]{1,0:T(8,128)(2,1)}, bf16[1024,256]{1,0:T(8,128)(2,1)S(1)}, u32[]{:S(2)}, u32[]{:S(2)}) collective-permute-start(bf16[1024,256]{1,0:T(8,128)(2,1)} %get-tuple-element.130.refs_0_.mixed), channel_id=1, source_target_pairs={{0,4},{1,5},{4,8},{5,9},{8,12},{9,13},{12,14},{13,15},{14,10},{15,... | collective-permute-start | bytes 1572872 | tf_op jit(solution)/shard_map/attended_ring/ppermute | solution.py:40
  150.7 13.9 %collective-permute-start.19 = (bf16[1024,256]{1,0:T(8,128)(2,1)}, bf16[1024,256]{1,0:T(8,128)(2,1)S(1)}, u32[]{:S(2)}, u32[]{:S(2)}) collective-permute-start(bf16[1024,256]{1,0:T(8,128)(2,1)} %get-tuple-element.130.refs_0_.mixed), channel_id=1, source_target_pairs={{0,2},{1,3},{4,0},{5,1},{8,4},{9,5},{12,8},{13,9},{14,12},{15,13},... | collective-permute-start | bytes 1572872 | tf_op jit(solution)/shard_map/attended_ring/ppermute | solution.py:40
  164.6 13.0 %collective-permute-start.21 = (bf16[1024,256]{1,0:T(8,128)(2,1)S(1)}, bf16[1024,256]{1,0:T(8,128)(2,1)}, u32[]{:S(2)}, u32[]{:S(2)}) collective-permute-start(bf16[1024,256]{1,0:T(8,128)(2,1)S(1)} %collective-permute-done.18.refs_7_), channel_id=1, source_target_pairs={{0,4},{1,5},{4,8},{5,9},{8,12},{9,13},{12,14},{13,15},{14,10},{15,... | collective-permute-start | bytes 1572872 | tf_op jit(solution)/shard_map/attended_ring/ppermute | solution.py:40
  165.3 12.8 %collective-permute-start.22 = (bf16[1024,256]{1,0:T(8,128)(2,1)S(1)}, bf16[1024,256]{1,0:T(8,128)(2,1)}, u32[]{:S(2)}, u32[]{:S(2)}) collective-permute-start(bf16[1024,256]{1,0:T(8,128)(2,1)S(1)} %collective-permute-done.19.refs_1_), channel_id=1, source_target_pairs={{0,2},{1,3},{4,0},{5,1},{8,4},{9,5},{12,8},{13,9},{14,12},{15,13},... | collective-permute-start | bytes 1572872 | tf_op jit(solution)/shard_map/attended_ring/ppermute | solution.py:40
  166.6 13.3 %collective-permute-start.20 = (bf16[8,64,1600]{2,1,0:T(8,128)(2,1)S(1)}, bf16[8,64,1600]{2,1,0:T(8,128)(2,1)S(1)}, u32[]{:S(2)}, u32[]{:S(2)}) collective-permute-start(bf16[8,64,1600]{2,1,0:T(8,128)(2,1)S(1)} %copy-done.18), channel_id=1, source_target_pairs={{0,1},{1,0},{2,3},{3,2},{4,5},{5,4},{6,7},{7,6},{8,9},{9,8},{10,11... | collective-permute-start | bytes 4915208 | tf_op jit(solution)/shard_map/output_weight/ppermute | solution.py:44
  178.0 28.6 %collective-permute-start.24 = (bf16[400,1600]{1,0:T(8,128)(2,1)S(1)}, bf16[400,1600]{1,0:T(8,128)(2,1)S(1)}, u32[]{:S(2)}, u32[]{:S(2)}) collective-permute-start(bf16[400,1600]{1,0:T(8,128)(2,1)S(1)} %maximum_select_fusion.up_own), channel_id=1, source_target_pairs={{0,1},{1,0},{2,3},{3,2},{4,5},{5,4},{6,7},{7,6},{8,9},{9,8},{10,11... | collective-permute-start | bytes 3840008 | tf_op jit(solution)/shard_map/feed_forward_weights/ppermute | solution.py:44
  178.5 28.1 %collective-permute-start.25 = (bf16[400,1600]{1,0:T(8,128)(2,1)S(1)}, bf16[400,1600]{1,0:T(8,128)(2,1)}, u32[]{:S(2)}, u32[]{:S(2)}) collective-permute-start(bf16[400,1600]{1,0:T(8,128)(2,1)S(1)} %maximum_select_fusion.1.down_own), channel_id=1, source_target_pairs={{0,1},{1,0},{2,3},{3,2},{4,5},{5,4},{6,7},{7,6},{8,9},{9,8},{10,11... | collective-permute-start | bytes 3840008 | tf_op jit(solution)/shard_map/feed_forward_weights/ppermute | solution.py:44
  178.5 15.6 %collective-permute-start.27 = (bf16[1024,256]{1,0:T(8,128)(2,1)}, bf16[1024,256]{1,0:T(8,128)(2,1)}, u32[]{:S(2)}, u32[]{:S(2)}) collective-permute-start(bf16[1024,256]{1,0:T(8,128)(2,1)} %collective-permute-done.22.refs_2_), channel_id=1, source_target_pairs={{0,2},{1,3},{4,0},{5,1},{8,4},{9,5},{12,8},{13,9},{14,12},{15,13},... | collective-permute-start | bytes 1572872 | tf_op jit(solution)/shard_map/attended_ring/ppermute | solution.py:40
  181.1 14.5 %collective-permute-start.28 = (bf16[1024,256]{1,0:T(8,128)(2,1)}, bf16[1024,256]{1,0:T(8,128)(2,1)}, u32[]{:S(2)}, u32[]{:S(2)}) collective-permute-start(bf16[1024,256]{1,0:T(8,128)(2,1)} %collective-permute-done.21.refs_6_), channel_id=1, source_target_pairs={{0,4},{1,5},{4,8},{5,9},{8,12},{9,13},{12,14},{13,15},{14,10},{15,... | collective-permute-start | bytes 1572872 | tf_op jit(solution)/shard_map/attended_ring/ppermute | solution.py:40
  257.6 13.4 %collective-permute-start.36 = (bf16[64,1600]{1,0:T(8,128)(2,1)S(1)}, bf16[64,1600]{1,0:T(8,128)(2,1)S(1)}, u32[]{:S(2)}, u32[]{:S(2)}) collective-permute-start(bf16[64,1600]{1,0:T(8,128)(2,1)S(1)} %get-tuple-element.143), channel_id=1, source_target_pairs={{0,4},{1,5},{4,8},{5,9},{8,12},{9,13},{12,14},{13,15},{14,10},{15,... | collective-permute-start | bytes 614408 | tf_op jit(solution)/shard_map/normed_two_back_ring/ppermute | solution.py:40
  259.8 13.1 %collective-permute-start.35 = (bf16[64,1600]{1,0:T(8,128)(2,1)S(1)}, bf16[64,1600]{1,0:T(8,128)(2,1)S(1)}, u32[]{:S(2)}, u32[]{:S(2)}) collective-permute-start(bf16[64,1600]{1,0:T(8,128)(2,1)S(1)} %fusion.32), channel_id=1, source_target_pairs={{0,2},{1,3},{4,0},{5,1},{8,4},{9,5},{12,8},{13,9},{14,12},{15,13},... | collective-permute-start | bytes 614408 | tf_op jit(solution)/shard_map/normed_two_back_ring/ppermute | solution.py:40
  267.2 44.6 %collective-permute-start.47 = (f32[400,1600]{1,0:T(8,128)}, f32[400,1600]{1,0:T(8,128)}, u32[]{:S(2)}, u32[]{:S(2)}) collective-permute-start(f32[400,1600]{1,0:T(8,128)} %fusion.53), channel_id=1, source_target_pairs={{0,1},{1,0},{2,3},{3,2},{4,5},{5,4},{6,7},{7,6},{8,9},{9,8},{10,11... | collective-permute-start | bytes 7680008 | tf_op jit(solution)/shard_map/up_gradient/ppermute | solution.py:44
  267.2 51.9 %collective-permute-start.48 = (f32[400,1600]{1,0:T(8,128)}, f32[400,1600]{1,0:T(8,128)}, u32[]{:S(2)}, u32[]{:S(2)}) collective-permute-start(f32[400,1600]{1,0:T(8,128)} %fusion.54), channel_id=1, source_target_pairs={{0,1},{1,0},{2,3},{3,2},{4,5},{5,4},{6,7},{7,6},{8,9},{9,8},{10,11... | collective-permute-start | bytes 7680008 | tf_op jit(solution)/shard_map/down_gradient/ppermute | solution.py:44
  300.8 27.0 %all-to-all-start.1 = ((bf16[8,128,512]{2,1,0:T(8,128)(2,1)}), bf16[8,128,512]{2,1,0:T(8,128)(2,1)}, u32[]{:S(2)}, u32[]{:S(2)}) async-start(bf16[8,128,512]{2,1,0:T(8,128)(2,1)} %get-tuple-element.161), calls=%async_computation.1 | async-start | bytes 2097152 | tf_op jit(solution)/shard_map/back_exchange/all_to_all | solution.py:129
  317.9 31.4 %collective-permute-start.51 = (bf16[400,800]{1,0:T(8,128)(2,1)}, bf16[400,800]{1,0:T(8,128)(2,1)}, u32[]{:S(2)}, u32[]{:S(2)}) collective-permute-start(bf16[400,800]{1,0:T(8,128)(2,1)} %select_convert_fusion.2), channel_id=1, source_target_pairs={{0,16},{16,0},{1,17},{17,1},{2,18},{18,2},{3,19},{19,3},{4,20},{20... | collective-permute-start | bytes 1920008 | tf_op jit(solution)/shard_map/up_gradient/ppermute | solution.py:48
  329.0 20.3 %collective-permute-start.52 = (bf16[128,1600]{1,0:T(8,128)(2,1)S(1)}, bf16[128,1600]{1,0:T(8,128)(2,1)S(1)}, u32[]{:S(2)}, u32[]{:S(2)}) collective-permute-start(bf16[128,1600]{1,0:T(8,128)(2,1)S(1)} %pad_maximum_fusion.4), channel_id=1, source_target_pairs={{0,4},{1,5},{4,8},{5,9},{8,12},{9,13},{12,14},{13,15},{14,10},{15,... | collective-permute-start | bytes 1228808 | tf_op jit(solution)/shard_map/down_ring/ppermute | solution.py:40
  331.2 18.1 %collective-permute-start.53 = (bf16[128,1600]{1,0:T(8,128)(2,1)}, bf16[128,1600]{1,0:T(8,128)(2,1)S(1)}, u32[]{:S(2)}, u32[]{:S(2)}) collective-permute-start(bf16[128,1600]{1,0:T(8,128)(2,1)} %pad_maximum_fusion.5), channel_id=1, source_target_pairs={{0,2},{1,3},{4,0},{5,1},{8,4},{9,5},{12,8},{13,9},{14,12},{15,13},... | collective-permute-start | bytes 1228808 | tf_op jit(solution)/shard_map/down_ring/ppermute | solution.py:40
  351.2 26.7 %collective-permute-start.55 = (bf16[128,1600]{1,0:T(8,128)(2,1)}, bf16[128,1600]{1,0:T(8,128)(2,1)S(1)}, u32[]{:S(2)}, u32[]{:S(2)}) collective-permute-start(bf16[128,1600]{1,0:T(8,128)(2,1)} %fusion.16), channel_id=1, source_target_pairs={{0,4},{1,5},{4,8},{5,9},{8,12},{9,13},{12,14},{13,15},{14,10},{15,... | collective-permute-start | bytes 1228808 | tf_op jit(solution)/shard_map/down_ring/ppermute | solution.py:40
  353.5 24.5 %collective-permute-start.56 = (bf16[128,1600]{1,0:T(8,128)(2,1)}, bf16[128,1600]{1,0:T(8,128)(2,1)S(1)}, u32[]{:S(2)}, u32[]{:S(2)}) collective-permute-start(bf16[128,1600]{1,0:T(8,128)(2,1)} %fusion.15), channel_id=1, source_target_pairs={{0,2},{1,3},{4,0},{5,1},{8,4},{9,5},{12,8},{13,9},{14,12},{15,13},... | collective-permute-start | bytes 1228808 | tf_op jit(solution)/shard_map/down_ring/ppermute | solution.py:40
  356.5 57.4 %collective-permute-start.69 = (bf16[400,800]{1,0:T(8,128)(2,1)}, bf16[400,800]{1,0:T(8,128)(2,1)}, u32[]{:S(2)}, u32[]{:S(2)}) collective-permute-start(bf16[400,800]{1,0:T(8,128)(2,1)} %select_convert_fusion.1), channel_id=1, source_target_pairs={{0,16},{16,0},{1,17},{17,1},{2,18},{18,2},{3,19},{19,3},{4,20},{20... | collective-permute-start | bytes 1920008 | tf_op jit(solution)/shard_map/down_gradient/ppermute | solution.py:48
  378.7 18.8 %collective-permute-start.60 = (f32[416,1600]{1,0:T(8,128)}, f32[416,1600]{1,0:T(8,128)S(1)}, u32[]{:S(2)}, u32[]{:S(2)}) collective-permute-start(f32[416,1600]{1,0:T(8,128)} %get-tuple-element.186), channel_id=1, source_target_pairs={{0,1},{1,0},{2,3},{3,2},{4,5},{5,4},{6,7},{7,6},{8,9},{9,8},{10,11... | collective-permute-start | bytes 7987208 | tf_op jit(solution)/shard_map/joint_gradient/ppermute | solution.py:44
  390.2 12.8 %collective-permute-start.58 = (bf16[128,1600]{1,0:T(8,128)(2,1)S(1)}, bf16[128,1600]{1,0:T(8,128)(2,1)S(1)}, u32[]{:S(2)}, u32[]{:S(2)}) collective-permute-start(bf16[128,1600]{1,0:T(8,128)(2,1)S(1)} %pad_maximum_fusion.6), channel_id=1, source_target_pairs={{0,4},{1,5},{4,8},{5,9},{8,12},{9,13},{12,14},{13,15},{14,10},{15,... | collective-permute-start | bytes 1228808 | tf_op jit(solution)/shard_map/last_ring/ppermute | solution.py:40
  391.6 14.4 %collective-permute-start.62 = (bf16[128,1600]{1,0:T(8,128)(2,1)S(1)}, bf16[128,1600]{1,0:T(8,128)(2,1)S(1)}, u32[]{:S(2)}, u32[]{:S(2)}) collective-permute-start(bf16[128,1600]{1,0:T(8,128)(2,1)S(1)} %pad_maximum_fusion.7), channel_id=1, source_target_pairs={{0,2},{1,3},{4,0},{5,1},{8,4},{9,5},{12,8},{13,9},{14,12},{15,13},... | collective-permute-start | bytes 1228808 | tf_op jit(solution)/shard_map/last_ring/ppermute | solution.py:40
  395.2 32.9 %collective-permute-start.64 = (bf16[128,1600]{1,0:T(8,128)(2,1)}, bf16[128,1600]{1,0:T(8,128)(2,1)}, u32[]{:S(2)}, u32[]{:S(2)}) collective-permute-start(bf16[128,1600]{1,0:T(8,128)(2,1)} %fusion.13), channel_id=1, source_target_pairs={{0,4},{1,5},{4,8},{5,9},{8,12},{9,13},{12,14},{13,15},{14,10},{15,... | collective-permute-start | bytes 1228808 | tf_op jit(solution)/shard_map/down_ring/ppermute | solution.py:40
  397.5 30.6 %collective-permute-start.65 = (bf16[128,1600]{1,0:T(8,128)(2,1)}, bf16[128,1600]{1,0:T(8,128)(2,1)}, u32[]{:S(2)}, u32[]{:S(2)}) collective-permute-start(bf16[128,1600]{1,0:T(8,128)(2,1)} %fusion.12), channel_id=1, source_target_pairs={{0,2},{1,3},{4,0},{5,1},{8,4},{9,5},{12,8},{13,9},{14,12},{15,13},... | collective-permute-start | bytes 1228808 | tf_op jit(solution)/shard_map/down_ring/ppermute | solution.py:40
  403.0 19.9 %collective-permute-start.63 = (bf16[416,800]{1,0:T(8,128)(2,1)}, bf16[416,800]{1,0:T(8,128)(2,1)}, u32[]{:S(2)}, u32[]{:S(2)}) collective-permute-start(bf16[416,800]{1,0:T(8,128)(2,1)} %select_convert_fusion), channel_id=1, source_target_pairs={{0,16},{16,0},{1,17},{17,1},{2,18},{18,2},{3,19},{19,3},{4,20},{20... | collective-permute-start | bytes 1996808 | tf_op jit(solution)/shard_map/joint_gradient/ppermute | solution.py:48
  406.0 22.1 %collective-permute-start.61 = (bf16[128,1600]{1,0:T(8,128)(2,1)}, bf16[128,1600]{1,0:T(8,128)(2,1)}, u32[]{:S(2)}, u32[]{:S(2)}) collective-permute-start(bf16[128,1600]{1,0:T(8,128)(2,1)} %fusion.17), channel_id=1, source_target_pairs={{0,4},{1,5},{4,8},{5,9},{8,12},{9,13},{12,14},{13,15},{14,10},{15,... | collective-permute-start | bytes 1228808 | tf_op jit(solution)/shard_map/last_ring/ppermute | solution.py:40
  413.9 15.5 %collective-permute-start.66 = (bf16[128,1600]{1,0:T(8,128)(2,1)}, bf16[128,1600]{1,0:T(8,128)(2,1)}, u32[]{:S(2)}, u32[]{:S(2)}) collective-permute-start(bf16[128,1600]{1,0:T(8,128)(2,1)} %fusion.14), channel_id=1, source_target_pairs={{0,2},{1,3},{4,0},{5,1},{8,4},{9,5},{12,8},{13,9},{14,12},{15,13},... | collective-permute-start | bytes 1228808 | tf_op jit(solution)/shard_map/last_ring/ppermute | solution.py:40
  422.9 17.5 %collective-permute-start.70 = (f32[100,2048]{1,0:T(8,128)}, f32[100,2048]{1,0:T(8,128)}, u32[]{:S(2)}, u32[]{:S(2)}) collective-permute-start(f32[100,2048]{1,0:T(8,128)} %fusion.38), channel_id=1, source_target_pairs={{0,1},{1,0},{2,3},{3,2},{4,5},{5,4},{6,7},{7,6},{8,9},{9,8},{10,11... | collective-permute-start | bytes 2457608 | tf_op jit(solution)/shard_map/output_gradient/ppermute | solution.py:44
  430.6 14.0 %collective-permute-start.68 = (bf16[128,1600]{1,0:T(8,128)(2,1)S(1)}, bf16[128,1600]{1,0:T(8,128)(2,1)}, u32[]{:S(2)}, u32[]{:S(2)}) collective-permute-start(bf16[128,1600]{1,0:T(8,128)(2,1)S(1)} %fusion.11), channel_id=1, source_target_pairs={{0,2},{1,3},{4,0},{5,1},{8,4},{9,5},{12,8},{13,9},{14,12},{15,13},... | collective-permute-start | bytes 1228808 | tf_op jit(solution)/shard_map/last_ring/ppermute | solution.py:40
  432.3 12.8 %collective-permute-start.67 = (bf16[128,1600]{1,0:T(8,128)(2,1)S(1)}, bf16[128,1600]{1,0:T(8,128)(2,1)}, u32[]{:S(2)}, u32[]{:S(2)}) collective-permute-start(bf16[128,1600]{1,0:T(8,128)(2,1)S(1)} %fusion.18), channel_id=1, source_target_pairs={{0,4},{1,5},{4,8},{5,9},{8,12},{9,13},{12,14},{13,15},{14,10},{15,... | collective-permute-start | bytes 1228808 | tf_op jit(solution)/shard_map/last_ring/ppermute | solution.py:40
  432.7 22.0 %collective-permute-start.71 = (bf16[256,896]{1,0:T(8,128)(2,1)}, bf16[256,896]{1,0:T(8,128)(2,1)S(1)}, u32[]{:S(2)}, u32[]{:S(2)}) collective-permute-start(bf16[256,896]{1,0:T(8,128)(2,1)} %get-tuple-element.197), channel_id=1, source_target_pairs={{15,15},{14,10},{0,0},{1,5},{3,11},{5,1},{7,7},{9,13},{11,3},{13,9... | collective-permute-start | bytes 1376264 | tf_op jit(solution)/shard_map/joint_gradient/ppermute | solution.py:191
  437.3 21.8 %collective-permute-start.72 = (bf16[160,896]{1,0:T(8,128)(2,1)}, bf16[160,896]{1,0:T(8,128)(2,1)}, u32[]{:S(2)}, u32[]{:S(2)}) collective-permute-start(bf16[160,896]{1,0:T(8,128)(2,1)} %get-tuple-element.198), channel_id=1, source_target_pairs={{14,4},{12,14},{10,8},{8,2},{6,12},{4,6},{2,0},{0,10},{15,5},{1,11... | collective-permute-start | bytes 860168 | tf_op jit(solution)/shard_map/joint_gradient/ppermute | solution.py:191
  440.4 19.8 %collective-permute-start.73 = (bf16[64,896]{1,0:T(8,128)(2,1)S(1)}, bf16[64,896]{1,0:T(8,128)(2,1)S(1)}, u32[]{:S(2)}, u32[]{:S(2)}) collective-permute-start(bf16[64,896]{1,0:T(8,128)(2,1)S(1)} %copy-done.51), channel_id=1, source_target_pairs={{15,9},{13,3},{11,13},{9,7},{7,1},{5,11},{3,5},{31,25},{29,19},{27... | collective-permute-start | bytes 344072 | tf_op jit(solution)/shard_map/joint_gradient/ppermute | solution.py:191
  (82 other events, 1073.6 us)

commit v5 on v4

--- a/solution.py
+++ b/solution.py
@@ -238,8 +238,11 @@
     return (rows == places).astype(bf16)
 
 
-def choose_kernel(rows, matrix, *outs):
-    found = rows_by_rows(chosen_by(rows[0:1], matrix.shape[0]), matrix[...])
+def choose_kernel(more, rows, matrix, *outs):
+    values = matrix[...]
+    if more:
+        values, outs = (values + outs[0][...].astype(f32)).astype(bf16), outs[1:]
+    found = rows_by_rows(chosen_by(rows[0:1], matrix.shape[0]), values)
     first = 0
     columns = matrix.shape[1]
     for out in outs:
@@ -248,17 +251,17 @@
         first += out.shape[0]
 
 
-def choose_rows(rows, matrix, sizes):
+def choose_rows(rows, matrix, sizes, *more):
     return pl.pallas_call(
-        choose_kernel,
+        functools.partial(choose_kernel, len(more)),
         out_shape=[
             jax.ShapeDtypeStruct((count, -(-matrix.shape[1] // LANES) * LANES), bf16)
             for count in sizes
         ],
-        in_specs=[pl.BlockSpec(memory_space=pltpu.VMEM) for _ in range(2)],
+        in_specs=[pl.BlockSpec(memory_space=pltpu.VMEM) for _ in range(2 + len(more))],
         out_specs=[pl.BlockSpec(memory_space=pltpu.VMEM) for _ in sizes],
         compiler_params=pltpu.CompilerParams(vmem_limit_bytes=vmem_bytes),
-    )(rows, matrix)
+    )(rows, matrix, *more)
 
 
 def pick_kernel(flag, own_rows, mate_rows, own, got, mate_own, mate_got, out):
@@ -524,8 +527,7 @@
 
 
 def project_kernel(rows, table, weight, bias, vectors, *refs):
-    blocks, (inputs, below, cotangent, normed, query, pair) = refs[:-6], refs[-6:]
-    last = blocks[0].shape[0] - rows
+    blocks, (inputs, below, normed, query, pair) = refs[:-5], refs[-5:]
     width = query.shape[1]
     for o in range(0, len(blocks), 2):
         values = jnp.concatenate([blocks[o][:rows], blocks[o + 1][:rows]], axis=0)
@@ -536,8 +538,7 @@
             here = slice(part * rows, (part + 1) * rows)
             place = pl.ds(pl.multiple_of(table[o + part] * rows, rows), rows)
             inputs[place] = values[here]
-            below[table[o + part]] = blocks[o + part][rows:last]
-            cotangent[place] = blocks[o + part][last:]
+            below[table[o + part]] = blocks[o + part][rows:]
             normed[place] = normed_low[here]
             query[place] = product[here, :width]
             pair[0, place] = product[here, width : 2 * width]
@@ -555,7 +556,7 @@
         by_chip = lambda value, axis: taken(value, table[chips + 1 :], axis)
         joined = []
         for number, parts in enumerate(zip(*found)):
-            axis = 1 if number == 5 else 0
+            axis = 1 if number == 4 else 0
             value = jnp.concatenate(parts, axis=axis)
             shape = value.shape
             split = shape[:axis] + (chips, shape[axis] // chips) + shape[axis + 1 :]
@@ -566,15 +567,14 @@
         functools.partial(project_kernel, rows),
         out_shape=[
             jax.ShapeDtypeStruct((total, features), bf16),
-            jax.ShapeDtypeStruct((chips, count - 2 * rows, features), bf16),
-            jax.ShapeDtypeStruct((total, features), bf16),
+            jax.ShapeDtypeStruct((chips, count - rows, features), bf16),
             jax.ShapeDtypeStruct((total, features), bf16),
             jax.ShapeDtypeStruct((total, width), bf16),
             jax.ShapeDtypeStruct((2, total, width), bf16),
         ],
         in_specs=[pl.BlockSpec(memory_space=pltpu.SMEM)]
         + [pl.BlockSpec(memory_space=pltpu.VMEM) for _ in range(3 + chips)],
-        out_specs=[pl.BlockSpec(memory_space=pltpu.VMEM) for _ in range(6)],
+        out_specs=[pl.BlockSpec(memory_space=pltpu.VMEM) for _ in range(5)],
         cost_estimate=cost_of(6 * total * features * width, 8 * total * features),
         compiler_params=pltpu.CompilerParams(vmem_limit_bytes=vmem_bytes),
     )(table, weight, bias, vectors, *blocks)
@@ -602,13 +602,12 @@
 
 
 def feed_forward_kernel(
-    table, inputs, cotangent, output_full, up_own, up_mate, down_own, down_mate, shift, vectors,
-    *refs
+    chips, table, inputs, output_full, up_own, up_mate, down_own, down_mate, shift, vectors, *refs
 ):
-    attended, refs = refs[:-9], refs[-9:]
+    attended, cotangent, refs = refs[:chips], refs[chips:-10], refs[-10:]
     (
         normed, hidden_own, hidden_mate, back_own, back_mate, parts, bias_sum, residual_own,
-        attended_wide,
+        attended_wide, cotangent_all,
     ) = refs
     step = pl.program_id(0)
     rows, features = residual_own.shape
@@ -618,7 +617,17 @@
         attended_wide[:, columns] = ref[...]
     residual = inputs[...].astype(f32) + vectors[0:1]
     residual += cols_by_cols(attended_wide[...], output_full[...])
-    cotangent_rows = cotangent[...]
+    if len(cotangent) == 1:
+        cotangent_all[...] = cotangent[0][...]
+    else:
+        for part in range(inputs.shape[0] // rows):
+            for o, ref in enumerate(cotangent):
+
+                @pl.when(table[o] == step * (inputs.shape[0] // rows) + part)
+                def _():
+                    cotangent_all[part * rows : (part + 1) * rows] = ref[...]
+
+    cotangent_rows = cotangent_all[...]
     for part in range(inputs.shape[0] // rows):
 
         @pl.when(table[0] == step * (inputs.shape[0] // rows) + part)
@@ -666,17 +675,18 @@
 ):
     chips, (total, width) = len(attended), attended[0].shape
     features = inputs.shape[1]
+    if chips > most_resident:
+        cotangent = [taken(jnp.stack(cotangent), table[chips + 1 :], 0).reshape(total, features)]
     units = up_own.shape[0]
     block = 2 * rows
     along = lambda columns: pl.BlockSpec((block, columns), lambda i, table: (i, 0))
     whole = lambda shape: pl.BlockSpec(shape, lambda i, table: (0, 0))
     return pl.pallas_call(
-        feed_forward_kernel,
+        functools.partial(feed_forward_kernel, chips),
         grid_spec=pltpu.PrefetchScalarGridSpec(
             num_scalar_prefetch=1,
             grid=(total // block,),
             in_specs=[
-                along(features),
                 along(features),
                 whole(output_full.shape),
                 whole(up_own.shape),
@@ -686,7 +696,8 @@
                 whole(shift.shape),
                 whole(vectors.shape),
             ]
-            + [along(width) for _ in attended],
+            + [along(width) for _ in attended]
+            + [along(features) if len(cotangent) == 1 else whole(c.shape) for c in cotangent],
             out_specs=[along(features)]
             + [along(units) for _ in range(4)]
             + [
@@ -694,6 +705,7 @@
                 whole(shift.shape),
                 whole((rows, features)),
                 along(chips * width),
+                along(features),
             ],
         ),
         out_shape=[jax.ShapeDtypeStruct((total, features), bf16)]
@@ -703,14 +715,15 @@
             jax.ShapeDtypeStruct(shift.shape, f32),
             jax.ShapeDtypeStruct((rows, features), f32),
             jax.ShapeDtypeStruct((total, chips * width), bf16),
+            jax.ShapeDtypeStruct((total, features), bf16),
         ],
         cost_estimate=cost_of(
             2 * total * features * (chips * width + 6 * units), 16 * total * features
         ),
         compiler_params=pltpu.CompilerParams(vmem_limit_bytes=vmem_bytes),
     )(
-        table, inputs, cotangent, output_full, up_own, up_mate, down_own, down_mate, shift, vectors,
-        *attended
+        table, inputs, output_full, up_own, up_mate, down_own, down_mate, shift, vectors, *attended,
+        *cotangent
     )
 
 
@@ -792,6 +805,42 @@
     )(table, query_back, own_back, mate_back, weight, inputs, normed, own_rows, mate_rows)
 
 
+def vectors_kernel(size, chip, norm_sums, query_sum, value_sum, middle_sums, out, whole):
+    chips = out.shape[0] // 4
+    whole[...] = jnp.zeros_like(whole)
+    whole[0:2] = norm_sums[0:2]
+    whole[4:8] = middle_sums[0:4]
+    firsts = head_spans(chips)[0]
+    for number in range(chips):
+        low, high = firsts[number] * size, firsts[number + 1] * size
+        if low < high:
+
+            @pl.when(chip[0] == number)
+            def _():
+                whole[2:3, low:high] = query_sum[0:1, : high - low]
+                whole[3:4, low:high] = value_sum[0:1, : high - low]
+
+    count = whole.shape[1] // (2 * chips)
+    out[...] = jnp.zeros_like(out)
+    for number in range(4 * chips):
+        half, column = divmod(number, 2 * chips)
+        out[number, :, :count] = whole[4 * half : 4 * half + 4, column * count : (column + 1) * count]
+
+
+def vectors_pieces(chip, norm_sums, query_sum, value_sum, middle_sums, size, chips):
+    features = norm_sums.shape[1]
+    lanes = -(-features // (2 * chips) // LANES) * LANES
+    return pl.pallas_call(
+        functools.partial(vectors_kernel, size),
+        out_shape=jax.ShapeDtypeStruct((4 * chips, 4, lanes), f32),
+        in_specs=[pl.BlockSpec(memory_space=pltpu.SMEM)]
+        + [pl.BlockSpec(memory_space=pltpu.VMEM) for _ in range(4)],
+        out_specs=pl.BlockSpec(memory_space=pltpu.VMEM),
+        scratch_shapes=[pltpu.VMEM((8, features), f32)],
+        compiler_params=pltpu.CompilerParams(vmem_limit_bytes=vmem_bytes),
+    )(chip, norm_sums, query_sum, value_sum, middle_sums)
+
+
 def shards(
     block_input,
     segments,
@@ -896,7 +945,7 @@
         fold = output_rows.shape[0] // 2
         output_rows = jnp.concatenate([output_rows[:fold], output_rows[fold:]], axis=1)
         output_rows = jnp.pad(output_rows, ((0, -fold % 16), (0, 0)))
-        block = jnp.concatenate([block_input[0], output_rows, cotangent[0]], axis=0)
+        block = jnp.concatenate([block_input[0], output_rows], axis=0)
         input_ring = ring_gather(block)
         next(input_ring)
         arrived = next(input_ring)
@@ -941,6 +990,10 @@
                 arrived = next(input_ring)
         input_blocks = next(input_ring)
         joint_heads = after(joint_heads, (up_got, bias))
+    with jax.named_scope("cotangent_ring"):
+        cotangent_ring = ring_gather(cotangent[0])
+        next(cotangent_ring)
+        crossing = cotangent_ring.send(arrived)
     with jax.named_scope("projection"):
         first_column = jnp.array(firsts[:chips], jnp.int32)[chip] * size
         last_column = jnp.array(firsts[1:], jnp.int32)[chip] * size
@@ -950,14 +1003,10 @@
             row = lax.dynamic_slice_in_dim(jnp.pad(row, (0, width)), first_column, width)
             return jnp.where(inside, row, 0.0)
 
-        def at_heads(row):
-            whole = jnp.zeros((features + width,), f32)
-            return lax.dynamic_update_slice_in_dim(whole, row, first_column, 0)[:features]
-
         head_bias = jnp.concatenate(
             [of_heads(params[2]), jnp.zeros((width,), f32), of_heads(params[3])]
         )
-        inputs, below, cotangent_all, normed_one, query, own = project(
+        inputs, below, normed_one, query, own = project(
             input_blocks,
             table,
             joint_heads,
@@ -978,30 +1027,44 @@
                 jnp.concatenate([got, mine], axis=-1),
             )
 
-        up_own, down_own = both_halves(up_mine, up_got), both_halves(down_mine, down_got)
-    mate = core_swap(after(own, down_got))
+        below_mate = core_swap(below)
+    mate = core_swap(after(own, (down_got, crossing)))
+    with jax.named_scope("cotangent_ring"):
+        crossing = cotangent_ring.send(own)
     attended, log_total = attend_forward(odd_core, bias, query, own, mate, scale)
     with jax.named_scope("attended_ring"):
         attended_ring = ring_gather(attended)
         next(attended_ring)
-        arrived = next(attended_ring)
+        arrived = attended_ring.send((crossing, below_mate))
+    with jax.named_scope("cotangent_ring"):
+        crossing = cotangent_ring.send(attended)
+    with jax.named_scope("feed_forward_weights"):
+        up_got, down_got = after((up_got, down_got), attended)
+        up_own, down_own = both_halves(up_mine, up_got), both_halves(down_mine, down_got)
     arrived_first = arrived
     with jax.named_scope("attended_ring"):
-        arrived = attended_ring.send((up_own, down_own))
+        arrived = attended_ring.send((up_own, down_own, crossing))
     with jax.named_scope("output_weight"):
         below_got = data_swap(below)
-        below_mate = core_swap(after(below, arrived_first))
         below_both = core_swap(after(below_got, arrived))
         flags = jnp.stack([half_index, core]).astype(jnp.int32)
         output_full = join_weight(
             flags, below, below_got, below_mate, below_both, size, output_cols
         )
-    with jax.named_scope("feed_forward_weights"):
-        up_mate, down_mate = core_swap(up_own), core_swap(down_own)
+    with jax.named_scope("cotangent_ring"):
+        crossing_last = next(cotangent_ring)
+        for step in range(5, chips // 2 + 1):
+            crossing_last = next(cotangent_ring)
+        cotangent_blocks = next(cotangent_ring)
     with jax.named_scope("attended_ring"):
-        arrived = next(attended_ring)
+        up_mate, down_mate = core_swap(after(up_own, arrived)), core_swap(after(down_own, arrived))
+        arrived = attended_ring.send(crossing_last)
+    with jax.named_scope("attended_ring"):
         for step in range(4, chips // 2 + 1):
-            arrived = attended_ring.send(output_full) if step == 4 else next(attended_ring)
+            if step == 4:
+                arrived = attended_ring.send((output_full, up_mate, down_mate))
+            else:
+                arrived = next(attended_ring)
         attended_blocks = next(attended_ring)
 
     (
@@ -1014,12 +1077,13 @@
         bias_sum,
         residual,
         attended_wide,
+        cotangent_all,
     ) = (
         feed_forward(
             table,
             attended_blocks,
             inputs,
-            cotangent_all,
+            cotangent_blocks,
             output_full,
             up_own,
             up_mate,
@@ -1108,7 +1172,7 @@
         table,
         query_back,
         own_back,
-        after(mate_back, up_gradient),
+        after(mate_back, (up_gradient, down_arrived)),
         joint_heads,
         inputs,
         normed_one,
@@ -1117,22 +1181,8 @@
         rows,
     )
 
-    vectors_sum = jnp.stack(
-        [
-            norm_sums[0],
-            norm_sums[1],
-            at_heads(query_sum[0]),
-            at_heads(value_sum[0]),
-            middle_sums[0],
-            middle_sums[1],
-            middle_sums[2],
-            middle_sums[3],
-        ]
-    )
-    vectors_cut = (
-        vectors_sum.reshape(data, vectors.shape[0], context, vectors.shape[1])
-        .transpose(0, 2, 1, 3)
-        .reshape((data * context,) + vectors.shape)
+    vectors_cut = vectors_pieces(
+        table[:1], norm_sums, query_sum, value_sum, middle_sums, size, chips
     )
     with jax.named_scope("last_ring"):
         normed_parts = by_place(normed_parts, table)
@@ -1143,13 +1193,16 @@
     with jax.named_scope("joint_gradient"):
         mine, joint_given = halves_of(joint_own + core_swap(after(joint_other, arrived)))
     with jax.named_scope("last_ring"):
-        sent, _ = next(ring)
+        sent, _ = ring.send(joint_given)
     with jax.named_scope("down_ring"):
         _, arrived = down_ring.send(sent)
         for step in range(4, chips // 2):
             _, arrived = next(down_ring)
+    with jax.named_scope("joint_gradient"):
+        joint_arrived = after(data_swap(joint_given), sent)
+        joint_sent = choose_rows(rows_here[5], mine, back_route[1], joint_arrived)
     with jax.named_scope("last_ring"):
-        sent, _ = ring.send(joint_given)
+        sent, _ = ring.send((joint_sent, arrived))
     with jax.named_scope("output_gradient"):
         low = after(back_all, sent)[:, width:]
 
@@ -1163,19 +1216,14 @@
             )
 
         output_other = rows_by_rows(low[:, output_cols : 2 * output_cols], attended_wide)
+    with jax.named_scope("last_ring"):
+        for step in range(3, chips // 2):
+            if step == 3:
+                sent, _ = ring.send(output_other)
+            else:
+                sent, _ = next(ring)
     with jax.named_scope("down_gradient"):
         down_gradient = down_kept + after(down_arrived, sent).astype(f32)
-    with jax.named_scope("vectors_gradient"):
-        vectors_gradient = jnp.sum(
-            lax.all_to_all(after(vectors_cut, sent), ("dp", "ctx"), 0, 0, tiled=True), axis=0
-        )
-    with jax.named_scope("joint_gradient"):
-        joint_arrived = after(data_swap(joint_given), vectors_gradient)
-        mine = (mine + joint_arrived.astype(f32)).astype(bf16)
-        joint_sent = choose_rows(rows_here[5], mine, back_route[1])
-    with jax.named_scope("last_ring"):
-        for step in range(3, chips // 2):
-            sent, _ = ring.send((output_other, joint_sent, arrived)) if step == 3 else next(ring)
     with jax.named_scope("down_ring"):
         block_output = (after(residual, sent) + next(down_ring) + params[7]).astype(bf16)
     with jax.named_scope("output_gradient"):
@@ -1186,9 +1234,14 @@
         mine = routed = run_route(joint_sent, back_route[0])
         joint_gradient = rows_by_rows(chosen_by(rows_here[6], mine.shape[0]), mine)[:, :half].T
     with jax.named_scope("output_gradient"):
-        output_gradient = finish(output_kept, after(output_given, routed)).T
+        output_arrived = data_swap(after(output_given, routed))
+        output_gradient = (output_kept + output_arrived.astype(f32)).T
+    with jax.named_scope("vectors_gradient"):
+        vectors_gradient = jnp.sum(
+            lax.all_to_all(after(vectors_cut, sent), ("dp", "ctx"), 0, 0, tiled=True), axis=0
+        )[:, : vectors.shape[1]]
     with jax.named_scope("last_ring"):
-        normed_one_back = after(next(ring), (down_gradient, output_given, routed))
+        normed_one_back = after(next(ring), (down_gradient, output_arrived, routed))
     with jax.named_scope("input_gradient"):
         _, first_pull = jax.vjp(layer_norm, rows_float, params[0], params[1])
         input_gradient = residual_back + first_pull(normed_one_back)[0]

time: 477 us -> 472 us (0.990)
  the two profiles are of different devices: /device:TPU:8 before, /device:TPU:0 now
where the time goes in v5:
time: 472 us; the launch traced here: 464 us
  Pallas kernels  122 us (26%)
  waiting for transfers between devices  116 us (25%)
  starting transfers between devices  102 us (22%)
  other arithmetic  65.2 us (14%)
  local copies, waits for them, and re-layouts  32.4 us (7%)
  matrix products  23.9 us (5%)
    ppermute x54, waiting for transfers between devices, send(): return lax.ppermute(value, 'ctx', pairs)  88.1 us
    ppermute x54, starting transfers between devices, send(): return lax.ppermute(value, 'ctx', pairs)  56.3 us
    pallas_call x1, Pallas kernels, feed_forward(): pl.pallas_call(functools.partial(feed_forward_kernel, chips), grid_spec=p...  39.5 us
    dot_general x7, matrix products, rows_by_rows(): lax.dot_general(left_side, right_side, (((0,), (0,)), ((), ())), preferre...  23.9 us
    convert_element_type x18, other arithmetic, ring_scatter(): piece = piece.astype(bf16)  23.7 us
    ppermute x9, waiting for transfers between devices, data_swap(): lax.ppermute(value, 'dp', [(i, i ^ 1) for i in range(lax.axis_size('dp'))])  17.8 us
    pallas_call x1, Pallas kernels, back_through(): pl.pallas_call(functools.partial(back_through_kernel, chips), grid_spec=p...  16.5 us
    ppermute x6, starting transfers between devices, run_route(): lax.ppermute(piece, 'ctx', group)  13.9 us
  transfers between devices with their start and end apart: 86, of which 42 were waited for; matrix products, arithmetic and copies ran while one was open for 24% of the time, Pallas kernels for 17%

profile of v5, /device:TPU:0, one launch (start us, length us, event | category | flops | bytes accessed | tf_op | source)
XLA Modules:
  0.0 464.3 jit_solution(3400218039386562509)
XLA Ops:
  2.0 2.6 joint_weight.2
  4.6 5.2 %collective-permute-start = (bf16[256,896]{1,0:T(8,128)(2,1)}, bf16[256,896]{1,0:T(8,128)(2,1)}, u32[]{:S(2)}, u32[]{:S(2)}) collective-permute-start(bf16[256,896]{1,0:T(8,128)(2,1)} %get-tuple-element.122), channel_id=1, source_target_pairs={{15,15},{10,14},{0,0},{1,5},{3,11},{5,1},{7,7},{9,13},{11,3},{13,9... | collective-permute-start | bytes 1376264 | tf_op jit(solution)/shard_map/joint_weight/ppermute | solution.py:191
  13.2 8.9 %all-to-all-start = ((bf16[32,4,100]{2,1,0:T(4,128)(2,1)}), bf16[32,4,100]{2,1,0:T(4,128)(2,1)S(1)}, u32[]{:S(2)}, u32[]{:S(2)}) async-start(bf16[32,4,100]{2,1,0:T(4,128)(2,1)} %broadcast_in_dim.53), calls=%async_computation | async-start | bytes 65536 | tf_op jit(solution)/shard_map/parameters/all_to_all | solution.py:956
  26.6 5.0 %all-to-all-done = bf16[32,4,100]{2,1,0:T(4,128)(2,1)S(1)} async-done(((bf16[32,4,100]{2,1,0:T(4,128)(2,1)}), bf16[32,4,100]{2,1,0:T(4,128)(2,1)S(1)}, u32[]{:S(2)}, u32[]{:S(2)}) %all-to-all-start) | async-done | bytes 25632 | tf_op jit(solution)/shard_map/parameters/all_to_all | solution.py:956
  34.1 7.3 %collective-permute-done.7.refs_1_ = bf16[192,1600]{1,0:T(8,128)(2,1)S(1)} collective-permute-done((bf16[192,1600]{1,0:T(8,128)(2,1)S(1)}, bf16[192,1600]{1,0:T(8,128)(2,1)S(1)}, u32[]{:S(2)}, u32[]{:S(2)}) %collective-permute-start.7) | collective-permute-done | bytes 614432 | tf_op jit(solution)/shard_map/input_ring/ppermute | solution.py:40
  45.0 9.4 %collective-permute-done.3.got = bf16[480,896]{1,0:T(8,128)(2,1)} collective-permute-done((bf16[480,896]{1,0:T(8,128)(2,1)S(1)}, bf16[480,896]{1,0:T(8,128)(2,1)}, u32[]{:S(2)}, u32[]{:S(2)}) %collective-permute-start.3) | collective-permute-done | bytes 860192 | tf_op jit(solution)/shard_map/joint_weight/ppermute | solution.py:48
  56.4 2.2 collective-permute-done.10.refs_6_
  67.7 7.0 %joint_weight.3.weight = bf16[768,1600]{1,0:T(8,128)(2,1)} custom-call(s32[1]{0:T(128)} %bitcast.1.flag, s32[1,768]{1,0:T(1,128)} %get-tuple-element.286.own_rows, s32[1,768]{1,0:T(1,128)} %get-tuple-element.285.mate_rows, bf16[480,896]{1,0:T(8,128)(2,1)} %copy-done.9, bf16[480,896]{1,0:T(8,128)(2,1)} %collective-permute-done.3.got, ...), custom_call_target="tpu_custom_call" | custom-call | tf_op jit(solution)/shard_map/joint_weight/pallas_call | solution.py:280
  77.9 2.3 collective-permute-start.14
  83.2 2.8 collective-permute-done.13
  87.5 10.9 %projection.1 = (bf16[1024,1600]{1,0:T(8,128)(2,1)}, bf16[8,64,1600]{2,1,0:T(8,128)(2,1)}, bf16[1024,1600]{1,0:T(8,128)(2,1)}, bf16[1024,256]{1,0:T(8,128)(2,1)}, bf16[2,1024,256]{2,1,0:T(8,128)(2,1)}) custom-call(s32[17]{0:T(128)} %pad_add_fusion.table, bf16[768,1600]{1,0:T(8,128)(2,1)} %joint_weight.3.weight, f32[8,768]{1,0:T(8,128)} %pad.34.bias, ...), custom_call_target="tpu_custom_call" | custom-call | tf_op jit(solution)/shard_map/projection/pallas_call | solution.py:566
  101.8 10.2 %collective-permute-done.18.refs_15_ = bf16[128,1600]{1,0:T(8,128)(2,1)S(1)} collective-permute-done((bf16[128,1600]{1,0:T(8,128)(2,1)S(1)}, bf16[128,1600]{1,0:T(8,128)(2,1)S(1)}, u32[]{:S(2)}, u32[]{:S(2)}) %collective-permute-start.18) | collective-permute-done | bytes 409632 | tf_op jit(solution)/shard_map/cotangent_ring/ppermute | solution.py:40
  117.1 10.3 %shard_map.179 = (bf16[1024,256]{1,0:T(8,128)(2,1)}, f32[8,2,256,1]{3,2,1,0:T(8,128)}) custom-call(s32[1]{0:T(128)} %bitcast.odd_core, f32[8,128,384]{2,1,0:T(8,128)} %and_select_fusion.bias, bf16[1024,256]{1,0:T(8,128)(2,1)} %get-tuple-element.138.query, bf16[2,1024,256]{2,1,0:T(8,128)(2,1)} %get-tuple-element.143.far.own, bf16[2,1024,256]{2,1,0:T(8,128)(2,1)} %copy-done.7, ...), custom_call_target="tpu_custom_call" | custom-call | tf_op jit(solution)/shard_map/pallas_call | solution.py:480
  131.6 2.2 maximum_select_fusion.1.down_own
  133.9 2.7 maximum_select_fusion.up_own
  136.6 3.9 collective-permute-done.25.refs_13_
  141.5 8.9 %collective-permute-done.23.refs_7_ = bf16[1024,256]{1,0:T(8,128)(2,1)S(1)} collective-permute-done((bf16[1024,256]{1,0:T(8,128)(2,1)}, bf16[1024,256]{1,0:T(8,128)(2,1)S(1)}, u32[]{:S(2)}, u32[]{:S(2)}) %collective-permute-start.23) | collective-permute-done | bytes 524320 | tf_op jit(solution)/shard_map/attended_ring/ppermute | solution.py:40
  152.8 10.4 %collective-permute-done.27.refs_6_ = bf16[1024,256]{1,0:T(8,128)(2,1)} collective-permute-done((bf16[1024,256]{1,0:T(8,128)(2,1)S(1)}, bf16[1024,256]{1,0:T(8,128)(2,1)}, u32[]{:S(2)}, u32[]{:S(2)}) %collective-permute-start.27) | collective-permute-done | bytes 524320 | tf_op jit(solution)/shard_map/attended_ring/ppermute | solution.py:40
  167.3 5.6 %collective-permute-done.33 = bf16[64,1600]{1,0:T(8,128)(2,1)S(1)} collective-permute-done((bf16[64,1600]{1,0:T(8,128)(2,1)S(1)}, bf16[64,1600]{1,0:T(8,128)(2,1)S(1)}, u32[]{:S(2)}, u32[]{:S(2)}) %collective-permute-start.33) | collective-permute-done | bytes 204832 | tf_op jit(solution)/shard_map/cotangent_ring/ppermute | solution.py:40
  177.4 9.8 %output_weight.1.output_full.weight = bf16[1600,2048]{1,0:T(8,128)(2,1)} custom-call(s32[2]{0:T(128)} %pad_add_fusion.1.flags, bf16[8,64,1600]{2,1,0:T(8,128)(2,1)} %get-tuple-element.137.own, bf16[8,64,1600]{2,1,0:T(8,128)(2,1)} %collective-permute-done.15.got, bf16[8,64,1600]{2,1,0:T(8,128)(2,1)} %collective-permute-done.16.mate_own, ...), custom_call_target="tpu_custom_call" | custom-call | tf_op jit(solution)/shard_map/output_weight/pallas_call | solution.py:321
  199.1 39.5 %shard_map.180 = (bf16[1024,1600]{1,0:T(8,128)(2,1)}, bf16[1024,400]{1,0:T(8,128)(2,1)}, bf16[1024,400]{1,0:T(8,128)(2,1)}, bf16[1024,400]{1,0:T(8,128)(2,1)}, b...) custom-call(s32[17]{0:T(128)} %pad_add_fusion.table, ...), custom_call_target="tpu_custom_call" | custom-call | tf_op jit(solution)/shard_map/pallas_call | solution.py:684
  242.5 3.8 collective-permute-done.39
  252.7 3.3 fusion.54
  256.0 3.3 fusion.53
  266.9 2.1 collective-permute-done.42
  279.2 4.0 collective-permute-done.52.back_two
  288.3 3.2 collective-permute-done.46.ahead_one
  292.2 6.6 %shard_map.181 = (bf16[8,128,512]{2,1,0:T(8,128)(2,1)}, f32[128,1600]{1,0:T(8,128)}, f32[8,1600]{1,0:T(8,128)}) custom-call(s32[1]{0:T(128)} %bitcast.odd_core, bf16[128,1600]{1,0:T(8,128)(2,1)} %slice_bitcast_fusion.own, bf16[64,1600]{1,0:T(8,128)(2,1)} %copy-done.39, bf16[64,1600]{1,0:T(8,128)(2,1)} %copy-done.37, bf16[64,1600]{1,0:T(8,128)(2,1)} %copy-done.38, ...), custom_call_target="tpu_custom_call" | custom-call | tf_op jit(solution)/shard_map/pallas_call | solution.py:369
  298.8 4.3 all-to-all-start.1
  309.2 4.9 %convolution_add_fusion.1 = f32[400,1600]{1,0:T(8,128)S(1)} fusion(f32[400,1600]{1,0:T(8,128)} %collective-permute-done.55, bf16[1024,400]{1,0:T(8,128)(2,1)} %get-tuple-element.189, bf16[1024,1600]{1,0:T(8,128)(2,1)} %get-tuple-element.176), kind=kOutput, calls=%fused_computation.1 | convolution fusion | flops 1311360000 | bytes 9216000 | tf_op jit(solution)/shard_map/up_gradient/dot_general | solution.py:217
  317.2 3.5 convolution_add_fusion
  329.1 2.3 collective-permute-start.61
  333.3 13.6 %shard_map.182 = (bf16[1024,256]{1,0:T(8,128)(2,1)}, f32[2,1024,256]{2,1,0:T(8,128)}, bf16[2,1024,256]{2,1,0:T(8,128)(2,1)}, f32[8,256]{1,0:T(8,128)}) custom-call(s32[1]{0:T(128)} %bitcast.odd_core, f32[8,128,384]{2,1,0:T(8,128)} %and_select_fusion.bias, bf16[1024,256]{1,0:T(8,128)(2,1)} %get-tuple-element.138.query, ...), custom_call_target="tpu_custom_call" | custom-call | tf_op jit(solution)/shard_map/pallas_call | solution.py:503
  350.8 2.0 collective-permute-start.65
  354.2 2.6 convert_add_fusion.1
  356.9 16.5 %shard_map.183 = (f32[416,1600]{1,0:T(8,128)}, f32[416,1600]{1,0:T(8,128)}, bf16[8,128,1600]{2,1,0:T(8,128)(2,1)}, f32[8,1600]{1,0:T(8,128)}, f32[8,256]{1,0:T(8,128)}) custom-call(s32[17]{0:T(128)} %pad_add_fusion.table, bf16[1024,256]{1,0:T(8,128)(2,1)} %get-tuple-element.194.query_back, f32[2,1024,256]{2,1,0:T(8,128)} %get-tuple-element.195.own_back, ...), custom_call_target="tpu_custom_call" | custom-call | tf_op jit(solution)/shard_map/pallas_call | solution.py:773
  378.8 2.1 add.277
  393.0 2.4 shard_map.184
  398.8 2.1 collective-permute-done.70.outs_0_
  401.9 3.1 joint_gradient.1
  407.1 4.6 collective-permute-done.74
  414.0 5.1 %collective-permute-start.79 = (bf16[256,896]{1,0:T(8,128)(2,1)}, bf16[256,896]{1,0:T(8,128)(2,1)}, u32[]{:S(2)}, u32[]{:S(2)}) collective-permute-start(bf16[256,896]{1,0:T(8,128)(2,1)} %get-tuple-element.214), channel_id=1, source_target_pairs={{15,15},{14,10},{0,0},{1,5},{3,11},{5,1},{7,7},{9,13},{11,3},{13,9... | collective-permute-start | bytes 1376264 | tf_op jit(solution)/shard_map/joint_gradient/ppermute | solution.py:191
  422.5 4.2 fusion.38
  426.6 1.9 fusion.18
  432.7 4.7 %all-to-all-start.2 = ((f32[32,4,128]{2,1,0:T(4,128)}), f32[32,4,128]{2,1,0:T(4,128)}, u32[]{:S(2)}, u32[]{:S(2)}) async-start(f32[32,4,128]{2,1,0:T(4,128)} %shard_map.184), calls=%async_computation.2 | async-start | bytes 131072 | tf_op jit(solution)/shard_map/vectors_gradient/all_to_all | solution.py:1241
  440.2 2.7 convert_add_fusion
  450.8 3.2 convolution_add_fusion.2
  457.2 3.7 collective-permute-done.82
  (358 shorter events, 178.9 us)
Async XLA Ops:
  4.6 27.9 %collective-permute-start = (bf16[256,896]{1,0:T(8,128)(2,1)}, bf16[256,896]{1,0:T(8,128)(2,1)}, u32[]{:S(2)}, u32[]{:S(2)}) collective-permute-start(bf16[256,896]{1,0:T(8,128)(2,1)} %get-tuple-element.122), channel_id=1, source_target_pairs={{15,15},{10,14},{0,0},{1,5},{3,11},{5,1},{7,7},{9,13},{11,3},{13,9... | collective-permute-start | bytes 1376264 | tf_op jit(solution)/shard_map/joint_weight/ppermute | solution.py:191
  9.8 22.0 %collective-permute-start.1 = (bf16[160,896]{1,0:T(8,128)(2,1)}, bf16[160,896]{1,0:T(8,128)(2,1)S(1)}, u32[]{:S(2)}, u32[]{:S(2)}) collective-permute-start(bf16[160,896]{1,0:T(8,128)(2,1)} %get-tuple-element.123), channel_id=1, source_target_pairs={{4,14},{14,12},{8,10},{2,8},{12,6},{6,4},{0,2},{5,15},{10,0},{11,1... | collective-permute-start | bytes 860168 | tf_op jit(solution)/shard_map/joint_weight/ppermute | solution.py:191
  11.2 20.6 %collective-permute-start.2 = (bf16[64,896]{1,0:T(8,128)(2,1)}, bf16[64,896]{1,0:T(8,128)(2,1)S(1)}, u32[]{:S(2)}, u32[]{:S(2)}) collective-permute-start(bf16[64,896]{1,0:T(8,128)(2,1)} %get-tuple-element.124), channel_id=1, source_target_pairs={{9,15},{3,13},{13,11},{7,9},{1,7},{11,5},{5,3},{25,31},{19,29},{29... | collective-permute-start | bytes 344072 | tf_op jit(solution)/shard_map/joint_weight/ppermute | solution.py:191
  13.2 18.5 %all-to-all-start = ((bf16[32,4,100]{2,1,0:T(4,128)(2,1)}), bf16[32,4,100]{2,1,0:T(4,128)(2,1)S(1)}, u32[]{:S(2)}, u32[]{:S(2)}) async-start(bf16[32,4,100]{2,1,0:T(4,128)(2,1)} %broadcast_in_dim.53), calls=%async_computation | async-start | bytes 65536 | tf_op jit(solution)/shard_map/parameters/all_to_all | solution.py:956
  24.6 16.9 %collective-permute-start.7 = (bf16[192,1600]{1,0:T(8,128)(2,1)S(1)}, bf16[192,1600]{1,0:T(8,128)(2,1)S(1)}, u32[]{:S(2)}, u32[]{:S(2)}) collective-permute-start(bf16[192,1600]{1,0:T(8,128)(2,1)S(1)} %pad_maximum_fusion.1.refs_0_), channel_id=1, source_target_pairs={{0,2},{1,3},{4,0},{5,1},{8,4},{9,5},{12,8},{13,9},{14,12},{15,13},... | collective-permute-start | bytes 1843208 | tf_op jit(solution)/shard_map/input_ring/ppermute | solution.py:40
  26.4 16.2 %collective-permute-start.8 = (bf16[192,1600]{1,0:T(8,128)(2,1)S(1)}, bf16[192,1600]{1,0:T(8,128)(2,1)S(1)}, u32[]{:S(2)}, u32[]{:S(2)}) collective-permute-start(bf16[192,1600]{1,0:T(8,128)(2,1)S(1)} %pad_maximum_fusion.1.refs_0_), channel_id=1, source_target_pairs={{0,4},{1,5},{4,8},{5,9},{8,12},{9,13},{12,14},{13,15},{14,10},{15,... | collective-permute-start | bytes 1843208 | tf_op jit(solution)/shard_map/input_ring/ppermute | solution.py:40
  33.7 20.7 %collective-permute-start.3 = (bf16[480,896]{1,0:T(8,128)(2,1)S(1)}, bf16[480,896]{1,0:T(8,128)(2,1)}, u32[]{:S(2)}, u32[]{:S(2)}) collective-permute-start(bf16[480,896]{1,0:T(8,128)(2,1)S(1)} %pad_maximum_fusion.own), channel_id=1, source_target_pairs={{0,16},{16,0},{1,17},{17,1},{2,18},{18,2},{3,19},{19,3},{4,20},{20... | collective-permute-start | bytes 2580488 | tf_op jit(solution)/shard_map/joint_weight/ppermute | solution.py:48
  42.6 16.0 %collective-permute-start.10 = (bf16[192,1600]{1,0:T(8,128)(2,1)S(1)}, bf16[192,1600]{1,0:T(8,128)(2,1)}, u32[]{:S(2)}, u32[]{:S(2)}) collective-permute-start(bf16[192,1600]{1,0:T(8,128)(2,1)S(1)} %collective-permute-done.8.refs_7_), channel_id=1, source_target_pairs={{0,4},{1,5},{4,8},{5,9},{8,12},{9,13},{12,14},{13,15},{14,10},{15,... | collective-permute-start | bytes 1843208 | tf_op jit(solution)/shard_map/input_ring/ppermute | solution.py:40
  43.8 16.1 %collective-permute-start.9 = (bf16[192,1600]{1,0:T(8,128)(2,1)S(1)}, bf16[192,1600]{1,0:T(8,128)(2,1)}, u32[]{:S(2)}, u32[]{:S(2)}) collective-permute-start(bf16[192,1600]{1,0:T(8,128)(2,1)S(1)} %collective-permute-done.7.refs_1_), channel_id=1, source_target_pairs={{0,2},{1,3},{4,0},{5,1},{8,4},{9,5},{12,8},{13,9},{14,12},{15,13},... | collective-permute-start | bytes 1843208 | tf_op jit(solution)/shard_map/input_ring/ppermute | solution.py:40
  60.0 15.7 %collective-permute-start.11 = (bf16[192,1600]{1,0:T(8,128)(2,1)}, bf16[192,1600]{1,0:T(8,128)(2,1)S(1)}, u32[]{:S(2)}, u32[]{:S(2)}) collective-permute-start(bf16[192,1600]{1,0:T(8,128)(2,1)} %collective-permute-done.9.refs_2_), channel_id=1, source_target_pairs={{0,2},{1,3},{4,0},{5,1},{8,4},{9,5},{12,8},{13,9},{14,12},{15,13},... | collective-permute-start | bytes 1843208 | tf_op jit(solution)/shard_map/input_ring/ppermute | solution.py:40
  61.3 16.2 %collective-permute-start.12 = (bf16[192,1600]{1,0:T(8,128)(2,1)}, bf16[192,1600]{1,0:T(8,128)(2,1)S(1)}, u32[]{:S(2)}, u32[]{:S(2)}) collective-permute-start(bf16[192,1600]{1,0:T(8,128)(2,1)} %collective-permute-done.10.refs_6_), channel_id=1, source_target_pairs={{0,4},{1,5},{4,8},{5,9},{8,12},{9,13},{12,14},{13,15},{14,10},{15,... | collective-permute-start | bytes 1843208 | tf_op jit(solution)/shard_map/input_ring/ppermute | solution.py:40
  65.4 17.9 %collective-permute-start.6 = (bf16[400,800]{1,0:T(8,128)(2,1)}, bf16[400,800]{1,0:T(8,128)(2,1)}, u32[]{:S(2)}, u32[]{:S(2)}) collective-permute-start(bf16[400,800]{1,0:T(8,128)(2,1)} %bitcast.158), channel_id=1, source_target_pairs={{0,16},{16,0},{1,17},{17,1},{2,18},{18,2},{3,19},{19,3},{4,20},{20... | collective-permute-start | bytes 1920008 | tf_op jit(solution)/shard_map/feed_forward_weights/ppermute | solution.py:48
  81.0 20.9 %collective-permute-start.17 = (bf16[400,800]{1,0:T(8,128)(2,1)}, bf16[400,800]{1,0:T(8,128)(2,1)S(1)}, u32[]{:S(2)}, u32[]{:S(2)}) collective-permute-start(bf16[400,800]{1,0:T(8,128)(2,1)} %param.17), channel_id=1, source_target_pairs={{0,16},{16,0},{1,17},{17,1},{2,18},{18,2},{3,19},{19,3},{4,20},{20... | collective-permute-start | bytes 1920008 | tf_op jit(solution)/shard_map/feed_forward_weights/ppermute | solution.py:48
  98.5 31.1 %collective-permute-start.16 = (bf16[8,64,1600]{2,1,0:T(8,128)(2,1)}, bf16[8,64,1600]{2,1,0:T(8,128)(2,1)}, u32[]{:S(2)}, u32[]{:S(2)}) collective-permute-start(bf16[8,64,1600]{2,1,0:T(8,128)(2,1)} %get-tuple-element.137.own), channel_id=1, source_target_pairs={{0,1},{1,0},{2,3},{3,2},{4,5},{5,4},{6,7},{7,6},{8,9},{9,8},{10,11... | collective-permute-start | bytes 4915208 | tf_op jit(solution)/shard_map/feed_forward_weights/ppermute | solution.py:44
  112.4 40.5 %collective-permute-start.15 = (bf16[8,64,1600]{2,1,0:T(8,128)(2,1)}, bf16[8,64,1600]{2,1,0:T(8,128)(2,1)}, u32[]{:S(2)}, u32[]{:S(2)}) collective-permute-start(bf16[8,64,1600]{2,1,0:T(8,128)(2,1)} %get-tuple-element.137.own), channel_id=1, source_target_pairs={{0,16},{16,0},{1,17},{17,1},{2,18},{18,2},{3,19},{19,3},{4,20},{20... | collective-permute-start | bytes 4915208 | tf_op jit(solution)/shard_map/output_weight/ppermute | solution.py:48
  114.1 13.3 %collective-permute-start.21 = (bf16[128,1600]{1,0:T(8,128)(2,1)S(1)}, bf16[128,1600]{1,0:T(8,128)(2,1)}, u32[]{:S(2)}, u32[]{:S(2)}) collective-permute-start(bf16[128,1600]{1,0:T(8,128)(2,1)S(1)} %collective-permute-done.18.refs_15_), channel_id=1, source_target_pairs={{0,4},{1,5},{4,8},{5,9},{8,12},{9,13},{12,14},{13,15},{14,10},{15,... | collective-permute-start | bytes 1228808 | tf_op jit(solution)/shard_map/cotangent_ring/ppermute | solution.py:40
  129.6 20.8 %collective-permute-start.23 = (bf16[1024,256]{1,0:T(8,128)(2,1)}, bf16[1024,256]{1,0:T(8,128)(2,1)S(1)}, u32[]{:S(2)}, u32[]{:S(2)}) collective-permute-start(bf16[1024,256]{1,0:T(8,128)(2,1)} %get-tuple-element.148.refs_0_.mixed), channel_id=1, source_target_pairs={{0,4},{1,5},{4,8},{5,9},{8,12},{9,13},{12,14},{13,15},{14,10},{15,... | collective-permute-start | bytes 1572872 | tf_op jit(solution)/shard_map/attended_ring/ppermute | solution.py:40
  130.6 20.2 %collective-permute-start.24 = (bf16[1024,256]{1,0:T(8,128)(2,1)}, bf16[1024,256]{1,0:T(8,128)(2,1)S(1)}, u32[]{:S(2)}, u32[]{:S(2)}) collective-permute-start(bf16[1024,256]{1,0:T(8,128)(2,1)} %get-tuple-element.148.refs_0_.mixed), channel_id=1, source_target_pairs={{0,2},{1,3},{4,0},{5,1},{8,4},{9,5},{12,8},{13,9},{14,12},{15,13},... | collective-permute-start | bytes 1572872 | tf_op jit(solution)/shard_map/attended_ring/ppermute | solution.py:40
  164.6 24.1 %collective-permute-start.31 = (bf16[400,1600]{1,0:T(8,128)(2,1)S(1)}, bf16[400,1600]{1,0:T(8,128)(2,1)}, u32[]{:S(2)}, u32[]{:S(2)}) collective-permute-start(bf16[400,1600]{1,0:T(8,128)(2,1)S(1)} %maximum_select_fusion.1.down_own), channel_id=1, source_target_pairs={{0,1},{1,0},{2,3},{3,2},{4,5},{5,4},{6,7},{7,6},{8,9},{9,8},{10,11... | collective-permute-start | bytes 3840008 | tf_op jit(solution)/shard_map/attended_ring/ppermute | solution.py:44
  165.1 23.6 %collective-permute-start.30 = (bf16[400,1600]{1,0:T(8,128)(2,1)S(1)}, bf16[400,1600]{1,0:T(8,128)(2,1)}, u32[]{:S(2)}, u32[]{:S(2)}) collective-permute-start(bf16[400,1600]{1,0:T(8,128)(2,1)S(1)} %maximum_select_fusion.up_own), channel_id=1, source_target_pairs={{0,1},{1,0},{2,3},{3,2},{4,5},{5,4},{6,7},{7,6},{8,9},{9,8},{10,11... | collective-permute-start | bytes 3840008 | tf_op jit(solution)/shard_map/attended_ring/ppermute | solution.py:44
  174.4 13.4 %collective-permute-start.35 = (bf16[1024,256]{1,0:T(8,128)(2,1)}, bf16[1024,256]{1,0:T(8,128)(2,1)S(1)}, u32[]{:S(2)}, u32[]{:S(2)}) collective-permute-start(bf16[1024,256]{1,0:T(8,128)(2,1)} %collective-permute-done.28.refs_2_), channel_id=1, source_target_pairs={{0,2},{1,3},{4,0},{5,1},{8,4},{9,5},{12,8},{13,9},{14,12},{15,13},... | collective-permute-start | bytes 1572872 | tf_op jit(solution)/shard_map/attended_ring/ppermute | solution.py:40
  175.1 13.7 %collective-permute-start.36 = (bf16[1024,256]{1,0:T(8,128)(2,1)}, bf16[1024,256]{1,0:T(8,128)(2,1)}, u32[]{:S(2)}, u32[]{:S(2)}) collective-permute-start(bf16[1024,256]{1,0:T(8,128)(2,1)} %collective-permute-done.27.refs_6_), channel_id=1, source_target_pairs={{0,4},{1,5},{4,8},{5,9},{8,12},{9,13},{12,14},{13,15},{14,10},{15,... | collective-permute-start | bytes 1572872 | tf_op jit(solution)/shard_map/attended_ring/ppermute | solution.py:40
  176.7 15.2 %collective-permute-start.32 = (f32[1,400]{1,0:T(1,128)S(1)}, f32[1,400]{1,0:T(1,128)S(1)}, u32[]{:S(2)}, u32[]{:S(2)}) collective-permute-start(f32[1,400]{1,0:T(1,128)S(1)} %bitcast.164), channel_id=1, source_target_pairs={{0,1},{1,0},{2,3},{3,2},{4,5},{5,4},{6,7},{7,6},{8,9},{9,8},{10,11... | collective-permute-start | bytes 4808 | tf_op jit(solution)/shard_map/feed_forward_weights/ppermute | solution.py:44
  249.4 13.3 %collective-permute-start.44 = (bf16[64,1600]{1,0:T(8,128)(2,1)S(1)}, bf16[64,1600]{1,0:T(8,128)(2,1)S(1)}, u32[]{:S(2)}, u32[]{:S(2)}) collective-permute-start(bf16[64,1600]{1,0:T(8,128)(2,1)S(1)} %get-tuple-element.168), channel_id=1, source_target_pairs={{0,4},{1,5},{4,8},{5,9},{8,12},{9,13},{12,14},{13,15},{14,10},{15,... | collective-permute-start | bytes 614408 | tf_op jit(solution)/shard_map/normed_two_back_ring/ppermute | solution.py:40
  251.3 13.6 %collective-permute-start.43 = (bf16[64,1600]{1,0:T(8,128)(2,1)S(1)}, bf16[64,1600]{1,0:T(8,128)(2,1)S(1)}, u32[]{:S(2)}, u32[]{:S(2)}) collective-permute-start(bf16[64,1600]{1,0:T(8,128)(2,1)S(1)} %fusion.32), channel_id=1, source_target_pairs={{0,2},{1,3},{4,0},{5,1},{8,4},{9,5},{12,8},{13,9},{14,12},{15,13},... | collective-permute-start | bytes 614408 | tf_op jit(solution)/shard_map/normed_two_back_ring/ppermute | solution.py:40
  256.0 61.2 %collective-permute-start.56 = (f32[400,1600]{1,0:T(8,128)}, f32[400,1600]{1,0:T(8,128)}, u32[]{:S(2)}, u32[]{:S(2)}) collective-permute-start(f32[400,1600]{1,0:T(8,128)} %fusion.54), channel_id=1, source_target_pairs={{0,1},{1,0},{2,3},{3,2},{4,5},{5,4},{6,7},{7,6},{8,9},{9,8},{10,11... | collective-permute-start | bytes 7680008 | tf_op jit(solution)/shard_map/down_gradient/ppermute | solution.py:44
  259.3 50.0 %collective-permute-start.55 = (f32[400,1600]{1,0:T(8,128)}, f32[400,1600]{1,0:T(8,128)}, u32[]{:S(2)}, u32[]{:S(2)}) collective-permute-start(f32[400,1600]{1,0:T(8,128)} %fusion.53), channel_id=1, source_target_pairs={{0,1},{1,0},{2,3},{3,2},{4,5},{5,4},{6,7},{7,6},{8,9},{9,8},{10,11... | collective-permute-start | bytes 7680008 | tf_op jit(solution)/shard_map/up_gradient/ppermute | solution.py:44
  283.2 15.6 %collective-permute-start.53 = (bf16[64,1600]{1,0:T(8,128)(2,1)S(1)}, bf16[64,1600]{1,0:T(8,128)(2,1)}, u32[]{:S(2)}, u32[]{:S(2)}) collective-permute-start(bf16[64,1600]{1,0:T(8,128)(2,1)S(1)} %get-tuple-element.185), channel_id=1, source_target_pairs={{0,4},{1,5},{4,8},{5,9},{8,12},{9,13},{12,14},{13,15},{14,10},{15,... | collective-permute-start | bytes 614408 | tf_op jit(solution)/shard_map/down_ring/ppermute | solution.py:40
  298.8 26.4 %all-to-all-start.1 = ((bf16[8,128,512]{2,1,0:T(8,128)(2,1)}), bf16[8,128,512]{2,1,0:T(8,128)(2,1)}, u32[]{:S(2)}, u32[]{:S(2)}) async-start(bf16[8,128,512]{2,1,0:T(8,128)(2,1)} %get-tuple-element.187), calls=%async_computation.1 | async-start | bytes 2097152 | tf_op jit(solution)/shard_map/back_exchange/all_to_all | solution.py:129
  315.4 31.6 %collective-permute-start.59 = (bf16[400,800]{1,0:T(8,128)(2,1)}, bf16[400,800]{1,0:T(8,128)(2,1)}, u32[]{:S(2)}, u32[]{:S(2)}) collective-permute-start(bf16[400,800]{1,0:T(8,128)(2,1)} %select_convert_fusion.2), channel_id=1, source_target_pairs={{0,16},{16,0},{1,17},{17,1},{2,18},{18,2},{3,19},{19,3},{4,20},{20... | collective-permute-start | bytes 1920008 | tf_op jit(solution)/shard_map/up_gradient/ppermute | solution.py:48
  327.1 19.8 %collective-permute-start.60 = (bf16[128,1600]{1,0:T(8,128)(2,1)}, bf16[128,1600]{1,0:T(8,128)(2,1)S(1)}, u32[]{:S(2)}, u32[]{:S(2)}) collective-permute-start(bf16[128,1600]{1,0:T(8,128)(2,1)} %pad_maximum_fusion.5), channel_id=1, source_target_pairs={{0,4},{1,5},{4,8},{5,9},{8,12},{9,13},{12,14},{13,15},{14,10},{15,... | collective-permute-start | bytes 1228808 | tf_op jit(solution)/shard_map/down_ring/ppermute | solution.py:40
  329.1 17.8 %collective-permute-start.61 = (bf16[128,1600]{1,0:T(8,128)(2,1)}, bf16[128,1600]{1,0:T(8,128)(2,1)S(1)}, u32[]{:S(2)}, u32[]{:S(2)}) collective-permute-start(bf16[128,1600]{1,0:T(8,128)(2,1)} %pad_maximum_fusion.6), channel_id=1, source_target_pairs={{0,2},{1,3},{4,0},{5,1},{8,4},{9,5},{12,8},{13,9},{14,12},{15,13},... | collective-permute-start | bytes 1228808 | tf_op jit(solution)/shard_map/down_ring/ppermute | solution.py:40
  331.4 25.4 %collective-permute-start.63 = (bf16[400,800]{1,0:T(8,128)(2,1)}, bf16[400,800]{1,0:T(8,128)(2,1)}, u32[]{:S(2)}, u32[]{:S(2)}) collective-permute-start(bf16[400,800]{1,0:T(8,128)(2,1)} %select_convert_fusion.1), channel_id=1, source_target_pairs={{0,16},{16,0},{1,17},{17,1},{2,18},{18,2},{3,19},{19,3},{4,20},{20... | collective-permute-start | bytes 1920008 | tf_op jit(solution)/shard_map/down_gradient/ppermute | solution.py:48
  348.9 24.4 %collective-permute-start.64 = (bf16[128,1600]{1,0:T(8,128)(2,1)}, bf16[128,1600]{1,0:T(8,128)(2,1)S(1)}, u32[]{:S(2)}, u32[]{:S(2)}) collective-permute-start(bf16[128,1600]{1,0:T(8,128)(2,1)} %fusion.16), channel_id=1, source_target_pairs={{0,4},{1,5},{4,8},{5,9},{8,12},{9,13},{12,14},{13,15},{14,10},{15,... | collective-permute-start | bytes 1228808 | tf_op jit(solution)/shard_map/down_ring/ppermute | solution.py:40
  350.8 22.5 %collective-permute-start.65 = (bf16[128,1600]{1,0:T(8,128)(2,1)}, bf16[128,1600]{1,0:T(8,128)(2,1)S(1)}, u32[]{:S(2)}, u32[]{:S(2)}) collective-permute-start(bf16[128,1600]{1,0:T(8,128)(2,1)} %fusion.15), channel_id=1, source_target_pairs={{0,2},{1,3},{4,0},{5,1},{8,4},{9,5},{12,8},{13,9},{14,12},{15,13},... | collective-permute-start | bytes 1228808 | tf_op jit(solution)/shard_map/down_ring/ppermute | solution.py:40
  382.1 18.9 %collective-permute-start.70 = (bf16[416,800]{1,0:T(8,128)(2,1)}, bf16[416,800]{1,0:T(8,128)(2,1)S(1)}, u32[]{:S(2)}, u32[]{:S(2)}) collective-permute-start(bf16[416,800]{1,0:T(8,128)(2,1)} %select_convert_fusion), channel_id=1, source_target_pairs={{0,16},{16,0},{1,17},{17,1},{2,18},{18,2},{3,19},{19,3},{4,20},{20... | collective-permute-start | bytes 1996808 | tf_op jit(solution)/shard_map/joint_gradient/ppermute | solution.py:48
  384.4 20.9 %collective-permute-start.68 = (bf16[128,1600]{1,0:T(8,128)(2,1)}, bf16[128,1600]{1,0:T(8,128)(2,1)}, u32[]{:S(2)}, u32[]{:S(2)}) collective-permute-start(bf16[128,1600]{1,0:T(8,128)(2,1)} %pad_maximum_fusion.7), channel_id=1, source_target_pairs={{0,4},{1,5},{4,8},{5,9},{8,12},{9,13},{12,14},{13,15},{14,10},{15,... | collective-permute-start | bytes 1228808 | tf_op jit(solution)/shard_map/last_ring/ppermute | solution.py:40
  388.4 16.9 %collective-permute-start.71 = (bf16[128,1600]{1,0:T(8,128)(2,1)}, bf16[128,1600]{1,0:T(8,128)(2,1)}, u32[]{:S(2)}, u32[]{:S(2)}) collective-permute-start(bf16[128,1600]{1,0:T(8,128)(2,1)} %fusion.14), channel_id=1, source_target_pairs={{0,4},{1,5},{4,8},{5,9},{8,12},{9,13},{12,14},{13,15},{14,10},{15,... | collective-permute-start | bytes 1228808 | tf_op jit(solution)/shard_map/down_ring/ppermute | solution.py:40
  391.2 13.8 %collective-permute-start.72 = (bf16[128,1600]{1,0:T(8,128)(2,1)}, bf16[128,1600]{1,0:T(8,128)(2,1)}, u32[]{:S(2)}, u32[]{:S(2)}) collective-permute-start(bf16[128,1600]{1,0:T(8,128)(2,1)} %fusion.13), channel_id=1, source_target_pairs={{0,2},{1,3},{4,0},{5,1},{8,4},{9,5},{12,8},{13,9},{14,12},{15,13},... | collective-permute-start | bytes 1228808 | tf_op jit(solution)/shard_map/down_ring/ppermute | solution.py:40
  395.4 16.3 %collective-permute-start.74 = (bf16[128,1600]{1,0:T(8,128)(2,1)}, bf16[128,1600]{1,0:T(8,128)(2,1)}, u32[]{:S(2)}, u32[]{:S(2)}) collective-permute-start(bf16[128,1600]{1,0:T(8,128)(2,1)} %pad_maximum_fusion.8), channel_id=1, source_target_pairs={{0,2},{1,3},{4,0},{5,1},{8,4},{9,5},{12,8},{13,9},{14,12},{15,13},... | collective-permute-start | bytes 1228808 | tf_op jit(solution)/shard_map/last_ring/ppermute | solution.py:40
  406.6 20.1 %collective-permute-start.73 = (bf16[128,1600]{1,0:T(8,128)(2,1)S(1)}, bf16[128,1600]{1,0:T(8,128)(2,1)S(1)}, u32[]{:S(2)}, u32[]{:S(2)}) collective-permute-start(bf16[128,1600]{1,0:T(8,128)(2,1)S(1)} %fusion.17), channel_id=1, source_target_pairs={{0,4},{1,5},{4,8},{5,9},{8,12},{9,13},{12,14},{13,15},{14,10},{15,... | collective-permute-start | bytes 1228808 | tf_op jit(solution)/shard_map/last_ring/ppermute | solution.py:40
  412.9 16.9 %collective-permute-start.75 = (bf16[128,1600]{1,0:T(8,128)(2,1)S(1)}, bf16[128,1600]{1,0:T(8,128)(2,1)S(1)}, u32[]{:S(2)}, u32[]{:S(2)}) collective-permute-start(bf16[128,1600]{1,0:T(8,128)(2,1)S(1)} %fusion.12), channel_id=1, source_target_pairs={{0,2},{1,3},{4,0},{5,1},{8,4},{9,5},{12,8},{13,9},{14,12},{15,13},... | collective-permute-start | bytes 1228808 | tf_op jit(solution)/shard_map/last_ring/ppermute | solution.py:40
  414.0 28.9 %collective-permute-start.79 = (bf16[256,896]{1,0:T(8,128)(2,1)}, bf16[256,896]{1,0:T(8,128)(2,1)}, u32[]{:S(2)}, u32[]{:S(2)}) collective-permute-start(bf16[256,896]{1,0:T(8,128)(2,1)} %get-tuple-element.214), channel_id=1, source_target_pairs={{15,15},{14,10},{0,0},{1,5},{3,11},{5,1},{7,7},{9,13},{11,3},{13,9... | collective-permute-start | bytes 1376264 | tf_op jit(solution)/shard_map/joint_gradient/ppermute | solution.py:191
  419.1 26.8 %collective-permute-start.80 = (bf16[160,896]{1,0:T(8,128)(2,1)}, bf16[160,896]{1,0:T(8,128)(2,1)}, u32[]{:S(2)}, u32[]{:S(2)}) collective-permute-start(bf16[160,896]{1,0:T(8,128)(2,1)} %get-tuple-element.215), channel_id=1, source_target_pairs={{14,4},{12,14},{10,8},{8,2},{6,12},{4,6},{2,0},{0,10},{15,5},{1,11... | collective-permute-start | bytes 860168 | tf_op jit(solution)/shard_map/joint_gradient/ppermute | solution.py:191
  419.3 27.5 %collective-permute-start.81 = (bf16[64,896]{1,0:T(8,128)(2,1)}, bf16[64,896]{1,0:T(8,128)(2,1)}, u32[]{:S(2)}, u32[]{:S(2)}) collective-permute-start(bf16[64,896]{1,0:T(8,128)(2,1)} %get-tuple-element.216), channel_id=1, source_target_pairs={{15,9},{13,3},{11,13},{9,7},{7,1},{5,11},{3,5},{31,25},{29,19},{27... | collective-permute-start | bytes 344072 | tf_op jit(solution)/shard_map/joint_gradient/ppermute | solution.py:191
  426.6 24.1 %collective-permute-start.78 = (f32[100,2048]{1,0:T(8,128)}, f32[100,2048]{1,0:T(8,128)}, u32[]{:S(2)}, u32[]{:S(2)}) collective-permute-start(f32[100,2048]{1,0:T(8,128)} %fusion.38), channel_id=1, source_target_pairs={{0,1},{1,0},{2,3},{3,2},{4,5},{5,4},{6,7},{7,6},{8,9},{9,8},{10,11... | collective-permute-start | bytes 2457608 | tf_op jit(solution)/shard_map/output_gradient/ppermute | solution.py:44
  431.7 24.2 %collective-permute-start.77 = (bf16[128,1600]{1,0:T(8,128)(2,1)}, bf16[128,1600]{1,0:T(8,128)(2,1)}, u32[]{:S(2)}, u32[]{:S(2)}) collective-permute-start(bf16[128,1600]{1,0:T(8,128)(2,1)} %fusion.11), channel_id=1, source_target_pairs={{0,2},{1,3},{4,0},{5,1},{8,4},{9,5},{12,8},{13,9},{14,12},{15,13},... | collective-permute-start | bytes 1228808 | tf_op jit(solution)/shard_map/last_ring/ppermute | solution.py:40
  432.7 16.6 %all-to-all-start.2 = ((f32[32,4,128]{2,1,0:T(4,128)}), f32[32,4,128]{2,1,0:T(4,128)}, u32[]{:S(2)}, u32[]{:S(2)}) async-start(f32[32,4,128]{2,1,0:T(4,128)} %shard_map.184), calls=%async_computation.2 | async-start | bytes 131072 | tf_op jit(solution)/shard_map/vectors_gradient/all_to_all | solution.py:1241
  (87 other events, 1223.1 us)

commit v6 on v5

--- a/solution.py
+++ b/solution.py
@@ -1028,7 +1028,7 @@
             )
 
         below_mate = core_swap(below)
-    mate = core_swap(after(own, (down_got, crossing)))
+    mate = core_swap(after(own, crossing))
     with jax.named_scope("cotangent_ring"):
         crossing = cotangent_ring.send(own)
     attended, log_total = attend_forward(odd_core, bias, query, own, mate, scale)

time: 472 us -> 464 us (0.983)
  waiting for transfers between devices: 116 us -> 106 us
    ppermute x54, waiting for transfers between devices: 88.1 us -> 62.2 us  [send(): return lax.ppermute(value, 'ctx', pairs)]
    ppermute x9, waiting for transfers between devices: 17.8 us -> 32 us  [data_swap(): lax.ppermute(value, 'dp', [(i, i ^ 1) for i in range(lax.axis_size('dp'))])]
    unnamed x104 -> x98, local copies, waits for them, and re-layouts: 11.8 us -> 9.55 us
  transfers between devices with their start and end apart: 86 -> 86, of which waited for: 42 -> 42; matrix products, arithmetic and copies ran while one was open for 24% -> 24% of each run, Pallas kernels for 17% -> 18%
where the time goes in v6:
time: 464 us; the launch traced here: 455 us
  Pallas kernels  122 us (26%)
  waiting for transfers between devices  106 us (23%)
  starting transfers between devices  105 us (23%)
  other arithmetic  66.4 us (14%)
  local copies, waits for them, and re-layouts  29.9 us (6%)
  matrix products  23.8 us (5%)
    ppermute x54, waiting for transfers between devices, send(): return lax.ppermute(value, 'ctx', pairs)  62.2 us
    ppermute x54, starting transfers between devices, send(): return lax.ppermute(value, 'ctx', pairs)  59.9 us
    pallas_call x1, Pallas kernels, feed_forward(): pl.pallas_call(functools.partial(feed_forward_kernel, chips), grid_spec=p...  39.5 us
    ppermute x9, waiting for transfers between devices, data_swap(): lax.ppermute(value, 'dp', [(i, i ^ 1) for i in range(lax.axis_size('dp'))])  32 us
    dot_general x7, matrix products, rows_by_rows(): lax.dot_general(left_side, right_side, (((0,), (0,)), ((), ())), preferre...  23.8 us
    convert_element_type x18, other arithmetic, ring_scatter(): piece = piece.astype(bf16)  23.8 us
    pallas_call x1, Pallas kernels, back_through(): pl.pallas_call(functools.partial(back_through_kernel, chips), grid_spec=p...  16.5 us
    ppermute x6, starting transfers between devices, run_route(): lax.ppermute(piece, 'ctx', group)  13.6 us
  transfers between devices with their start and end apart: 86, of which 42 were waited for; matrix products, arithmetic and copies ran while one was open for 24% of the time, Pallas kernels for 18%

profile of v6, /device:TPU:0, one launch (start us, length us, event | category | flops | bytes accessed | tf_op | source)
XLA Modules:
  0.0 455.5 jit_solution(12635938872231451543)
XLA Ops:
  2.0 2.6 joint_weight.2
  4.6 5.2 %collective-permute-start = (bf16[256,896]{1,0:T(8,128)(2,1)}, bf16[256,896]{1,0:T(8,128)(2,1)}, u32[]{:S(2)}, u32[]{:S(2)}) collective-permute-start(bf16[256,896]{1,0:T(8,128)(2,1)} %get-tuple-element.122), channel_id=1, source_target_pairs={{15,15},{10,14},{0,0},{1,5},{3,11},{5,1},{7,7},{9,13},{11,3},{13,9... | collective-permute-start | bytes 1376264 | tf_op jit(solution)/shard_map/joint_weight/ppermute | solution.py:191
  13.2 8.9 %all-to-all-start = ((bf16[32,4,100]{2,1,0:T(4,128)(2,1)}), bf16[32,4,100]{2,1,0:T(4,128)(2,1)S(1)}, u32[]{:S(2)}, u32[]{:S(2)}) async-start(bf16[32,4,100]{2,1,0:T(4,128)(2,1)} %broadcast_in_dim.53), calls=%async_computation | async-start | bytes 65536 | tf_op jit(solution)/shard_map/parameters/all_to_all | solution.py:956
  26.6 5.1 %all-to-all-done = bf16[32,4,100]{2,1,0:T(4,128)(2,1)S(1)} async-done(((bf16[32,4,100]{2,1,0:T(4,128)(2,1)}), bf16[32,4,100]{2,1,0:T(4,128)(2,1)S(1)}, u32[]{:S(2)}, u32[]{:S(2)}) %all-to-all-start) | async-done | bytes 25632 | tf_op jit(solution)/shard_map/parameters/all_to_all | solution.py:956
  34.2 7.3 %collective-permute-done.7.refs_1_ = bf16[192,1600]{1,0:T(8,128)(2,1)S(1)} collective-permute-done((bf16[192,1600]{1,0:T(8,128)(2,1)S(1)}, bf16[192,1600]{1,0:T(8,128)(2,1)S(1)}, u32[]{:S(2)}, u32[]{:S(2)}) %collective-permute-start.7) | collective-permute-done | bytes 614432 | tf_op jit(solution)/shard_map/input_ring/ppermute | solution.py:40
  45.1 9.3 %collective-permute-done.3.got = bf16[480,896]{1,0:T(8,128)(2,1)} collective-permute-done((bf16[480,896]{1,0:T(8,128)(2,1)S(1)}, bf16[480,896]{1,0:T(8,128)(2,1)}, u32[]{:S(2)}, u32[]{:S(2)}) %collective-permute-start.3) | collective-permute-done | bytes 860192 | tf_op jit(solution)/shard_map/joint_weight/ppermute | solution.py:48
  56.4 2.4 collective-permute-done.10.refs_6_
  68.5 7.0 %joint_weight.3.weight = bf16[768,1600]{1,0:T(8,128)(2,1)} custom-call(s32[1]{0:T(128)} %bitcast.1.flag, s32[1,768]{1,0:T(1,128)} %get-tuple-element.286.own_rows, s32[1,768]{1,0:T(1,128)} %get-tuple-element.285.mate_rows, bf16[480,896]{1,0:T(8,128)(2,1)} %copy-done.9, bf16[480,896]{1,0:T(8,128)(2,1)} %collective-permute-done.3.got, ...), custom_call_target="tpu_custom_call" | custom-call | tf_op jit(solution)/shard_map/joint_weight/pallas_call | solution.py:280
  81.5 2.1 collective-permute-done.6
  83.6 3.2 collective-permute-done.13
  90.3 11.0 %projection.1 = (bf16[1024,1600]{1,0:T(8,128)(2,1)}, bf16[8,64,1600]{2,1,0:T(8,128)(2,1)}, bf16[1024,1600]{1,0:T(8,128)(2,1)}, bf16[1024,256]{1,0:T(8,128)(2,1)}, bf16[2,1024,256]{2,1,0:T(8,128)(2,1)}) custom-call(s32[17]{0:T(128)} %pad_add_fusion.table, bf16[768,1600]{1,0:T(8,128)(2,1)} %joint_weight.3.weight, f32[8,768]{1,0:T(8,128)} %pad.34.bias, ...), custom_call_target="tpu_custom_call" | custom-call | tf_op jit(solution)/shard_map/projection/pallas_call | solution.py:566
  108.3 10.4 %shard_map.179 = (bf16[1024,256]{1,0:T(8,128)(2,1)}, f32[8,2,256,1]{3,2,1,0:T(8,128)}) custom-call(s32[1]{0:T(128)} %bitcast.odd_core, f32[8,128,384]{2,1,0:T(8,128)} %and_select_fusion.bias, bf16[1024,256]{1,0:T(8,128)(2,1)} %get-tuple-element.138.query, bf16[2,1024,256]{2,1,0:T(8,128)(2,1)} %get-tuple-element.142.far.own, bf16[2,1024,256]{2,1,0:T(8,128)(2,1)} %copy-done.7, ...), custom_call_target="tpu_custom_call" | custom-call | tf_op jit(solution)/shard_map/pallas_call | solution.py:480
  123.1 2.8 maximum_select_fusion.1.down_own
  125.8 2.7 maximum_select_fusion.up_own
  128.6 3.1 collective-permute-done.25.refs_13_
  132.6 9.2 %collective-permute-done.22.refs_7_ = bf16[1024,256]{1,0:T(8,128)(2,1)S(1)} collective-permute-done((bf16[1024,256]{1,0:T(8,128)(2,1)}, bf16[1024,256]{1,0:T(8,128)(2,1)S(1)}, u32[]{:S(2)}, u32[]{:S(2)}) %collective-permute-start.22) | collective-permute-done | bytes 524320 | tf_op jit(solution)/shard_map/attended_ring/ppermute | solution.py:40
  143.9 12.8 %collective-permute-done.15.got = bf16[8,64,1600]{2,1,0:T(8,128)(2,1)} collective-permute-done((bf16[8,64,1600]{2,1,0:T(8,128)(2,1)}, bf16[8,64,1600]{2,1,0:T(8,128)(2,1)}, u32[]{:S(2)}, u32[]{:S(2)}) %collective-permute-start.15) | collective-permute-done | bytes 1638432 | tf_op jit(solution)/shard_map/output_weight/ppermute | solution.py:48
  159.4 5.5 %collective-permute-done.33 = bf16[64,1600]{1,0:T(8,128)(2,1)S(1)} collective-permute-done((bf16[64,1600]{1,0:T(8,128)(2,1)S(1)}, bf16[64,1600]{1,0:T(8,128)(2,1)S(1)}, u32[]{:S(2)}, u32[]{:S(2)}) %collective-permute-start.33) | collective-permute-done | bytes 204832 | tf_op jit(solution)/shard_map/cotangent_ring/ppermute | solution.py:40
  168.5 9.8 %output_weight.1.output_full.weight = bf16[1600,2048]{1,0:T(8,128)(2,1)} custom-call(s32[2]{0:T(128)} %pad_add_fusion.1.flags, bf16[8,64,1600]{2,1,0:T(8,128)(2,1)} %get-tuple-element.137.own, bf16[8,64,1600]{2,1,0:T(8,128)(2,1)} %collective-permute-done.15.got, bf16[8,64,1600]{2,1,0:T(8,128)(2,1)} %copy-done.12, ...), custom_call_target="tpu_custom_call" | custom-call | tf_op jit(solution)/shard_map/output_weight/pallas_call | solution.py:321
  189.9 39.5 %shard_map.180 = (bf16[1024,1600]{1,0:T(8,128)(2,1)}, bf16[1024,400]{1,0:T(8,128)(2,1)}, bf16[1024,400]{1,0:T(8,128)(2,1)}, bf16[1024,400]{1,0:T(8,128)(2,1)}, b...) custom-call(s32[17]{0:T(128)} %pad_add_fusion.table, ...), custom_call_target="tpu_custom_call" | custom-call | tf_op jit(solution)/shard_map/pallas_call | solution.py:684
  233.3 3.8 collective-permute-done.39
  243.5 3.3 fusion.54
  246.8 3.2 fusion.53
  270.3 4.0 collective-permute-done.52.back_two
  279.5 3.1 collective-permute-done.46.ahead_one
  283.3 6.6 %shard_map.181 = (bf16[8,128,512]{2,1,0:T(8,128)(2,1)}, f32[128,1600]{1,0:T(8,128)}, f32[8,1600]{1,0:T(8,128)}) custom-call(s32[1]{0:T(128)} %bitcast.odd_core, bf16[128,1600]{1,0:T(8,128)(2,1)} %slice_bitcast_fusion.own, bf16[64,1600]{1,0:T(8,128)(2,1)} %copy-done.34, bf16[64,1600]{1,0:T(8,128)(2,1)} %copy-done.32, bf16[64,1600]{1,0:T(8,128)(2,1)} %copy-done.33, ...), custom_call_target="tpu_custom_call" | custom-call | tf_op jit(solution)/shard_map/pallas_call | solution.py:369
  290.0 5.1 %all-to-all-start.1 = ((bf16[8,128,512]{2,1,0:T(8,128)(2,1)}), bf16[8,128,512]{2,1,0:T(8,128)(2,1)}, u32[]{:S(2)}, u32[]{:S(2)}) async-start(bf16[8,128,512]{2,1,0:T(8,128)(2,1)} %get-tuple-element.187), calls=%async_computation.1 | async-start | bytes 2097152 | tf_op jit(solution)/shard_map/back_exchange/all_to_all | solution.py:129
  298.5 2.1 collective-permute-done.58
  301.2 4.9 %convolution_add_fusion.1 = f32[400,1600]{1,0:T(8,128)S(1)} fusion(f32[400,1600]{1,0:T(8,128)} %collective-permute-done.55, bf16[1024,400]{1,0:T(8,128)(2,1)} %get-tuple-element.189, bf16[1024,1600]{1,0:T(8,128)(2,1)} %get-tuple-element.176), kind=kOutput, calls=%fused_computation.1 | convolution fusion | flops 1311360000 | bytes 9216000 | tf_op jit(solution)/shard_map/up_gradient/dot_general | solution.py:217
  308.8 3.5 convolution_add_fusion
  315.0 2.5 all-to-all-done.1
  321.4 2.4 collective-permute-start.61
  325.2 13.6 %shard_map.182 = (bf16[1024,256]{1,0:T(8,128)(2,1)}, f32[2,1024,256]{2,1,0:T(8,128)}, bf16[2,1024,256]{2,1,0:T(8,128)(2,1)}, f32[8,256]{1,0:T(8,128)}) custom-call(s32[1]{0:T(128)} %bitcast.odd_core, f32[8,128,384]{2,1,0:T(8,128)} %and_select_fusion.bias, bf16[1024,256]{1,0:T(8,128)(2,1)} %get-tuple-element.138.query, ...), custom_call_target="tpu_custom_call" | custom-call | tf_op jit(solution)/shard_map/pallas_call | solution.py:503
  342.8 2.0 collective-permute-start.65
  345.4 2.6 convert_add_fusion.1
  348.0 16.5 %shard_map.183 = (f32[416,1600]{1,0:T(8,128)}, f32[416,1600]{1,0:T(8,128)}, bf16[8,128,1600]{2,1,0:T(8,128)(2,1)}, f32[8,1600]{1,0:T(8,128)}, f32[8,256]{1,0:T(8,128)}) custom-call(s32[17]{0:T(128)} %pad_add_fusion.table, bf16[1024,256]{1,0:T(8,128)(2,1)} %get-tuple-element.194.query_back, f32[2,1024,256]{2,1,0:T(8,128)} %get-tuple-element.195.own_back, ...), custom_call_target="tpu_custom_call" | custom-call | tf_op jit(solution)/shard_map/pallas_call | solution.py:773
  369.9 2.1 add.277
  384.6 2.3 shard_map.184
  393.0 3.1 joint_gradient.1
  398.7 4.0 collective-permute-done.74
  405.7 5.0 %collective-permute-start.79 = (bf16[256,896]{1,0:T(8,128)(2,1)}, bf16[256,896]{1,0:T(8,128)(2,1)}, u32[]{:S(2)}, u32[]{:S(2)}) collective-permute-start(bf16[256,896]{1,0:T(8,128)(2,1)} %get-tuple-element.214), channel_id=1, source_target_pairs={{15,15},{14,10},{0,0},{1,5},{3,11},{5,1},{7,7},{9,13},{11,3},{13,9... | collective-permute-start | bytes 1376264 | tf_op jit(solution)/shard_map/joint_gradient/ppermute | solution.py:191
  414.0 4.2 fusion.38
  418.1 1.9 fusion.18
  420.8 2.0 fusion.11
  424.3 4.2 all-to-all-start.2
  431.3 2.7 convert_add_fusion
  441.9 3.2 convolution_add_fusion.2
  448.3 3.7 collective-permute-done.82
  (352 shorter events, 175.6 us)
Async XLA Ops:
  4.6 27.9 %collective-permute-start = (bf16[256,896]{1,0:T(8,128)(2,1)}, bf16[256,896]{1,0:T(8,128)(2,1)}, u32[]{:S(2)}, u32[]{:S(2)}) collective-permute-start(bf16[256,896]{1,0:T(8,128)(2,1)} %get-tuple-element.122), channel_id=1, source_target_pairs={{15,15},{10,14},{0,0},{1,5},{3,11},{5,1},{7,7},{9,13},{11,3},{13,9... | collective-permute-start | bytes 1376264 | tf_op jit(solution)/shard_map/joint_weight/ppermute | solution.py:191
  9.8 22.0 %collective-permute-start.1 = (bf16[160,896]{1,0:T(8,128)(2,1)}, bf16[160,896]{1,0:T(8,128)(2,1)S(1)}, u32[]{:S(2)}, u32[]{:S(2)}) collective-permute-start(bf16[160,896]{1,0:T(8,128)(2,1)} %get-tuple-element.123), channel_id=1, source_target_pairs={{4,14},{14,12},{8,10},{2,8},{12,6},{6,4},{0,2},{5,15},{10,0},{11,1... | collective-permute-start | bytes 860168 | tf_op jit(solution)/shard_map/joint_weight/ppermute | solution.py:191
  11.2 20.6 %collective-permute-start.2 = (bf16[64,896]{1,0:T(8,128)(2,1)}, bf16[64,896]{1,0:T(8,128)(2,1)S(1)}, u32[]{:S(2)}, u32[]{:S(2)}) collective-permute-start(bf16[64,896]{1,0:T(8,128)(2,1)} %get-tuple-element.124), channel_id=1, source_target_pairs={{9,15},{3,13},{13,11},{7,9},{1,7},{11,5},{5,3},{25,31},{19,29},{29... | collective-permute-start | bytes 344072 | tf_op jit(solution)/shard_map/joint_weight/ppermute | solution.py:191
  13.2 18.5 %all-to-all-start = ((bf16[32,4,100]{2,1,0:T(4,128)(2,1)}), bf16[32,4,100]{2,1,0:T(4,128)(2,1)S(1)}, u32[]{:S(2)}, u32[]{:S(2)}) async-start(bf16[32,4,100]{2,1,0:T(4,128)(2,1)} %broadcast_in_dim.53), calls=%async_computation | async-start | bytes 65536 | tf_op jit(solution)/shard_map/parameters/all_to_all | solution.py:956
  24.5 16.9 %collective-permute-start.7 = (bf16[192,1600]{1,0:T(8,128)(2,1)S(1)}, bf16[192,1600]{1,0:T(8,128)(2,1)S(1)}, u32[]{:S(2)}, u32[]{:S(2)}) collective-permute-start(bf16[192,1600]{1,0:T(8,128)(2,1)S(1)} %pad_maximum_fusion.1.refs_0_), channel_id=1, source_target_pairs={{0,2},{1,3},{4,0},{5,1},{8,4},{9,5},{12,8},{13,9},{14,12},{15,13},... | collective-permute-start | bytes 1843208 | tf_op jit(solution)/shard_map/input_ring/ppermute | solution.py:40
  26.4 16.3 %collective-permute-start.8 = (bf16[192,1600]{1,0:T(8,128)(2,1)S(1)}, bf16[192,1600]{1,0:T(8,128)(2,1)}, u32[]{:S(2)}, u32[]{:S(2)}) collective-permute-start(bf16[192,1600]{1,0:T(8,128)(2,1)S(1)} %pad_maximum_fusion.1.refs_0_), channel_id=1, source_target_pairs={{0,4},{1,5},{4,8},{5,9},{8,12},{9,13},{12,14},{13,15},{14,10},{15,... | collective-permute-start | bytes 1843208 | tf_op jit(solution)/shard_map/input_ring/ppermute | solution.py:40
  33.6 20.7 %collective-permute-start.3 = (bf16[480,896]{1,0:T(8,128)(2,1)S(1)}, bf16[480,896]{1,0:T(8,128)(2,1)}, u32[]{:S(2)}, u32[]{:S(2)}) collective-permute-start(bf16[480,896]{1,0:T(8,128)(2,1)S(1)} %pad_maximum_fusion.own), channel_id=1, source_target_pairs={{0,16},{16,0},{1,17},{17,1},{2,18},{18,2},{3,19},{19,3},{4,20},{20... | collective-permute-start | bytes 2580488 | tf_op jit(solution)/shard_map/joint_weight/ppermute | solution.py:48
  42.7 16.1 %collective-permute-start.10 = (bf16[192,1600]{1,0:T(8,128)(2,1)}, bf16[192,1600]{1,0:T(8,128)(2,1)}, u32[]{:S(2)}, u32[]{:S(2)}) collective-permute-start(bf16[192,1600]{1,0:T(8,128)(2,1)} %collective-permute-done.8.refs_7_), channel_id=1, source_target_pairs={{0,4},{1,5},{4,8},{5,9},{8,12},{9,13},{12,14},{13,15},{14,10},{15,... | collective-permute-start | bytes 1843208 | tf_op jit(solution)/shard_map/input_ring/ppermute | solution.py:40
  43.8 16.2 %collective-permute-start.9 = (bf16[192,1600]{1,0:T(8,128)(2,1)S(1)}, bf16[192,1600]{1,0:T(8,128)(2,1)}, u32[]{:S(2)}, u32[]{:S(2)}) collective-permute-start(bf16[192,1600]{1,0:T(8,128)(2,1)S(1)} %collective-permute-done.7.refs_1_), channel_id=1, source_target_pairs={{0,2},{1,3},{4,0},{5,1},{8,4},{9,5},{12,8},{13,9},{14,12},{15,13},... | collective-permute-start | bytes 1843208 | tf_op jit(solution)/shard_map/input_ring/ppermute | solution.py:40
  54.4 14.1 %collective-permute-start.4 = (bf16[480,896]{1,0:T(8,128)(2,1)S(1)}, bf16[480,896]{1,0:T(8,128)(2,1)}, u32[]{:S(2)}, u32[]{:S(2)}) collective-permute-start(bf16[480,896]{1,0:T(8,128)(2,1)S(1)} %pad_maximum_fusion.own), channel_id=1, source_target_pairs={{0,1},{1,0},{2,3},{3,2},{4,5},{5,4},{6,7},{7,6},{8,9},{9,8},{10,11... | collective-permute-start | bytes 2580488 | tf_op jit(solution)/shard_map/joint_weight/ppermute | solution.py:44
  54.4 14.1 %collective-permute-start.5 = (bf16[480,896]{1,0:T(8,128)(2,1)}, bf16[480,896]{1,0:T(8,128)(2,1)}, u32[]{:S(2)}, u32[]{:S(2)}) collective-permute-start(bf16[480,896]{1,0:T(8,128)(2,1)} %collective-permute-done.3.got), channel_id=1, source_target_pairs={{0,1},{1,0},{2,3},{3,2},{4,5},{5,4},{6,7},{7,6},{8,9},{9,8},{10,11... | collective-permute-start | bytes 2580488 | tf_op jit(solution)/shard_map/joint_weight/ppermute | solution.py:44
  59.9 15.8 %collective-permute-start.11 = (bf16[192,1600]{1,0:T(8,128)(2,1)}, bf16[192,1600]{1,0:T(8,128)(2,1)S(1)}, u32[]{:S(2)}, u32[]{:S(2)}) collective-permute-start(bf16[192,1600]{1,0:T(8,128)(2,1)} %collective-permute-done.9.refs_2_), channel_id=1, source_target_pairs={{0,2},{1,3},{4,0},{5,1},{8,4},{9,5},{12,8},{13,9},{14,12},{15,13},... | collective-permute-start | bytes 1843208 | tf_op jit(solution)/shard_map/input_ring/ppermute | solution.py:40
  61.4 16.2 %collective-permute-start.12 = (bf16[192,1600]{1,0:T(8,128)(2,1)}, bf16[192,1600]{1,0:T(8,128)(2,1)}, u32[]{:S(2)}, u32[]{:S(2)}) collective-permute-start(bf16[192,1600]{1,0:T(8,128)(2,1)} %collective-permute-done.10.refs_6_), channel_id=1, source_target_pairs={{0,4},{1,5},{4,8},{5,9},{8,12},{9,13},{12,14},{13,15},{14,10},{15,... | collective-permute-start | bytes 1843208 | tf_op jit(solution)/shard_map/input_ring/ppermute | solution.py:40
  66.2 17.3 %collective-permute-start.6 = (bf16[400,800]{1,0:T(8,128)(2,1)}, bf16[400,800]{1,0:T(8,128)(2,1)}, u32[]{:S(2)}, u32[]{:S(2)}) collective-permute-start(bf16[400,800]{1,0:T(8,128)(2,1)} %bitcast.158), channel_id=1, source_target_pairs={{0,16},{16,0},{1,17},{17,1},{2,18},{18,2},{3,19},{19,3},{4,20},{20... | collective-permute-start | bytes 1920008 | tf_op jit(solution)/shard_map/feed_forward_weights/ppermute | solution.py:48
  86.9 14.4 %collective-permute-start.17 = (bf16[128,1600]{1,0:T(8,128)(2,1)S(1)}, bf16[128,1600]{1,0:T(8,128)(2,1)}, u32[]{:S(2)}, u32[]{:S(2)}) collective-permute-start(bf16[128,1600]{1,0:T(8,128)(2,1)S(1)} %bitcast.153), channel_id=1, source_target_pairs={{0,4},{1,5},{4,8},{5,9},{8,12},{9,13},{12,14},{13,15},{14,10},{15,... | collective-permute-start | bytes 1228808 | tf_op jit(solution)/shard_map/cotangent_ring/ppermute | solution.py:40
  101.3 19.7 %collective-permute-start.16 = (bf16[8,64,1600]{2,1,0:T(8,128)(2,1)}, bf16[8,64,1600]{2,1,0:T(8,128)(2,1)S(1)}, u32[]{:S(2)}, u32[]{:S(2)}) collective-permute-start(bf16[8,64,1600]{2,1,0:T(8,128)(2,1)} %get-tuple-element.137.own), channel_id=1, source_target_pairs={{0,1},{1,0},{2,3},{3,2},{4,5},{5,4},{6,7},{7,6},{8,9},{9,8},{10,11... | collective-permute-start | bytes 4915208 | tf_op jit(solution)/shard_map/feed_forward_weights/ppermute | solution.py:44
  101.8 19.2 %collective-permute-start.24 = (bf16[400,800]{1,0:T(8,128)(2,1)}, bf16[400,800]{1,0:T(8,128)(2,1)}, u32[]{:S(2)}, u32[]{:S(2)}) collective-permute-start(bf16[400,800]{1,0:T(8,128)(2,1)} %param.17), channel_id=1, source_target_pairs={{0,16},{16,0},{1,17},{17,1},{2,18},{18,2},{3,19},{19,3},{4,20},{20... | collective-permute-start | bytes 1920008 | tf_op jit(solution)/shard_map/feed_forward_weights/ppermute | solution.py:48
  103.3 53.4 %collective-permute-start.15 = (bf16[8,64,1600]{2,1,0:T(8,128)(2,1)}, bf16[8,64,1600]{2,1,0:T(8,128)(2,1)}, u32[]{:S(2)}, u32[]{:S(2)}) collective-permute-start(bf16[8,64,1600]{2,1,0:T(8,128)(2,1)} %get-tuple-element.137.own), channel_id=1, source_target_pairs={{0,16},{16,0},{1,17},{17,1},{2,18},{18,2},{3,19},{19,3},{4,20},{20... | collective-permute-start | bytes 4915208 | tf_op jit(solution)/shard_map/output_weight/ppermute | solution.py:48
  103.8 14.9 %collective-permute-start.20 = (bf16[128,1600]{1,0:T(8,128)(2,1)}, bf16[128,1600]{1,0:T(8,128)(2,1)}, u32[]{:S(2)}, u32[]{:S(2)}) collective-permute-start(bf16[128,1600]{1,0:T(8,128)(2,1)} %collective-permute-done.17.refs_15_), channel_id=1, source_target_pairs={{0,4},{1,5},{4,8},{5,9},{8,12},{9,13},{12,14},{13,15},{14,10},{15,... | collective-permute-start | bytes 1228808 | tf_op jit(solution)/shard_map/cotangent_ring/ppermute | solution.py:40
  121.0 20.8 %collective-permute-start.22 = (bf16[1024,256]{1,0:T(8,128)(2,1)}, bf16[1024,256]{1,0:T(8,128)(2,1)S(1)}, u32[]{:S(2)}, u32[]{:S(2)}) collective-permute-start(bf16[1024,256]{1,0:T(8,128)(2,1)} %get-tuple-element.147.refs_0_.mixed), channel_id=1, source_target_pairs={{0,4},{1,5},{4,8},{5,9},{8,12},{9,13},{12,14},{13,15},{14,10},{15,... | collective-permute-start | bytes 1572872 | tf_op jit(solution)/shard_map/attended_ring/ppermute | solution.py:40
  121.9 20.0 %collective-permute-start.23 = (bf16[1024,256]{1,0:T(8,128)(2,1)}, bf16[1024,256]{1,0:T(8,128)(2,1)S(1)}, u32[]{:S(2)}, u32[]{:S(2)}) collective-permute-start(bf16[1024,256]{1,0:T(8,128)(2,1)} %get-tuple-element.147.refs_0_.mixed), channel_id=1, source_target_pairs={{0,2},{1,3},{4,0},{5,1},{8,4},{9,5},{12,8},{13,9},{14,12},{15,13},... | collective-permute-start | bytes 1572872 | tf_op jit(solution)/shard_map/attended_ring/ppermute | solution.py:40
  141.9 14.8 %collective-permute-start.27 = (bf16[1024,256]{1,0:T(8,128)(2,1)S(1)}, bf16[1024,256]{1,0:T(8,128)(2,1)}, u32[]{:S(2)}, u32[]{:S(2)}) collective-permute-start(bf16[1024,256]{1,0:T(8,128)(2,1)S(1)} %collective-permute-done.22.refs_7_), channel_id=1, source_target_pairs={{0,4},{1,5},{4,8},{5,9},{8,12},{9,13},{12,14},{13,15},{14,10},{15,... | collective-permute-start | bytes 1572872 | tf_op jit(solution)/shard_map/attended_ring/ppermute | solution.py:40
  156.7 23.8 %collective-permute-start.31 = (bf16[400,1600]{1,0:T(8,128)(2,1)S(1)}, bf16[400,1600]{1,0:T(8,128)(2,1)}, u32[]{:S(2)}, u32[]{:S(2)}) collective-permute-start(bf16[400,1600]{1,0:T(8,128)(2,1)S(1)} %maximum_select_fusion.1.down_own), channel_id=1, source_target_pairs={{0,1},{1,0},{2,3},{3,2},{4,5},{5,4},{6,7},{7,6},{8,9},{9,8},{10,11... | collective-permute-start | bytes 3840008 | tf_op jit(solution)/shard_map/attended_ring/ppermute | solution.py:44
  157.2 23.3 %collective-permute-start.30 = (bf16[400,1600]{1,0:T(8,128)(2,1)S(1)}, bf16[400,1600]{1,0:T(8,128)(2,1)}, u32[]{:S(2)}, u32[]{:S(2)}) collective-permute-start(bf16[400,1600]{1,0:T(8,128)(2,1)S(1)} %maximum_select_fusion.up_own), channel_id=1, source_target_pairs={{0,1},{1,0},{2,3},{3,2},{4,5},{5,4},{6,7},{7,6},{8,9},{9,8},{10,11... | collective-permute-start | bytes 3840008 | tf_op jit(solution)/shard_map/attended_ring/ppermute | solution.py:44
  167.9 15.7 %collective-permute-start.32 = (f32[1,400]{1,0:T(1,128)S(1)}, f32[1,400]{1,0:T(1,128)S(1)}, u32[]{:S(2)}, u32[]{:S(2)}) collective-permute-start(f32[1,400]{1,0:T(1,128)S(1)} %bitcast.164), channel_id=1, source_target_pairs={{0,1},{1,0},{2,3},{3,2},{4,5},{5,4},{6,7},{7,6},{8,9},{9,8},{10,11... | collective-permute-start | bytes 4808 | tf_op jit(solution)/shard_map/feed_forward_weights/ppermute | solution.py:44
  240.2 14.1 %collective-permute-start.44 = (bf16[64,1600]{1,0:T(8,128)(2,1)S(1)}, bf16[64,1600]{1,0:T(8,128)(2,1)S(1)}, u32[]{:S(2)}, u32[]{:S(2)}) collective-permute-start(bf16[64,1600]{1,0:T(8,128)(2,1)S(1)} %get-tuple-element.168), channel_id=1, source_target_pairs={{0,4},{1,5},{4,8},{5,9},{8,12},{9,13},{12,14},{13,15},{14,10},{15,... | collective-permute-start | bytes 614408 | tf_op jit(solution)/shard_map/normed_two_back_ring/ppermute | solution.py:40
  246.8 62.0 %collective-permute-start.56 = (f32[400,1600]{1,0:T(8,128)}, f32[400,1600]{1,0:T(8,128)}, u32[]{:S(2)}, u32[]{:S(2)}) collective-permute-start(f32[400,1600]{1,0:T(8,128)} %fusion.54), channel_id=1, source_target_pairs={{0,1},{1,0},{2,3},{3,2},{4,5},{5,4},{6,7},{7,6},{8,9},{9,8},{10,11... | collective-permute-start | bytes 7680008 | tf_op jit(solution)/shard_map/down_gradient/ppermute | solution.py:44
  250.0 51.2 %collective-permute-start.55 = (f32[400,1600]{1,0:T(8,128)}, f32[400,1600]{1,0:T(8,128)}, u32[]{:S(2)}, u32[]{:S(2)}) collective-permute-start(f32[400,1600]{1,0:T(8,128)} %fusion.53), channel_id=1, source_target_pairs={{0,1},{1,0},{2,3},{3,2},{4,5},{5,4},{6,7},{7,6},{8,9},{9,8},{10,11... | collective-permute-start | bytes 7680008 | tf_op jit(solution)/shard_map/up_gradient/ppermute | solution.py:44
  274.4 15.6 %collective-permute-start.53 = (bf16[64,1600]{1,0:T(8,128)(2,1)S(1)}, bf16[64,1600]{1,0:T(8,128)(2,1)}, u32[]{:S(2)}, u32[]{:S(2)}) collective-permute-start(bf16[64,1600]{1,0:T(8,128)(2,1)S(1)} %get-tuple-element.185), channel_id=1, source_target_pairs={{0,4},{1,5},{4,8},{5,9},{8,12},{9,13},{12,14},{13,15},{14,10},{15,... | collective-permute-start | bytes 614408 | tf_op jit(solution)/shard_map/down_ring/ppermute | solution.py:40
  290.0 27.6 %all-to-all-start.1 = ((bf16[8,128,512]{2,1,0:T(8,128)(2,1)}), bf16[8,128,512]{2,1,0:T(8,128)(2,1)}, u32[]{:S(2)}, u32[]{:S(2)}) async-start(bf16[8,128,512]{2,1,0:T(8,128)(2,1)} %get-tuple-element.187), calls=%async_computation.1 | async-start | bytes 2097152 | tf_op jit(solution)/shard_map/back_exchange/all_to_all | solution.py:129
  307.3 31.6 %collective-permute-start.59 = (bf16[400,800]{1,0:T(8,128)(2,1)}, bf16[400,800]{1,0:T(8,128)(2,1)}, u32[]{:S(2)}, u32[]{:S(2)}) collective-permute-start(bf16[400,800]{1,0:T(8,128)(2,1)} %select_convert_fusion.2), channel_id=1, source_target_pairs={{0,16},{16,0},{1,17},{17,1},{2,18},{18,2},{3,19},{19,3},{4,20},{20... | collective-permute-start | bytes 1920008 | tf_op jit(solution)/shard_map/up_gradient/ppermute | solution.py:48
  319.5 19.4 %collective-permute-start.60 = (bf16[128,1600]{1,0:T(8,128)(2,1)}, bf16[128,1600]{1,0:T(8,128)(2,1)S(1)}, u32[]{:S(2)}, u32[]{:S(2)}) collective-permute-start(bf16[128,1600]{1,0:T(8,128)(2,1)} %pad_maximum_fusion.5), channel_id=1, source_target_pairs={{0,4},{1,5},{4,8},{5,9},{8,12},{9,13},{12,14},{13,15},{14,10},{15,... | collective-permute-start | bytes 1228808 | tf_op jit(solution)/shard_map/down_ring/ppermute | solution.py:40
  321.4 17.5 %collective-permute-start.61 = (bf16[128,1600]{1,0:T(8,128)(2,1)}, bf16[128,1600]{1,0:T(8,128)(2,1)S(1)}, u32[]{:S(2)}, u32[]{:S(2)}) collective-permute-start(bf16[128,1600]{1,0:T(8,128)(2,1)} %pad_maximum_fusion.6), channel_id=1, source_target_pairs={{0,2},{1,3},{4,0},{5,1},{8,4},{9,5},{12,8},{13,9},{14,12},{15,13},... | collective-permute-start | bytes 1228808 | tf_op jit(solution)/shard_map/down_ring/ppermute | solution.py:40
  323.8 24.3 %collective-permute-start.63 = (bf16[400,800]{1,0:T(8,128)(2,1)}, bf16[400,800]{1,0:T(8,128)(2,1)}, u32[]{:S(2)}, u32[]{:S(2)}) collective-permute-start(bf16[400,800]{1,0:T(8,128)(2,1)} %select_convert_fusion.1), channel_id=1, source_target_pairs={{0,16},{16,0},{1,17},{17,1},{2,18},{18,2},{3,19},{19,3},{4,20},{20... | collective-permute-start | bytes 1920008 | tf_op jit(solution)/shard_map/down_gradient/ppermute | solution.py:48
  340.9 23.7 %collective-permute-start.64 = (bf16[128,1600]{1,0:T(8,128)(2,1)}, bf16[128,1600]{1,0:T(8,128)(2,1)S(1)}, u32[]{:S(2)}, u32[]{:S(2)}) collective-permute-start(bf16[128,1600]{1,0:T(8,128)(2,1)} %fusion.16), channel_id=1, source_target_pairs={{0,4},{1,5},{4,8},{5,9},{8,12},{9,13},{12,14},{13,15},{14,10},{15,... | collective-permute-start | bytes 1228808 | tf_op jit(solution)/shard_map/down_ring/ppermute | solution.py:40
  342.8 21.7 %collective-permute-start.65 = (bf16[128,1600]{1,0:T(8,128)(2,1)}, bf16[128,1600]{1,0:T(8,128)(2,1)S(1)}, u32[]{:S(2)}, u32[]{:S(2)}) collective-permute-start(bf16[128,1600]{1,0:T(8,128)(2,1)} %fusion.15), channel_id=1, source_target_pairs={{0,2},{1,3},{4,0},{5,1},{8,4},{9,5},{12,8},{13,9},{14,12},{15,13},... | collective-permute-start | bytes 1228808 | tf_op jit(solution)/shard_map/down_ring/ppermute | solution.py:40
  373.2 18.9 %collective-permute-start.70 = (bf16[416,800]{1,0:T(8,128)(2,1)}, bf16[416,800]{1,0:T(8,128)(2,1)S(1)}, u32[]{:S(2)}, u32[]{:S(2)}) collective-permute-start(bf16[416,800]{1,0:T(8,128)(2,1)} %select_convert_fusion), channel_id=1, source_target_pairs={{0,16},{16,0},{1,17},{17,1},{2,18},{18,2},{3,19},{19,3},{4,20},{20... | collective-permute-start | bytes 1996808 | tf_op jit(solution)/shard_map/joint_gradient/ppermute | solution.py:48
  376.2 20.9 %collective-permute-start.68 = (bf16[128,1600]{1,0:T(8,128)(2,1)}, bf16[128,1600]{1,0:T(8,128)(2,1)}, u32[]{:S(2)}, u32[]{:S(2)}) collective-permute-start(bf16[128,1600]{1,0:T(8,128)(2,1)} %pad_maximum_fusion.7), channel_id=1, source_target_pairs={{0,4},{1,5},{4,8},{5,9},{8,12},{9,13},{12,14},{13,15},{14,10},{15,... | collective-permute-start | bytes 1228808 | tf_op jit(solution)/shard_map/last_ring/ppermute | solution.py:40
  380.1 16.9 %collective-permute-start.71 = (bf16[128,1600]{1,0:T(8,128)(2,1)}, bf16[128,1600]{1,0:T(8,128)(2,1)}, u32[]{:S(2)}, u32[]{:S(2)}) collective-permute-start(bf16[128,1600]{1,0:T(8,128)(2,1)} %fusion.14), channel_id=1, source_target_pairs={{0,4},{1,5},{4,8},{5,9},{8,12},{9,13},{12,14},{13,15},{14,10},{15,... | collective-permute-start | bytes 1228808 | tf_op jit(solution)/shard_map/down_ring/ppermute | solution.py:40
  386.9 15.8 %collective-permute-start.74 = (bf16[128,1600]{1,0:T(8,128)(2,1)}, bf16[128,1600]{1,0:T(8,128)(2,1)}, u32[]{:S(2)}, u32[]{:S(2)}) collective-permute-start(bf16[128,1600]{1,0:T(8,128)(2,1)} %pad_maximum_fusion.8), channel_id=1, source_target_pairs={{0,2},{1,3},{4,0},{5,1},{8,4},{9,5},{12,8},{13,9},{14,12},{15,13},... | collective-permute-start | bytes 1228808 | tf_op jit(solution)/shard_map/last_ring/ppermute | solution.py:40
  398.3 19.8 %collective-permute-start.73 = (bf16[128,1600]{1,0:T(8,128)(2,1)S(1)}, bf16[128,1600]{1,0:T(8,128)(2,1)S(1)}, u32[]{:S(2)}, u32[]{:S(2)}) collective-permute-start(bf16[128,1600]{1,0:T(8,128)(2,1)S(1)} %fusion.17), channel_id=1, source_target_pairs={{0,4},{1,5},{4,8},{5,9},{8,12},{9,13},{12,14},{13,15},{14,10},{15,... | collective-permute-start | bytes 1228808 | tf_op jit(solution)/shard_map/last_ring/ppermute | solution.py:40
  404.0 16.8 %collective-permute-start.75 = (bf16[128,1600]{1,0:T(8,128)(2,1)S(1)}, bf16[128,1600]{1,0:T(8,128)(2,1)S(1)}, u32[]{:S(2)}, u32[]{:S(2)}) collective-permute-start(bf16[128,1600]{1,0:T(8,128)(2,1)S(1)} %fusion.12), channel_id=1, source_target_pairs={{0,2},{1,3},{4,0},{5,1},{8,4},{9,5},{12,8},{13,9},{14,12},{15,13},... | collective-permute-start | bytes 1228808 | tf_op jit(solution)/shard_map/last_ring/ppermute | solution.py:40
  405.7 28.2 %collective-permute-start.79 = (bf16[256,896]{1,0:T(8,128)(2,1)}, bf16[256,896]{1,0:T(8,128)(2,1)}, u32[]{:S(2)}, u32[]{:S(2)}) collective-permute-start(bf16[256,896]{1,0:T(8,128)(2,1)} %get-tuple-element.214), channel_id=1, source_target_pairs={{15,15},{14,10},{0,0},{1,5},{3,11},{5,1},{7,7},{9,13},{11,3},{13,9... | collective-permute-start | bytes 1376264 | tf_op jit(solution)/shard_map/joint_gradient/ppermute | solution.py:191
  410.8 26.2 %collective-permute-start.80 = (bf16[160,896]{1,0:T(8,128)(2,1)}, bf16[160,896]{1,0:T(8,128)(2,1)}, u32[]{:S(2)}, u32[]{:S(2)}) collective-permute-start(bf16[160,896]{1,0:T(8,128)(2,1)} %get-tuple-element.215), channel_id=1, source_target_pairs={{14,4},{12,14},{10,8},{8,2},{6,12},{4,6},{2,0},{0,10},{15,5},{1,11... | collective-permute-start | bytes 860168 | tf_op jit(solution)/shard_map/joint_gradient/ppermute | solution.py:191
  410.8 27.2 %collective-permute-start.81 = (bf16[64,896]{1,0:T(8,128)(2,1)}, bf16[64,896]{1,0:T(8,128)(2,1)}, u32[]{:S(2)}, u32[]{:S(2)}) collective-permute-start(bf16[64,896]{1,0:T(8,128)(2,1)} %get-tuple-element.216), channel_id=1, source_target_pairs={{15,9},{13,3},{11,13},{9,7},{7,1},{5,11},{3,5},{31,25},{29,19},{27... | collective-permute-start | bytes 344072 | tf_op jit(solution)/shard_map/joint_gradient/ppermute | solution.py:191
  418.1 23.8 %collective-permute-start.78 = (f32[100,2048]{1,0:T(8,128)}, f32[100,2048]{1,0:T(8,128)}, u32[]{:S(2)}, u32[]{:S(2)}) collective-permute-start(f32[100,2048]{1,0:T(8,128)} %fusion.38), channel_id=1, source_target_pairs={{0,1},{1,0},{2,3},{3,2},{4,5},{5,4},{6,7},{7,6},{8,9},{9,8},{10,11... | collective-permute-start | bytes 2457608 | tf_op jit(solution)/shard_map/output_gradient/ppermute | solution.py:44
  422.7 24.3 %collective-permute-start.77 = (bf16[128,1600]{1,0:T(8,128)(2,1)}, bf16[128,1600]{1,0:T(8,128)(2,1)}, u32[]{:S(2)}, u32[]{:S(2)}) collective-permute-start(bf16[128,1600]{1,0:T(8,128)(2,1)} %fusion.11), channel_id=1, source_target_pairs={{0,2},{1,3},{4,0},{5,1},{8,4},{9,5},{12,8},{13,9},{14,12},{15,13},... | collective-permute-start | bytes 1228808 | tf_op jit(solution)/shard_map/last_ring/ppermute | solution.py:40
  424.3 16.1 %all-to-all-start.2 = ((f32[32,4,128]{2,1,0:T(4,128)}), f32[32,4,128]{2,1,0:T(4,128)}, u32[]{:S(2)}, u32[]{:S(2)}) async-start(f32[32,4,128]{2,1,0:T(4,128)} %shard_map.184), calls=%async_computation.2 | async-start | bytes 131072 | tf_op jit(solution)/shard_map/vectors_gradient/all_to_all | solution.py:1241
  (84 other events, 1091.7 us)

commit v7 on v6

--- a/solution.py
+++ b/solution.py
@@ -359,13 +359,19 @@
         out[chip, :, :width] = back[:, chip * width : (chip + 1) * width]
         piece = total[:, chip * both : (chip + 1) * both].astype(bf16).astype(f32)
         piece = jnp.where(odd, jnp.concatenate([piece[:, half:], piece[:, :half]], axis=1), piece)
-        out[chip, :, width : width + both] = piece.astype(out.dtype)
-        out[chip, :, width + both :] = jnp.zeros((rows, out.shape[2] - width - both), out.dtype)
+        step = -(-half // LANES) * LANES
+        for side in range(2):
+            first = width + side * step
+            low_half = piece[:, side * half : (side + 1) * half].astype(out.dtype)
+            out[chip, :, first : first + half] = low_half
+            if half < step:
+                rest = jnp.zeros((rows, step - half), out.dtype)
+                out[chip, :, first + half : first + step] = rest
 
 
 def between(odd_core, terms, residual, cotangent, weight, vectors, chips):
     rows, features = residual.shape
-    columns = (weight.shape[1] + features) // chips
+    columns = weight.shape[1] // chips + 2 * (-(-features // (2 * chips) // LANES) * LANES)
     return pl.pallas_call(
         functools.partial(between_kernel, chips),
         out_shape=[
@@ -989,7 +995,7 @@
             else:
                 arrived = next(input_ring)
         input_blocks = next(input_ring)
-        joint_heads = after(joint_heads, (up_got, bias))
+        joint_heads = after(joint_heads, (up_got, bias, rows_here[3:]))
     with jax.named_scope("cotangent_ring"):
         cotangent_ring = ring_gather(cotangent[0])
         next(cotangent_ring)
@@ -1215,7 +1221,8 @@
                 axis=1,
             )
 
-        output_other = rows_by_rows(low[:, output_cols : 2 * output_cols], attended_wide)
+        step = -(-output_cols // LANES) * LANES
+        output_other = rows_by_rows(low[:, step : step + output_cols], attended_wide)
     with jax.named_scope("last_ring"):
         for step in range(3, chips // 2):
             if step == 3:
@@ -1238,7 +1245,8 @@
         output_gradient = (output_kept + output_arrived.astype(f32)).T
     with jax.named_scope("vectors_gradient"):
         vectors_gradient = jnp.sum(
-            lax.all_to_all(after(vectors_cut, sent), ("dp", "ctx"), 0, 0, tiled=True), axis=0
+            lax.all_to_all(after(vectors_cut, (sent, output_given)), ("dp", "ctx"), 0, 0, tiled=True),
+            axis=0,
         )[:, : vectors.shape[1]]
     with jax.named_scope("last_ring"):
         normed_one_back = after(next(ring), (down_gradient, output_arrived, routed))

time: 464 us -> 462 us (level)
    ppermute x9, waiting for transfers between devices: 32 us -> 26.8 us  [data_swap(): lax.ppermute(value, 'dp', [(i, i ^ 1) for i in range(lax.axis_size('dp'))])]
    unnamed x98 -> x104, local copies, waits for them, and re-layouts: 9.55 us -> 9.53 us
where the time goes in v7:
time: 462 us; the launch traced here: 454 us
  Pallas kernels  122 us (26%)
  waiting for transfers between devices  106 us (23%)
  starting transfers between devices  104 us (23%)
  other arithmetic  66.7 us (14%)
  local copies, waits for them, and re-layouts  29.9 us (6%)
  matrix products  22.5 us (5%)
    ppermute x54, waiting for transfers between devices, send(): return lax.ppermute(value, 'ctx', pairs)  62.9 us
    ppermute x54, starting transfers between devices, send(): return lax.ppermute(value, 'ctx', pairs)  58.2 us
    pallas_call x1, Pallas kernels, feed_forward(): pl.pallas_call(functools.partial(feed_forward_kernel, chips), grid_spec=p...  39.5 us
    ppermute x9, waiting for transfers between devices, data_swap(): lax.ppermute(value, 'dp', [(i, i ^ 1) for i in range(lax.axis_size('dp'))])  26.8 us
    convert_element_type x18, other arithmetic, ring_scatter(): piece = piece.astype(bf16)  23.9 us
    dot_general x7, matrix products, rows_by_rows(): lax.dot_general(left_side, right_side, (((0,), (0,)), ((), ())), preferre...  22.5 us
    pallas_call x1, Pallas kernels, back_through(): pl.pallas_call(functools.partial(back_through_kernel, chips), grid_spec=p...  16.5 us
    pallas_call x1, Pallas kernels, attend_backward(): pl.pallas_call(functools.partial(backward_kernel, scale), grid_spec=pltpu...  13.6 us
  transfers between devices with their start and end apart: 86, of which 42 were waited for; matrix products, arithmetic and copies ran while one was open for 24% of the time, Pallas kernels for 18%

profile of v7, /device:TPU:0, one launch (start us, length us, event | category | flops | bytes accessed | tf_op | source)
XLA Modules:
  0.0 454.3 jit_solution(14260880918462700767)
XLA Ops:
  2.0 2.6 joint_weight.2
  4.6 5.1 %collective-permute-start = (bf16[256,896]{1,0:T(8,128)(2,1)}, bf16[256,896]{1,0:T(8,128)(2,1)}, u32[]{:S(2)}, u32[]{:S(2)}) collective-permute-start(bf16[256,896]{1,0:T(8,128)(2,1)} %get-tuple-element.122), channel_id=1, source_target_pairs={{15,15},{10,14},{0,0},{1,5},{3,11},{5,1},{7,7},{9,13},{11,3},{13,9... | collective-permute-start | bytes 1376264 | tf_op jit(solution)/shard_map/joint_weight/ppermute | solution.py:191
  13.1 8.9 %all-to-all-start = ((bf16[32,4,100]{2,1,0:T(4,128)(2,1)}), bf16[32,4,100]{2,1,0:T(4,128)(2,1)S(1)}, u32[]{:S(2)}, u32[]{:S(2)}) async-start(bf16[32,4,100]{2,1,0:T(4,128)(2,1)} %broadcast_in_dim.53), calls=%async_computation | async-start | bytes 65536 | tf_op jit(solution)/shard_map/parameters/all_to_all | solution.py:962
  26.5 5.0 %all-to-all-done = bf16[32,4,100]{2,1,0:T(4,128)(2,1)S(1)} async-done(((bf16[32,4,100]{2,1,0:T(4,128)(2,1)}), bf16[32,4,100]{2,1,0:T(4,128)(2,1)S(1)}, u32[]{:S(2)}, u32[]{:S(2)}) %all-to-all-start) | async-done | bytes 25632 | tf_op jit(solution)/shard_map/parameters/all_to_all | solution.py:962
  34.1 7.3 %collective-permute-done.7.refs_1_ = bf16[192,1600]{1,0:T(8,128)(2,1)S(1)} collective-permute-done((bf16[192,1600]{1,0:T(8,128)(2,1)S(1)}, bf16[192,1600]{1,0:T(8,128)(2,1)S(1)}, u32[]{:S(2)}, u32[]{:S(2)}) %collective-permute-start.7) | collective-permute-done | bytes 614432 | tf_op jit(solution)/shard_map/input_ring/ppermute | solution.py:40
  46.4 7.8 %collective-permute-done.3.got = bf16[480,896]{1,0:T(8,128)(2,1)} collective-permute-done((bf16[480,896]{1,0:T(8,128)(2,1)S(1)}, bf16[480,896]{1,0:T(8,128)(2,1)}, u32[]{:S(2)}, u32[]{:S(2)}) %collective-permute-start.3) | collective-permute-done | bytes 860192 | tf_op jit(solution)/shard_map/joint_weight/ppermute | solution.py:48
  55.3 3.4 collective-permute-done.10.refs_6_
  68.4 7.0 %joint_weight.3.weight = bf16[768,1600]{1,0:T(8,128)(2,1)} custom-call(s32[1]{0:T(128)} %bitcast.1.flag, s32[1,768]{1,0:T(1,128)} %get-tuple-element.286.own_rows, s32[1,768]{1,0:T(1,128)} %get-tuple-element.285.mate_rows, bf16[480,896]{1,0:T(8,128)(2,1)} %copy-done.10, bf16[480,896]{1,0:T(8,128)(2,1)} %collective-permute-done.3.got, ...), custom_call_target="tpu_custom_call" | custom-call | tf_op jit(solution)/shard_map/joint_weight/pallas_call | solution.py:280
  75.5 2.0 collective-permute-done.12.refs_5_
  81.3 2.1 collective-permute-done.6
  83.4 3.2 collective-permute-done.13
  90.1 10.9 %projection.1 = (bf16[1024,1600]{1,0:T(8,128)(2,1)}, bf16[8,64,1600]{2,1,0:T(8,128)(2,1)}, bf16[1024,1600]{1,0:T(8,128)(2,1)}, bf16[1024,256]{1,0:T(8,128)(2,1)}, bf16[2,1024,256]{2,1,0:T(8,128)(2,1)}) custom-call(s32[17]{0:T(128)} %pad_add_fusion.table, bf16[768,1600]{1,0:T(8,128)(2,1)} %joint_weight.3.weight, f32[8,768]{1,0:T(8,128)} %pad.34.bias, ...), custom_call_target="tpu_custom_call" | custom-call | tf_op jit(solution)/shard_map/projection/pallas_call | solution.py:572
  104.3 2.0 collective-permute-done.19.near
  108.1 10.4 %shard_map.179 = (bf16[1024,256]{1,0:T(8,128)(2,1)}, f32[8,2,256,1]{3,2,1,0:T(8,128)}) custom-call(s32[1]{0:T(128)} %bitcast.odd_core, f32[8,128,384]{2,1,0:T(8,128)} %and_select_fusion.bias, bf16[1024,256]{1,0:T(8,128)(2,1)} %get-tuple-element.138.query, bf16[2,1024,256]{2,1,0:T(8,128)(2,1)} %get-tuple-element.142.far.own, bf16[2,1024,256]{2,1,0:T(8,128)(2,1)} %copy-done.8, ...), custom_call_target="tpu_custom_call" | custom-call | tf_op jit(solution)/shard_map/pallas_call | solution.py:486
  122.8 2.8 maximum_select_fusion.1.down_own
  125.6 2.7 maximum_select_fusion.up_own
  128.4 3.1 collective-permute-done.25.refs_13_
  132.2 9.3 %collective-permute-done.22.refs_7_ = bf16[1024,256]{1,0:T(8,128)(2,1)S(1)} collective-permute-done((bf16[1024,256]{1,0:T(8,128)(2,1)}, bf16[1024,256]{1,0:T(8,128)(2,1)S(1)}, u32[]{:S(2)}, u32[]{:S(2)}) %collective-permute-start.22) | collective-permute-done | bytes 524320 | tf_op jit(solution)/shard_map/attended_ring/ppermute | solution.py:40
  143.6 12.8 %collective-permute-done.15.got = bf16[8,64,1600]{2,1,0:T(8,128)(2,1)} collective-permute-done((bf16[8,64,1600]{2,1,0:T(8,128)(2,1)}, bf16[8,64,1600]{2,1,0:T(8,128)(2,1)}, u32[]{:S(2)}, u32[]{:S(2)}) %collective-permute-start.15) | collective-permute-done | bytes 1638432 | tf_op jit(solution)/shard_map/output_weight/ppermute | solution.py:48
  159.2 5.5 %collective-permute-done.33 = bf16[64,1600]{1,0:T(8,128)(2,1)S(1)} collective-permute-done((bf16[64,1600]{1,0:T(8,128)(2,1)S(1)}, bf16[64,1600]{1,0:T(8,128)(2,1)S(1)}, u32[]{:S(2)}, u32[]{:S(2)}) %collective-permute-start.33) | collective-permute-done | bytes 204832 | tf_op jit(solution)/shard_map/cotangent_ring/ppermute | solution.py:40
  168.2 9.8 %output_weight.1.output_full.weight = bf16[1600,2048]{1,0:T(8,128)(2,1)} custom-call(s32[2]{0:T(128)} %pad_add_fusion.1.flags, bf16[8,64,1600]{2,1,0:T(8,128)(2,1)} %get-tuple-element.137.own, bf16[8,64,1600]{2,1,0:T(8,128)(2,1)} %collective-permute-done.15.got, bf16[8,64,1600]{2,1,0:T(8,128)(2,1)} %copy-done.14, ...), custom_call_target="tpu_custom_call" | custom-call | tf_op jit(solution)/shard_map/output_weight/pallas_call | solution.py:321
  189.7 39.5 %shard_map.180 = (bf16[1024,1600]{1,0:T(8,128)(2,1)}, bf16[1024,400]{1,0:T(8,128)(2,1)}, bf16[1024,400]{1,0:T(8,128)(2,1)}, bf16[1024,400]{1,0:T(8,128)(2,1)}, b...) custom-call(s32[17]{0:T(128)} %pad_add_fusion.table, ...), custom_call_target="tpu_custom_call" | custom-call | tf_op jit(solution)/shard_map/pallas_call | solution.py:690
  233.1 3.8 collective-permute-done.39
  243.3 3.3 fusion.54
  246.6 3.3 fusion.53
  270.0 4.2 collective-permute-done.52.back_two
  279.5 2.8 collective-permute-done.46.ahead_one
  283.0 6.6 %shard_map.181 = (bf16[8,128,512]{2,1,0:T(8,128)(2,1)}, f32[128,1600]{1,0:T(8,128)}, f32[8,1600]{1,0:T(8,128)}) custom-call(s32[1]{0:T(128)} %bitcast.odd_core, bf16[128,1600]{1,0:T(8,128)(2,1)} %slice_bitcast_fusion.own, bf16[64,1600]{1,0:T(8,128)(2,1)} %copy-done.35, bf16[64,1600]{1,0:T(8,128)(2,1)} %copy-done.33, bf16[64,1600]{1,0:T(8,128)(2,1)} %copy-done.34, ...), custom_call_target="tpu_custom_call" | custom-call | tf_op jit(solution)/shard_map/pallas_call | solution.py:375
  289.6 5.3 %all-to-all-start.1 = ((bf16[8,128,512]{2,1,0:T(8,128)(2,1)}), bf16[8,128,512]{2,1,0:T(8,128)(2,1)}, u32[]{:S(2)}, u32[]{:S(2)}) async-start(bf16[8,128,512]{2,1,0:T(8,128)(2,1)} %get-tuple-element.187), calls=%async_computation.1 | async-start | bytes 2097152 | tf_op jit(solution)/shard_map/back_exchange/all_to_all | solution.py:129
  298.3 2.1 collective-permute-done.58
  301.1 4.9 %convolution_add_fusion.1 = f32[400,1600]{1,0:T(8,128)S(1)} fusion(f32[400,1600]{1,0:T(8,128)} %collective-permute-done.55, bf16[1024,400]{1,0:T(8,128)(2,1)} %get-tuple-element.189, bf16[1024,1600]{1,0:T(8,128)(2,1)} %get-tuple-element.176), kind=kOutput, calls=%fused_computation.1 | convolution fusion | flops 1311360000 | bytes 9216000 | tf_op jit(solution)/shard_map/up_gradient/dot_general | solution.py:217
  308.6 3.5 convolution_add_fusion
  314.9 2.6 all-to-all-done.1
  321.2 2.4 collective-permute-start.61
  325.2 13.6 %shard_map.182 = (bf16[1024,256]{1,0:T(8,128)(2,1)}, f32[2,1024,256]{2,1,0:T(8,128)}, bf16[2,1024,256]{2,1,0:T(8,128)(2,1)}, f32[8,256]{1,0:T(8,128)}) custom-call(s32[1]{0:T(128)} %bitcast.odd_core, f32[8,128,384]{2,1,0:T(8,128)} %and_select_fusion.bias, bf16[1024,256]{1,0:T(8,128)(2,1)} %get-tuple-element.138.query, ...), custom_call_target="tpu_custom_call" | custom-call | tf_op jit(solution)/shard_map/pallas_call | solution.py:509
  344.7 2.6 convert_add_fusion.1
  347.4 16.5 %shard_map.183 = (f32[416,1600]{1,0:T(8,128)}, f32[416,1600]{1,0:T(8,128)}, bf16[8,128,1600]{2,1,0:T(8,128)(2,1)}, f32[8,1600]{1,0:T(8,128)}, f32[8,256]{1,0:T(8,128)}) custom-call(s32[17]{0:T(128)} %pad_add_fusion.table, bf16[1024,256]{1,0:T(8,128)(2,1)} %get-tuple-element.194.query_back, f32[2,1024,256]{2,1,0:T(8,128)} %get-tuple-element.195.own_back, ...), custom_call_target="tpu_custom_call" | custom-call | tf_op jit(solution)/shard_map/pallas_call | solution.py:779
  369.3 2.1 add.277
  383.9 2.4 shard_map.184
  392.3 3.1 joint_gradient.1
  398.0 4.0 collective-permute-done.74
  405.0 5.1 %collective-permute-start.79 = (bf16[256,896]{1,0:T(8,128)(2,1)}, bf16[256,896]{1,0:T(8,128)(2,1)}, u32[]{:S(2)}, u32[]{:S(2)}) collective-permute-start(bf16[256,896]{1,0:T(8,128)(2,1)} %get-tuple-element.214), channel_id=1, source_target_pairs={{15,15},{14,10},{0,0},{1,5},{3,11},{5,1},{7,7},{9,13},{11,3},{13,9... | collective-permute-start | bytes 1376264 | tf_op jit(solution)/shard_map/joint_gradient/ppermute | solution.py:191
  413.2 4.1 fusion.38
  417.3 2.1 fusion.18
  426.0 2.8 convert_add_fusion
  433.9 2.0 convolution_add_fusion.2
  436.3 5.3 %all-to-all-start.2 = ((f32[32,4,128]{2,1,0:T(4,128)}), f32[32,4,128]{2,1,0:T(4,128)S(1)}, u32[]{:S(2)}, u32[]{:S(2)}) async-start(f32[32,4,128]{2,1,0:T(4,128)} %shard_map.184), calls=%async_computation.2 | async-start | bytes 131072 | tf_op jit(solution)/shard_map/vectors_gradient/all_to_all | solution.py:1248
  444.7 4.3 all-to-all-done.2
  (358 shorter events, 174.1 us)
Async XLA Ops:
  4.6 27.7 %collective-permute-start = (bf16[256,896]{1,0:T(8,128)(2,1)}, bf16[256,896]{1,0:T(8,128)(2,1)}, u32[]{:S(2)}, u32[]{:S(2)}) collective-permute-start(bf16[256,896]{1,0:T(8,128)(2,1)} %get-tuple-element.122), channel_id=1, source_target_pairs={{15,15},{10,14},{0,0},{1,5},{3,11},{5,1},{7,7},{9,13},{11,3},{13,9... | collective-permute-start | bytes 1376264 | tf_op jit(solution)/shard_map/joint_weight/ppermute | solution.py:191
  9.7 22.0 %collective-permute-start.1 = (bf16[160,896]{1,0:T(8,128)(2,1)}, bf16[160,896]{1,0:T(8,128)(2,1)S(1)}, u32[]{:S(2)}, u32[]{:S(2)}) collective-permute-start(bf16[160,896]{1,0:T(8,128)(2,1)} %get-tuple-element.123), channel_id=1, source_target_pairs={{4,14},{14,12},{8,10},{2,8},{12,6},{6,4},{0,2},{5,15},{10,0},{11,1... | collective-permute-start | bytes 860168 | tf_op jit(solution)/shard_map/joint_weight/ppermute | solution.py:191
  11.1 20.6 %collective-permute-start.2 = (bf16[64,896]{1,0:T(8,128)(2,1)}, bf16[64,896]{1,0:T(8,128)(2,1)S(1)}, u32[]{:S(2)}, u32[]{:S(2)}) collective-permute-start(bf16[64,896]{1,0:T(8,128)(2,1)} %get-tuple-element.124), channel_id=1, source_target_pairs={{9,15},{3,13},{13,11},{7,9},{1,7},{11,5},{5,3},{25,31},{19,29},{29... | collective-permute-start | bytes 344072 | tf_op jit(solution)/shard_map/joint_weight/ppermute | solution.py:191
  13.1 18.5 %all-to-all-start = ((bf16[32,4,100]{2,1,0:T(4,128)(2,1)}), bf16[32,4,100]{2,1,0:T(4,128)(2,1)S(1)}, u32[]{:S(2)}, u32[]{:S(2)}) async-start(bf16[32,4,100]{2,1,0:T(4,128)(2,1)} %broadcast_in_dim.53), calls=%async_computation | async-start | bytes 65536 | tf_op jit(solution)/shard_map/parameters/all_to_all | solution.py:962
  24.4 16.9 %collective-permute-start.7 = (bf16[192,1600]{1,0:T(8,128)(2,1)S(1)}, bf16[192,1600]{1,0:T(8,128)(2,1)S(1)}, u32[]{:S(2)}, u32[]{:S(2)}) collective-permute-start(bf16[192,1600]{1,0:T(8,128)(2,1)S(1)} %pad_maximum_fusion.1.refs_0_), channel_id=1, source_target_pairs={{0,2},{1,3},{4,0},{5,1},{8,4},{9,5},{12,8},{13,9},{14,12},{15,13},... | collective-permute-start | bytes 1843208 | tf_op jit(solution)/shard_map/input_ring/ppermute | solution.py:40
  26.3 16.3 %collective-permute-start.8 = (bf16[192,1600]{1,0:T(8,128)(2,1)S(1)}, bf16[192,1600]{1,0:T(8,128)(2,1)}, u32[]{:S(2)}, u32[]{:S(2)}) collective-permute-start(bf16[192,1600]{1,0:T(8,128)(2,1)S(1)} %pad_maximum_fusion.1.refs_0_), channel_id=1, source_target_pairs={{0,4},{1,5},{4,8},{5,9},{8,12},{9,13},{12,14},{13,15},{14,10},{15,... | collective-permute-start | bytes 1843208 | tf_op jit(solution)/shard_map/input_ring/ppermute | solution.py:40
  33.5 20.7 %collective-permute-start.3 = (bf16[480,896]{1,0:T(8,128)(2,1)S(1)}, bf16[480,896]{1,0:T(8,128)(2,1)}, u32[]{:S(2)}, u32[]{:S(2)}) collective-permute-start(bf16[480,896]{1,0:T(8,128)(2,1)S(1)} %pad_maximum_fusion.own), channel_id=1, source_target_pairs={{0,16},{16,0},{1,17},{17,1},{2,18},{18,2},{3,19},{19,3},{4,20},{20... | collective-permute-start | bytes 2580488 | tf_op jit(solution)/shard_map/joint_weight/ppermute | solution.py:48
  42.6 16.1 %collective-permute-start.10 = (bf16[192,1600]{1,0:T(8,128)(2,1)}, bf16[192,1600]{1,0:T(8,128)(2,1)}, u32[]{:S(2)}, u32[]{:S(2)}) collective-permute-start(bf16[192,1600]{1,0:T(8,128)(2,1)} %collective-permute-done.8.refs_7_), channel_id=1, source_target_pairs={{0,4},{1,5},{4,8},{5,9},{8,12},{9,13},{12,14},{13,15},{14,10},{15,... | collective-permute-start | bytes 1843208 | tf_op jit(solution)/shard_map/input_ring/ppermute | solution.py:40
  43.6 16.1 %collective-permute-start.9 = (bf16[192,1600]{1,0:T(8,128)(2,1)S(1)}, bf16[192,1600]{1,0:T(8,128)(2,1)}, u32[]{:S(2)}, u32[]{:S(2)}) collective-permute-start(bf16[192,1600]{1,0:T(8,128)(2,1)S(1)} %collective-permute-done.7.refs_1_), channel_id=1, source_target_pairs={{0,2},{1,3},{4,0},{5,1},{8,4},{9,5},{12,8},{13,9},{14,12},{15,13},... | collective-permute-start | bytes 1843208 | tf_op jit(solution)/shard_map/input_ring/ppermute | solution.py:40
  54.2 14.1 %collective-permute-start.4 = (bf16[480,896]{1,0:T(8,128)(2,1)S(1)}, bf16[480,896]{1,0:T(8,128)(2,1)}, u32[]{:S(2)}, u32[]{:S(2)}) collective-permute-start(bf16[480,896]{1,0:T(8,128)(2,1)S(1)} %pad_maximum_fusion.own), channel_id=1, source_target_pairs={{0,1},{1,0},{2,3},{3,2},{4,5},{5,4},{6,7},{7,6},{8,9},{9,8},{10,11... | collective-permute-start | bytes 2580488 | tf_op jit(solution)/shard_map/joint_weight/ppermute | solution.py:44
  54.2 14.1 %collective-permute-start.5 = (bf16[480,896]{1,0:T(8,128)(2,1)}, bf16[480,896]{1,0:T(8,128)(2,1)}, u32[]{:S(2)}, u32[]{:S(2)}) collective-permute-start(bf16[480,896]{1,0:T(8,128)(2,1)} %collective-permute-done.3.got), channel_id=1, source_target_pairs={{0,1},{1,0},{2,3},{3,2},{4,5},{5,4},{6,7},{7,6},{8,9},{9,8},{10,11... | collective-permute-start | bytes 2580488 | tf_op jit(solution)/shard_map/joint_weight/ppermute | solution.py:44
  59.8 15.7 %collective-permute-start.11 = (bf16[192,1600]{1,0:T(8,128)(2,1)}, bf16[192,1600]{1,0:T(8,128)(2,1)S(1)}, u32[]{:S(2)}, u32[]{:S(2)}) collective-permute-start(bf16[192,1600]{1,0:T(8,128)(2,1)} %collective-permute-done.9.refs_2_), channel_id=1, source_target_pairs={{0,2},{1,3},{4,0},{5,1},{8,4},{9,5},{12,8},{13,9},{14,12},{15,13},... | collective-permute-start | bytes 1843208 | tf_op jit(solution)/shard_map/input_ring/ppermute | solution.py:40
  61.3 16.2 %collective-permute-start.12 = (bf16[192,1600]{1,0:T(8,128)(2,1)}, bf16[192,1600]{1,0:T(8,128)(2,1)}, u32[]{:S(2)}, u32[]{:S(2)}) collective-permute-start(bf16[192,1600]{1,0:T(8,128)(2,1)} %collective-permute-done.10.refs_6_), channel_id=1, source_target_pairs={{0,4},{1,5},{4,8},{5,9},{8,12},{9,13},{12,14},{13,15},{14,10},{15,... | collective-permute-start | bytes 1843208 | tf_op jit(solution)/shard_map/input_ring/ppermute | solution.py:40
  66.1 17.3 %collective-permute-start.6 = (bf16[400,800]{1,0:T(8,128)(2,1)}, bf16[400,800]{1,0:T(8,128)(2,1)}, u32[]{:S(2)}, u32[]{:S(2)}) collective-permute-start(bf16[400,800]{1,0:T(8,128)(2,1)} %bitcast.158), channel_id=1, source_target_pairs={{0,16},{16,0},{1,17},{17,1},{2,18},{18,2},{3,19},{19,3},{4,20},{20... | collective-permute-start | bytes 1920008 | tf_op jit(solution)/shard_map/feed_forward_weights/ppermute | solution.py:48
  86.7 14.4 %collective-permute-start.17 = (bf16[128,1600]{1,0:T(8,128)(2,1)S(1)}, bf16[128,1600]{1,0:T(8,128)(2,1)}, u32[]{:S(2)}, u32[]{:S(2)}) collective-permute-start(bf16[128,1600]{1,0:T(8,128)(2,1)S(1)} %bitcast.153), channel_id=1, source_target_pairs={{0,4},{1,5},{4,8},{5,9},{8,12},{9,13},{12,14},{13,15},{14,10},{15,... | collective-permute-start | bytes 1228808 | tf_op jit(solution)/shard_map/cotangent_ring/ppermute | solution.py:40
  101.0 19.7 %collective-permute-start.16 = (bf16[8,64,1600]{2,1,0:T(8,128)(2,1)}, bf16[8,64,1600]{2,1,0:T(8,128)(2,1)S(1)}, u32[]{:S(2)}, u32[]{:S(2)}) collective-permute-start(bf16[8,64,1600]{2,1,0:T(8,128)(2,1)} %get-tuple-element.137.own), channel_id=1, source_target_pairs={{0,1},{1,0},{2,3},{3,2},{4,5},{5,4},{6,7},{7,6},{8,9},{9,8},{10,11... | collective-permute-start | bytes 4915208 | tf_op jit(solution)/shard_map/feed_forward_weights/ppermute | solution.py:44
  101.6 19.2 %collective-permute-start.24 = (bf16[400,800]{1,0:T(8,128)(2,1)}, bf16[400,800]{1,0:T(8,128)(2,1)}, u32[]{:S(2)}, u32[]{:S(2)}) collective-permute-start(bf16[400,800]{1,0:T(8,128)(2,1)} %param.17), channel_id=1, source_target_pairs={{0,16},{16,0},{1,17},{17,1},{2,18},{18,2},{3,19},{19,3},{4,20},{20... | collective-permute-start | bytes 1920008 | tf_op jit(solution)/shard_map/feed_forward_weights/ppermute | solution.py:48
  103.1 53.3 %collective-permute-start.15 = (bf16[8,64,1600]{2,1,0:T(8,128)(2,1)}, bf16[8,64,1600]{2,1,0:T(8,128)(2,1)}, u32[]{:S(2)}, u32[]{:S(2)}) collective-permute-start(bf16[8,64,1600]{2,1,0:T(8,128)(2,1)} %get-tuple-element.137.own), channel_id=1, source_target_pairs={{0,16},{16,0},{1,17},{17,1},{2,18},{18,2},{3,19},{19,3},{4,20},{20... | collective-permute-start | bytes 4915208 | tf_op jit(solution)/shard_map/output_weight/ppermute | solution.py:48
  103.6 14.9 %collective-permute-start.20 = (bf16[128,1600]{1,0:T(8,128)(2,1)}, bf16[128,1600]{1,0:T(8,128)(2,1)}, u32[]{:S(2)}, u32[]{:S(2)}) collective-permute-start(bf16[128,1600]{1,0:T(8,128)(2,1)} %collective-permute-done.17.refs_15_), channel_id=1, source_target_pairs={{0,4},{1,5},{4,8},{5,9},{8,12},{9,13},{12,14},{13,15},{14,10},{15,... | collective-permute-start | bytes 1228808 | tf_op jit(solution)/shard_map/cotangent_ring/ppermute | solution.py:40
  120.8 20.8 %collective-permute-start.22 = (bf16[1024,256]{1,0:T(8,128)(2,1)}, bf16[1024,256]{1,0:T(8,128)(2,1)S(1)}, u32[]{:S(2)}, u32[]{:S(2)}) collective-permute-start(bf16[1024,256]{1,0:T(8,128)(2,1)} %get-tuple-element.147.refs_0_.mixed), channel_id=1, source_target_pairs={{0,4},{1,5},{4,8},{5,9},{8,12},{9,13},{12,14},{13,15},{14,10},{15,... | collective-permute-start | bytes 1572872 | tf_op jit(solution)/shard_map/attended_ring/ppermute | solution.py:40
  121.5 20.1 %collective-permute-start.23 = (bf16[1024,256]{1,0:T(8,128)(2,1)}, bf16[1024,256]{1,0:T(8,128)(2,1)S(1)}, u32[]{:S(2)}, u32[]{:S(2)}) collective-permute-start(bf16[1024,256]{1,0:T(8,128)(2,1)} %get-tuple-element.147.refs_0_.mixed), channel_id=1, source_target_pairs={{0,2},{1,3},{4,0},{5,1},{8,4},{9,5},{12,8},{13,9},{14,12},{15,13},... | collective-permute-start | bytes 1572872 | tf_op jit(solution)/shard_map/attended_ring/ppermute | solution.py:40
  141.6 14.8 %collective-permute-start.27 = (bf16[1024,256]{1,0:T(8,128)(2,1)S(1)}, bf16[1024,256]{1,0:T(8,128)(2,1)}, u32[]{:S(2)}, u32[]{:S(2)}) collective-permute-start(bf16[1024,256]{1,0:T(8,128)(2,1)S(1)} %collective-permute-done.22.refs_7_), channel_id=1, source_target_pairs={{0,4},{1,5},{4,8},{5,9},{8,12},{9,13},{12,14},{13,15},{14,10},{15,... | collective-permute-start | bytes 1572872 | tf_op jit(solution)/shard_map/attended_ring/ppermute | solution.py:40
  156.4 23.8 %collective-permute-start.31 = (bf16[400,1600]{1,0:T(8,128)(2,1)S(1)}, bf16[400,1600]{1,0:T(8,128)(2,1)}, u32[]{:S(2)}, u32[]{:S(2)}) collective-permute-start(bf16[400,1600]{1,0:T(8,128)(2,1)S(1)} %maximum_select_fusion.1.down_own), channel_id=1, source_target_pairs={{0,1},{1,0},{2,3},{3,2},{4,5},{5,4},{6,7},{7,6},{8,9},{9,8},{10,11... | collective-permute-start | bytes 3840008 | tf_op jit(solution)/shard_map/attended_ring/ppermute | solution.py:44
  156.9 23.3 %collective-permute-start.30 = (bf16[400,1600]{1,0:T(8,128)(2,1)S(1)}, bf16[400,1600]{1,0:T(8,128)(2,1)}, u32[]{:S(2)}, u32[]{:S(2)}) collective-permute-start(bf16[400,1600]{1,0:T(8,128)(2,1)S(1)} %maximum_select_fusion.up_own), channel_id=1, source_target_pairs={{0,1},{1,0},{2,3},{3,2},{4,5},{5,4},{6,7},{7,6},{8,9},{9,8},{10,11... | collective-permute-start | bytes 3840008 | tf_op jit(solution)/shard_map/attended_ring/ppermute | solution.py:44
  167.5 15.8 %collective-permute-start.32 = (f32[1,400]{1,0:T(1,128)S(1)}, f32[1,400]{1,0:T(1,128)S(1)}, u32[]{:S(2)}, u32[]{:S(2)}) collective-permute-start(f32[1,400]{1,0:T(1,128)S(1)} %bitcast.164), channel_id=1, source_target_pairs={{0,1},{1,0},{2,3},{3,2},{4,5},{5,4},{6,7},{7,6},{8,9},{9,8},{10,11... | collective-permute-start | bytes 4808 | tf_op jit(solution)/shard_map/feed_forward_weights/ppermute | solution.py:44
  240.0 14.2 %collective-permute-start.44 = (bf16[64,1600]{1,0:T(8,128)(2,1)S(1)}, bf16[64,1600]{1,0:T(8,128)(2,1)S(1)}, u32[]{:S(2)}, u32[]{:S(2)}) collective-permute-start(bf16[64,1600]{1,0:T(8,128)(2,1)S(1)} %get-tuple-element.168), channel_id=1, source_target_pairs={{0,4},{1,5},{4,8},{5,9},{8,12},{9,13},{12,14},{13,15},{14,10},{15,... | collective-permute-start | bytes 614408 | tf_op jit(solution)/shard_map/normed_two_back_ring/ppermute | solution.py:40
  246.6 62.0 %collective-permute-start.56 = (f32[400,1600]{1,0:T(8,128)}, f32[400,1600]{1,0:T(8,128)}, u32[]{:S(2)}, u32[]{:S(2)}) collective-permute-start(f32[400,1600]{1,0:T(8,128)} %fusion.54), channel_id=1, source_target_pairs={{0,1},{1,0},{2,3},{3,2},{4,5},{5,4},{6,7},{7,6},{8,9},{9,8},{10,11... | collective-permute-start | bytes 7680008 | tf_op jit(solution)/shard_map/down_gradient/ppermute | solution.py:44
  249.9 51.2 %collective-permute-start.55 = (f32[400,1600]{1,0:T(8,128)}, f32[400,1600]{1,0:T(8,128)}, u32[]{:S(2)}, u32[]{:S(2)}) collective-permute-start(f32[400,1600]{1,0:T(8,128)} %fusion.53), channel_id=1, source_target_pairs={{0,1},{1,0},{2,3},{3,2},{4,5},{5,4},{6,7},{7,6},{8,9},{9,8},{10,11... | collective-permute-start | bytes 7680008 | tf_op jit(solution)/shard_map/up_gradient/ppermute | solution.py:44
  274.2 15.4 %collective-permute-start.53 = (bf16[64,1600]{1,0:T(8,128)(2,1)S(1)}, bf16[64,1600]{1,0:T(8,128)(2,1)}, u32[]{:S(2)}, u32[]{:S(2)}) collective-permute-start(bf16[64,1600]{1,0:T(8,128)(2,1)S(1)} %get-tuple-element.185), channel_id=1, source_target_pairs={{0,4},{1,5},{4,8},{5,9},{8,12},{9,13},{12,14},{13,15},{14,10},{15,... | collective-permute-start | bytes 614408 | tf_op jit(solution)/shard_map/down_ring/ppermute | solution.py:40
  289.6 27.8 %all-to-all-start.1 = ((bf16[8,128,512]{2,1,0:T(8,128)(2,1)}), bf16[8,128,512]{2,1,0:T(8,128)(2,1)}, u32[]{:S(2)}, u32[]{:S(2)}) async-start(bf16[8,128,512]{2,1,0:T(8,128)(2,1)} %get-tuple-element.187), calls=%async_computation.1 | async-start | bytes 2097152 | tf_op jit(solution)/shard_map/back_exchange/all_to_all | solution.py:129
  307.2 31.6 %collective-permute-start.59 = (bf16[400,800]{1,0:T(8,128)(2,1)}, bf16[400,800]{1,0:T(8,128)(2,1)}, u32[]{:S(2)}, u32[]{:S(2)}) collective-permute-start(bf16[400,800]{1,0:T(8,128)(2,1)} %select_convert_fusion.2), channel_id=1, source_target_pairs={{0,16},{16,0},{1,17},{17,1},{2,18},{18,2},{3,19},{19,3},{4,20},{20... | collective-permute-start | bytes 1920008 | tf_op jit(solution)/shard_map/up_gradient/ppermute | solution.py:48
  319.4 19.4 %collective-permute-start.60 = (bf16[128,1600]{1,0:T(8,128)(2,1)}, bf16[128,1600]{1,0:T(8,128)(2,1)S(1)}, u32[]{:S(2)}, u32[]{:S(2)}) collective-permute-start(bf16[128,1600]{1,0:T(8,128)(2,1)} %pad_maximum_fusion.5), channel_id=1, source_target_pairs={{0,4},{1,5},{4,8},{5,9},{8,12},{9,13},{12,14},{13,15},{14,10},{15,... | collective-permute-start | bytes 1228808 | tf_op jit(solution)/shard_map/down_ring/ppermute | solution.py:40
  321.2 17.6 %collective-permute-start.61 = (bf16[128,1600]{1,0:T(8,128)(2,1)}, bf16[128,1600]{1,0:T(8,128)(2,1)S(1)}, u32[]{:S(2)}, u32[]{:S(2)}) collective-permute-start(bf16[128,1600]{1,0:T(8,128)(2,1)} %pad_maximum_fusion.6), channel_id=1, source_target_pairs={{0,2},{1,3},{4,0},{5,1},{8,4},{9,5},{12,8},{13,9},{14,12},{15,13},... | collective-permute-start | bytes 1228808 | tf_op jit(solution)/shard_map/down_ring/ppermute | solution.py:40
  323.7 23.7 %collective-permute-start.63 = (bf16[400,800]{1,0:T(8,128)(2,1)}, bf16[400,800]{1,0:T(8,128)(2,1)}, u32[]{:S(2)}, u32[]{:S(2)}) collective-permute-start(bf16[400,800]{1,0:T(8,128)(2,1)} %select_convert_fusion.1), channel_id=1, source_target_pairs={{0,16},{16,0},{1,17},{17,1},{2,18},{18,2},{3,19},{19,3},{4,20},{20... | collective-permute-start | bytes 1920008 | tf_op jit(solution)/shard_map/down_gradient/ppermute | solution.py:48
  342.7 21.1 %collective-permute-start.65 = (bf16[128,1600]{1,0:T(8,128)(2,1)}, bf16[128,1600]{1,0:T(8,128)(2,1)S(1)}, u32[]{:S(2)}, u32[]{:S(2)}) collective-permute-start(bf16[128,1600]{1,0:T(8,128)(2,1)} %fusion.15), channel_id=1, source_target_pairs={{0,2},{1,3},{4,0},{5,1},{8,4},{9,5},{12,8},{13,9},{14,12},{15,13},... | collective-permute-start | bytes 1228808 | tf_op jit(solution)/shard_map/down_ring/ppermute | solution.py:40
  343.9 20.0 %collective-permute-start.64 = (bf16[128,1600]{1,0:T(8,128)(2,1)}, bf16[128,1600]{1,0:T(8,128)(2,1)S(1)}, u32[]{:S(2)}, u32[]{:S(2)}) collective-permute-start(bf16[128,1600]{1,0:T(8,128)(2,1)} %fusion.16), channel_id=1, source_target_pairs={{0,4},{1,5},{4,8},{5,9},{8,12},{9,13},{12,14},{13,15},{14,10},{15,... | collective-permute-start | bytes 1228808 | tf_op jit(solution)/shard_map/down_ring/ppermute | solution.py:40
  372.6 18.9 %collective-permute-start.70 = (bf16[416,800]{1,0:T(8,128)(2,1)}, bf16[416,800]{1,0:T(8,128)(2,1)S(1)}, u32[]{:S(2)}, u32[]{:S(2)}) collective-permute-start(bf16[416,800]{1,0:T(8,128)(2,1)} %select_convert_fusion), channel_id=1, source_target_pairs={{0,16},{16,0},{1,17},{17,1},{2,18},{18,2},{3,19},{19,3},{4,20},{20... | collective-permute-start | bytes 1996808 | tf_op jit(solution)/shard_map/joint_gradient/ppermute | solution.py:48
  375.4 20.9 %collective-permute-start.68 = (bf16[128,1600]{1,0:T(8,128)(2,1)}, bf16[128,1600]{1,0:T(8,128)(2,1)}, u32[]{:S(2)}, u32[]{:S(2)}) collective-permute-start(bf16[128,1600]{1,0:T(8,128)(2,1)} %pad_maximum_fusion.7), channel_id=1, source_target_pairs={{0,4},{1,5},{4,8},{5,9},{8,12},{9,13},{12,14},{13,15},{14,10},{15,... | collective-permute-start | bytes 1228808 | tf_op jit(solution)/shard_map/last_ring/ppermute | solution.py:40
  379.4 16.9 %collective-permute-start.71 = (bf16[128,1600]{1,0:T(8,128)(2,1)}, bf16[128,1600]{1,0:T(8,128)(2,1)}, u32[]{:S(2)}, u32[]{:S(2)}) collective-permute-start(bf16[128,1600]{1,0:T(8,128)(2,1)} %fusion.14), channel_id=1, source_target_pairs={{0,4},{1,5},{4,8},{5,9},{8,12},{9,13},{12,14},{13,15},{14,10},{15,... | collective-permute-start | bytes 1228808 | tf_op jit(solution)/shard_map/down_ring/ppermute | solution.py:40
  386.2 15.7 %collective-permute-start.74 = (bf16[128,1600]{1,0:T(8,128)(2,1)}, bf16[128,1600]{1,0:T(8,128)(2,1)}, u32[]{:S(2)}, u32[]{:S(2)}) collective-permute-start(bf16[128,1600]{1,0:T(8,128)(2,1)} %pad_maximum_fusion.8), channel_id=1, source_target_pairs={{0,2},{1,3},{4,0},{5,1},{8,4},{9,5},{12,8},{13,9},{14,12},{15,13},... | collective-permute-start | bytes 1228808 | tf_op jit(solution)/shard_map/last_ring/ppermute | solution.py:40
  397.5 19.8 %collective-permute-start.73 = (bf16[128,1600]{1,0:T(8,128)(2,1)S(1)}, bf16[128,1600]{1,0:T(8,128)(2,1)S(1)}, u32[]{:S(2)}, u32[]{:S(2)}) collective-permute-start(bf16[128,1600]{1,0:T(8,128)(2,1)S(1)} %fusion.17), channel_id=1, source_target_pairs={{0,4},{1,5},{4,8},{5,9},{8,12},{9,13},{12,14},{13,15},{14,10},{15,... | collective-permute-start | bytes 1228808 | tf_op jit(solution)/shard_map/last_ring/ppermute | solution.py:40
  403.2 16.8 %collective-permute-start.75 = (bf16[128,1600]{1,0:T(8,128)(2,1)S(1)}, bf16[128,1600]{1,0:T(8,128)(2,1)S(1)}, u32[]{:S(2)}, u32[]{:S(2)}) collective-permute-start(bf16[128,1600]{1,0:T(8,128)(2,1)S(1)} %fusion.12), channel_id=1, source_target_pairs={{0,2},{1,3},{4,0},{5,1},{8,4},{9,5},{12,8},{13,9},{14,12},{15,13},... | collective-permute-start | bytes 1228808 | tf_op jit(solution)/shard_map/last_ring/ppermute | solution.py:40
  405.0 23.8 %collective-permute-start.79 = (bf16[256,896]{1,0:T(8,128)(2,1)}, bf16[256,896]{1,0:T(8,128)(2,1)}, u32[]{:S(2)}, u32[]{:S(2)}) collective-permute-start(bf16[256,896]{1,0:T(8,128)(2,1)} %get-tuple-element.214), channel_id=1, source_target_pairs={{15,15},{14,10},{0,0},{1,5},{3,11},{5,1},{7,7},{9,13},{11,3},{13,9... | collective-permute-start | bytes 1376264 | tf_op jit(solution)/shard_map/joint_gradient/ppermute | solution.py:191
  410.0 20.4 %collective-permute-start.80 = (bf16[160,896]{1,0:T(8,128)(2,1)}, bf16[160,896]{1,0:T(8,128)(2,1)}, u32[]{:S(2)}, u32[]{:S(2)}) collective-permute-start(bf16[160,896]{1,0:T(8,128)(2,1)} %get-tuple-element.215), channel_id=1, source_target_pairs={{14,4},{12,14},{10,8},{8,2},{6,12},{4,6},{2,0},{0,10},{15,5},{1,11... | collective-permute-start | bytes 860168 | tf_op jit(solution)/shard_map/joint_gradient/ppermute | solution.py:191
  410.0 21.4 %collective-permute-start.81 = (bf16[64,896]{1,0:T(8,128)(2,1)}, bf16[64,896]{1,0:T(8,128)(2,1)}, u32[]{:S(2)}, u32[]{:S(2)}) collective-permute-start(bf16[64,896]{1,0:T(8,128)(2,1)} %get-tuple-element.216), channel_id=1, source_target_pairs={{15,9},{13,3},{11,13},{9,7},{7,1},{5,11},{3,5},{31,25},{29,19},{27... | collective-permute-start | bytes 344072 | tf_op jit(solution)/shard_map/joint_gradient/ppermute | solution.py:191
  417.3 16.6 %collective-permute-start.78 = (f32[100,2048]{1,0:T(8,128)}, f32[100,2048]{1,0:T(8,128)}, u32[]{:S(2)}, u32[]{:S(2)}) collective-permute-start(f32[100,2048]{1,0:T(8,128)} %fusion.38), channel_id=1, source_target_pairs={{0,1},{1,0},{2,3},{3,2},{4,5},{5,4},{6,7},{7,6},{8,9},{9,8},{10,11... | collective-permute-start | bytes 2457608 | tf_op jit(solution)/shard_map/output_gradient/ppermute | solution.py:44
  421.9 21.6 %collective-permute-start.77 = (bf16[128,1600]{1,0:T(8,128)(2,1)}, bf16[128,1600]{1,0:T(8,128)(2,1)}, u32[]{:S(2)}, u32[]{:S(2)}) collective-permute-start(bf16[128,1600]{1,0:T(8,128)(2,1)} %fusion.11), channel_id=1, source_target_pairs={{0,2},{1,3},{4,0},{5,1},{8,4},{9,5},{12,8},{13,9},{14,12},{15,13},... | collective-permute-start | bytes 1228808 | tf_op jit(solution)/shard_map/last_ring/ppermute | solution.py:40
  428.8 14.7 %collective-permute-start.76 = (bf16[128,1600]{1,0:T(8,128)(2,1)S(1)}, bf16[128,1600]{1,0:T(8,128)(2,1)S(1)}, u32[]{:S(2)}, u32[]{:S(2)}) collective-permute-start(bf16[128,1600]{1,0:T(8,128)(2,1)S(1)} %copy-done.29), channel_id=1, source_target_pairs={{0,4},{1,5},{4,8},{5,9},{8,12},{9,13},{12,14},{13,15},{14,10},{15,... | collective-permute-start | bytes 1228808 | tf_op jit(solution)/shard_map/last_ring/ppermute | solution.py:40
  (87 other events, 1098.7 us)
